TPU v7x, 32 devices: a whole 2x2x4 slice. The times are simulated.
32 devices in a mesh: row: 4 (over z), col: 8 (over y, x, core).
Axes of the slice: x: 2, y: 2, z: 4, core: 2. Of those that a mesh axis runs over, the one named last changes fastest.
Arguments:
- tiles: float32 [4, 8, 256, 128, 128], P('row', 'col'), may hold values from -0.125 to 0.125
- tile_rows: int32 [4, 8, 256], P('row', 'col'), may hold values from 0 to 127, as said below
- tile_cols: int32 [4, 8, 256], P('row', 'col'), may hold values from 0 to 63, as said below
- tile_counts: int32 [4, 8], P('row', 'col'), may hold values from 1 to 256, as said below
- block_now: float32 [8, 65536], P(None, ('row', 'col')), may hold values from -6 to 6
- block_prev: float32 [8, 65536], P(None, ('row', 'col')), may hold values from -6 to 6
- coupling: float32 [8, 8], replicated, may hold values from -3 to 3
- diag_energy: float32 [65536], P(('row', 'col')), may hold values from 1 to 4
Outputs:
- next_block: float32 [8, 65536], P(None, ('row', 'col'))
- alpha: float32 [8, 8], replicated
- beta: float32 [8, 8], replicated
Inputs may be any that keep to these rules, and one draw needn't show every extreme that they name: `tile_rows`: every slot, used or not, holds a local tile row below 128; used tiles lie on or below the global diagonal. `tile_cols`: every slot holds a local tile column below 64. `tile_counts`: devices on the last block row use all 256 slots.
All inputs are finite; a program needn't handle non-finite values.
Results may differ from a plain program's by a relative error of at most 0.0003.
Values sent between devices are 32-bit elements; how exact they have to be, the bound alone decides.
No kernel may reach another device: no remote copies, remote signals or barrier semaphores. Data moves between devices by JAX's collectives and lax.ppermute only.
A program may use at most 64 MiB of HBM per device.

v0:
```python
import jax
import jax.numpy as jnp
from jax import lax
from jax.sharding import PartitionSpec as P


def tile_products(
    tiles, tile_rows, tile_cols, tile_total, row_vec, col_vec, block_size, with_rows, with_cols
):
    vectors = row_vec.shape[0]
    tile_width = tiles.shape[-1]
    row_tiles = row_vec.reshape(vectors, -1, tile_width)
    col_tiles = col_vec.reshape(vectors, -1, tile_width)
    row_blocks = row_tiles.shape[1]
    col_blocks = col_tiles.shape[1]
    offsets = jnp.arange(block_size, dtype=jnp.int32)
    row_range = jnp.arange(row_blocks, dtype=jnp.int32)
    col_range = jnp.arange(col_blocks, dtype=jnp.int32)

    def advance(block_step, carry):
        acc_rows, acc_cols = carry
        first_slot = block_step * block_size
        tile_block = lax.dynamic_slice_in_dim(tiles, first_slot, block_size, 0)
        row_index = lax.dynamic_slice_in_dim(tile_rows, first_slot, block_size, 0)
        col_index = lax.dynamic_slice_in_dim(tile_cols, first_slot, block_size, 0)
        alive_mask = (first_slot + offsets < tile_total).astype(jnp.float32)
        if with_rows:
            picked = jnp.take(col_tiles, col_index, axis=1)
            images = jnp.einsum("vmk,mjk->vmj", picked, tile_block, precision=lax.Precision.HIGHEST)
            one_hot = (row_index[:, None] == row_range[None, :]).astype(jnp.float32) * alive_mask[
                :, None
            ]
            acc_rows = acc_rows + jnp.einsum(
                "vmj,ms->vsj", images, one_hot, precision=lax.Precision.HIGHEST
            )
        if with_cols:
            picked_rows = jnp.take(row_tiles, row_index, axis=1)
            images_back = jnp.einsum(
                "vmj,mjk->vmk", picked_rows, tile_block, precision=lax.Precision.HIGHEST
            )
            one_hot_cols = (col_index[:, None] == col_range[None, :]).astype(
                jnp.float32
            ) * alive_mask[:, None]
            acc_cols = acc_cols + jnp.einsum(
                "vmk,mt->vtk", images_back, one_hot_cols, precision=lax.Precision.HIGHEST
            )
        return (acc_rows, acc_cols)

    block_count = (tile_total + block_size - 1) // block_size
    initial = (
        jnp.zeros((vectors, row_blocks, tile_width), jnp.float32),
        jnp.zeros((vectors, col_blocks, tile_width), jnp.float32),
    )
    acc_rows, acc_cols = lax.fori_loop(0, block_count, advance, initial)
    return (acc_rows.reshape(vectors, -1), acc_cols.reshape(vectors, -1))


def inner_products(left, right):
    return jnp.dot(
        left, right.T, precision=lax.Precision.HIGHEST, preferred_element_type=jnp.float32
    )


def local(tiles, tile_rows, tile_cols, tile_counts, block_now, block_prev, coupling, diag_energy):
    own_tiles = tiles[0, 0]
    own_rows = tile_rows[0, 0]
    own_cols = tile_cols[0, 0]
    tile_total = tile_counts[0, 0]
    slot_count = own_tiles.shape[0]
    block_size = min(32, slot_count // 8)
    row_vec = lax.all_gather(block_now, "col", axis=1, tiled=True)
    col_vec = lax.all_gather(block_now, "row", axis=1, tiled=True)
    part_rows, _ = tile_products(
        own_tiles, own_rows, own_cols, tile_total, row_vec, col_vec, block_size, True, False
    )
    _, part_cols = tile_products(
        own_tiles, own_rows, own_cols, tile_total, row_vec, col_vec, block_size, False, True
    )
    row_sum = lax.psum_scatter(part_rows, "col", scatter_dimension=1, tiled=True)
    col_sum = lax.psum_scatter(part_cols, "row", scatter_dimension=1, tiled=True)
    image = row_sum + col_sum + diag_energy[None, :] * block_now
    total_states = block_now.shape[1] * lax.axis_size("row") * lax.axis_size("col")
    sums = lax.psum(
        (
            inner_products(image, image),
            inner_products(block_now, image),
            inner_products(block_prev, image),
            inner_products(block_now, block_now),
            inner_products(block_prev, block_now),
            inner_products(block_prev, block_prev),
        ),
        ("row", "col"),
    )
    image_gram = sums[0] / total_states
    alpha = sums[1] / total_states
    prev_image = sums[2] / total_states
    now_gram = sums[3] / total_states
    prev_now = sums[4] / total_states
    prev_gram = sums[5] / total_states
    residual = (
        image
        - jnp.dot(alpha.T, block_now, precision=lax.Precision.HIGHEST)
        - jnp.dot(coupling, block_prev, precision=lax.Precision.HIGHEST)
    )

    def mult(left, right):
        return jnp.dot(left, right, precision=lax.Precision.HIGHEST)

    gram_matrix = (
        image_gram
        - 2.0 * mult(alpha.T, alpha)
        - mult(prev_image.T, coupling.T)
        + mult(mult(alpha.T, now_gram), alpha)
        + mult(mult(alpha.T, prev_now.T), coupling.T)
        - mult(coupling, prev_image)
        + mult(mult(coupling, prev_now), alpha)
        + mult(mult(coupling, prev_gram), coupling.T)
    )
    factor = jnp.linalg.cholesky(gram_matrix)
    next_block = jax.scipy.linalg.solve_triangular(factor, residual, lower=True)
    return (next_block, alpha, factor.T)


def solution(mesh):
    return jax.shard_map(
        local,
        mesh=mesh,
        in_specs=(
            P("row", "col", None, None, None),
            P("row", "col", None),
            P("row", "col", None),
            P("row", "col"),
            P(None, ("row", "col")),
            P(None, ("row", "col")),
            P(),
            P(("row", "col")),
        ),
        out_specs=(P(None, ("row", "col")), P(), P()),
        check_vma=False,
    )
```

profile of v0, /device:TPU:0, one launch (start us, length us, event | category | flops | bytes accessed | tf_op | source)
XLA Modules:
  0.0 250.0 jit_solution(8011270188232333913)
XLA Ops:
  7.9 11.6 %all_gather.7 = f32[8,16384]{1,0:T(8,128)S(1)} all-gather(f32[8,2048]{1,0:T(8,128)} %param.16), channel_id=1, replica_groups=mesh['row'=4,'col'=8] {'col'}, dimensions={1}, use_global_device_ids=true | all-gather | bytes 589824 | tf_op jit(solution)/shard_map/all_gather | solution.py:71
  19.6 13.6 %while.23 = (s32[]{:T(128)}, f32[8,64,128]{2,1,0:T(8,128)S(1)}, s32[]{:T(128)}, s32[256]{0:T(256)}, s32[]{:T(128)}, /*index=5*/f32[256,128,128]{2,1,0:T(8,128)},...) while((s32[]{:T(128)}, f32[8,64,128]{2,1,0:T(8,128)S(1)}, ...), condition=%wide.region_4.5_spmd.clone, body=%wide.region_3.4_spmd.clone.sunk | while | flops 75601184 | bytes 3282295 | solution.py:54
  19.6 1.4 compare_and_fusion.5
  21.0 0.6 gather_fusion.1
  21.6 3.5 %fusion.120 = f32[32,128,8]{1,2,0:T(8,128)S(1)} fusion(f32[256,128,128]{2,1,0:T(8,128)} %get-tuple-element.380, s32[]{:T(128)S(6)} %select_n.71, f32[32,8,128]{2,1,0:T(8,128)S(1)} %gather_fusion.1, pred[32]{0:T(512)(128)(4,1)S(1)} %get-tuple-element.313), kind=kOutput, calls=%fused_computation.30.clone.1 | convolution fusion | flops 50364416 | bytes 2359332 | tf_op jit(solution)/shard_map/while/body/vmj,mjk->vmk/dot_general | solution.py:38
  25.1 0.8 dynamic_slice.39
  25.8 0.5 fusion.121
  26.4 1.4 compare_and_fusion.5
  27.8 0.6 gather_fusion.1
  28.4 3.5 %fusion.120 = f32[32,128,8]{1,2,0:T(8,128)S(1)} fusion(f32[256,128,128]{2,1,0:T(8,128)} %get-tuple-element.380, s32[]{:T(128)S(6)} %select_n.71, f32[32,8,128]{2,1,0:T(8,128)S(1)} %gather_fusion.1, pred[32]{0:T(512)(128)(4,1)S(1)} %get-tuple-element.313), kind=kOutput, calls=%fused_computation.30.clone.1 | convolution fusion | flops 50364416 | bytes 2359332 | tf_op jit(solution)/shard_map/while/body/vmj,mjk->vmk/dot_general | solution.py:38
  31.9 0.8 dynamic_slice.39
  32.7 0.5 fusion.121
  33.2 0.8 copy.57
  34.1 56.2 %all_gather.6 = f32[8,8192]{1,0:T(8,128)S(1)} all-gather(f32[8,2048]{1,0:T(8,128)S(1)} %copy-done.1), channel_id=1, replica_groups=mesh['row'=4,'col'=8] {'row'}, dimensions={1}, use_global_device_ids=true | all-gather | bytes 327680 | tf_op jit(solution)/shard_map/all_gather | solution.py:72
  90.3 17.2 %while.22 = (s32[]{:T(128)}, f32[8,128,128]{2,1,0:T(8,128)S(1)}, s32[]{:T(128)}, s32[256]{0:T(256)}, s32[]{:T(128)}, /*index=5*/f32[256,128,128]{2,1,0:T(8,128)}...) while((s32[]{:T(128)}, f32[8,128,128]{2,1,0:T(8,128)S(1)}, ...), condition=%wide.region_1.2_spmd.clone, body=%wide.region_0.1_spmd.clone.sunk | while | flops 100836640 | bytes 3806583 | solution.py:54
  90.4 1.4 compare_and_fusion.4
  91.8 0.6 gather_fusion
  92.4 5.0 %fusion.114 = f32[32,128,8]{1,2,0:T(8,128)S(1)} fusion(f32[256,128,128]{2,1,0:T(8,128)} %get-tuple-element.344, s32[]{:T(128)S(6)} %select_n.69, f32[32,8,128]{2,1,0:T(8,128)S(1)} %gather_fusion, pred[32]{0:T(512)(128)(4,1)S(1)} %get-tuple-element.302), kind=kOutput, calls=%fused_computation.6.clone.1 | convolution fusion | flops 50364416 | bytes 2359332 | tf_op jit(solution)/shard_map/while/body/vmk,mjk->vmj/dot_general | solution.py:29
  97.3 0.8 dynamic_slice.37
  98.1 0.8 fusion.115
  98.9 1.4 compare_and_fusion.4
  100.4 0.6 gather_fusion
  101.0 5.0 %fusion.114 = f32[32,128,8]{1,2,0:T(8,128)S(1)} fusion(f32[256,128,128]{2,1,0:T(8,128)} %get-tuple-element.344, s32[]{:T(128)S(6)} %select_n.69, f32[32,8,128]{2,1,0:T(8,128)S(1)} %gather_fusion, pred[32]{0:T(512)(128)(4,1)S(1)} %get-tuple-element.302), kind=kOutput, calls=%fused_computation.6.clone.1 | convolution fusion | flops 50364416 | bytes 2359332 | tf_op jit(solution)/shard_map/while/body/vmk,mjk->vmj/dot_general | solution.py:29
  105.9 0.8 dynamic_slice.37
  106.7 0.8 fusion.115
  107.5 1.1 copy.56
  108.6 0.2 fusion.70
  108.8 0.3 fusion.71
  109.1 0.3 fusion.72
  109.3 85.6 %reduce-scatter.3.cloned.1.call-done = f32[8,2048]{1,0:T(8,128)} async-done(((f32[8,16384]{1,0:T(8,128)}), f32[8,2048]{1,0:T(8,128)}) %reduce-scatter.3.cloned.1.call-update) | async-done | bytes 65552 | tf_op jit(solution)/shard_map/reduce_scatter | solution.py:79
  194.9 0.9 multiply_add_fusion
  195.8 0.2 convolution_bitcast_fusion.2
  196.0 0.3 convolution_bitcast_fusion.3
  196.3 0.3 fusion.69
  196.6 39.7 %all-reduce = (f32[8,8]{0,1:T(8,128)S(1)}, f32[8,8]{0,1:T(8,128)S(1)}, f32[8,8]{0,1:T(8,128)S(1)}, f32[8,8]{0,1:T(8,128)S(1)}, f32[8,8]{0,1:T(8,128)S(1)}, /*index=5*/f32[8,8]{0,1:T(8,128)S(1)}) all-reduce(f32[8,8]{0,1:T(8,128)S(1)} %convolution_bitcast_fusion.3, ...), channel_id=1, replica_groups=mesh['row'=4,'col'=8] {'row','col'}, use_global_device_ids=true, to_apply=%region_7.8 | all-reduce | flops 384 | bytes 3072 | tf_op jit(solution)/shard_map/psum | solution.py:83
  236.3 0.2 convolution_subtract_fusion.1
  237.2 0.1 fusion.44
  237.4 0.1 convolution_add_fusion.3
  237.5 0.1 fusion.42
  237.7 0.1 convolution_add_fusion.1
  238.0 0.7 cholesky.16
  238.8 0.6 compare_reduce_fusion
  239.4 0.6 fusion.58
  240.1 0.6 custom-call.7
  240.7 0.2 convolution_subtract_fusion
  240.9 0.7 copy.34
  241.6 0.7 copy.33
  242.2 0.9 fusion.45
  (30 shorter events, 1.2 us)
Async XLA Ops:
  7.2 101.7 %copy-start = (f32[8,2048]{1,0:T(8,128)S(1)}, f32[8,2048]{1,0:T(8,128)}, u32[]{:S(2)}) copy-start(f32[8,2048]{1,0:T(8,128)} %param.17) | copy-start | bytes 196612
  7.2 26.9 %copy-start.1 = (f32[8,2048]{1,0:T(8,128)S(1)}, f32[8,2048]{1,0:T(8,128)}, u32[]{:S(2)}) copy-start(f32[8,2048]{1,0:T(8,128)} %param.16) | copy-start | bytes 196612
  7.2 102.1 %reduce-scatter.5.cloned.1.call-start = ((), (), s32[]{:S(2)}) async-start(), calls=%async_computation.3 | async-start | bytes 327680 | tf_op jit(solution)/shard_map/reduce_scatter | solution.py:80
  19.6 175.4 %copy-start.3 = (f32[2048]{0:T(1024)S(1)}, f32[2048]{0:T(1024)}, u32[]{:S(2)}) copy-start(f32[2048]{0:T(1024)} %param.19) | copy-start | bytes 24580
  19.6 217.2 %copy-start.2 = (f32[8,8]{1,0:T(8,128)S(1)}, f32[8,8]{1,0:T(8,128)}, u32[]{:S(2)}) copy-start(f32[8,8]{1,0:T(8,128)} %param.18) | copy-start | bytes 772
  34.1 160.9 %reduce-scatter.3.cloned.1.call-start = ((), (), s32[]{:S(2)}) async-start(), calls=%async_computation.2 | async-start | bytes 589824 | tf_op jit(solution)/shard_map/reduce_scatter | solution.py:79
Sparse Core Ops, SparseCore 0:
  34.2 61.7 reduce-scatter.4
  108.7 86.1 reduce-scatter.2
where the time goes:
time: 251 us; the launch traced here: 250 us
  blocking collectives  108 us (43%)
  waiting for transfers between devices  85.6 us (34%)
  matrix products  23.6 us (9%)
  between operations  14.8 us (6%)
  other arithmetic  9.23 us (4%)
  local copies, waits for them, and re-layouts  8.87 us (4%)
    reduce_scatter x1, waiting for transfers between devices, local(): lax.psum_scatter(part_rows, 'col', scatter_dimension=1, tiled=True)  85.6 us
    all_gather x1, blocking collectives, local(): col_vec = lax.all_gather(block_now, 'row', axis=1, tiled=True)  56.2 us
    psum x1, blocking collectives, local(): lax.psum((inner_products(image, image), inner_products(block_now, image),...  39.7 us
    all_gather x1, blocking collectives, local(): row_vec = lax.all_gather(block_now, 'col', axis=1, tiled=True)  11.6 us
    dot_general x2, matrix products, advance(): jnp.einsum('vmk,mjk->vmj', picked, tile_block, precision=lax.Precision.HI...  9.95 us
    dot_general x2, matrix products, advance(): jnp.einsum('vmj,mjk->vmk', picked_rows, tile_block, precision=lax.Precisi...  6.95 us
  transfers between devices with their start and end apart: 2, of which 1 were waited for; matrix products, arithmetic and copies ran while one was open for 8% of the time, Pallas kernels for 0%

commit v1 on v0

v1 whole, which is shorter than its diff:
```python
import functools

import jax
import jax.numpy as jnp
from jax import lax
from jax.experimental import pallas as pl
from jax.experimental.pallas import tpu as pltpu
from jax.sharding import PartitionSpec as P

VMEM = pltpu.VMEM
SMEM = pltpu.SMEM
GROUP = 8
MIB = 1 << 20


def halves(x):
    high = x.astype(jnp.bfloat16)
    low = (x - high.astype(jnp.float32)).astype(jnp.bfloat16)
    return high, low


def contract(left, right):
    return lax.dot_general(
        left,
        right,
        (((1,), (1,)), ((), ())),
        precision=lax.Precision.HIGHEST,
        preferred_element_type=jnp.float32,
    )


def matmul(left, right):
    return jnp.dot(
        left, right, precision=lax.Precision.HIGHEST, preferred_element_type=jnp.float32
    )


def products_kernel(rows, planes, piece_tiles, width, *refs):
    row_idx, col_idx, count, tiles, diag = refs[:5]
    plane_in = refs[5 : 5 + planes]
    core_in = refs[5 + planes : 5 + 2 * planes]
    row_in = refs[5 + 2 * planes : 4 + 2 * planes + rows]
    keep_out, send_out, col_out, vec_rows, vec_cols, acc_rows, acc_cols = refs[
        4 + 2 * planes + rows :
    ]
    row = lax.axis_index("row")
    col = lax.axis_index("col")
    plane, core = col // 2, col % 2

    def store_split(target, base, source):
        for t in range(piece_tiles):
            high, low = halves(source[:, t * width : (t + 1) * width])
            target[base + t] = jnp.concatenate([high, low], axis=0)

    own = plane_in[0]
    for s in range(planes):
        base = jnp.bitwise_xor(plane, s) * 2 * piece_tiles
        store_split(vec_rows, base + core * piece_tiles, plane_in[s])
        store_split(vec_rows, base + (1 - core) * piece_tiles, core_in[s])
    store_split(vec_cols, row * piece_tiles, own)
    for s in range(1, rows):
        store_split(vec_cols, jnp.bitwise_xor(row, s) * piece_tiles, row_in[s - 1])
    acc_rows[...] = jnp.zeros_like(acc_rows)
    acc_cols[...] = jnp.zeros_like(acc_cols)

    total = count[0]
    spare_row = acc_rows.shape[0] - 1
    spare_col = acc_cols.shape[0] - 1

    def step(group, carry):
        for k in range(GROUP):
            m = group * GROUP + k
            alive = m < total
            r, c = row_idx[m], col_idx[m]
            high, low = halves(tiles[m])
            from_row = vec_rows[r]
            from_col = vec_cols[c]
            back = jnp.dot(
                jnp.concatenate([from_row, from_row], axis=1),
                jnp.concatenate([high, low], axis=0),
                preferred_element_type=jnp.float32,
            )
            ahead = lax.dot_general(
                jnp.concatenate([from_col, from_col], axis=1),
                jnp.concatenate([high, low], axis=1),
                (((1,), (1,)), ((), ())),
                preferred_element_type=jnp.float32,
            )
            acc_rows[jnp.where(alive, r, spare_row)] += ahead[:8] + ahead[8:]
            acc_cols[jnp.where(alive, c, spare_col)] += back[:8] + back[8:]
        return carry

    lax.fori_loop(0, (total + GROUP - 1) // GROUP, step, 0)

    for s in range(planes):
        base = jnp.bitwise_xor(plane, s) * 2 * piece_tiles
        for t in range(piece_tiles):
            at = slice(t * width, (t + 1) * width)
            keep_out[s, :, at] = acc_rows[base + core * piece_tiles + t]
            send_out[s, :, at] = acc_rows[base + (1 - core) * piece_tiles + t]
    for s in range(rows):
        base = jnp.bitwise_xor(row, s) * piece_tiles
        for t in range(piece_tiles):
            at = slice(t * width, (t + 1) * width)
            piece = acc_cols[base + t]
            if s == 0:
                piece = piece + own[:, at] * diag[:, at]
            col_out[s, :, at] = piece


def image_kernel(planes, rows, copies, *refs):
    now, prev, keep, core, cols = refs[:5]
    plane_in = refs[5 : 4 + planes]
    row_in = refs[4 + planes : 3 + planes + rows]
    image_out, sums_out = refs[3 + planes + rows :]
    image = keep[...] + core[...] + cols[...]
    for ref in plane_in + row_in:
        image = image + ref[...]
    image_out[...] = image
    block, last = now[...], prev[...]
    vectors = image.shape[0]
    both = jnp.concatenate([block, last], axis=0)
    against = contract(image, jnp.concatenate([image, both], axis=0))
    fixed = contract(both, both)
    used = against.shape[1] + 2 * fixed.shape[1]
    sums = jnp.concatenate(
        [
            against,
            fixed[:vectors],
            fixed[vectors:],
            jnp.zeros((vectors, sums_out.shape[2] - used), jnp.float32),
        ],
        axis=1,
    )
    for k in range(copies):
        sums_out[k] = sums


def finish_kernel(states, sums_in, image, now, prev, coupling, next_out, alpha_out, beta_out):
    vectors = image.shape[0]
    sums = jnp.sum(sums_in[...], axis=0) / states
    image_gram = sums[:, :vectors]
    alpha_t = sums[:, vectors : 2 * vectors]
    image_prev = sums[:, 2 * vectors : 3 * vectors]
    fixed = jnp.concatenate(
        [sums[:, 3 * vectors : 5 * vectors], sums[:, 5 * vectors : 7 * vectors]], axis=0
    )
    pair = coupling[...]
    left = jnp.concatenate([alpha_t, pair], axis=1)
    seen = jnp.concatenate([alpha_t, image_prev], axis=1)
    gram = image_gram + contract(
        jnp.concatenate([matmul(left, fixed) - seen, -left], axis=1),
        jnp.concatenate([left, seen], axis=1),
    )
    row_at = lax.broadcasted_iota(jnp.int32, (vectors, vectors), 0)
    col_at = lax.broadcasted_iota(jnp.int32, (vectors, vectors), 1)
    eye = (row_at == col_at).astype(jnp.float32)
    alpha_out[...] = contract(eye, alpha_t)
    work = jnp.concatenate([gram, eye, -left], axis=1)
    below = lax.broadcasted_iota(jnp.int32, (vectors, 1), 0)
    pivots = jnp.zeros((vectors, 1), jnp.float32)
    for j in range(vectors):
        pivot = work[j : j + 1, j : j + 1]
        line = work[j : j + 1, :]
        pivots = jnp.where(below == j, pivot, pivots)
        if j + 1 < vectors:
            factor = jnp.where(below > j, work[:, j : j + 1] / pivot, 0.0)
            work = work - factor * line
    work = work / jnp.sqrt(pivots)
    beta_out[...] = jnp.where(col_at >= row_at, work[:, :vectors], 0.0)
    next_out[...] = matmul(
        work[:, vectors:], jnp.concatenate([image[...], now[...], prev[...]], axis=0)
    )


def local(rows, cols, tiles, tile_rows, tile_cols, tile_counts, block_now, block_prev, coupling, diag_energy):
    slots, width = tiles.shape[2], tiles.shape[4]
    vectors, piece = block_now.shape
    piece_tiles = piece // width
    planes = cols // 2
    f32 = jnp.float32
    piece_shape = jax.ShapeDtypeStruct((vectors, piece), f32)

    def along_col(x, s):
        return lax.ppermute(x, "col", [(i, i ^ s) for i in range(cols)])

    def along_row(x, s):
        return lax.ppermute(x, "row", [(i, i ^ s) for i in range(rows)])

    row_in = [along_row(block_now, s) for s in range(1, rows)]
    plane_in = [block_now] + [along_col(block_now, 2 * s) for s in range(1, planes)]
    core_in = [along_col(x, 1) for x in plane_in]

    in_vmem = pl.BlockSpec(memory_space=VMEM)
    in_smem = pl.BlockSpec(memory_space=SMEM)
    held = pltpu.with_memory_space_constraint(tiles.reshape(slots, width, width), VMEM)
    keep, send, col_parts = pl.pallas_call(
        functools.partial(products_kernel, rows, planes, piece_tiles, width),
        out_shape=(
            jax.ShapeDtypeStruct((planes, vectors, piece), f32),
            jax.ShapeDtypeStruct((planes, vectors, piece), f32),
            jax.ShapeDtypeStruct((rows, vectors, piece), f32),
        ),
        in_specs=[in_smem] * 3 + [in_vmem] * (2 * planes + rows + 1),
        out_specs=(in_vmem,) * 3,
        scratch_shapes=[
            VMEM((cols * piece_tiles, 2 * vectors, width), jnp.bfloat16),
            VMEM((rows * piece_tiles, 2 * vectors, width), jnp.bfloat16),
            VMEM((cols * piece_tiles + 1, vectors, width), f32),
            VMEM((rows * piece_tiles + 1, vectors, width), f32),
        ],
        compiler_params=pltpu.CompilerParams(vmem_limit_bytes=24 * MIB),
        name="products",
    )(
        tile_rows.reshape(slots),
        tile_cols.reshape(slots),
        tile_counts.reshape(1),
        held,
        diag_energy.reshape(1, piece),
        *plane_in,
        *core_in,
        *row_in,
    )

    back_rows = [along_row(col_parts[s], s) for s in range(1, rows)]
    from_core = along_col(send, 1)
    summed = [keep[s] + from_core[s] for s in range(1, planes)]
    back_planes = [along_col(summed[s - 1], 2 * s) for s in range(1, planes)]

    devices = rows * cols
    image, sums = pl.pallas_call(
        functools.partial(image_kernel, planes, rows, devices),
        out_shape=(piece_shape, jax.ShapeDtypeStruct((devices, vectors, 128), f32)),
        in_specs=[in_vmem] * (3 + planes + rows),
        out_specs=(in_vmem,) * 2,
        compiler_params=pltpu.CompilerParams(vmem_limit_bytes=16 * MIB),
        name="image",
    )(block_now, block_prev, keep[0], from_core[0], col_parts[0], *back_planes, *back_rows)

    sums = lax.all_to_all(sums, ("row", "col"), 0, 0)
    return pl.pallas_call(
        functools.partial(finish_kernel, float(piece * devices)),
        out_shape=(
            piece_shape,
            jax.ShapeDtypeStruct((vectors, vectors), f32),
            jax.ShapeDtypeStruct((vectors, vectors), f32),
        ),
        in_specs=[in_vmem] * 5,
        out_specs=(in_vmem,) * 3,
        compiler_params=pltpu.CompilerParams(vmem_limit_bytes=16 * MIB),
        name="finish",
    )(sums, image, block_now, block_prev, coupling)


def solution(mesh):
    return jax.shard_map(
        functools.partial(local, mesh.shape["row"], mesh.shape["col"]),
        mesh=mesh,
        in_specs=(
            P("row", "col", None, None, None),
            P("row", "col", None),
            P("row", "col", None),
            P("row", "col"),
            P(None, ("row", "col")),
            P(None, ("row", "col")),
            P(),
            P(("row", "col")),
        ),
        out_specs=(P(None, ("row", "col")), P(), P()),
        check_vma=False,
    )
```

time: 251 us -> 61.8 us (0.25)
  blocking collectives: 108 us -> 13.4 us
  waiting for transfers between devices: 85.6 us -> 5.61 us
  starting transfers between devices: 0.08 us -> 26.9 us
  matrix products: 23.6 us -> 0 us
  between operations: 14.8 us -> 1.36 us
  other arithmetic: 9.23 us -> 0.03 us
  Pallas kernels: 0 us -> 5.57 us
    reduce_scatter x2 -> x0, waiting for transfers between devices: 85.6 us -> none  [the longest x1 85.6 us: local(): lax.psum_scatter(part_rows, 'col', scatter_dimension=1, tiled=True)]
    all_gather x2 -> x0, blocking collectives: 67.8 us -> none  [the longest x1 56.2 us: local(): col_vec = lax.all_gather(block_now, 'row', axis=1, tiled=True)]
    psum x1 -> x0, blocking collectives: 39.7 us -> none  [local(): lax.psum((inner_products(image, image), inner_products(block_now, image),...]
    ppermute x0 -> x17, starting transfers between devices: none -> 26.9 us  [the longest x6 18.2 us: along_row(): return lax.ppermute(x, 'row', [(i, i ^ s) for i in range(rows)])]
    dot_general x26 -> x0, matrix products: 22.7 us -> none  [the longest x2 9.95 us: advance(): jnp.einsum('vmk,mjk->vmj', picked, tile_block, precision=lax.Precision.HI...]
    all_to_all x0 -> x1, blocking collectives: none -> 13.4 us  [local(): sums = lax.all_to_all(sums, ('row', 'col'), 0, 0)]
    and x4 -> x0, other arithmetic: 5.63 us -> none  [the longest x2 2.82 us: advance(): picked = jnp.take(col_tiles, col_index, axis=1)]
    ppermute x0 -> x17, waiting for transfers between devices: none -> 5.61 us  [the longest x11 3.87 us: along_col(): return lax.ppermute(x, 'col', [(i, i ^ s) for i in range(cols)])]
  transfers between devices with their start and end apart: 2 -> 17, of which waited for: 1 -> 9; matrix products, arithmetic and copies ran while one was open for 8% -> 0% of each run, Pallas kernels for 0% -> 0%
where the time goes in v1:
time: 61.8 us; the launch traced here: 61.5 us
  starting transfers between devices  26.9 us (44%)
  blocking collectives  13.4 us (22%)
  local copies, waits for them, and re-layouts  8.69 us (14%)
  waiting for transfers between devices  5.61 us (9%)
  Pallas kernels  5.57 us (9%)
  between operations  1.36 us (2%)
    ppermute x6, starting transfers between devices, along_row(): return lax.ppermute(x, 'row', [(i, i ^ s) for i in range(rows)])  18.2 us
    all_to_all x1, blocking collectives, local(): sums = lax.all_to_all(sums, ('row', 'col'), 0, 0)  13.4 us
    ppermute x11, starting transfers between devices, along_col(): return lax.ppermute(x, 'col', [(i, i ^ s) for i in range(cols)])  8.67 us
    unnamed x14, local copies, waits for them, and re-layouts  8.67 us
    ppermute x11, waiting for transfers between devices, along_col(): return lax.ppermute(x, 'col', [(i, i ^ s) for i in range(cols)])  3.87 us
    pallas_call x1, Pallas kernels, local(): pl.pallas_call(functools.partial(products_kernel, rows, planes, piece_til...  2.92 us
    pallas_call x1, Pallas kernels, local(): pl.pallas_call(functools.partial(finish_kernel, float(piece * devices)),...  2.05 us
    ppermute x6, waiting for transfers between devices, along_row(): return lax.ppermute(x, 'row', [(i, i ^ s) for i in range(rows)])  1.73 us
  transfers between devices with their start and end apart: 17, of which 9 were waited for; matrix products, arithmetic and copies ran while one was open for 0% of the time, Pallas kernels for 0%

profile of v1, /device:TPU:0, one launch (start us, length us, event | category | flops | bytes accessed | tf_op | source)
XLA Modules:
  0.0 61.5 jit_solution(16951168663230422630)
XLA Ops:
  0.6 0.0 copy-start.4
  0.6 5.1 %collective-permute-start.9 = (f32[8,2048]{1,0:T(8,128)}, f32[8,2048]{1,0:T(8,128)S(1)}, u32[]{:S(2)}, u32[]{:S(2)}) collective-permute-start(f32[8,2048]{1,0:T(8,128)} %now.1), channel_id=1, source_target_pairs={{0,24},{8,16},{16,8},{24,0},{1,25},{9,17},{17,9},{25,1},{2,26},{10... | collective-permute-start | bytes 196616 | tf_op jit(solution)/shard_map/ppermute | solution.py:188
  5.8 0.0 collective-permute-start.8
  5.8 2.4 %collective-permute-start.2 = (f32[8,2048]{1,0:T(8,128)}, f32[8,2048]{1,0:T(8,128)S(1)}, u32[]{:S(2)}, u32[]{:S(2)}) collective-permute-start(f32[8,2048]{1,0:T(8,128)} %now.1), channel_id=1, source_target_pairs={{0,6},{1,7},{2,4},{3,5},{4,2},{5,3},{6,0},{7,1},{8,14},{9,15},{10,... | collective-permute-start | bytes 196616 | tf_op jit(solution)/shard_map/ppermute | solution.py:185
  8.2 0.5 collective-permute-start.1
  8.7 0.5 collective-permute-start
  9.3 0.0 collective-permute-done.9.refs_15_
  9.3 1.9 %collective-permute-start.7 = (f32[8,2048]{1,0:T(8,128)}, f32[8,2048]{1,0:T(8,128)S(1)}, u32[]{:S(2)}, u32[]{:S(2)}) collective-permute-start(f32[8,2048]{1,0:T(8,128)} %now.1), channel_id=1, source_target_pairs={{0,8},{8,0},{16,24},{24,16},{1,9},{9,1},{17,25},{25,17},{2,10},{10... | collective-permute-start | bytes 196616 | tf_op jit(solution)/shard_map/ppermute | solution.py:188
  11.2 0.5 collective-permute-done.8.refs_14_
  11.7 0.0 collective-permute-start.3
  11.7 0.0 collective-permute-done.2.refs_8_
  11.7 0.5 collective-permute-start.6
  12.2 0.5 collective-permute-done.1.refs_7_
  12.7 0.0 collective-permute-start.5
  12.7 0.5 collective-permute-done.refs_6_
  13.2 0.0 collective-permute-start.4
  13.9 0.0 collective-permute-done.7.refs_13_
  13.9 0.0 collective-permute-done.3.refs_9_
  13.9 0.0 collective-permute-done.6.refs_12_
  13.9 0.1 collective-permute-done.5.refs_11_
  13.9 0.5 collective-permute-done.4.refs_10_
  14.4 0.0 copy-start
  14.4 5.8 %copy-done = f32[1,1,256,128,128]{4,3,2,1,0:T(8,128)S(1)} copy-done((f32[1,1,256,128,128]{4,3,2,1,0:T(8,128)S(1)}, f32[1,1,256,128,128]{4,3,2,1,0:T(8,128)}, u32[]{:S(2)}) %copy-start) | copy-done | bytes 16777240
  20.2 0.0 copy-start.1
  20.2 0.8 %copy-done.1 = f32[8,2048]{1,0:T(8,128)S(1)} copy-done((f32[8,2048]{1,0:T(8,128)S(1)}, f32[8,2048]{1,0:T(8,128)}, u32[]{:S(2)}) %copy-start.1) | copy-done | bytes 65560
  21.1 0.7 %copy-done.3 = f32[2048]{0:T(1024)S(1)} copy-done((f32[2048]{0:T(1024)S(1)}, f32[2048]{0:T(1024)}, u32[]{:S(2)}) %copy-start.3) | copy-done | bytes 8216
  21.8 0.7 %copy-done.5 = s32[1,1,256]{2,1,0:T(1,128)S(1)} copy-done((s32[1,1,256]{2,1,0:T(1,128)S(1)}, s32[1,1,256]{2,1,0:T(1,128)}, u32[]{:S(2)}) %copy-start.5) | copy-done | bytes 1048
  22.4 0.7 %copy-done.6 = s32[1,1,256]{2,1,0:T(1,128)S(1)} copy-done((s32[1,1,256]{2,1,0:T(1,128)S(1)}, s32[1,1,256]{2,1,0:T(1,128)}, u32[]{:S(2)}) %copy-start.6) | copy-done | bytes 1048
  23.1 2.9 %products.1 = (f32[4,8,2048]{2,1,0:T(8,128)S(1)}, f32[4,8,2048]{2,1,0:T(8,128)S(1)}, f32[4,8,2048]{2,1,0:T(8,128)S(1)}) custom-call(s32[256]{0:T(256)S(1)} %bitcast.26, s32[256]{0:T(256)S(1)} %bitcast.27, s32[1]{0:T(128)} %bitcast.23.refs_2_, f32[256,128,128]{2,1,0:T(8,128)S(1)} %bitcast.24, f32[1,2048]{1,0:T(1,128)S(1)} %bitcast.25, ...), custom_call_target="tpu_custom_call" | custom-call | tf_op jit(solution)/shard_map/products/pallas_call | solution.py:197
  26.0 0.9 %collective-permute-start.10 = (f32[4,8,2048]{2,1,0:T(8,128)S(1)}, f32[4,8,2048]{2,1,0:T(8,128)S(1)}, u32[]{:S(2)}, u32[]{:S(2)}) collective-permute-start(f32[4,8,2048]{2,1,0:T(8,128)S(1)} %get-tuple-element.9), channel_id=1, source_target_pairs={{0,1},{1,0},{2,3},{3,2},{4,5},{5,4},{6,7},{7,6},{8,9},{9,8},{10,11... | collective-permute-start | bytes 786440 | tf_op jit(solution)/shard_map/ppermute | solution.py:185
  27.0 10.5 %collective-permute-start.16 = (f32[8,2048]{1,0:T(8,128)S(1)}, f32[8,2048]{1,0:T(8,128)S(1)}, u32[]{:S(2)}, u32[]{:S(2)}) collective-permute-start(f32[8,2048]{1,0:T(8,128)S(1)} %get-tuple-element.16), channel_id=1, source_target_pairs={{0,24},{8,16},{16,8},{24,0},{1,25},{9,17},{17,9},{25,1},{2,26},{10... | collective-permute-start | bytes 196616 | tf_op jit(solution)/shard_map/ppermute | solution.py:188
  37.5 0.0 collective-permute-start.15
  37.5 0.6 %collective-permute-start.14 = (f32[8,2048]{1,0:T(8,128)S(1)}, f32[8,2048]{1,0:T(8,128)S(1)}, u32[]{:S(2)}, u32[]{:S(2)}) collective-permute-start(f32[8,2048]{1,0:T(8,128)S(1)} %get-tuple-element.18), channel_id=1, source_target_pairs={{0,8},{8,0},{16,24},{24,16},{1,9},{9,1},{17,25},{25,17},{2,10},{10... | collective-permute-start | bytes 196616 | tf_op jit(solution)/shard_map/ppermute | solution.py:188
  38.1 0.0 collective-permute-done.10
  38.2 2.5 %collective-permute-start.13 = (f32[8,2048]{1,0:T(8,128)S(1)}, f32[8,2048]{1,0:T(8,128)S(1)}, u32[]{:S(2)}, u32[]{:S(2)}) collective-permute-start(f32[8,2048]{1,0:T(8,128)S(1)} %get-tuple-element.13), channel_id=1, source_target_pairs={{0,6},{1,7},{2,4},{3,5},{4,2},{5,3},{6,0},{7,1},{8,14},{9,15},{10,... | collective-permute-start | bytes 196616 | tf_op jit(solution)/shard_map/ppermute | solution.py:185
  40.7 0.5 collective-permute-start.12
  41.2 0.0 collective-permute-done.16.refs_10_
  41.2 0.7 %collective-permute-start.11 = (f32[8,2048]{1,0:T(8,128)S(1)}, f32[8,2048]{1,0:T(8,128)S(1)}, u32[]{:S(2)}, u32[]{:S(2)}) collective-permute-start(f32[8,2048]{1,0:T(8,128)S(1)} %get-tuple-element.15), channel_id=1, source_target_pairs={{0,2},{1,3},{2,0},{3,1},{4,6},{5,7},{6,4},{7,5},{8,10},{9,11},{10,... | collective-permute-start | bytes 196616 | tf_op jit(solution)/shard_map/ppermute | solution.py:185
  41.9 1.2 %collective-permute-done.15.refs_9_ = f32[8,2048]{1,0:T(8,128)S(1)} collective-permute-done((f32[8,2048]{1,0:T(8,128)S(1)}, f32[8,2048]{1,0:T(8,128)S(1)}, u32[]{:S(2)}, u32[]{:S(2)}) %collective-permute-start.15) | collective-permute-done | bytes 65568 | tf_op jit(solution)/shard_map/ppermute | solution.py:188
  43.1 0.0 collective-permute-done.14.refs_8_
  43.2 0.3 collective-permute-done.13.refs_7_
  43.4 1.5 %collective-permute-done.12.refs_6_ = f32[8,2048]{1,0:T(8,128)S(1)} collective-permute-done((f32[8,2048]{1,0:T(8,128)S(1)}, f32[8,2048]{1,0:T(8,128)S(1)}, u32[]{:S(2)}, u32[]{:S(2)}) %collective-permute-start.12) | collective-permute-done | bytes 65568 | tf_op jit(solution)/shard_map/ppermute | solution.py:185
  44.9 0.5 collective-permute-done.11.refs_5_
  45.4 0.0 copy-done.2
  45.5 0.6 image.1
  46.1 13.4 %all_to_all.5.sums_in = f32[32,8,128]{2,1,0:T(8,128)S(1)} all-to-all(f32[32,8,128]{2,1,0:T(8,128)S(1)} %get-tuple-element.11), channel_id=1, replica_groups=mesh['row'=4,'col'=8] {'row','col'}, dimensions={0} | all-to-all | bytes 262144 | tf_op jit(solution)/shard_map/all_to_all | solution.py:240
  59.4 0.0 copy-done.4
  59.4 2.0 %finish.1 = (f32[8,2048]{1,0:T(8,128)}, f32[8,8]{1,0:T(8,128)}, f32[8,8]{1,0:T(8,128)}) custom-call(f32[32,8,128]{2,1,0:T(8,128)S(1)} %all_to_all.5.sums_in, f32[8,2048]{1,0:T(8,128)S(1)} %get-tuple-element.12.image, f32[8,2048]{1,0:T(8,128)S(1)} %copy-done.1, f32[8,2048]{1,0:T(8,128)S(1)} %copy-done.2, f32[8,8]{1,0:T(8,128)S(1)} %copy-done.4), custom_call_target="tpu_custom_call" | custom-call | tf_op jit(solution)/shard_map/finish/pallas_call | solution.py:241
  (6 shorter events, 0.1 us)
Async XLA Ops:
  0.6 58.8 %copy-start.4 = (f32[8,8]{1,0:T(8,128)S(1)}, f32[8,8]{1,0:T(8,128)}, u32[]{:S(2)}) copy-start(f32[8,8]{1,0:T(8,128)} %coupling.1) | copy-start | bytes 772
  0.6 8.6 %collective-permute-start.9 = (f32[8,2048]{1,0:T(8,128)}, f32[8,2048]{1,0:T(8,128)S(1)}, u32[]{:S(2)}, u32[]{:S(2)}) collective-permute-start(f32[8,2048]{1,0:T(8,128)} %now.1), channel_id=1, source_target_pairs={{0,24},{8,16},{16,8},{24,0},{1,25},{9,17},{17,9},{25,1},{2,26},{10... | collective-permute-start | bytes 196616 | tf_op jit(solution)/shard_map/ppermute | solution.py:188
  5.8 5.9 %collective-permute-start.8 = (f32[8,2048]{1,0:T(8,128)}, f32[8,2048]{1,0:T(8,128)S(1)}, u32[]{:S(2)}, u32[]{:S(2)}) collective-permute-start(f32[8,2048]{1,0:T(8,128)} %now.1), channel_id=1, source_target_pairs={{0,16},{8,24},{16,0},{24,8},{1,17},{9,25},{17,1},{25,9},{2,18},{10... | collective-permute-start | bytes 196616 | tf_op jit(solution)/shard_map/ppermute | solution.py:188
  5.8 5.9 %collective-permute-start.2 = (f32[8,2048]{1,0:T(8,128)}, f32[8,2048]{1,0:T(8,128)S(1)}, u32[]{:S(2)}, u32[]{:S(2)}) collective-permute-start(f32[8,2048]{1,0:T(8,128)} %now.1), channel_id=1, source_target_pairs={{0,6},{1,7},{2,4},{3,5},{4,2},{5,3},{6,0},{7,1},{8,14},{9,15},{10,... | collective-permute-start | bytes 196616 | tf_op jit(solution)/shard_map/ppermute | solution.py:185
  8.2 4.5 %collective-permute-start.1 = (f32[8,2048]{1,0:T(8,128)}, f32[8,2048]{1,0:T(8,128)S(1)}, u32[]{:S(2)}, u32[]{:S(2)}) collective-permute-start(f32[8,2048]{1,0:T(8,128)} %now.1), channel_id=1, source_target_pairs={{0,4},{1,5},{2,6},{3,7},{4,0},{5,1},{6,2},{7,3},{8,12},{9,13},{10,... | collective-permute-start | bytes 196616 | tf_op jit(solution)/shard_map/ppermute | solution.py:185
  8.7 4.5 %collective-permute-start = (f32[8,2048]{1,0:T(8,128)}, f32[8,2048]{1,0:T(8,128)S(1)}, u32[]{:S(2)}, u32[]{:S(2)}) collective-permute-start(f32[8,2048]{1,0:T(8,128)} %now.1), channel_id=1, source_target_pairs={{0,2},{1,3},{2,0},{3,1},{4,6},{5,7},{6,4},{7,5},{8,10},{9,11},{10,... | collective-permute-start | bytes 196616 | tf_op jit(solution)/shard_map/ppermute | solution.py:185
  9.3 4.6 %collective-permute-start.7 = (f32[8,2048]{1,0:T(8,128)}, f32[8,2048]{1,0:T(8,128)S(1)}, u32[]{:S(2)}, u32[]{:S(2)}) collective-permute-start(f32[8,2048]{1,0:T(8,128)} %now.1), channel_id=1, source_target_pairs={{0,8},{8,0},{16,24},{24,16},{1,9},{9,1},{17,25},{25,17},{2,10},{10... | collective-permute-start | bytes 196616 | tf_op jit(solution)/shard_map/ppermute | solution.py:188
  11.7 2.2 %collective-permute-start.3 = (f32[8,2048]{1,0:T(8,128)}, f32[8,2048]{1,0:T(8,128)S(1)}, u32[]{:S(2)}, u32[]{:S(2)}) collective-permute-start(f32[8,2048]{1,0:T(8,128)} %now.1), channel_id=1, source_target_pairs={{0,1},{1,0},{2,3},{3,2},{4,5},{5,4},{6,7},{7,6},{8,9},{9,8},{10,11... | collective-permute-start | bytes 196616 | tf_op jit(solution)/shard_map/ppermute | solution.py:185
  11.7 2.2 %collective-permute-start.6 = (f32[8,2048]{1,0:T(8,128)S(1)}, f32[8,2048]{1,0:T(8,128)S(1)}, u32[]{:S(2)}, u32[]{:S(2)}) collective-permute-start(f32[8,2048]{1,0:T(8,128)S(1)} %collective-permute-done.2.refs_8_), channel_id=1, source_target_pairs={{0,1},{1,0},{2,3},{3,2},{4,5},{5,4},{6,7},{7,6},{8,9},{9,8},{10,11... | collective-permute-start | bytes 196616 | tf_op jit(solution)/shard_map/ppermute | solution.py:185
  12.7 1.3 %collective-permute-start.5 = (f32[8,2048]{1,0:T(8,128)S(1)}, f32[8,2048]{1,0:T(8,128)S(1)}, u32[]{:S(2)}, u32[]{:S(2)}) collective-permute-start(f32[8,2048]{1,0:T(8,128)S(1)} %collective-permute-done.1.refs_7_), channel_id=1, source_target_pairs={{0,1},{1,0},{2,3},{3,2},{4,5},{5,4},{6,7},{7,6},{8,9},{9,8},{10,11... | collective-permute-start | bytes 196616 | tf_op jit(solution)/shard_map/ppermute | solution.py:185
  13.2 1.3 %collective-permute-start.4 = (f32[8,2048]{1,0:T(8,128)S(1)}, f32[8,2048]{1,0:T(8,128)S(1)}, u32[]{:S(2)}, u32[]{:S(2)}) collective-permute-start(f32[8,2048]{1,0:T(8,128)S(1)} %collective-permute-done.refs_6_), channel_id=1, source_target_pairs={{0,1},{1,0},{2,3},{3,2},{4,5},{5,4},{6,7},{7,6},{8,9},{9,8},{10,11... | collective-permute-start | bytes 196616 | tf_op jit(solution)/shard_map/ppermute | solution.py:185
  14.4 5.8 %copy-start = (f32[1,1,256,128,128]{4,3,2,1,0:T(8,128)S(1)}, f32[1,1,256,128,128]{4,3,2,1,0:T(8,128)}, u32[]{:S(2)}) copy-start(f32[1,1,256,128,128]{4,3,2,1,0:T(8,128)} %param.8) | copy-start | bytes 50331652
  20.2 0.8 %copy-start.1 = (f32[8,2048]{1,0:T(8,128)S(1)}, f32[8,2048]{1,0:T(8,128)}, u32[]{:S(2)}) copy-start(f32[8,2048]{1,0:T(8,128)} %now.1) | copy-start | bytes 196612
  21.1 0.7 %copy-start.3 = (f32[2048]{0:T(1024)S(1)}, f32[2048]{0:T(1024)}, u32[]{:S(2)}) copy-start(f32[2048]{0:T(1024)} %param.15) | copy-start | bytes 24580
  21.8 0.7 %copy-start.5 = (s32[1,1,256]{2,1,0:T(1,128)S(1)}, s32[1,1,256]{2,1,0:T(1,128)}, u32[]{:S(2)}) copy-start(s32[1,1,256]{2,1,0:T(1,128)} %param.9) | copy-start | bytes 3076
  22.4 0.7 %copy-start.6 = (s32[1,1,256]{2,1,0:T(1,128)S(1)}, s32[1,1,256]{2,1,0:T(1,128)}, u32[]{:S(2)}) copy-start(s32[1,1,256]{2,1,0:T(1,128)} %param.10) | copy-start | bytes 3076
  23.1 22.3 %copy-start.2 = (f32[8,2048]{1,0:T(8,128)S(1)}, f32[8,2048]{1,0:T(8,128)}, u32[]{:S(2)}) copy-start(f32[8,2048]{1,0:T(8,128)} %prev.1) | copy-start | bytes 196612
  26.0 12.1 %collective-permute-start.10 = (f32[4,8,2048]{2,1,0:T(8,128)S(1)}, f32[4,8,2048]{2,1,0:T(8,128)S(1)}, u32[]{:S(2)}, u32[]{:S(2)}) collective-permute-start(f32[4,8,2048]{2,1,0:T(8,128)S(1)} %get-tuple-element.9), channel_id=1, source_target_pairs={{0,1},{1,0},{2,3},{3,2},{4,5},{5,4},{6,7},{7,6},{8,9},{9,8},{10,11... | collective-permute-start | bytes 786440 | tf_op jit(solution)/shard_map/ppermute | solution.py:185
  27.0 14.2 %collective-permute-start.16 = (f32[8,2048]{1,0:T(8,128)S(1)}, f32[8,2048]{1,0:T(8,128)S(1)}, u32[]{:S(2)}, u32[]{:S(2)}) collective-permute-start(f32[8,2048]{1,0:T(8,128)S(1)} %get-tuple-element.16), channel_id=1, source_target_pairs={{0,24},{8,16},{16,8},{24,0},{1,25},{9,17},{17,9},{25,1},{2,26},{10... | collective-permute-start | bytes 196616 | tf_op jit(solution)/shard_map/ppermute | solution.py:188
  37.5 5.7 %collective-permute-start.15 = (f32[8,2048]{1,0:T(8,128)S(1)}, f32[8,2048]{1,0:T(8,128)S(1)}, u32[]{:S(2)}, u32[]{:S(2)}) collective-permute-start(f32[8,2048]{1,0:T(8,128)S(1)} %get-tuple-element.17), channel_id=1, source_target_pairs={{0,16},{8,24},{16,0},{24,8},{1,17},{9,25},{17,1},{25,9},{2,18},{10... | collective-permute-start | bytes 196616 | tf_op jit(solution)/shard_map/ppermute | solution.py:188
  37.5 5.7 %collective-permute-start.14 = (f32[8,2048]{1,0:T(8,128)S(1)}, f32[8,2048]{1,0:T(8,128)S(1)}, u32[]{:S(2)}, u32[]{:S(2)}) collective-permute-start(f32[8,2048]{1,0:T(8,128)S(1)} %get-tuple-element.18), channel_id=1, source_target_pairs={{0,8},{8,0},{16,24},{24,16},{1,9},{9,1},{17,25},{25,17},{2,10},{10... | collective-permute-start | bytes 196616 | tf_op jit(solution)/shard_map/ppermute | solution.py:188
  38.2 5.3 %collective-permute-start.13 = (f32[8,2048]{1,0:T(8,128)S(1)}, f32[8,2048]{1,0:T(8,128)S(1)}, u32[]{:S(2)}, u32[]{:S(2)}) collective-permute-start(f32[8,2048]{1,0:T(8,128)S(1)} %get-tuple-element.13), channel_id=1, source_target_pairs={{0,6},{1,7},{2,4},{3,5},{4,2},{5,3},{6,0},{7,1},{8,14},{9,15},{10,... | collective-permute-start | bytes 196616 | tf_op jit(solution)/shard_map/ppermute | solution.py:185
  40.7 4.3 %collective-permute-start.12 = (f32[8,2048]{1,0:T(8,128)S(1)}, f32[8,2048]{1,0:T(8,128)S(1)}, u32[]{:S(2)}, u32[]{:S(2)}) collective-permute-start(f32[8,2048]{1,0:T(8,128)S(1)} %get-tuple-element.14), channel_id=1, source_target_pairs={{0,4},{1,5},{2,6},{3,7},{4,0},{5,1},{6,2},{7,3},{8,12},{9,13},{10,... | collective-permute-start | bytes 196616 | tf_op jit(solution)/shard_map/ppermute | solution.py:185
  41.2 4.3 %collective-permute-start.11 = (f32[8,2048]{1,0:T(8,128)S(1)}, f32[8,2048]{1,0:T(8,128)S(1)}, u32[]{:S(2)}, u32[]{:S(2)}) collective-permute-start(f32[8,2048]{1,0:T(8,128)S(1)} %get-tuple-element.15), channel_id=1, source_target_pairs={{0,2},{1,3},{2,0},{3,1},{4,6},{5,7},{6,4},{7,5},{8,10},{9,11},{10,... | collective-permute-start | bytes 196616 | tf_op jit(solution)/shard_map/ppermute | solution.py:185

commit v2 on v1

--- a/solution.py
+++ b/solution.py
@@ -1,4 +1,5 @@
 import functools
+import math
 
 import jax
 import jax.numpy as jnp
@@ -9,7 +10,7 @@
 
 VMEM = pltpu.VMEM
 SMEM = pltpu.SMEM
-GROUP = 8
+GROUP = 32
 MIB = 1 << 20
 
 
@@ -35,43 +36,93 @@
     )
 
 
-def products_kernel(rows, planes, piece_tiles, width, *refs):
-    row_idx, col_idx, count, tiles, diag = refs[:5]
-    plane_in = refs[5 : 5 + planes]
-    core_in = refs[5 + planes : 5 + 2 * planes]
-    row_in = refs[5 + 2 * planes : 4 + 2 * planes + rows]
-    keep_out, send_out, col_out, vec_rows, vec_cols, acc_rows, acc_cols = refs[
-        4 + 2 * planes + rows :
-    ]
+def products_kernel(rows, planes, group, *refs):
+    tiles_hbm, row_idx_hbm, col_idx_hbm, count_hbm, diag_hbm, own_hbm = refs[:6]
+    refs = refs[6:]
+    plane_in = refs[: planes - 1]
+    core_in = refs[planes - 1 : 2 * planes - 1]
+    row_in = refs[2 * planes - 1 : 2 * planes + rows - 2]
+    (
+        keep_out,
+        send_out,
+        col_out,
+        tiles,
+        row_idx,
+        col_idx,
+        count,
+        diag,
+        own,
+        vec_rows,
+        vec_cols,
+        acc_rows,
+        acc_cols,
+        small_sems,
+        tile_sems,
+    ) = refs[2 * planes + rows - 2 :]
     row = lax.axis_index("row")
     col = lax.axis_index("col")
     plane, core = col // 2, col % 2
+    width = tiles.shape[-1]
+    piece_tiles = own.shape[1] // width
+
+    small = [
+        pltpu.make_async_copy(source, target, small_sems.at[k])
+        for k, (source, target) in enumerate(
+            (
+                (count_hbm, count),
+                (row_idx_hbm, row_idx),
+                (col_idx_hbm, col_idx),
+                (own_hbm, own),
+                (diag_hbm, diag),
+            )
+        )
+    ]
+
+    def tile_copy(g):
+        at = pl.ds(g * group, group)
+        return pltpu.make_async_copy(tiles_hbm.at[at], tiles.at[at], tile_sems.at[g])
+
+    for copy in small:
+        copy.start()
+    small[0].wait()
+    total = count[0, 0]
+    groups = (total + group - 1) // group
+
+    def start_tiles(g, carry):
+        tile_copy(g).start()
+        return carry
+
+    lax.fori_loop(0, groups, start_tiles, 0)
+    acc_rows[...] = jnp.zeros_like(acc_rows)
+    acc_cols[...] = jnp.zeros_like(acc_cols)
 
     def store_split(target, base, source):
         for t in range(piece_tiles):
             high, low = halves(source[:, t * width : (t + 1) * width])
             target[base + t] = jnp.concatenate([high, low], axis=0)
 
-    own = plane_in[0]
+    for s in range(1, planes):
+        base = jnp.bitwise_xor(plane, s) * 2 * piece_tiles
+        store_split(vec_rows, base + core * piece_tiles, plane_in[s - 1])
     for s in range(planes):
         base = jnp.bitwise_xor(plane, s) * 2 * piece_tiles
-        store_split(vec_rows, base + core * piece_tiles, plane_in[s])
         store_split(vec_rows, base + (1 - core) * piece_tiles, core_in[s])
-    store_split(vec_cols, row * piece_tiles, own)
     for s in range(1, rows):
         store_split(vec_cols, jnp.bitwise_xor(row, s) * piece_tiles, row_in[s - 1])
-    acc_rows[...] = jnp.zeros_like(acc_rows)
-    acc_cols[...] = jnp.zeros_like(acc_cols)
-
-    total = count[0]
+    for copy in small[1:]:
+        copy.wait()
+    store_split(vec_rows, col * piece_tiles, own)
+    store_split(vec_cols, row * piece_tiles, own)
+
     spare_row = acc_rows.shape[0] - 1
     spare_col = acc_cols.shape[0] - 1
 
-    def step(group, carry):
-        for k in range(GROUP):
-            m = group * GROUP + k
+    def step(g, carry):
+        tile_copy(g).wait()
+        for k in range(group):
+            m = g * group + k
             alive = m < total
-            r, c = row_idx[m], col_idx[m]
+            r, c = row_idx[0, 0, m], col_idx[0, 0, m]
             high, low = halves(tiles[m])
             from_row = vec_rows[r]
             from_col = vec_cols[c]
@@ -81,16 +132,16 @@
                 preferred_element_type=jnp.float32,
             )
             ahead = lax.dot_general(
+                jnp.concatenate([high, low], axis=1),
                 jnp.concatenate([from_col, from_col], axis=1),
-                jnp.concatenate([high, low], axis=1),
                 (((1,), (1,)), ((), ())),
                 preferred_element_type=jnp.float32,
-            )
+            ).T
             acc_rows[jnp.where(alive, r, spare_row)] += ahead[:8] + ahead[8:]
             acc_cols[jnp.where(alive, c, spare_col)] += back[:8] + back[8:]
         return carry
 
-    lax.fori_loop(0, (total + GROUP - 1) // GROUP, step, 0)
+    lax.fori_loop(0, groups, step, 0)
 
     for s in range(planes):
         base = jnp.bitwise_xor(plane, s) * 2 * piece_tiles
@@ -192,32 +243,45 @@
     core_in = [along_col(x, 1) for x in plane_in]
 
     in_vmem = pl.BlockSpec(memory_space=VMEM)
-    in_smem = pl.BlockSpec(memory_space=SMEM)
-    held = pltpu.with_memory_space_constraint(tiles.reshape(slots, width, width), VMEM)
+    in_hbm = pl.BlockSpec(memory_space=pltpu.HBM)
+    group = math.gcd(slots, GROUP)
+
+    def stay(x):
+        return pltpu.with_memory_space_constraint(x, pltpu.HBM)
+
     keep, send, col_parts = pl.pallas_call(
-        functools.partial(products_kernel, rows, planes, piece_tiles, width),
+        functools.partial(products_kernel, rows, planes, group),
         out_shape=(
             jax.ShapeDtypeStruct((planes, vectors, piece), f32),
             jax.ShapeDtypeStruct((planes, vectors, piece), f32),
             jax.ShapeDtypeStruct((rows, vectors, piece), f32),
         ),
-        in_specs=[in_smem] * 3 + [in_vmem] * (2 * planes + rows + 1),
+        in_specs=[in_hbm] * 3 + [pl.BlockSpec(memory_space=pl.ANY)] + [in_hbm] * 2 + [in_vmem] * (2 * planes + rows - 2),
         out_specs=(in_vmem,) * 3,
         scratch_shapes=[
+            VMEM((slots, width, width), f32),
+            SMEM(tile_rows.shape, jnp.int32),
+            SMEM(tile_cols.shape, jnp.int32),
+            SMEM(tile_counts.shape, jnp.int32),
+            VMEM((1, piece), f32),
+            VMEM((vectors, piece), f32),
             VMEM((cols * piece_tiles, 2 * vectors, width), jnp.bfloat16),
             VMEM((rows * piece_tiles, 2 * vectors, width), jnp.bfloat16),
             VMEM((cols * piece_tiles + 1, vectors, width), f32),
             VMEM((rows * piece_tiles + 1, vectors, width), f32),
+            pltpu.SemaphoreType.DMA((5,)),
+            pltpu.SemaphoreType.DMA((slots // group,)),
         ],
-        compiler_params=pltpu.CompilerParams(vmem_limit_bytes=24 * MIB),
+        compiler_params=pltpu.CompilerParams(vmem_limit_bytes=40 * MIB),
         name="products",
     )(
-        tile_rows.reshape(slots),
-        tile_cols.reshape(slots),
-        tile_counts.reshape(1),
-        held,
-        diag_energy.reshape(1, piece),
-        *plane_in,
+        stay(tiles.reshape(slots, width, width)),
+        stay(tile_rows),
+        stay(tile_cols),
+        tile_counts,
+        stay(diag_energy.reshape(1, piece)),
+        stay(block_now),
+        *plane_in[1:],
         *core_in,
         *row_in,
     )

time: 61.8 us -> 50.1 us (0.81)
  local copies, waits for them, and re-layouts: 8.69 us -> 0.03 us
  starting transfers between devices: 26.9 us -> 23 us
  Pallas kernels: 5.57 us -> 6.62 us
    unnamed x14 -> x6, local copies, waits for them, and re-layouts: 8.67 us -> 0.01 us
    ppermute x6, starting transfers between devices: 18.2 us -> 15 us  [along_row(): return lax.ppermute(x, 'row', [(i, i ^ s) for i in range(rows)])]
    pallas_call x1, Pallas kernels: 2.92 us -> 3.97 us  [local(): pl.pallas_call(functools.partial(products_kernel, rows, planes, group), o...]
    ppermute x11, starting transfers between devices: 8.67 us -> 8.04 us  [along_col(): return lax.ppermute(x, 'col', [(i, i ^ s) for i in range(cols)])]
where the time goes in v2:
time: 50.1 us; the launch traced here: 50 us
  starting transfers between devices  23 us (46%)
  blocking collectives  13.3 us (27%)
  Pallas kernels  6.62 us (13%)
  waiting for transfers between devices  5.55 us (11%)
  between operations  1.37 us (3%)
    ppermute x6, starting transfers between devices, along_row(): return lax.ppermute(x, 'row', [(i, i ^ s) for i in range(rows)])  15 us
    all_to_all x1, blocking collectives, local(): sums = lax.all_to_all(sums, ('row', 'col'), 0, 0)  13.3 us
    ppermute x11, starting transfers between devices, along_col(): return lax.ppermute(x, 'col', [(i, i ^ s) for i in range(cols)])  8.04 us
    pallas_call x1, Pallas kernels, local(): pl.pallas_call(functools.partial(products_kernel, rows, planes, group), o...  3.97 us
    ppermute x11, waiting for transfers between devices, along_col(): return lax.ppermute(x, 'col', [(i, i ^ s) for i in range(cols)])  3.77 us
    pallas_call x1, Pallas kernels, local(): pl.pallas_call(functools.partial(finish_kernel, float(piece * devices)),...  2.05 us
    ppermute x6, waiting for transfers between devices, along_row(): return lax.ppermute(x, 'row', [(i, i ^ s) for i in range(rows)])  1.78 us
  transfers between devices with their start and end apart: 17, of which 9 were waited for; matrix products, arithmetic and copies ran while one was open for 0% of the time, Pallas kernels for 0%

profile of v2, /device:TPU:0, one launch (start us, length us, event | category | flops | bytes accessed | tf_op | source)
XLA Modules:
  0.0 50.0 jit_solution(4277778043005826291)
XLA Ops:
  0.6 0.0 copy-start
  0.6 0.0 copy-start.1
  0.7 0.0 copy-start.2
  0.7 5.1 %collective-permute-start.9 = (f32[8,2048]{1,0:T(8,128)}, f32[8,2048]{1,0:T(8,128)S(1)}, u32[]{:S(2)}, u32[]{:S(2)}) collective-permute-start(f32[8,2048]{1,0:T(8,128)} %now.1), channel_id=1, source_target_pairs={{0,24},{8,16},{16,8},{24,0},{1,25},{9,17},{17,9},{25,1},{2,26},{10... | collective-permute-start | bytes 196616 | tf_op jit(solution)/shard_map/ppermute | solution.py:239
  5.8 0.0 collective-permute-start.8
  5.8 2.4 %collective-permute-start.2 = (f32[8,2048]{1,0:T(8,128)}, f32[8,2048]{1,0:T(8,128)S(1)}, u32[]{:S(2)}, u32[]{:S(2)}) collective-permute-start(f32[8,2048]{1,0:T(8,128)} %now.1), channel_id=1, source_target_pairs={{0,6},{1,7},{2,4},{3,5},{4,2},{5,3},{6,0},{7,1},{8,14},{9,15},{10,... | collective-permute-start | bytes 196616 | tf_op jit(solution)/shard_map/ppermute | solution.py:236
  8.2 0.5 %collective-permute-start.1 = (f32[8,2048]{1,0:T(8,128)}, f32[8,2048]{1,0:T(8,128)S(1)}, u32[]{:S(2)}, u32[]{:S(2)}) collective-permute-start(f32[8,2048]{1,0:T(8,128)} %now.1), channel_id=1, source_target_pairs={{0,4},{1,5},{2,6},{3,7},{4,0},{5,1},{6,2},{7,3},{8,12},{9,13},{10,... | collective-permute-start | bytes 196616 | tf_op jit(solution)/shard_map/ppermute | solution.py:236
  8.7 0.5 %collective-permute-start = (f32[8,2048]{1,0:T(8,128)}, f32[8,2048]{1,0:T(8,128)S(1)}, u32[]{:S(2)}, u32[]{:S(2)}) collective-permute-start(f32[8,2048]{1,0:T(8,128)} %now.1), channel_id=1, source_target_pairs={{0,2},{1,3},{2,0},{3,1},{4,6},{5,7},{6,4},{7,5},{8,10},{9,11},{10,... | collective-permute-start | bytes 196616 | tf_op jit(solution)/shard_map/ppermute | solution.py:236
  9.3 0.0 collective-permute-done.9.refs_15_
  9.3 1.9 %collective-permute-start.7 = (f32[8,2048]{1,0:T(8,128)}, f32[8,2048]{1,0:T(8,128)S(1)}, u32[]{:S(2)}, u32[]{:S(2)}) collective-permute-start(f32[8,2048]{1,0:T(8,128)} %now.1), channel_id=1, source_target_pairs={{0,8},{8,0},{16,24},{24,16},{1,9},{9,1},{17,25},{25,17},{2,10},{10... | collective-permute-start | bytes 196616 | tf_op jit(solution)/shard_map/ppermute | solution.py:239
  11.2 0.5 collective-permute-done.8.refs_14_
  11.7 0.0 collective-permute-start.3
  11.7 0.0 collective-permute-done.2.refs_8_
  11.7 0.5 %collective-permute-start.6 = (f32[8,2048]{1,0:T(8,128)S(1)}, f32[8,2048]{1,0:T(8,128)S(1)}, u32[]{:S(2)}, u32[]{:S(2)}) collective-permute-start(f32[8,2048]{1,0:T(8,128)S(1)} %collective-permute-done.2.refs_8_), channel_id=1, source_target_pairs={{0,1},{1,0},{2,3},{3,2},{4,5},{5,4},{6,7},{7,6},{8,9},{9,8},{10,11... | collective-permute-start | bytes 196616 | tf_op jit(solution)/shard_map/ppermute | solution.py:236
  12.2 0.5 %collective-permute-done.1.refs_7_ = f32[8,2048]{1,0:T(8,128)S(1)} collective-permute-done((f32[8,2048]{1,0:T(8,128)}, f32[8,2048]{1,0:T(8,128)S(1)}, u32[]{:S(2)}, u32[]{:S(2)}) %collective-permute-start.1) | collective-permute-done | bytes 65568 | tf_op jit(solution)/shard_map/ppermute | solution.py:236
  12.7 0.0 collective-permute-start.5
  12.7 0.5 %collective-permute-done.refs_6_ = f32[8,2048]{1,0:T(8,128)S(1)} collective-permute-done((f32[8,2048]{1,0:T(8,128)}, f32[8,2048]{1,0:T(8,128)S(1)}, u32[]{:S(2)}, u32[]{:S(2)}) %collective-permute-start) | collective-permute-done | bytes 65568 | tf_op jit(solution)/shard_map/ppermute | solution.py:236
  13.2 0.0 collective-permute-start.4
  13.9 0.0 collective-permute-done.7.refs_13_
  13.9 0.0 collective-permute-done.3.refs_9_
  13.9 0.0 collective-permute-done.6.refs_12_
  13.9 0.1 collective-permute-done.5.refs_11_
  14.0 0.5 %collective-permute-done.4.refs_10_ = f32[8,2048]{1,0:T(8,128)S(1)} collective-permute-done((f32[8,2048]{1,0:T(8,128)S(1)}, f32[8,2048]{1,0:T(8,128)S(1)}, u32[]{:S(2)}, u32[]{:S(2)}) %collective-permute-start.4) | collective-permute-done | bytes 65568 | tf_op jit(solution)/shard_map/ppermute | solution.py:236
  14.5 4.0 %products.1 = (f32[4,8,2048]{2,1,0:T(8,128)S(1)}, f32[4,8,2048]{2,1,0:T(8,128)S(1)}, f32[4,8,2048]{2,1,0:T(8,128)S(1)}) custom-call(f32[256,128,128]{2,1,0:T(8,128)} %bitcast.20, s32[1,1,256]{2,1,0:T(1,128)} %refs_1_.2, s32[1,1,256]{2,1,0:T(1,128)} %refs_2_.1, s32[1,1]{1,0:T(1,128)S(6)} %copy.11.refs_3_, f32[1,2048]{1,0:T(1,128)} %bitcast.21, ...), custom_call_target="tpu_custom_call" | custom-call | tf_op jit(solution)/shard_map/products/pallas_call | solution.py:252
  18.4 0.2 collective-permute-start.10
  18.7 7.3 %collective-permute-start.16 = (f32[8,2048]{1,0:T(8,128)S(1)}, f32[8,2048]{1,0:T(8,128)S(1)}, u32[]{:S(2)}, u32[]{:S(2)}) collective-permute-start(f32[8,2048]{1,0:T(8,128)S(1)} %get-tuple-element.16), channel_id=1, source_target_pairs={{0,24},{8,16},{16,8},{24,0},{1,25},{9,17},{17,9},{25,1},{2,26},{10... | collective-permute-start | bytes 196616 | tf_op jit(solution)/shard_map/ppermute | solution.py:239
  26.0 0.0 collective-permute-start.15
  26.0 0.6 %collective-permute-start.14 = (f32[8,2048]{1,0:T(8,128)S(1)}, f32[8,2048]{1,0:T(8,128)S(1)}, u32[]{:S(2)}, u32[]{:S(2)}) collective-permute-start(f32[8,2048]{1,0:T(8,128)S(1)} %get-tuple-element.18), channel_id=1, source_target_pairs={{0,8},{8,0},{16,24},{24,16},{1,9},{9,1},{17,25},{25,17},{2,10},{10... | collective-permute-start | bytes 196616 | tf_op jit(solution)/shard_map/ppermute | solution.py:239
  26.6 0.0 collective-permute-done.10
  26.7 2.5 %collective-permute-start.13 = (f32[8,2048]{1,0:T(8,128)S(1)}, f32[8,2048]{1,0:T(8,128)S(1)}, u32[]{:S(2)}, u32[]{:S(2)}) collective-permute-start(f32[8,2048]{1,0:T(8,128)S(1)} %get-tuple-element.13), channel_id=1, source_target_pairs={{0,6},{1,7},{2,4},{3,5},{4,2},{5,3},{6,0},{7,1},{8,14},{9,15},{10,... | collective-permute-start | bytes 196616 | tf_op jit(solution)/shard_map/ppermute | solution.py:236
  29.2 0.5 %collective-permute-start.12 = (f32[8,2048]{1,0:T(8,128)S(1)}, f32[8,2048]{1,0:T(8,128)S(1)}, u32[]{:S(2)}, u32[]{:S(2)}) collective-permute-start(f32[8,2048]{1,0:T(8,128)S(1)} %get-tuple-element.14), channel_id=1, source_target_pairs={{0,4},{1,5},{2,6},{3,7},{4,0},{5,1},{6,2},{7,3},{8,12},{9,13},{10,... | collective-permute-start | bytes 196616 | tf_op jit(solution)/shard_map/ppermute | solution.py:236
  29.7 0.0 collective-permute-done.16.refs_10_
  29.7 0.8 %collective-permute-start.11 = (f32[8,2048]{1,0:T(8,128)S(1)}, f32[8,2048]{1,0:T(8,128)S(1)}, u32[]{:S(2)}, u32[]{:S(2)}) collective-permute-start(f32[8,2048]{1,0:T(8,128)S(1)} %get-tuple-element.15), channel_id=1, source_target_pairs={{0,2},{1,3},{2,0},{3,1},{4,6},{5,7},{6,4},{7,5},{8,10},{9,11},{10,... | collective-permute-start | bytes 196616 | tf_op jit(solution)/shard_map/ppermute | solution.py:236
  30.5 1.3 %collective-permute-done.15.refs_9_ = f32[8,2048]{1,0:T(8,128)S(1)} collective-permute-done((f32[8,2048]{1,0:T(8,128)S(1)}, f32[8,2048]{1,0:T(8,128)S(1)}, u32[]{:S(2)}, u32[]{:S(2)}) %collective-permute-start.15) | collective-permute-done | bytes 65568 | tf_op jit(solution)/shard_map/ppermute | solution.py:239
  31.8 0.0 collective-permute-done.14.refs_8_
  31.8 0.2 collective-permute-done.13.refs_7_
  31.9 1.5 %collective-permute-done.12.refs_6_ = f32[8,2048]{1,0:T(8,128)S(1)} collective-permute-done((f32[8,2048]{1,0:T(8,128)S(1)}, f32[8,2048]{1,0:T(8,128)S(1)}, u32[]{:S(2)}, u32[]{:S(2)}) %collective-permute-start.12) | collective-permute-done | bytes 65568 | tf_op jit(solution)/shard_map/ppermute | solution.py:236
  33.4 0.5 %collective-permute-done.11.refs_5_ = f32[8,2048]{1,0:T(8,128)S(1)} collective-permute-done((f32[8,2048]{1,0:T(8,128)S(1)}, f32[8,2048]{1,0:T(8,128)S(1)}, u32[]{:S(2)}, u32[]{:S(2)}) %collective-permute-start.11) | collective-permute-done | bytes 65568 | tf_op jit(solution)/shard_map/ppermute | solution.py:236
  34.0 0.0 copy-done
  34.0 0.0 copy-done.1
  34.0 0.6 %image.1 = (f32[8,2048]{1,0:T(8,128)S(1)}, f32[32,8,128]{2,1,0:T(8,128)S(1)}) custom-call(f32[8,2048]{1,0:T(8,128)S(1)} %copy-done, f32[8,2048]{1,0:T(8,128)S(1)} %copy-done.1, f32[8,2048]{1,0:T(8,128)S(1)} %get-tuple-element.20.refs_2_, f32[8,2048]{1,0:T(8,128)S(1)} %get-tuple-element.21.refs_3_, f32[8,2048]{1,0:T(8,128)S(1)} %get-tuple-element.19.refs_4_, ...), custom_call_target="tpu_custom_call" | custom-call | tf_op jit(solution)/shard_map/image/pallas_call | solution.py:295
  34.6 13.3 %all_to_all.5.sums_in = f32[32,8,128]{2,1,0:T(8,128)S(1)} all-to-all(f32[32,8,128]{2,1,0:T(8,128)S(1)} %get-tuple-element.11), channel_id=1, replica_groups=mesh['row'=4,'col'=8] {'row','col'}, dimensions={0} | all-to-all | bytes 262144 | tf_op jit(solution)/shard_map/all_to_all | solution.py:304
  47.9 0.0 copy-done.2
  47.9 2.0 %finish.1 = (f32[8,2048]{1,0:T(8,128)}, f32[8,8]{1,0:T(8,128)}, f32[8,8]{1,0:T(8,128)}) custom-call(f32[32,8,128]{2,1,0:T(8,128)S(1)} %all_to_all.5.sums_in, f32[8,2048]{1,0:T(8,128)S(1)} %get-tuple-element.12.image, f32[8,2048]{1,0:T(8,128)S(1)} %copy-done, f32[8,2048]{1,0:T(8,128)S(1)} %copy-done.1, f32[8,8]{1,0:T(8,128)S(1)} %copy-done.2), custom_call_target="tpu_custom_call" | custom-call | tf_op jit(solution)/shard_map/finish/pallas_call | solution.py:305
  (2 shorter events, 0.0 us)
Async XLA Ops:
  0.6 33.3 %copy-start = (f32[8,2048]{1,0:T(8,128)S(1)}, f32[8,2048]{1,0:T(8,128)}, u32[]{:S(2)}) copy-start(f32[8,2048]{1,0:T(8,128)} %now.1) | copy-start | bytes 196612
  0.6 33.3 %copy-start.1 = (f32[8,2048]{1,0:T(8,128)S(1)}, f32[8,2048]{1,0:T(8,128)}, u32[]{:S(2)}) copy-start(f32[8,2048]{1,0:T(8,128)} %prev.1) | copy-start | bytes 196612
  0.7 47.3 %copy-start.2 = (f32[8,8]{1,0:T(8,128)S(1)}, f32[8,8]{1,0:T(8,128)}, u32[]{:S(2)}) copy-start(f32[8,8]{1,0:T(8,128)} %coupling.1) | copy-start | bytes 772
  0.7 8.6 %collective-permute-start.9 = (f32[8,2048]{1,0:T(8,128)}, f32[8,2048]{1,0:T(8,128)S(1)}, u32[]{:S(2)}, u32[]{:S(2)}) collective-permute-start(f32[8,2048]{1,0:T(8,128)} %now.1), channel_id=1, source_target_pairs={{0,24},{8,16},{16,8},{24,0},{1,25},{9,17},{17,9},{25,1},{2,26},{10... | collective-permute-start | bytes 196616 | tf_op jit(solution)/shard_map/ppermute | solution.py:239
  5.8 5.9 %collective-permute-start.8 = (f32[8,2048]{1,0:T(8,128)}, f32[8,2048]{1,0:T(8,128)S(1)}, u32[]{:S(2)}, u32[]{:S(2)}) collective-permute-start(f32[8,2048]{1,0:T(8,128)} %now.1), channel_id=1, source_target_pairs={{0,16},{8,24},{16,0},{24,8},{1,17},{9,25},{17,1},{25,9},{2,18},{10... | collective-permute-start | bytes 196616 | tf_op jit(solution)/shard_map/ppermute | solution.py:239
  5.8 5.9 %collective-permute-start.2 = (f32[8,2048]{1,0:T(8,128)}, f32[8,2048]{1,0:T(8,128)S(1)}, u32[]{:S(2)}, u32[]{:S(2)}) collective-permute-start(f32[8,2048]{1,0:T(8,128)} %now.1), channel_id=1, source_target_pairs={{0,6},{1,7},{2,4},{3,5},{4,2},{5,3},{6,0},{7,1},{8,14},{9,15},{10,... | collective-permute-start | bytes 196616 | tf_op jit(solution)/shard_map/ppermute | solution.py:236
  8.2 4.5 %collective-permute-start.1 = (f32[8,2048]{1,0:T(8,128)}, f32[8,2048]{1,0:T(8,128)S(1)}, u32[]{:S(2)}, u32[]{:S(2)}) collective-permute-start(f32[8,2048]{1,0:T(8,128)} %now.1), channel_id=1, source_target_pairs={{0,4},{1,5},{2,6},{3,7},{4,0},{5,1},{6,2},{7,3},{8,12},{9,13},{10,... | collective-permute-start | bytes 196616 | tf_op jit(solution)/shard_map/ppermute | solution.py:236
  8.7 4.5 %collective-permute-start = (f32[8,2048]{1,0:T(8,128)}, f32[8,2048]{1,0:T(8,128)S(1)}, u32[]{:S(2)}, u32[]{:S(2)}) collective-permute-start(f32[8,2048]{1,0:T(8,128)} %now.1), channel_id=1, source_target_pairs={{0,2},{1,3},{2,0},{3,1},{4,6},{5,7},{6,4},{7,5},{8,10},{9,11},{10,... | collective-permute-start | bytes 196616 | tf_op jit(solution)/shard_map/ppermute | solution.py:236
  9.3 4.6 %collective-permute-start.7 = (f32[8,2048]{1,0:T(8,128)}, f32[8,2048]{1,0:T(8,128)S(1)}, u32[]{:S(2)}, u32[]{:S(2)}) collective-permute-start(f32[8,2048]{1,0:T(8,128)} %now.1), channel_id=1, source_target_pairs={{0,8},{8,0},{16,24},{24,16},{1,9},{9,1},{17,25},{25,17},{2,10},{10... | collective-permute-start | bytes 196616 | tf_op jit(solution)/shard_map/ppermute | solution.py:239
  11.7 2.2 %collective-permute-start.3 = (f32[8,2048]{1,0:T(8,128)}, f32[8,2048]{1,0:T(8,128)S(1)}, u32[]{:S(2)}, u32[]{:S(2)}) collective-permute-start(f32[8,2048]{1,0:T(8,128)} %now.1), channel_id=1, source_target_pairs={{0,1},{1,0},{2,3},{3,2},{4,5},{5,4},{6,7},{7,6},{8,9},{9,8},{10,11... | collective-permute-start | bytes 196616 | tf_op jit(solution)/shard_map/ppermute | solution.py:236
  11.7 2.2 %collective-permute-start.6 = (f32[8,2048]{1,0:T(8,128)S(1)}, f32[8,2048]{1,0:T(8,128)S(1)}, u32[]{:S(2)}, u32[]{:S(2)}) collective-permute-start(f32[8,2048]{1,0:T(8,128)S(1)} %collective-permute-done.2.refs_8_), channel_id=1, source_target_pairs={{0,1},{1,0},{2,3},{3,2},{4,5},{5,4},{6,7},{7,6},{8,9},{9,8},{10,11... | collective-permute-start | bytes 196616 | tf_op jit(solution)/shard_map/ppermute | solution.py:236
  12.7 1.3 %collective-permute-start.5 = (f32[8,2048]{1,0:T(8,128)S(1)}, f32[8,2048]{1,0:T(8,128)S(1)}, u32[]{:S(2)}, u32[]{:S(2)}) collective-permute-start(f32[8,2048]{1,0:T(8,128)S(1)} %collective-permute-done.1.refs_7_), channel_id=1, source_target_pairs={{0,1},{1,0},{2,3},{3,2},{4,5},{5,4},{6,7},{7,6},{8,9},{9,8},{10,11... | collective-permute-start | bytes 196616 | tf_op jit(solution)/shard_map/ppermute | solution.py:236
  13.2 1.3 %collective-permute-start.4 = (f32[8,2048]{1,0:T(8,128)S(1)}, f32[8,2048]{1,0:T(8,128)S(1)}, u32[]{:S(2)}, u32[]{:S(2)}) collective-permute-start(f32[8,2048]{1,0:T(8,128)S(1)} %collective-permute-done.refs_6_), channel_id=1, source_target_pairs={{0,1},{1,0},{2,3},{3,2},{4,5},{5,4},{6,7},{7,6},{8,9},{9,8},{10,11... | collective-permute-start | bytes 196616 | tf_op jit(solution)/shard_map/ppermute | solution.py:236
  18.4 8.2 %collective-permute-start.10 = (f32[4,8,2048]{2,1,0:T(8,128)S(1)}, f32[4,8,2048]{2,1,0:T(8,128)S(1)}, u32[]{:S(2)}, u32[]{:S(2)}) collective-permute-start(f32[4,8,2048]{2,1,0:T(8,128)S(1)} %get-tuple-element.9), channel_id=1, source_target_pairs={{0,1},{1,0},{2,3},{3,2},{4,5},{5,4},{6,7},{7,6},{8,9},{9,8},{10,11... | collective-permute-start | bytes 786440 | tf_op jit(solution)/shard_map/ppermute | solution.py:236
  18.7 11.0 %collective-permute-start.16 = (f32[8,2048]{1,0:T(8,128)S(1)}, f32[8,2048]{1,0:T(8,128)S(1)}, u32[]{:S(2)}, u32[]{:S(2)}) collective-permute-start(f32[8,2048]{1,0:T(8,128)S(1)} %get-tuple-element.16), channel_id=1, source_target_pairs={{0,24},{8,16},{16,8},{24,0},{1,25},{9,17},{17,9},{25,1},{2,26},{10... | collective-permute-start | bytes 196616 | tf_op jit(solution)/shard_map/ppermute | solution.py:239
  26.0 5.8 %collective-permute-start.15 = (f32[8,2048]{1,0:T(8,128)S(1)}, f32[8,2048]{1,0:T(8,128)S(1)}, u32[]{:S(2)}, u32[]{:S(2)}) collective-permute-start(f32[8,2048]{1,0:T(8,128)S(1)} %get-tuple-element.17), channel_id=1, source_target_pairs={{0,16},{8,24},{16,0},{24,8},{1,17},{9,25},{17,1},{25,9},{2,18},{10... | collective-permute-start | bytes 196616 | tf_op jit(solution)/shard_map/ppermute | solution.py:239
  26.0 5.8 %collective-permute-start.14 = (f32[8,2048]{1,0:T(8,128)S(1)}, f32[8,2048]{1,0:T(8,128)S(1)}, u32[]{:S(2)}, u32[]{:S(2)}) collective-permute-start(f32[8,2048]{1,0:T(8,128)S(1)} %get-tuple-element.18), channel_id=1, source_target_pairs={{0,8},{8,0},{16,24},{24,16},{1,9},{9,1},{17,25},{25,17},{2,10},{10... | collective-permute-start | bytes 196616 | tf_op jit(solution)/shard_map/ppermute | solution.py:239
  26.7 5.3 %collective-permute-start.13 = (f32[8,2048]{1,0:T(8,128)S(1)}, f32[8,2048]{1,0:T(8,128)S(1)}, u32[]{:S(2)}, u32[]{:S(2)}) collective-permute-start(f32[8,2048]{1,0:T(8,128)S(1)} %get-tuple-element.13), channel_id=1, source_target_pairs={{0,6},{1,7},{2,4},{3,5},{4,2},{5,3},{6,0},{7,1},{8,14},{9,15},{10,... | collective-permute-start | bytes 196616 | tf_op jit(solution)/shard_map/ppermute | solution.py:236
  29.2 4.3 %collective-permute-start.12 = (f32[8,2048]{1,0:T(8,128)S(1)}, f32[8,2048]{1,0:T(8,128)S(1)}, u32[]{:S(2)}, u32[]{:S(2)}) collective-permute-start(f32[8,2048]{1,0:T(8,128)S(1)} %get-tuple-element.14), channel_id=1, source_target_pairs={{0,4},{1,5},{2,6},{3,7},{4,0},{5,1},{6,2},{7,3},{8,12},{9,13},{10,... | collective-permute-start | bytes 196616 | tf_op jit(solution)/shard_map/ppermute | solution.py:236
  29.7 4.3 %collective-permute-start.11 = (f32[8,2048]{1,0:T(8,128)S(1)}, f32[8,2048]{1,0:T(8,128)S(1)}, u32[]{:S(2)}, u32[]{:S(2)}) collective-permute-start(f32[8,2048]{1,0:T(8,128)S(1)} %get-tuple-element.15), channel_id=1, source_target_pairs={{0,2},{1,3},{2,0},{3,1},{4,6},{5,7},{6,4},{7,5},{8,10},{9,11},{10,... | collective-permute-start | bytes 196616 | tf_op jit(solution)/shard_map/ppermute | solution.py:236

commit v3 on v2

--- a/solution.py
+++ b/solution.py
@@ -12,6 +12,26 @@
 SMEM = pltpu.SMEM
 GROUP = 32
 MIB = 1 << 20
+
+
+def pair_steps(count):
+    last = [0] * count
+    steps = []
+    for high in range(1, count):
+        for low in range(high):
+            at = max(last[low], last[high])
+            last[low] = last[high] = at + 1
+            if at == len(steps):
+                steps.append(list(range(count)))
+            steps[at][low], steps[at][high] = high, low
+    return steps
+
+
+def partner(step, mine):
+    found = jnp.int32(step[0])
+    for k in range(1, len(step)):
+        found = jnp.where(mine == k, step[k], found)
+    return found
 
 
 def halves(x):
@@ -36,20 +56,20 @@
     )
 
 
-def products_kernel(rows, planes, group, *refs):
-    tiles_hbm, row_idx_hbm, col_idx_hbm, count_hbm, diag_hbm, own_hbm = refs[:6]
+def products_kernel(steps, planes, group, *refs):
+    count, tiles_hbm, row_idx_hbm, col_idx_hbm, diag_hbm, own_hbm = refs[:6]
     refs = refs[6:]
     plane_in = refs[: planes - 1]
     core_in = refs[planes - 1 : 2 * planes - 1]
-    row_in = refs[2 * planes - 1 : 2 * planes + rows - 2]
+    row_in = refs[2 * planes - 1 : 2 * planes - 1 + len(steps)]
     (
         keep_out,
         send_out,
+        col_own,
         col_out,
         tiles,
         row_idx,
         col_idx,
-        count,
         diag,
         own,
         vec_rows,
@@ -58,7 +78,7 @@
         acc_cols,
         small_sems,
         tile_sems,
-    ) = refs[2 * planes + rows - 2 :]
+    ) = refs[2 * planes - 1 + len(steps) :]
     row = lax.axis_index("row")
     col = lax.axis_index("col")
     plane, core = col // 2, col % 2
@@ -69,7 +89,6 @@
         pltpu.make_async_copy(source, target, small_sems.at[k])
         for k, (source, target) in enumerate(
             (
-                (count_hbm, count),
                 (row_idx_hbm, row_idx),
                 (col_idx_hbm, col_idx),
                 (own_hbm, own),
@@ -82,9 +101,6 @@
         at = pl.ds(g * group, group)
         return pltpu.make_async_copy(tiles_hbm.at[at], tiles.at[at], tile_sems.at[g])
 
-    for copy in small:
-        copy.start()
-    small[0].wait()
     total = count[0, 0]
     groups = (total + group - 1) // group
 
@@ -92,7 +108,10 @@
         tile_copy(g).start()
         return carry
 
-    lax.fori_loop(0, groups, start_tiles, 0)
+    tile_copy(0).start()
+    for copy in small:
+        copy.start()
+    lax.fori_loop(1, groups, start_tiles, 0)
     acc_rows[...] = jnp.zeros_like(acc_rows)
     acc_cols[...] = jnp.zeros_like(acc_cols)
 
@@ -107,9 +126,9 @@
     for s in range(planes):
         base = jnp.bitwise_xor(plane, s) * 2 * piece_tiles
         store_split(vec_rows, base + (1 - core) * piece_tiles, core_in[s])
-    for s in range(1, rows):
-        store_split(vec_cols, jnp.bitwise_xor(row, s) * piece_tiles, row_in[s - 1])
-    for copy in small[1:]:
+    for step, source in zip(steps, row_in):
+        store_split(vec_cols, partner(step, row) * piece_tiles, source)
+    for copy in small:
         copy.wait()
     store_split(vec_rows, col * piece_tiles, own)
     store_split(vec_cols, row * piece_tiles, own)
@@ -117,7 +136,7 @@
     spare_row = acc_rows.shape[0] - 1
     spare_col = acc_cols.shape[0] - 1
 
-    def step(g, carry):
+    def multiply(g, carry):
         tile_copy(g).wait()
         for k in range(group):
             m = g * group + k
@@ -141,7 +160,7 @@
             acc_cols[jnp.where(alive, c, spare_col)] += back[:8] + back[8:]
         return carry
 
-    lax.fori_loop(0, groups, step, 0)
+    lax.fori_loop(0, groups, multiply, 0)
 
     for s in range(planes):
         base = jnp.bitwise_xor(plane, s) * 2 * piece_tiles
@@ -149,23 +168,22 @@
             at = slice(t * width, (t + 1) * width)
             keep_out[s, :, at] = acc_rows[base + core * piece_tiles + t]
             send_out[s, :, at] = acc_rows[base + (1 - core) * piece_tiles + t]
-    for s in range(rows):
-        base = jnp.bitwise_xor(row, s) * piece_tiles
+    for t in range(piece_tiles):
+        at = slice(t * width, (t + 1) * width)
+        col_own[:, at] = acc_cols[row * piece_tiles + t] + own[:, at] * diag[:, at]
+    for k, step in enumerate(steps):
+        other = partner(step, row)
+        base = other * piece_tiles
         for t in range(piece_tiles):
             at = slice(t * width, (t + 1) * width)
-            piece = acc_cols[base + t]
-            if s == 0:
-                piece = piece + own[:, at] * diag[:, at]
-            col_out[s, :, at] = piece
-
-
-def image_kernel(planes, rows, copies, *refs):
-    now, prev, keep, core, cols = refs[:5]
-    plane_in = refs[5 : 4 + planes]
-    row_in = refs[4 + planes : 3 + planes + rows]
-    image_out, sums_out = refs[3 + planes + rows :]
-    image = keep[...] + core[...] + cols[...]
-    for ref in plane_in + row_in:
+            col_out[k, :, at] = jnp.where(other == row, 0.0, acc_cols[base + t])
+
+
+def image_kernel(copies, *refs):
+    now, prev = refs[:2]
+    image_out, sums_out = refs[-2:]
+    image = refs[2][...]
+    for ref in refs[3:-2]:
         image = image + ref[...]
     image_out[...] = image
     block, last = now[...], prev[...]
@@ -173,16 +191,18 @@
     both = jnp.concatenate([block, last], axis=0)
     against = contract(image, jnp.concatenate([image, both], axis=0))
     fixed = contract(both, both)
+    half = sums_out.shape[2] // 2
     used = against.shape[1] + 2 * fixed.shape[1]
     sums = jnp.concatenate(
         [
             against,
             fixed[:vectors],
             fixed[vectors:],
-            jnp.zeros((vectors, sums_out.shape[2] - used), jnp.float32),
+            jnp.zeros((vectors, half - used), jnp.float32),
         ],
         axis=1,
     )
+    sums = jnp.concatenate([sums[: vectors // 2], sums[vectors // 2 :]], axis=1)
     for k in range(copies):
         sums_out[k] = sums
 
@@ -190,6 +210,8 @@
 def finish_kernel(states, sums_in, image, now, prev, coupling, next_out, alpha_out, beta_out):
     vectors = image.shape[0]
     sums = jnp.sum(sums_in[...], axis=0) / states
+    half = sums.shape[1] // 2
+    sums = jnp.concatenate([sums[:, :half], sums[:, half:]], axis=0)
     image_gram = sums[:, :vectors]
     alpha_t = sums[:, vectors : 2 * vectors]
     image_prev = sums[:, 2 * vectors : 3 * vectors]
@@ -235,10 +257,11 @@
     def along_col(x, s):
         return lax.ppermute(x, "col", [(i, i ^ s) for i in range(cols)])
 
-    def along_row(x, s):
-        return lax.ppermute(x, "row", [(i, i ^ s) for i in range(rows)])
-
-    row_in = [along_row(block_now, s) for s in range(1, rows)]
+    def along_row(x, step):
+        return lax.ppermute(x, "row", list(enumerate(step)))
+
+    steps = pair_steps(rows)[::-1]
+    row_in = [along_row(block_now, step) for step in steps]
     plane_in = [block_now] + [along_col(block_now, 2 * s) for s in range(1, planes)]
     core_in = [along_col(x, 1) for x in plane_in]
 
@@ -249,36 +272,38 @@
     def stay(x):
         return pltpu.with_memory_space_constraint(x, pltpu.HBM)
 
-    keep, send, col_parts = pl.pallas_call(
-        functools.partial(products_kernel, rows, planes, group),
+    keep, send, col_own, col_parts = pl.pallas_call(
+        functools.partial(products_kernel, steps, planes, group),
         out_shape=(
             jax.ShapeDtypeStruct((planes, vectors, piece), f32),
             jax.ShapeDtypeStruct((planes, vectors, piece), f32),
-            jax.ShapeDtypeStruct((rows, vectors, piece), f32),
+            piece_shape,
+            jax.ShapeDtypeStruct((len(steps), vectors, piece), f32),
         ),
-        in_specs=[in_hbm] * 3 + [pl.BlockSpec(memory_space=pl.ANY)] + [in_hbm] * 2 + [in_vmem] * (2 * planes + rows - 2),
-        out_specs=(in_vmem,) * 3,
+        in_specs=[pl.BlockSpec(memory_space=SMEM)]
+        + [in_hbm] * 5
+        + [in_vmem] * (2 * planes - 1 + len(steps)),
+        out_specs=(in_vmem,) * 4,
         scratch_shapes=[
             VMEM((slots, width, width), f32),
             SMEM(tile_rows.shape, jnp.int32),
             SMEM(tile_cols.shape, jnp.int32),
-            SMEM(tile_counts.shape, jnp.int32),
             VMEM((1, piece), f32),
             VMEM((vectors, piece), f32),
             VMEM((cols * piece_tiles, 2 * vectors, width), jnp.bfloat16),
             VMEM((rows * piece_tiles, 2 * vectors, width), jnp.bfloat16),
             VMEM((cols * piece_tiles + 1, vectors, width), f32),
             VMEM((rows * piece_tiles + 1, vectors, width), f32),
-            pltpu.SemaphoreType.DMA((5,)),
+            pltpu.SemaphoreType.DMA((4,)),
             pltpu.SemaphoreType.DMA((slots // group,)),
         ],
         compiler_params=pltpu.CompilerParams(vmem_limit_bytes=40 * MIB),
         name="products",
     )(
+        tile_counts,
         stay(tiles.reshape(slots, width, width)),
         stay(tile_rows),
         stay(tile_cols),
-        tile_counts,
         stay(diag_energy.reshape(1, piece)),
         stay(block_now),
         *plane_in[1:],
@@ -286,20 +311,24 @@
         *row_in,
     )
 
-    back_rows = [along_row(col_parts[s], s) for s in range(1, rows)]
+    back_rows = [along_row(col_parts[k], step) for k, step in enumerate(steps)]
     from_core = along_col(send, 1)
     summed = [keep[s] + from_core[s] for s in range(1, planes)]
     back_planes = [along_col(summed[s - 1], 2 * s) for s in range(1, planes)]
+    terms = [keep[0], from_core[0], col_own, *back_planes, *back_rows]
 
     devices = rows * cols
     image, sums = pl.pallas_call(
-        functools.partial(image_kernel, planes, rows, devices),
-        out_shape=(piece_shape, jax.ShapeDtypeStruct((devices, vectors, 128), f32)),
-        in_specs=[in_vmem] * (3 + planes + rows),
+        functools.partial(image_kernel, devices),
+        out_shape=(
+            piece_shape,
+            jax.ShapeDtypeStruct((devices, vectors // 2, 128), f32),
+        ),
+        in_specs=[in_vmem] * (2 + len(terms)),
         out_specs=(in_vmem,) * 2,
         compiler_params=pltpu.CompilerParams(vmem_limit_bytes=16 * MIB),
         name="image",
-    )(block_now, block_prev, keep[0], from_core[0], col_parts[0], *back_planes, *back_rows)
+    )(block_now, block_prev, *terms)
 
     sums = lax.all_to_all(sums, ("row", "col"), 0, 0)
     return pl.pallas_call(

time: 50.1 us -> 61.9 us (1.24)
  starting transfers between devices: 23 us -> 34.1 us
  blocking collectives: 13.3 us -> 14.7 us
  waiting for transfers between devices: 5.55 us -> 4.93 us
    ppermute x6 -> x10, starting transfers between devices: 15 us -> 24.6 us  [along_row(): return lax.ppermute(x, 'row', list(enumerate(step)))]
    ppermute x11, starting transfers between devices: 8.04 us -> 9.52 us  [along_col(): return lax.ppermute(x, 'col', [(i, i ^ s) for i in range(cols)])]
    all_to_all x1, blocking collectives: 13.3 us -> 14.7 us  [local(): sums = lax.all_to_all(sums, ('row', 'col'), 0, 0)]
    ppermute x6 -> x10, waiting for transfers between devices: 1.78 us -> 0.46 us  [along_row(): return lax.ppermute(x, 'row', list(enumerate(step)))]
    ppermute x11, waiting for transfers between devices: 3.77 us -> 4.48 us  [along_col(): return lax.ppermute(x, 'col', [(i, i ^ s) for i in range(cols)])]
  transfers between devices with their start and end apart: 17 -> 21, of which waited for: 9 -> 6; matrix products, arithmetic and copies ran while one was open for 0% -> 0% of each run, Pallas kernels for 0% -> 0%
where the time goes in v3:
time: 61.9 us; the launch traced here: 61.5 us
  starting transfers between devices  34.1 us (55%)
  blocking collectives  14.7 us (24%)
  Pallas kernels  6.22 us (10%)
  waiting for transfers between devices  4.93 us (8%)
  between operations  1.47 us (2%)
    ppermute x10, starting transfers between devices, along_row(): return lax.ppermute(x, 'row', list(enumerate(step)))  24.6 us
    all_to_all x1, blocking collectives, local(): sums = lax.all_to_all(sums, ('row', 'col'), 0, 0)  14.7 us
    ppermute x11, starting transfers between devices, along_col(): return lax.ppermute(x, 'col', [(i, i ^ s) for i in range(cols)])  9.52 us
    ppermute x11, waiting for transfers between devices, along_col(): return lax.ppermute(x, 'col', [(i, i ^ s) for i in range(cols)])  4.48 us
    pallas_call x1, Pallas kernels, local(): pl.pallas_call(functools.partial(products_kernel, steps, planes, group),...  3.47 us
    pallas_call x1, Pallas kernels, local(): pl.pallas_call(functools.partial(finish_kernel, float(piece * devices)),...  2.1 us
  transfers between devices with their start and end apart: 21, of which 6 were waited for; matrix products, arithmetic and copies ran while one was open for 0% of the time, Pallas kernels for 0%

profile of v3, /device:TPU:0, one launch (start us, length us, event | category | flops | bytes accessed | tf_op | source)
XLA Modules:
  0.0 61.5 jit_solution(1424115586173452747)
XLA Ops:
  0.6 0.0 copy-start
  0.6 0.0 copy-start.1
  0.7 5.1 %collective-permute-start.11 = (f32[8,2048]{1,0:T(8,128)}, f32[8,2048]{1,0:T(8,128)S(1)}, u32[]{:S(2)}, u32[]{:S(2)}) collective-permute-start(f32[8,2048]{1,0:T(8,128)} %now.1), channel_id=1, source_target_pairs={{0,8},{8,0},{16,16},{24,24},{1,9},{9,1},{17,17},{25,25},{2,10},{10... | collective-permute-start | bytes 196616 | tf_op jit(solution)/shard_map/ppermute | solution.py:261
  5.7 2.5 %collective-permute-start.10 = (f32[8,2048]{1,0:T(8,128)}, f32[8,2048]{1,0:T(8,128)S(1)}, u32[]{:S(2)}, u32[]{:S(2)}) collective-permute-start(f32[8,2048]{1,0:T(8,128)} %now.1), channel_id=1, source_target_pairs={{0,16},{8,8},{16,0},{24,24},{1,17},{9,9},{17,1},{25,25},{2,18},{10... | collective-permute-start | bytes 196616 | tf_op jit(solution)/shard_map/ppermute | solution.py:261
  8.2 0.6 collective-permute-start.9
  8.8 1.5 %collective-permute-start.8 = (f32[8,2048]{1,0:T(8,128)}, f32[8,2048]{1,0:T(8,128)S(1)}, u32[]{:S(2)}, u32[]{:S(2)}) collective-permute-start(f32[8,2048]{1,0:T(8,128)} %now.1), channel_id=1, source_target_pairs={{0,0},{8,24},{16,16},{24,8},{1,1},{9,25},{17,17},{25,9},{2,2},{10,... | collective-permute-start | bytes 196616 | tf_op jit(solution)/shard_map/ppermute | solution.py:261
  10.3 2.4 %collective-permute-start.2 = (f32[8,2048]{1,0:T(8,128)}, f32[8,2048]{1,0:T(8,128)S(1)}, u32[]{:S(2)}, u32[]{:S(2)}) collective-permute-start(f32[8,2048]{1,0:T(8,128)} %now.1), channel_id=1, source_target_pairs={{0,6},{1,7},{2,4},{3,5},{4,2},{5,3},{6,0},{7,1},{8,14},{9,15},{10,... | collective-permute-start | bytes 196616 | tf_op jit(solution)/shard_map/ppermute | solution.py:258
  12.8 0.0 collective-permute-done.11.refs_17_
  12.8 0.5 collective-permute-start.1
  13.3 0.4 collective-permute-done.10.refs_16_
  13.7 1.5 %collective-permute-start = (f32[8,2048]{1,0:T(8,128)}, f32[8,2048]{1,0:T(8,128)S(1)}, u32[]{:S(2)}, u32[]{:S(2)}) collective-permute-start(f32[8,2048]{1,0:T(8,128)} %now.1), channel_id=1, source_target_pairs={{0,2},{1,3},{2,0},{3,1},{4,6},{5,7},{6,4},{7,5},{8,10},{9,11},{10,... | collective-permute-start | bytes 196616 | tf_op jit(solution)/shard_map/ppermute | solution.py:258
  15.2 0.0 collective-permute-done.9.refs_15_
  15.2 1.5 %collective-permute-start.7 = (f32[8,2048]{1,0:T(8,128)}, f32[8,2048]{1,0:T(8,128)S(1)}, u32[]{:S(2)}, u32[]{:S(2)}) collective-permute-start(f32[8,2048]{1,0:T(8,128)} %now.1), channel_id=1, source_target_pairs={{0,0},{8,8},{16,24},{24,16},{1,1},{9,9},{17,25},{25,17},{2,2},{10,... | collective-permute-start | bytes 196616 | tf_op jit(solution)/shard_map/ppermute | solution.py:261
  16.7 0.0 collective-permute-done.8.refs_14_
  16.7 0.0 collective-permute-start.3
  16.7 0.0 collective-permute-done.2.refs_8_
  16.7 0.5 collective-permute-start.6
  17.2 0.0 collective-permute-done.1.refs_7_
  17.2 0.0 collective-permute-start.5
  17.3 0.9 %collective-permute-done.refs_6_ = f32[8,2048]{1,0:T(8,128)S(1)} collective-permute-done((f32[8,2048]{1,0:T(8,128)}, f32[8,2048]{1,0:T(8,128)S(1)}, u32[]{:S(2)}, u32[]{:S(2)}) %collective-permute-start) | collective-permute-done | bytes 65568 | tf_op jit(solution)/shard_map/ppermute | solution.py:258
  18.2 0.0 collective-permute-start.4
  18.8 0.0 collective-permute-done.7.refs_13_
  18.8 0.0 collective-permute-done.3.refs_9_
  18.9 0.0 collective-permute-done.6.refs_12_
  18.9 0.0 collective-permute-done.5.refs_11_
  18.9 0.6 collective-permute-done.4.refs_10_
  19.4 3.5 %products.1 = (f32[4,8,2048]{2,1,0:T(8,128)S(1)}, f32[4,8,2048]{2,1,0:T(8,128)S(1)}, f32[8,2048]{1,0:T(8,128)S(1)}, f32[5,8,2048]{2,1,0:T(8,128)S(1)}) custom-call(s32[1,1]{1,0:T(1,128)S(6)} %copy.11.refs_0_, f32[256,128,128]{2,1,0:T(8,128)} %bitcast.22, s32[1,1,256]{2,1,0:T(1,128)} %refs_2_.1, s32[1,1,256]{2,1,0:T(1,128)} %refs_3_.1, f32[1,2048]{1,0:T(1,128)} %bitcast.23, ...), custom_call_target="tpu_custom_call" | custom-call | tf_op jit(solution)/shard_map/products/pallas_call | solution.py:275
  22.9 0.2 collective-permute-start.12
  23.2 7.4 %collective-permute-start.20 = (f32[8,2048]{1,0:T(8,128)S(1)}, f32[8,2048]{1,0:T(8,128)S(1)}, u32[]{:S(2)}, u32[]{:S(2)}) collective-permute-start(f32[8,2048]{1,0:T(8,128)S(1)} %get-tuple-element.18), channel_id=1, source_target_pairs={{0,8},{8,0},{16,16},{24,24},{1,9},{9,1},{17,17},{25,25},{2,10},{10... | collective-permute-start | bytes 196616 | tf_op jit(solution)/shard_map/ppermute | solution.py:261
  30.6 2.8 %collective-permute-start.19 = (f32[8,2048]{1,0:T(8,128)S(1)}, f32[8,2048]{1,0:T(8,128)S(1)}, u32[]{:S(2)}, u32[]{:S(2)}) collective-permute-start(f32[8,2048]{1,0:T(8,128)S(1)} %get-tuple-element.19), channel_id=1, source_target_pairs={{0,16},{8,8},{16,0},{24,24},{1,17},{9,9},{17,1},{25,25},{2,18},{10... | collective-permute-start | bytes 196616 | tf_op jit(solution)/shard_map/ppermute | solution.py:261
  33.5 1.9 %collective-permute-start.18 = (f32[8,2048]{1,0:T(8,128)S(1)}, f32[8,2048]{1,0:T(8,128)S(1)}, u32[]{:S(2)}, u32[]{:S(2)}) collective-permute-start(f32[8,2048]{1,0:T(8,128)S(1)} %get-tuple-element.20), channel_id=1, source_target_pairs={{0,24},{8,16},{16,8},{24,0},{1,25},{9,17},{17,9},{25,1},{2,26},{10... | collective-permute-start | bytes 196616 | tf_op jit(solution)/shard_map/ppermute | solution.py:261
  35.3 0.7 %collective-permute-start.17 = (f32[8,2048]{1,0:T(8,128)S(1)}, f32[8,2048]{1,0:T(8,128)S(1)}, u32[]{:S(2)}, u32[]{:S(2)}) collective-permute-start(f32[8,2048]{1,0:T(8,128)S(1)} %get-tuple-element.21), channel_id=1, source_target_pairs={{0,0},{8,24},{16,16},{24,8},{1,1},{9,25},{17,17},{25,9},{2,2},{10,... | collective-permute-start | bytes 196616 | tf_op jit(solution)/shard_map/ppermute | solution.py:261
  36.0 0.0 collective-permute-done.12
  36.0 0.7 %collective-permute-start.16 = (f32[8,2048]{1,0:T(8,128)S(1)}, f32[8,2048]{1,0:T(8,128)S(1)}, u32[]{:S(2)}, u32[]{:S(2)}) collective-permute-start(f32[8,2048]{1,0:T(8,128)S(1)} %get-tuple-element.22), channel_id=1, source_target_pairs={{0,0},{8,8},{16,24},{24,16},{1,1},{9,9},{17,25},{25,17},{2,2},{10,... | collective-permute-start | bytes 196616 | tf_op jit(solution)/shard_map/ppermute | solution.py:261
  36.7 0.0 collective-permute-done.20.refs_12_
  36.7 2.5 %collective-permute-start.15 = (f32[8,2048]{1,0:T(8,128)S(1)}, f32[8,2048]{1,0:T(8,128)S(1)}, u32[]{:S(2)}, u32[]{:S(2)}) collective-permute-start(f32[8,2048]{1,0:T(8,128)S(1)} %get-tuple-element.15), channel_id=1, source_target_pairs={{0,6},{1,7},{2,4},{3,5},{4,2},{5,3},{6,0},{7,1},{8,14},{9,15},{10,... | collective-permute-start | bytes 196616 | tf_op jit(solution)/shard_map/ppermute | solution.py:258
  39.2 0.0 collective-permute-done.19.refs_11_
  39.2 0.5 collective-permute-start.14
  39.7 0.0 collective-permute-done.18.refs_10_
  39.8 1.3 %collective-permute-start.13 = (f32[8,2048]{1,0:T(8,128)S(1)}, f32[8,2048]{1,0:T(8,128)S(1)}, u32[]{:S(2)}, u32[]{:S(2)}) collective-permute-start(f32[8,2048]{1,0:T(8,128)S(1)} %get-tuple-element.17), channel_id=1, source_target_pairs={{0,2},{1,3},{2,0},{3,1},{4,6},{5,7},{6,4},{7,5},{8,10},{9,11},{10,... | collective-permute-start | bytes 196616 | tf_op jit(solution)/shard_map/ppermute | solution.py:258
  41.0 0.0 collective-permute-done.17.refs_9_
  41.0 0.0 collective-permute-done.16.refs_8_
  41.0 0.9 %collective-permute-done.15.refs_7_ = f32[8,2048]{1,0:T(8,128)S(1)} collective-permute-done((f32[8,2048]{1,0:T(8,128)S(1)}, f32[8,2048]{1,0:T(8,128)S(1)}, u32[]{:S(2)}, u32[]{:S(2)}) %collective-permute-start.15) | collective-permute-done | bytes 65568 | tf_op jit(solution)/shard_map/ppermute | solution.py:258
  42.0 1.5 %collective-permute-done.14.refs_6_ = f32[8,2048]{1,0:T(8,128)S(1)} collective-permute-done((f32[8,2048]{1,0:T(8,128)S(1)}, f32[8,2048]{1,0:T(8,128)S(1)}, u32[]{:S(2)}, u32[]{:S(2)}) %collective-permute-start.14) | collective-permute-done | bytes 65568 | tf_op jit(solution)/shard_map/ppermute | solution.py:258
  43.5 0.5 collective-permute-done.13.refs_5_
  44.0 0.6 %image.1 = (f32[8,2048]{1,0:T(8,128)S(1)}, f32[32,4,128]{2,1,0:T(4,128)S(1)}) custom-call(f32[8,2048]{1,0:T(8,128)S(1)} %copy-done, f32[8,2048]{1,0:T(8,128)S(1)} %copy-done.1, f32[8,2048]{1,0:T(8,128)S(1)} %get-tuple-element.23.refs_2_, f32[8,2048]{1,0:T(8,128)S(1)} %get-tuple-element.24.refs_3_, f32[8,2048]{1,0:T(8,128)S(1)} %get-tuple-element.11.refs_4_, ...), custom_call_target="tpu_custom_call" | custom-call | tf_op jit(solution)/shard_map/image/pallas_call | solution.py:321
  44.7 14.7 %all_to_all.5.sums_in = f32[32,4,128]{2,1,0:T(4,128)S(1)} all-to-all(f32[32,4,128]{2,1,0:T(4,128)S(1)} %get-tuple-element.13), channel_id=1, replica_groups=mesh['row'=4,'col'=8] {'row','col'}, dimensions={0} | all-to-all | bytes 131072 | tf_op jit(solution)/shard_map/all_to_all | solution.py:333
  59.4 2.1 %finish.1 = (f32[8,2048]{1,0:T(8,128)}, f32[8,8]{1,0:T(8,128)}, f32[8,8]{1,0:T(8,128)}) custom-call(f32[32,4,128]{2,1,0:T(4,128)S(1)} %all_to_all.5.sums_in, f32[8,2048]{1,0:T(8,128)S(1)} %get-tuple-element.14.image, f32[8,2048]{1,0:T(8,128)S(1)} %copy-done, f32[8,2048]{1,0:T(8,128)S(1)} %copy-done.1, f32[8,8]{1,0:T(8,128)S(1)} %copy-done.2), custom_call_target="tpu_custom_call" | custom-call | tf_op jit(solution)/shard_map/finish/pallas_call | solution.py:334
  (6 shorter events, 0.1 us)
Async XLA Ops:
  0.6 43.4 %copy-start = (f32[8,2048]{1,0:T(8,128)S(1)}, f32[8,2048]{1,0:T(8,128)}, u32[]{:S(2)}) copy-start(f32[8,2048]{1,0:T(8,128)} %now.1) | copy-start | bytes 196612
  0.6 43.4 %copy-start.1 = (f32[8,2048]{1,0:T(8,128)S(1)}, f32[8,2048]{1,0:T(8,128)}, u32[]{:S(2)}) copy-start(f32[8,2048]{1,0:T(8,128)} %prev.1) | copy-start | bytes 196612
  0.7 58.8 %copy-start.2 = (f32[8,8]{1,0:T(8,128)S(1)}, f32[8,8]{1,0:T(8,128)}, u32[]{:S(2)}) copy-start(f32[8,8]{1,0:T(8,128)} %coupling.1) | copy-start | bytes 772
  0.7 12.1 %collective-permute-start.11 = (f32[8,2048]{1,0:T(8,128)}, f32[8,2048]{1,0:T(8,128)S(1)}, u32[]{:S(2)}, u32[]{:S(2)}) collective-permute-start(f32[8,2048]{1,0:T(8,128)} %now.1), channel_id=1, source_target_pairs={{0,8},{8,0},{16,16},{24,24},{1,9},{9,1},{17,17},{25,25},{2,10},{10... | collective-permute-start | bytes 196616 | tf_op jit(solution)/shard_map/ppermute | solution.py:261
  5.7 8.0 %collective-permute-start.10 = (f32[8,2048]{1,0:T(8,128)}, f32[8,2048]{1,0:T(8,128)S(1)}, u32[]{:S(2)}, u32[]{:S(2)}) collective-permute-start(f32[8,2048]{1,0:T(8,128)} %now.1), channel_id=1, source_target_pairs={{0,16},{8,8},{16,0},{24,24},{1,17},{9,9},{17,1},{25,25},{2,18},{10... | collective-permute-start | bytes 196616 | tf_op jit(solution)/shard_map/ppermute | solution.py:261
  8.2 7.0 %collective-permute-start.9 = (f32[8,2048]{1,0:T(8,128)}, f32[8,2048]{1,0:T(8,128)S(1)}, u32[]{:S(2)}, u32[]{:S(2)}) collective-permute-start(f32[8,2048]{1,0:T(8,128)} %now.1), channel_id=1, source_target_pairs={{0,24},{8,16},{16,8},{24,0},{1,25},{9,17},{17,9},{25,1},{2,26},{10... | collective-permute-start | bytes 196616 | tf_op jit(solution)/shard_map/ppermute | solution.py:261
  8.8 7.9 %collective-permute-start.8 = (f32[8,2048]{1,0:T(8,128)}, f32[8,2048]{1,0:T(8,128)S(1)}, u32[]{:S(2)}, u32[]{:S(2)}) collective-permute-start(f32[8,2048]{1,0:T(8,128)} %now.1), channel_id=1, source_target_pairs={{0,0},{8,24},{16,16},{24,8},{1,1},{9,25},{17,17},{25,9},{2,2},{10,... | collective-permute-start | bytes 196616 | tf_op jit(solution)/shard_map/ppermute | solution.py:261
  10.3 6.4 %collective-permute-start.2 = (f32[8,2048]{1,0:T(8,128)}, f32[8,2048]{1,0:T(8,128)S(1)}, u32[]{:S(2)}, u32[]{:S(2)}) collective-permute-start(f32[8,2048]{1,0:T(8,128)} %now.1), channel_id=1, source_target_pairs={{0,6},{1,7},{2,4},{3,5},{4,2},{5,3},{6,0},{7,1},{8,14},{9,15},{10,... | collective-permute-start | bytes 196616 | tf_op jit(solution)/shard_map/ppermute | solution.py:258
  12.8 4.5 %collective-permute-start.1 = (f32[8,2048]{1,0:T(8,128)}, f32[8,2048]{1,0:T(8,128)S(1)}, u32[]{:S(2)}, u32[]{:S(2)}) collective-permute-start(f32[8,2048]{1,0:T(8,128)} %now.1), channel_id=1, source_target_pairs={{0,4},{1,5},{2,6},{3,7},{4,0},{5,1},{6,2},{7,3},{8,12},{9,13},{10,... | collective-permute-start | bytes 196616 | tf_op jit(solution)/shard_map/ppermute | solution.py:258
  13.7 4.5 %collective-permute-start = (f32[8,2048]{1,0:T(8,128)}, f32[8,2048]{1,0:T(8,128)S(1)}, u32[]{:S(2)}, u32[]{:S(2)}) collective-permute-start(f32[8,2048]{1,0:T(8,128)} %now.1), channel_id=1, source_target_pairs={{0,2},{1,3},{2,0},{3,1},{4,6},{5,7},{6,4},{7,5},{8,10},{9,11},{10,... | collective-permute-start | bytes 196616 | tf_op jit(solution)/shard_map/ppermute | solution.py:258
  15.2 3.6 %collective-permute-start.7 = (f32[8,2048]{1,0:T(8,128)}, f32[8,2048]{1,0:T(8,128)S(1)}, u32[]{:S(2)}, u32[]{:S(2)}) collective-permute-start(f32[8,2048]{1,0:T(8,128)} %now.1), channel_id=1, source_target_pairs={{0,0},{8,8},{16,24},{24,16},{1,1},{9,9},{17,25},{25,17},{2,2},{10,... | collective-permute-start | bytes 196616 | tf_op jit(solution)/shard_map/ppermute | solution.py:261
  16.7 2.2 %collective-permute-start.3 = (f32[8,2048]{1,0:T(8,128)}, f32[8,2048]{1,0:T(8,128)S(1)}, u32[]{:S(2)}, u32[]{:S(2)}) collective-permute-start(f32[8,2048]{1,0:T(8,128)} %now.1), channel_id=1, source_target_pairs={{0,1},{1,0},{2,3},{3,2},{4,5},{5,4},{6,7},{7,6},{8,9},{9,8},{10,11... | collective-permute-start | bytes 196616 | tf_op jit(solution)/shard_map/ppermute | solution.py:258
  16.7 2.2 %collective-permute-start.6 = (f32[8,2048]{1,0:T(8,128)S(1)}, f32[8,2048]{1,0:T(8,128)S(1)}, u32[]{:S(2)}, u32[]{:S(2)}) collective-permute-start(f32[8,2048]{1,0:T(8,128)S(1)} %collective-permute-done.2.refs_8_), channel_id=1, source_target_pairs={{0,1},{1,0},{2,3},{3,2},{4,5},{5,4},{6,7},{7,6},{8,9},{9,8},{10,11... | collective-permute-start | bytes 196616 | tf_op jit(solution)/shard_map/ppermute | solution.py:258
  17.2 1.6 %collective-permute-start.5 = (f32[8,2048]{1,0:T(8,128)S(1)}, f32[8,2048]{1,0:T(8,128)S(1)}, u32[]{:S(2)}, u32[]{:S(2)}) collective-permute-start(f32[8,2048]{1,0:T(8,128)S(1)} %collective-permute-done.1.refs_7_), channel_id=1, source_target_pairs={{0,1},{1,0},{2,3},{3,2},{4,5},{5,4},{6,7},{7,6},{8,9},{9,8},{10,11... | collective-permute-start | bytes 196616 | tf_op jit(solution)/shard_map/ppermute | solution.py:258
  18.2 1.3 %collective-permute-start.4 = (f32[8,2048]{1,0:T(8,128)S(1)}, f32[8,2048]{1,0:T(8,128)S(1)}, u32[]{:S(2)}, u32[]{:S(2)}) collective-permute-start(f32[8,2048]{1,0:T(8,128)S(1)} %collective-permute-done.refs_6_), channel_id=1, source_target_pairs={{0,1},{1,0},{2,3},{3,2},{4,5},{5,4},{6,7},{7,6},{8,9},{9,8},{10,11... | collective-permute-start | bytes 196616 | tf_op jit(solution)/shard_map/ppermute | solution.py:258
  22.9 13.1 %collective-permute-start.12 = (f32[4,8,2048]{2,1,0:T(8,128)S(1)}, f32[4,8,2048]{2,1,0:T(8,128)S(1)}, u32[]{:S(2)}, u32[]{:S(2)}) collective-permute-start(f32[4,8,2048]{2,1,0:T(8,128)S(1)} %get-tuple-element.10), channel_id=1, source_target_pairs={{0,1},{1,0},{2,3},{3,2},{4,5},{5,4},{6,7},{7,6},{8,9},{9,8},{10,11... | collective-permute-start | bytes 786440 | tf_op jit(solution)/shard_map/ppermute | solution.py:258
  23.2 13.6 %collective-permute-start.20 = (f32[8,2048]{1,0:T(8,128)S(1)}, f32[8,2048]{1,0:T(8,128)S(1)}, u32[]{:S(2)}, u32[]{:S(2)}) collective-permute-start(f32[8,2048]{1,0:T(8,128)S(1)} %get-tuple-element.18), channel_id=1, source_target_pairs={{0,8},{8,0},{16,16},{24,24},{1,9},{9,1},{17,17},{25,25},{2,10},{10... | collective-permute-start | bytes 196616 | tf_op jit(solution)/shard_map/ppermute | solution.py:261
  30.6 8.6 %collective-permute-start.19 = (f32[8,2048]{1,0:T(8,128)S(1)}, f32[8,2048]{1,0:T(8,128)S(1)}, u32[]{:S(2)}, u32[]{:S(2)}) collective-permute-start(f32[8,2048]{1,0:T(8,128)S(1)} %get-tuple-element.19), channel_id=1, source_target_pairs={{0,16},{8,8},{16,0},{24,24},{1,17},{9,9},{17,1},{25,25},{2,18},{10... | collective-permute-start | bytes 196616 | tf_op jit(solution)/shard_map/ppermute | solution.py:261
  33.5 6.3 %collective-permute-start.18 = (f32[8,2048]{1,0:T(8,128)S(1)}, f32[8,2048]{1,0:T(8,128)S(1)}, u32[]{:S(2)}, u32[]{:S(2)}) collective-permute-start(f32[8,2048]{1,0:T(8,128)S(1)} %get-tuple-element.20), channel_id=1, source_target_pairs={{0,24},{8,16},{16,8},{24,0},{1,25},{9,17},{17,9},{25,1},{2,26},{10... | collective-permute-start | bytes 196616 | tf_op jit(solution)/shard_map/ppermute | solution.py:261
  35.3 5.7 %collective-permute-start.17 = (f32[8,2048]{1,0:T(8,128)S(1)}, f32[8,2048]{1,0:T(8,128)S(1)}, u32[]{:S(2)}, u32[]{:S(2)}) collective-permute-start(f32[8,2048]{1,0:T(8,128)S(1)} %get-tuple-element.21), channel_id=1, source_target_pairs={{0,0},{8,24},{16,16},{24,8},{1,1},{9,25},{17,17},{25,9},{2,2},{10,... | collective-permute-start | bytes 196616 | tf_op jit(solution)/shard_map/ppermute | solution.py:261
  36.0 5.0 %collective-permute-start.16 = (f32[8,2048]{1,0:T(8,128)S(1)}, f32[8,2048]{1,0:T(8,128)S(1)}, u32[]{:S(2)}, u32[]{:S(2)}) collective-permute-start(f32[8,2048]{1,0:T(8,128)S(1)} %get-tuple-element.22), channel_id=1, source_target_pairs={{0,0},{8,8},{16,24},{24,16},{1,1},{9,9},{17,25},{25,17},{2,2},{10,... | collective-permute-start | bytes 196616 | tf_op jit(solution)/shard_map/ppermute | solution.py:261
  36.7 5.2 %collective-permute-start.15 = (f32[8,2048]{1,0:T(8,128)S(1)}, f32[8,2048]{1,0:T(8,128)S(1)}, u32[]{:S(2)}, u32[]{:S(2)}) collective-permute-start(f32[8,2048]{1,0:T(8,128)S(1)} %get-tuple-element.15), channel_id=1, source_target_pairs={{0,6},{1,7},{2,4},{3,5},{4,2},{5,3},{6,0},{7,1},{8,14},{9,15},{10,... | collective-permute-start | bytes 196616 | tf_op jit(solution)/shard_map/ppermute | solution.py:258
  39.2 4.3 %collective-permute-start.14 = (f32[8,2048]{1,0:T(8,128)S(1)}, f32[8,2048]{1,0:T(8,128)S(1)}, u32[]{:S(2)}, u32[]{:S(2)}) collective-permute-start(f32[8,2048]{1,0:T(8,128)S(1)} %get-tuple-element.16), channel_id=1, source_target_pairs={{0,4},{1,5},{2,6},{3,7},{4,0},{5,1},{6,2},{7,3},{8,12},{9,13},{10,... | collective-permute-start | bytes 196616 | tf_op jit(solution)/shard_map/ppermute | solution.py:258
  39.8 4.3 %collective-permute-start.13 = (f32[8,2048]{1,0:T(8,128)S(1)}, f32[8,2048]{1,0:T(8,128)S(1)}, u32[]{:S(2)}, u32[]{:S(2)}) collective-permute-start(f32[8,2048]{1,0:T(8,128)S(1)} %get-tuple-element.17), channel_id=1, source_target_pairs={{0,2},{1,3},{2,0},{3,1},{4,6},{5,7},{6,4},{7,5},{8,10},{9,11},{10,... | collective-permute-start | bytes 196616 | tf_op jit(solution)/shard_map/ppermute | solution.py:258

commit v4 on v3

--- a/solution.py
+++ b/solution.py
@@ -12,26 +12,6 @@
 SMEM = pltpu.SMEM
 GROUP = 32
 MIB = 1 << 20
-
-
-def pair_steps(count):
-    last = [0] * count
-    steps = []
-    for high in range(1, count):
-        for low in range(high):
-            at = max(last[low], last[high])
-            last[low] = last[high] = at + 1
-            if at == len(steps):
-                steps.append(list(range(count)))
-            steps[at][low], steps[at][high] = high, low
-    return steps
-
-
-def partner(step, mine):
-    found = jnp.int32(step[0])
-    for k in range(1, len(step)):
-        found = jnp.where(mine == k, step[k], found)
-    return found
 
 
 def halves(x):
@@ -56,16 +36,14 @@
     )
 
 
-def products_kernel(steps, planes, group, *refs):
-    count, tiles_hbm, row_idx_hbm, col_idx_hbm, diag_hbm, own_hbm = refs[:6]
-    refs = refs[6:]
-    plane_in = refs[: planes - 1]
-    core_in = refs[planes - 1 : 2 * planes - 1]
-    row_in = refs[2 * planes - 1 : 2 * planes - 1 + len(steps)]
+def products_kernel(rows, planes, group, *refs):
+    peers = max(planes, rows) - 1
+    count, tiles_hbm, row_idx_hbm, col_idx_hbm, diag_hbm, own_hbm, beside = refs[:7]
+    fetched = refs[7 : 7 + peers]
+    passed = refs[7 + peers : 7 + 2 * peers]
     (
         keep_out,
         send_out,
-        col_own,
         col_out,
         tiles,
         row_idx,
@@ -78,12 +56,14 @@
         acc_cols,
         small_sems,
         tile_sems,
-    ) = refs[2 * planes - 1 + len(steps) :]
+    ) = refs[7 + 2 * peers :]
     row = lax.axis_index("row")
     col = lax.axis_index("col")
     plane, core = col // 2, col % 2
+    vectors = own.shape[0]
     width = tiles.shape[-1]
     piece_tiles = own.shape[1] // width
+    first = core == 0
 
     small = [
         pltpu.make_async_copy(source, target, small_sems.at[k])
@@ -115,23 +95,33 @@
     acc_rows[...] = jnp.zeros_like(acc_rows)
     acc_cols[...] = jnp.zeros_like(acc_cols)
 
-    def store_split(target, base, source):
+    def store_split(target, base, read):
         for t in range(piece_tiles):
-            high, low = halves(source[:, t * width : (t + 1) * width])
+            high, low = halves(read(slice(t * width, (t + 1) * width)))
             target[base + t] = jnp.concatenate([high, low], axis=0)
 
     for s in range(1, planes):
         base = jnp.bitwise_xor(plane, s) * 2 * piece_tiles
-        store_split(vec_rows, base + core * piece_tiles, plane_in[s - 1])
-    for s in range(planes):
-        base = jnp.bitwise_xor(plane, s) * 2 * piece_tiles
-        store_split(vec_rows, base + (1 - core) * piece_tiles, core_in[s])
-    for step, source in zip(steps, row_in):
-        store_split(vec_cols, partner(step, row) * piece_tiles, source)
+        for side in range(2):
+            part = slice(side * vectors, (side + 1) * vectors)
+            store_split(
+                vec_rows,
+                base + side * piece_tiles,
+                lambda at: jnp.where(first, fetched[s - 1][part, at], passed[s - 1][part, at]),
+            )
+    for s in range(1, rows):
+        store_split(
+            vec_cols,
+            jnp.bitwise_xor(row, s) * piece_tiles,
+            lambda at: jnp.where(
+                first, passed[s - 1][vectors:, at], fetched[s - 1][:vectors, at]
+            ),
+        )
+    store_split(vec_rows, (col + 1 - 2 * core) * piece_tiles, lambda at: beside[:, at])
     for copy in small:
         copy.wait()
-    store_split(vec_rows, col * piece_tiles, own)
-    store_split(vec_cols, row * piece_tiles, own)
+    store_split(vec_rows, col * piece_tiles, lambda at: own[:, at])
+    store_split(vec_cols, row * piece_tiles, lambda at: own[:, at])
 
     spare_row = acc_rows.shape[0] - 1
     spare_col = acc_cols.shape[0] - 1
@@ -168,15 +158,14 @@
             at = slice(t * width, (t + 1) * width)
             keep_out[s, :, at] = acc_rows[base + core * piece_tiles + t]
             send_out[s, :, at] = acc_rows[base + (1 - core) * piece_tiles + t]
-    for t in range(piece_tiles):
-        at = slice(t * width, (t + 1) * width)
-        col_own[:, at] = acc_cols[row * piece_tiles + t] + own[:, at] * diag[:, at]
-    for k, step in enumerate(steps):
-        other = partner(step, row)
-        base = other * piece_tiles
+    for s in range(rows):
+        base = jnp.bitwise_xor(row, s) * piece_tiles
         for t in range(piece_tiles):
             at = slice(t * width, (t + 1) * width)
-            col_out[k, :, at] = jnp.where(other == row, 0.0, acc_cols[base + t])
+            piece = acc_cols[base + t]
+            if s == 0:
+                piece = piece + own[:, at] * diag[:, at]
+            col_out[s, :, at] = piece
 
 
 def image_kernel(copies, *refs):
@@ -257,13 +246,25 @@
     def along_col(x, s):
         return lax.ppermute(x, "col", [(i, i ^ s) for i in range(cols)])
 
-    def along_row(x, step):
-        return lax.ppermute(x, "row", list(enumerate(step)))
-
-    steps = pair_steps(rows)[::-1]
-    row_in = [along_row(block_now, step) for step in steps]
-    plane_in = [block_now] + [along_col(block_now, 2 * s) for s in range(1, planes)]
-    core_in = [along_col(x, 1) for x in plane_in]
+    def along_row(x, s):
+        return lax.ppermute(x, "row", [(i, i ^ s) for i in range(rows)])
+
+    def apart(x, s):
+        pairs = []
+        for r in range(rows):
+            for c in range(cols):
+                if c % 2 == 0:
+                    to = (r, c ^ (2 * s) if s < planes else c)
+                else:
+                    to = (r ^ s if s < rows else r, c)
+                pairs.append((r * cols + c, to[0] * cols + to[1]))
+        return lax.ppermute(x, ("row", "col"), pairs)
+
+    beside = along_col(block_now, 1)
+    chip = jnp.concatenate([block_now, beside], axis=0)
+    peers = range(1, max(planes, rows))
+    fetched = [apart(chip, s) for s in peers]
+    passed = [along_col(x, 1) for x in fetched]
 
     in_vmem = pl.BlockSpec(memory_space=VMEM)
     in_hbm = pl.BlockSpec(memory_space=pltpu.HBM)
@@ -272,18 +273,17 @@
     def stay(x):
         return pltpu.with_memory_space_constraint(x, pltpu.HBM)
 
-    keep, send, col_own, col_parts = pl.pallas_call(
-        functools.partial(products_kernel, steps, planes, group),
+    keep, send, col_parts = pl.pallas_call(
+        functools.partial(products_kernel, rows, planes, group),
         out_shape=(
             jax.ShapeDtypeStruct((planes, vectors, piece), f32),
             jax.ShapeDtypeStruct((planes, vectors, piece), f32),
-            piece_shape,
-            jax.ShapeDtypeStruct((len(steps), vectors, piece), f32),
+            jax.ShapeDtypeStruct((rows, vectors, piece), f32),
         ),
         in_specs=[pl.BlockSpec(memory_space=SMEM)]
         + [in_hbm] * 5
-        + [in_vmem] * (2 * planes - 1 + len(steps)),
-        out_specs=(in_vmem,) * 4,
+        + [in_vmem] * (1 + 2 * len(peers)),
+        out_specs=(in_vmem,) * 3,
         scratch_shapes=[
             VMEM((slots, width, width), f32),
             SMEM(tile_rows.shape, jnp.int32),
@@ -306,16 +306,16 @@
         stay(tile_cols),
         stay(diag_energy.reshape(1, piece)),
         stay(block_now),
-        *plane_in[1:],
-        *core_in,
-        *row_in,
-    )
-
-    back_rows = [along_row(col_parts[k], step) for k, step in enumerate(steps)]
+        beside,
+        *fetched,
+        *passed,
+    )
+
+    back_rows = [along_row(col_parts[s], s) for s in range(1, rows)]
     from_core = along_col(send, 1)
     summed = [keep[s] + from_core[s] for s in range(1, planes)]
     back_planes = [along_col(summed[s - 1], 2 * s) for s in range(1, planes)]
-    terms = [keep[0], from_core[0], col_own, *back_planes, *back_rows]
+    terms = [keep[0], from_core[0], col_parts[0], *back_planes, *back_rows]
 
     devices = rows * cols
     image, sums = pl.pallas_call(

time: 61.9 us -> 48.9 us (0.79)
  starting transfers between devices: 34.1 us -> 19.2 us
  waiting for transfers between devices: 4.93 us -> 8.38 us
  blocking collectives: 14.7 us -> 12.6 us
  local copies, waits for them, and re-layouts: 0.03 us -> 0.88 us
    ppermute x10 -> x6, starting transfers between devices: 24.6 us -> 12.5 us  [the longest x3 8.08 us: along_row(): return lax.ppermute(x, 'row', [(i, i ^ s) for i in range(rows)])]
    ppermute x10 -> x6, waiting for transfers between devices: 0.46 us -> 5.12 us  [the longest x3 3.78 us: apart(): return lax.ppermute(x, ('row', 'col'), pairs)]
    ppermute x11 -> x8, starting transfers between devices: 9.52 us -> 6.74 us  [along_col(): return lax.ppermute(x, 'col', [(i, i ^ s) for i in range(cols)])]
    all_to_all x1, blocking collectives: 14.7 us -> 12.6 us  [local(): sums = lax.all_to_all(sums, ('row', 'col'), 0, 0)]
    ppermute x11 -> x8, waiting for transfers between devices: 4.48 us -> 3.26 us  [along_col(): return lax.ppermute(x, 'col', [(i, i ^ s) for i in range(cols)])]
    unnamed x6 -> x7, local copies, waits for them, and re-layouts: 0.01 us -> 0.86 us
  transfers between devices with their start and end apart: 21 -> 14, of which waited for: 6 -> 10; matrix products, arithmetic and copies ran while one was open for 0% -> 2% of each run, Pallas kernels for 0% -> 0%
where the time goes in v4:
time: 48.9 us; the launch traced here: 48.7 us
  starting transfers between devices  19.2 us (39%)
  blocking collectives  12.6 us (26%)
  waiting for transfers between devices  8.38 us (17%)
  Pallas kernels  6.2 us (13%)
  between operations  1.37 us (3%)
  local copies, waits for them, and re-layouts  0.88 us (2%)
    all_to_all x1, blocking collectives, local(): sums = lax.all_to_all(sums, ('row', 'col'), 0, 0)  12.6 us
    ppermute x3, starting transfers between devices, along_row(): return lax.ppermute(x, 'row', [(i, i ^ s) for i in range(rows)])  8.08 us
    ppermute x8, starting transfers between devices, along_col(): return lax.ppermute(x, 'col', [(i, i ^ s) for i in range(cols)])  6.74 us
    ppermute x3, starting transfers between devices, apart(): return lax.ppermute(x, ('row', 'col'), pairs)  4.43 us
    ppermute x3, waiting for transfers between devices, apart(): return lax.ppermute(x, ('row', 'col'), pairs)  3.78 us
    pallas_call x1, Pallas kernels, local(): pl.pallas_call(functools.partial(products_kernel, rows, planes, group), o...  3.46 us
    ppermute x8, waiting for transfers between devices, along_col(): return lax.ppermute(x, 'col', [(i, i ^ s) for i in range(cols)])  3.26 us
    pallas_call x1, Pallas kernels, local(): pl.pallas_call(functools.partial(finish_kernel, float(piece * devices)),...  2.1 us
  transfers between devices with their start and end apart: 14, of which 10 were waited for; matrix products, arithmetic and copies ran while one was open for 2% of the time, Pallas kernels for 0%

profile of v4, /device:TPU:0, one launch (start us, length us, event | category | flops | bytes accessed | tf_op | source)
XLA Modules:
  0.0 48.7 jit_solution(16722287023060108073)
XLA Ops:
  0.6 0.0 copy-start
  0.6 0.0 copy-start.1
  0.7 0.0 copy-start.2
  0.7 0.5 %collective-permute-start = (f32[8,2048]{1,0:T(8,128)}, f32[8,2048]{1,0:T(8,128)S(1)}, u32[]{:S(2)}, u32[]{:S(2)}) collective-permute-start(f32[8,2048]{1,0:T(8,128)} %now.1), channel_id=1, source_target_pairs={{0,1},{1,0},{2,3},{3,2},{4,5},{5,4},{6,7},{7,6},{8,9},{9,8},{10,11... | collective-permute-start | bytes 196616 | tf_op jit(solution)/shard_map/ppermute | solution.py:247
  1.2 0.8 %constant_dynamic-update-slice_fusion.1 = f32[16,2048]{1,0:T(8,128)S(1)} fusion(f32[8,2048]{1,0:T(8,128)} %now.1), kind=kLoop, calls=%fused_computation.13 | loop fusion | bytes 131072
  2.0 0.3 collective-permute-done.refs_6_
  2.3 3.8 %collective-permute-start.3 = (f32[16,2048]{1,0:T(8,128)S(1)}, f32[16,2048]{1,0:T(8,128)S(1)}, u32[]{:S(2)}, u32[]{:S(2)}) collective-permute-start(f32[16,2048]{1,0:T(8,128)S(1)} %constant_dynamic-update-slice_fusion), channel_id=1, source_target_pairs={{0,6},{1,25},{2,4},{3,27},{4,2},{5,29},{6,0},{7,31},{8,14},{9,17},... | collective-permute-start | bytes 393224 | tf_op jit(solution)/shard_map/ppermute | solution.py:261
  6.1 0.5 %collective-permute-start.2 = (f32[16,2048]{1,0:T(8,128)S(1)}, f32[16,2048]{1,0:T(8,128)S(1)}, u32[]{:S(2)}, u32[]{:S(2)}) collective-permute-start(f32[16,2048]{1,0:T(8,128)S(1)} %constant_dynamic-update-slice_fusion), channel_id=1, source_target_pairs={{0,4},{1,17},{2,6},{3,19},{4,0},{5,21},{6,2},{7,23},{8,12},{9,25},... | collective-permute-start | bytes 393224 | tf_op jit(solution)/shard_map/ppermute | solution.py:261
  6.6 0.1 collective-permute-start.1
  6.7 2.3 %collective-permute-done.3.refs_9_ = f32[16,2048]{1,0:T(8,128)S(1)} collective-permute-done((f32[16,2048]{1,0:T(8,128)S(1)}, f32[16,2048]{1,0:T(8,128)S(1)}, u32[]{:S(2)}, u32[]{:S(2)}) %collective-permute-start.3) | collective-permute-done | bytes 131104 | tf_op jit(solution)/shard_map/ppermute | solution.py:261
  9.0 0.5 %collective-permute-start.6 = (f32[16,2048]{1,0:T(8,128)S(1)}, f32[16,2048]{1,0:T(8,128)S(1)}, u32[]{:S(2)}, u32[]{:S(2)}) collective-permute-start(f32[16,2048]{1,0:T(8,128)S(1)} %collective-permute-done.3.refs_9_), channel_id=1, source_target_pairs={{0,1},{1,0},{2,3},{3,2},{4,5},{5,4},{6,7},{7,6},{8,9},{9,8},{10,11... | collective-permute-start | bytes 393224 | tf_op jit(solution)/shard_map/ppermute | solution.py:247
  9.6 1.5 %collective-permute-done.2.refs_8_ = f32[16,2048]{1,0:T(8,128)S(1)} collective-permute-done((f32[16,2048]{1,0:T(8,128)S(1)}, f32[16,2048]{1,0:T(8,128)S(1)}, u32[]{:S(2)}, u32[]{:S(2)}) %collective-permute-start.2) | collective-permute-done | bytes 131104 | tf_op jit(solution)/shard_map/ppermute | solution.py:261
  11.1 1.8 %collective-permute-start.5 = (f32[16,2048]{1,0:T(8,128)S(1)}, f32[16,2048]{1,0:T(8,128)S(1)}, u32[]{:S(2)}, u32[]{:S(2)}) collective-permute-start(f32[16,2048]{1,0:T(8,128)S(1)} %collective-permute-done.2.refs_8_), channel_id=1, source_target_pairs={{0,1},{1,0},{2,3},{3,2},{4,5},{5,4},{6,7},{7,6},{8,9},{9,8},{10,11... | collective-permute-start | bytes 393224 | tf_op jit(solution)/shard_map/ppermute | solution.py:247
  12.8 0.0 collective-permute-done.1.refs_7_
  12.9 0.0 collective-permute-start.4
  13.5 0.0 collective-permute-done.6.refs_12_
  13.5 0.3 collective-permute-done.5.refs_11_
  13.8 0.4 collective-permute-done.4.refs_10_
  14.2 3.5 %products.1 = (f32[4,8,2048]{2,1,0:T(8,128)S(1)}, f32[4,8,2048]{2,1,0:T(8,128)S(1)}, f32[4,8,2048]{2,1,0:T(8,128)S(1)}) custom-call(s32[1,1]{1,0:T(1,128)S(6)} %copy.12.refs_0_, f32[256,128,128]{2,1,0:T(8,128)} %bitcast.20, s32[1,1,256]{2,1,0:T(1,128)} %refs_2_.1, s32[1,1,256]{2,1,0:T(1,128)} %refs_3_.1, f32[1,2048]{1,0:T(1,128)} %bitcast.21, ...), custom_call_target="tpu_custom_call" | custom-call | tf_op jit(solution)/shard_map/products/pallas_call | solution.py:276
  17.7 0.2 collective-permute-start.7
  17.9 7.4 %collective-permute-start.13 = (f32[8,2048]{1,0:T(8,128)S(1)}, f32[8,2048]{1,0:T(8,128)S(1)}, u32[]{:S(2)}, u32[]{:S(2)}) collective-permute-start(f32[8,2048]{1,0:T(8,128)S(1)} %get-tuple-element.16), channel_id=1, source_target_pairs={{0,24},{8,16},{16,8},{24,0},{1,25},{9,17},{17,9},{25,1},{2,26},{10... | collective-permute-start | bytes 196616 | tf_op jit(solution)/shard_map/ppermute | solution.py:250
  25.4 0.0 collective-permute-start.12
  25.4 0.6 %collective-permute-start.11 = (f32[8,2048]{1,0:T(8,128)S(1)}, f32[8,2048]{1,0:T(8,128)S(1)}, u32[]{:S(2)}, u32[]{:S(2)}) collective-permute-start(f32[8,2048]{1,0:T(8,128)S(1)} %get-tuple-element.18), channel_id=1, source_target_pairs={{0,8},{8,0},{16,24},{24,16},{1,9},{9,1},{17,25},{25,17},{2,10},{10... | collective-permute-start | bytes 196616 | tf_op jit(solution)/shard_map/ppermute | solution.py:250
  26.0 0.0 collective-permute-done.7
  26.1 2.5 %collective-permute-start.10 = (f32[8,2048]{1,0:T(8,128)S(1)}, f32[8,2048]{1,0:T(8,128)S(1)}, u32[]{:S(2)}, u32[]{:S(2)}) collective-permute-start(f32[8,2048]{1,0:T(8,128)S(1)} %get-tuple-element.13), channel_id=1, source_target_pairs={{0,6},{1,7},{2,4},{3,5},{4,2},{5,3},{6,0},{7,1},{8,14},{9,15},{10,... | collective-permute-start | bytes 196616 | tf_op jit(solution)/shard_map/ppermute | solution.py:247
  28.6 0.5 %collective-permute-start.9 = (f32[8,2048]{1,0:T(8,128)S(1)}, f32[8,2048]{1,0:T(8,128)S(1)}, u32[]{:S(2)}, u32[]{:S(2)}) collective-permute-start(f32[8,2048]{1,0:T(8,128)S(1)} %get-tuple-element.14), channel_id=1, source_target_pairs={{0,4},{1,5},{2,6},{3,7},{4,0},{5,1},{6,2},{7,3},{8,12},{9,13},{10,... | collective-permute-start | bytes 196616 | tf_op jit(solution)/shard_map/ppermute | solution.py:247
  29.1 0.0 collective-permute-done.13.refs_10_
  29.1 0.6 %collective-permute-start.8 = (f32[8,2048]{1,0:T(8,128)S(1)}, f32[8,2048]{1,0:T(8,128)S(1)}, u32[]{:S(2)}, u32[]{:S(2)}) collective-permute-start(f32[8,2048]{1,0:T(8,128)S(1)} %get-tuple-element.15), channel_id=1, source_target_pairs={{0,2},{1,3},{2,0},{3,1},{4,6},{5,7},{6,4},{7,5},{8,10},{9,11},{10,... | collective-permute-start | bytes 196616 | tf_op jit(solution)/shard_map/ppermute | solution.py:247
  29.7 1.2 %collective-permute-done.12.refs_9_ = f32[8,2048]{1,0:T(8,128)S(1)} collective-permute-done((f32[8,2048]{1,0:T(8,128)S(1)}, f32[8,2048]{1,0:T(8,128)S(1)}, u32[]{:S(2)}, u32[]{:S(2)}) %collective-permute-start.12) | collective-permute-done | bytes 65568 | tf_op jit(solution)/shard_map/ppermute | solution.py:250
  30.9 0.2 collective-permute-done.11.refs_8_
  31.0 0.3 collective-permute-done.10.refs_7_
  31.4 1.5 %collective-permute-done.9.refs_6_ = f32[8,2048]{1,0:T(8,128)S(1)} collective-permute-done((f32[8,2048]{1,0:T(8,128)S(1)}, f32[8,2048]{1,0:T(8,128)S(1)}, u32[]{:S(2)}, u32[]{:S(2)}) %collective-permute-start.9) | collective-permute-done | bytes 65568 | tf_op jit(solution)/shard_map/ppermute | solution.py:247
  32.8 0.5 %collective-permute-done.8.refs_5_ = f32[8,2048]{1,0:T(8,128)S(1)} collective-permute-done((f32[8,2048]{1,0:T(8,128)S(1)}, f32[8,2048]{1,0:T(8,128)S(1)}, u32[]{:S(2)}, u32[]{:S(2)}) %collective-permute-start.8) | collective-permute-done | bytes 65568 | tf_op jit(solution)/shard_map/ppermute | solution.py:247
  33.3 0.0 copy-done
  33.3 0.0 copy-done.1
  33.4 0.6 %image.1 = (f32[8,2048]{1,0:T(8,128)S(1)}, f32[32,4,128]{2,1,0:T(4,128)S(1)}) custom-call(f32[8,2048]{1,0:T(8,128)S(1)} %copy-done, f32[8,2048]{1,0:T(8,128)S(1)} %copy-done.1, f32[8,2048]{1,0:T(8,128)S(1)} %get-tuple-element.20.refs_2_, f32[8,2048]{1,0:T(8,128)S(1)} %get-tuple-element.21.refs_3_, f32[8,2048]{1,0:T(8,128)S(1)} %get-tuple-element.19.refs_4_, ...), custom_call_target="tpu_custom_call" | custom-call | tf_op jit(solution)/shard_map/image/pallas_call | solution.py:321
  34.0 12.6 %all_to_all.5.sums_in = f32[32,4,128]{2,1,0:T(4,128)S(1)} all-to-all(f32[32,4,128]{2,1,0:T(4,128)S(1)} %get-tuple-element.11), channel_id=1, replica_groups=mesh['row'=4,'col'=8] {'row','col'}, dimensions={0} | all-to-all | bytes 131072 | tf_op jit(solution)/shard_map/all_to_all | solution.py:333
  46.6 0.0 copy-done.2
  46.6 2.1 %finish.1 = (f32[8,2048]{1,0:T(8,128)}, f32[8,8]{1,0:T(8,128)}, f32[8,8]{1,0:T(8,128)}) custom-call(f32[32,4,128]{2,1,0:T(4,128)S(1)} %all_to_all.5.sums_in, f32[8,2048]{1,0:T(8,128)S(1)} %get-tuple-element.12.image, f32[8,2048]{1,0:T(8,128)S(1)} %copy-done, f32[8,2048]{1,0:T(8,128)S(1)} %copy-done.1, f32[8,8]{1,0:T(8,128)S(1)} %copy-done.2), custom_call_target="tpu_custom_call" | custom-call | tf_op jit(solution)/shard_map/finish/pallas_call | solution.py:334
  (3 shorter events, 0.1 us)
Async XLA Ops:
  0.6 32.7 %copy-start = (f32[8,2048]{1,0:T(8,128)S(1)}, f32[8,2048]{1,0:T(8,128)}, u32[]{:S(2)}) copy-start(f32[8,2048]{1,0:T(8,128)} %now.1) | copy-start | bytes 196612
  0.6 32.7 %copy-start.1 = (f32[8,2048]{1,0:T(8,128)S(1)}, f32[8,2048]{1,0:T(8,128)}, u32[]{:S(2)}) copy-start(f32[8,2048]{1,0:T(8,128)} %prev.1) | copy-start | bytes 196612
  0.7 45.9 %copy-start.2 = (f32[8,8]{1,0:T(8,128)S(1)}, f32[8,8]{1,0:T(8,128)}, u32[]{:S(2)}) copy-start(f32[8,8]{1,0:T(8,128)} %coupling.1) | copy-start | bytes 772
  0.7 1.6 %collective-permute-start = (f32[8,2048]{1,0:T(8,128)}, f32[8,2048]{1,0:T(8,128)S(1)}, u32[]{:S(2)}, u32[]{:S(2)}) collective-permute-start(f32[8,2048]{1,0:T(8,128)} %now.1), channel_id=1, source_target_pairs={{0,1},{1,0},{2,3},{3,2},{4,5},{5,4},{6,7},{7,6},{8,9},{9,8},{10,11... | collective-permute-start | bytes 196616 | tf_op jit(solution)/shard_map/ppermute | solution.py:247
  2.3 6.7 %collective-permute-start.3 = (f32[16,2048]{1,0:T(8,128)S(1)}, f32[16,2048]{1,0:T(8,128)S(1)}, u32[]{:S(2)}, u32[]{:S(2)}) collective-permute-start(f32[16,2048]{1,0:T(8,128)S(1)} %constant_dynamic-update-slice_fusion), channel_id=1, source_target_pairs={{0,6},{1,25},{2,4},{3,27},{4,2},{5,29},{6,0},{7,31},{8,14},{9,17},... | collective-permute-start | bytes 393224 | tf_op jit(solution)/shard_map/ppermute | solution.py:261
  6.1 5.0 %collective-permute-start.2 = (f32[16,2048]{1,0:T(8,128)S(1)}, f32[16,2048]{1,0:T(8,128)S(1)}, u32[]{:S(2)}, u32[]{:S(2)}) collective-permute-start(f32[16,2048]{1,0:T(8,128)S(1)} %constant_dynamic-update-slice_fusion), channel_id=1, source_target_pairs={{0,4},{1,17},{2,6},{3,19},{4,0},{5,21},{6,2},{7,23},{8,12},{9,25},... | collective-permute-start | bytes 393224 | tf_op jit(solution)/shard_map/ppermute | solution.py:261
  6.6 6.3 %collective-permute-start.1 = (f32[16,2048]{1,0:T(8,128)S(1)}, f32[16,2048]{1,0:T(8,128)S(1)}, u32[]{:S(2)}, u32[]{:S(2)}) collective-permute-start(f32[16,2048]{1,0:T(8,128)S(1)} %constant_dynamic-update-slice_fusion), channel_id=1, source_target_pairs={{0,2},{1,9},{2,0},{3,11},{4,6},{5,13},{6,4},{7,15},{8,10},{9,1},{1... | collective-permute-start | bytes 393224 | tf_op jit(solution)/shard_map/ppermute | solution.py:261
  9.0 4.5 %collective-permute-start.6 = (f32[16,2048]{1,0:T(8,128)S(1)}, f32[16,2048]{1,0:T(8,128)S(1)}, u32[]{:S(2)}, u32[]{:S(2)}) collective-permute-start(f32[16,2048]{1,0:T(8,128)S(1)} %collective-permute-done.3.refs_9_), channel_id=1, source_target_pairs={{0,1},{1,0},{2,3},{3,2},{4,5},{5,4},{6,7},{7,6},{8,9},{9,8},{10,11... | collective-permute-start | bytes 393224 | tf_op jit(solution)/shard_map/ppermute | solution.py:247
  11.1 2.8 %collective-permute-start.5 = (f32[16,2048]{1,0:T(8,128)S(1)}, f32[16,2048]{1,0:T(8,128)S(1)}, u32[]{:S(2)}, u32[]{:S(2)}) collective-permute-start(f32[16,2048]{1,0:T(8,128)S(1)} %collective-permute-done.2.refs_8_), channel_id=1, source_target_pairs={{0,1},{1,0},{2,3},{3,2},{4,5},{5,4},{6,7},{7,6},{8,9},{9,8},{10,11... | collective-permute-start | bytes 393224 | tf_op jit(solution)/shard_map/ppermute | solution.py:247
  12.9 1.3 %collective-permute-start.4 = (f32[16,2048]{1,0:T(8,128)S(1)}, f32[16,2048]{1,0:T(8,128)S(1)}, u32[]{:S(2)}, u32[]{:S(2)}) collective-permute-start(f32[16,2048]{1,0:T(8,128)S(1)} %collective-permute-done.1.refs_7_), channel_id=1, source_target_pairs={{0,1},{1,0},{2,3},{3,2},{4,5},{5,4},{6,7},{7,6},{8,9},{9,8},{10,11... | collective-permute-start | bytes 393224 | tf_op jit(solution)/shard_map/ppermute | solution.py:247
  17.7 8.3 %collective-permute-start.7 = (f32[4,8,2048]{2,1,0:T(8,128)S(1)}, f32[4,8,2048]{2,1,0:T(8,128)S(1)}, u32[]{:S(2)}, u32[]{:S(2)}) collective-permute-start(f32[4,8,2048]{2,1,0:T(8,128)S(1)} %get-tuple-element.9), channel_id=1, source_target_pairs={{0,1},{1,0},{2,3},{3,2},{4,5},{5,4},{6,7},{7,6},{8,9},{9,8},{10,11... | collective-permute-start | bytes 786440 | tf_op jit(solution)/shard_map/ppermute | solution.py:247
  17.9 11.2 %collective-permute-start.13 = (f32[8,2048]{1,0:T(8,128)S(1)}, f32[8,2048]{1,0:T(8,128)S(1)}, u32[]{:S(2)}, u32[]{:S(2)}) collective-permute-start(f32[8,2048]{1,0:T(8,128)S(1)} %get-tuple-element.16), channel_id=1, source_target_pairs={{0,24},{8,16},{16,8},{24,0},{1,25},{9,17},{17,9},{25,1},{2,26},{10... | collective-permute-start | bytes 196616 | tf_op jit(solution)/shard_map/ppermute | solution.py:250
  25.4 5.5 %collective-permute-start.12 = (f32[8,2048]{1,0:T(8,128)S(1)}, f32[8,2048]{1,0:T(8,128)S(1)}, u32[]{:S(2)}, u32[]{:S(2)}) collective-permute-start(f32[8,2048]{1,0:T(8,128)S(1)} %get-tuple-element.17), channel_id=1, source_target_pairs={{0,16},{8,24},{16,0},{24,8},{1,17},{9,25},{17,1},{25,9},{2,18},{10... | collective-permute-start | bytes 196616 | tf_op jit(solution)/shard_map/ppermute | solution.py:250
  25.4 5.7 %collective-permute-start.11 = (f32[8,2048]{1,0:T(8,128)S(1)}, f32[8,2048]{1,0:T(8,128)S(1)}, u32[]{:S(2)}, u32[]{:S(2)}) collective-permute-start(f32[8,2048]{1,0:T(8,128)S(1)} %get-tuple-element.18), channel_id=1, source_target_pairs={{0,8},{8,0},{16,24},{24,16},{1,9},{9,1},{17,25},{25,17},{2,10},{10... | collective-permute-start | bytes 196616 | tf_op jit(solution)/shard_map/ppermute | solution.py:250
  26.1 5.3 %collective-permute-start.10 = (f32[8,2048]{1,0:T(8,128)S(1)}, f32[8,2048]{1,0:T(8,128)S(1)}, u32[]{:S(2)}, u32[]{:S(2)}) collective-permute-start(f32[8,2048]{1,0:T(8,128)S(1)} %get-tuple-element.13), channel_id=1, source_target_pairs={{0,6},{1,7},{2,4},{3,5},{4,2},{5,3},{6,0},{7,1},{8,14},{9,15},{10,... | collective-permute-start | bytes 196616 | tf_op jit(solution)/shard_map/ppermute | solution.py:247
  28.6 4.3 %collective-permute-start.9 = (f32[8,2048]{1,0:T(8,128)S(1)}, f32[8,2048]{1,0:T(8,128)S(1)}, u32[]{:S(2)}, u32[]{:S(2)}) collective-permute-start(f32[8,2048]{1,0:T(8,128)S(1)} %get-tuple-element.14), channel_id=1, source_target_pairs={{0,4},{1,5},{2,6},{3,7},{4,0},{5,1},{6,2},{7,3},{8,12},{9,13},{10,... | collective-permute-start | bytes 196616 | tf_op jit(solution)/shard_map/ppermute | solution.py:247
  29.1 4.3 %collective-permute-start.8 = (f32[8,2048]{1,0:T(8,128)S(1)}, f32[8,2048]{1,0:T(8,128)S(1)}, u32[]{:S(2)}, u32[]{:S(2)}) collective-permute-start(f32[8,2048]{1,0:T(8,128)S(1)} %get-tuple-element.15), channel_id=1, source_target_pairs={{0,2},{1,3},{2,0},{3,1},{4,6},{5,7},{6,4},{7,5},{8,10},{9,11},{10,... | collective-permute-start | bytes 196616 | tf_op jit(solution)/shard_map/ppermute | solution.py:247

commit v5 on v4

--- a/solution.py
+++ b/solution.py
@@ -11,6 +11,7 @@
 VMEM = pltpu.VMEM
 SMEM = pltpu.SMEM
 GROUP = 32
+WAIT_FLOPS = 20_000_000_000
 MIB = 1 << 20
 
 
@@ -38,14 +39,13 @@
 
 def products_kernel(rows, planes, group, *refs):
     peers = max(planes, rows) - 1
-    count, tiles_hbm, row_idx_hbm, col_idx_hbm, diag_hbm, own_hbm, beside = refs[:7]
+    count, tiles, row_idx_hbm, col_idx_hbm, diag_hbm, own_hbm, beside = refs[:7]
     fetched = refs[7 : 7 + peers]
     passed = refs[7 + peers : 7 + 2 * peers]
     (
         keep_out,
         send_out,
         col_out,
-        tiles,
         row_idx,
         col_idx,
         diag,
@@ -55,7 +55,6 @@
         acc_rows,
         acc_cols,
         small_sems,
-        tile_sems,
     ) = refs[7 + 2 * peers :]
     row = lax.axis_index("row")
     col = lax.axis_index("col")
@@ -77,21 +76,11 @@
         )
     ]
 
-    def tile_copy(g):
-        at = pl.ds(g * group, group)
-        return pltpu.make_async_copy(tiles_hbm.at[at], tiles.at[at], tile_sems.at[g])
-
     total = count[0, 0]
     groups = (total + group - 1) // group
 
-    def start_tiles(g, carry):
-        tile_copy(g).start()
-        return carry
-
-    tile_copy(0).start()
     for copy in small:
         copy.start()
-    lax.fori_loop(1, groups, start_tiles, 0)
     acc_rows[...] = jnp.zeros_like(acc_rows)
     acc_cols[...] = jnp.zeros_like(acc_cols)
 
@@ -127,7 +116,6 @@
     spare_col = acc_cols.shape[0] - 1
 
     def multiply(g, carry):
-        tile_copy(g).wait()
         for k in range(group):
             m = g * group + k
             alive = m < total
@@ -168,18 +156,31 @@
             col_out[s, :, at] = piece
 
 
+def fixed_kernel(now, prev, out, both, sems):
+    vectors = now.shape[0]
+    copies = [
+        pltpu.make_async_copy(now, both.at[pl.ds(0, vectors)], sems.at[0]),
+        pltpu.make_async_copy(prev, both.at[pl.ds(vectors, vectors)], sems.at[1]),
+    ]
+    for copy in copies:
+        copy.start()
+    for copy in copies:
+        copy.wait()
+    out[...] = contract(both[...], both[...])
+
+
 def image_kernel(copies, *refs):
-    now, prev = refs[:2]
+    now, prev, fixed_in = refs[:3]
     image_out, sums_out = refs[-2:]
-    image = refs[2][...]
-    for ref in refs[3:-2]:
+    image = refs[3][...]
+    for ref in refs[4:-2]:
         image = image + ref[...]
     image_out[...] = image
     block, last = now[...], prev[...]
     vectors = image.shape[0]
     both = jnp.concatenate([block, last], axis=0)
     against = contract(image, jnp.concatenate([image, both], axis=0))
-    fixed = contract(both, both)
+    fixed = fixed_in[...]
     half = sums_out.shape[2] // 2
     used = against.shape[1] + 2 * fixed.shape[1]
     sums = jnp.concatenate(
@@ -260,18 +261,35 @@
                 pairs.append((r * cols + c, to[0] * cols + to[1]))
         return lax.ppermute(x, ("row", "col"), pairs)
 
+    in_vmem = pl.BlockSpec(memory_space=VMEM)
+    in_hbm = pl.BlockSpec(memory_space=pltpu.HBM)
+
+    def stay(x):
+        return pltpu.with_memory_space_constraint(x, pltpu.HBM)
+
+    fixed = pl.pallas_call(
+        fixed_kernel,
+        out_shape=jax.ShapeDtypeStruct((2 * vectors, 2 * vectors), f32),
+        in_specs=[in_hbm] * 2,
+        out_specs=in_vmem,
+        scratch_shapes=[
+            VMEM((2 * vectors, piece), f32),
+            pltpu.SemaphoreType.DMA((2,)),
+        ],
+        compiler_params=pltpu.CompilerParams(vmem_limit_bytes=16 * MIB),
+        cost_estimate=pl.CostEstimate(
+            flops=WAIT_FLOPS, bytes_accessed=2 * vectors * piece * 4, transcendentals=0
+        ),
+        name="fixed",
+    )(stay(block_now), stay(block_prev))
     beside = along_col(block_now, 1)
     chip = jnp.concatenate([block_now, beside], axis=0)
     peers = range(1, max(planes, rows))
     fetched = [apart(chip, s) for s in peers]
+    fetched[-1], fixed = lax.optimization_barrier((fetched[-1], fixed))
     passed = [along_col(x, 1) for x in fetched]
 
-    in_vmem = pl.BlockSpec(memory_space=VMEM)
-    in_hbm = pl.BlockSpec(memory_space=pltpu.HBM)
     group = math.gcd(slots, GROUP)
-
-    def stay(x):
-        return pltpu.with_memory_space_constraint(x, pltpu.HBM)
 
     keep, send, col_parts = pl.pallas_call(
         functools.partial(products_kernel, rows, planes, group),
@@ -281,11 +299,11 @@
             jax.ShapeDtypeStruct((rows, vectors, piece), f32),
         ),
         in_specs=[pl.BlockSpec(memory_space=SMEM)]
-        + [in_hbm] * 5
+        + [in_vmem]
+        + [in_hbm] * 4
         + [in_vmem] * (1 + 2 * len(peers)),
         out_specs=(in_vmem,) * 3,
         scratch_shapes=[
-            VMEM((slots, width, width), f32),
             SMEM(tile_rows.shape, jnp.int32),
             SMEM(tile_cols.shape, jnp.int32),
             VMEM((1, piece), f32),
@@ -295,13 +313,12 @@
             VMEM((cols * piece_tiles + 1, vectors, width), f32),
             VMEM((rows * piece_tiles + 1, vectors, width), f32),
             pltpu.SemaphoreType.DMA((4,)),
-            pltpu.SemaphoreType.DMA((slots // group,)),
         ],
-        compiler_params=pltpu.CompilerParams(vmem_limit_bytes=40 * MIB),
+        compiler_params=pltpu.CompilerParams(vmem_limit_bytes=20 * MIB),
         name="products",
     )(
         tile_counts,
-        stay(tiles.reshape(slots, width, width)),
+        pltpu.with_memory_space_constraint(tiles.reshape(slots, width, width), VMEM),
         stay(tile_rows),
         stay(tile_cols),
         stay(diag_energy.reshape(1, piece)),
@@ -324,11 +341,11 @@
             piece_shape,
             jax.ShapeDtypeStruct((devices, vectors // 2, 128), f32),
         ),
-        in_specs=[in_vmem] * (2 + len(terms)),
+        in_specs=[in_vmem] * (3 + len(terms)),
         out_specs=(in_vmem,) * 2,
         compiler_params=pltpu.CompilerParams(vmem_limit_bytes=16 * MIB),
         name="image",
-    )(block_now, block_prev, *terms)
+    )(block_now, block_prev, fixed, *terms)
 
     sums = lax.all_to_all(sums, ("row", "col"), 0, 0)
     return pl.pallas_call(

time: 48.9 us -> 48.2 us (0.986)
  waiting for transfers between devices: 8.38 us -> 7.87 us
  starting transfers between devices: 19.2 us -> 18.7 us
    pallas_call x0 -> x1, Pallas kernels: none -> 1.51 us  [local(): pl.pallas_call(fixed_kernel, out_shape=jax.ShapeDtypeStruct((2 * vectors,...]
    ppermute x8, starting transfers between devices: 6.74 us -> 5.37 us  [along_col(): return lax.ppermute(x, 'col', [(i, i ^ s) for i in range(cols)])]
    ppermute x8, waiting for transfers between devices: 3.26 us -> 2.09 us  [along_col(): return lax.ppermute(x, 'col', [(i, i ^ s) for i in range(cols)])]
    pallas_call x1, Pallas kernels: 3.46 us -> 2.65 us  [local(): pl.pallas_call(functools.partial(products_kernel, rows, planes, group), o...]
    ppermute x3, starting transfers between devices: 8.08 us -> 8.82 us  [along_row(): return lax.ppermute(x, 'row', [(i, i ^ s) for i in range(rows)])]
  transfers between devices with their start and end apart: 14 -> 14, of which waited for: 10 -> 10; matrix products, arithmetic and copies ran while one was open for 2% -> 2% of each run, Pallas kernels for 0% -> 3%
where the time goes in v5:
time: 48.2 us; the launch traced here: 47.9 us
  starting transfers between devices  18.7 us (39%)
  blocking collectives  12.4 us (26%)
  waiting for transfers between devices  7.87 us (16%)
  Pallas kernels  6.64 us (14%)
  between operations  1.41 us (3%)
  local copies, waits for them, and re-layouts  0.9 us (2%)
    all_to_all x1, blocking collectives, local(): sums = lax.all_to_all(sums, ('row', 'col'), 0, 0)  12.4 us
    ppermute x3, starting transfers between devices, along_row(): return lax.ppermute(x, 'row', [(i, i ^ s) for i in range(rows)])  8.82 us
    ppermute x8, starting transfers between devices, along_col(): return lax.ppermute(x, 'col', [(i, i ^ s) for i in range(cols)])  5.37 us
    ppermute x3, starting transfers between devices, apart(): return lax.ppermute(x, ('row', 'col'), pairs)  4.48 us
    ppermute x3, waiting for transfers between devices, apart(): return lax.ppermute(x, ('row', 'col'), pairs)  4.27 us
    pallas_call x1, Pallas kernels, local(): pl.pallas_call(functools.partial(products_kernel, rows, planes, group), o...  2.65 us
    pallas_call x1, Pallas kernels, local(): pl.pallas_call(functools.partial(finish_kernel, float(piece * devices)),...  2.1 us
    ppermute x8, waiting for transfers between devices, along_col(): return lax.ppermute(x, 'col', [(i, i ^ s) for i in range(cols)])  2.09 us
  transfers between devices with their start and end apart: 14, of which 10 were waited for; matrix products, arithmetic and copies ran while one was open for 2% of the time, Pallas kernels for 3%

profile of v5, /device:TPU:0, one launch (start us, length us, event | category | flops | bytes accessed | tf_op | source)
XLA Modules:
  0.0 47.9 jit_solution(507420539059866193)
XLA Ops:
  0.6 0.5 %collective-permute-start = (f32[8,2048]{1,0:T(8,128)}, f32[8,2048]{1,0:T(8,128)S(1)}, u32[]{:S(2)}, u32[]{:S(2)}) collective-permute-start(f32[8,2048]{1,0:T(8,128)} %now.3), channel_id=1, source_target_pairs={{0,1},{1,0},{2,3},{3,2},{4,5},{5,4},{6,7},{7,6},{8,9},{9,8},{10,11... | collective-permute-start | bytes 196616 | tf_op jit(solution)/shard_map/ppermute | solution.py:248
  1.1 0.8 %constant_dynamic-update-slice_fusion.1 = f32[16,2048]{1,0:T(8,128)S(1)} fusion(f32[8,2048]{1,0:T(8,128)} %now.3), kind=kLoop, calls=%fused_computation.13 | loop fusion | bytes 131072
  2.0 0.3 collective-permute-done.refs_6_
  2.3 0.0 slice-start
  2.3 0.0 slice-start.1
  2.3 0.0 slice-start.2
  2.3 0.0 slice-start.3
  2.3 2.9 %collective-permute-start.3 = (f32[16,2048]{1,0:T(8,128)S(1)}, f32[16,2048]{1,0:T(8,128)S(1)}, u32[]{:S(2)}, u32[]{:S(2)}) collective-permute-start(f32[16,2048]{1,0:T(8,128)S(1)} %constant_dynamic-update-slice_fusion), channel_id=1, source_target_pairs={{0,4},{1,17},{2,6},{3,19},{4,0},{5,21},{6,2},{7,23},{8,12},{9,25},... | collective-permute-start | bytes 393224 | tf_op jit(solution)/shard_map/ppermute | solution.py:262
  5.2 1.5 %collective-permute-start.2 = (f32[16,2048]{1,0:T(8,128)S(1)}, f32[16,2048]{1,0:T(8,128)S(1)}, u32[]{:S(2)}, u32[]{:S(2)}) collective-permute-start(f32[16,2048]{1,0:T(8,128)S(1)} %constant_dynamic-update-slice_fusion), channel_id=1, source_target_pairs={{0,2},{1,9},{2,0},{3,11},{4,6},{5,13},{6,4},{7,15},{8,10},{9,1},{1... | collective-permute-start | bytes 393224 | tf_op jit(solution)/shard_map/ppermute | solution.py:262
  6.7 0.0 collective-permute-start.1
  6.8 1.5 %fixed.1.refs_2_ = f32[16,16]{1,0:T(8,128)S(1)} custom-call(f32[8,2048]{1,0:T(8,128)} %now.3, f32[8,2048]{1,0:T(8,128)} %prev.3), custom_call_target="tpu_custom_call" | custom-call | flops 20000000000 | bytes 131072 | tf_op jit(solution)/shard_map/fixed/pallas_call | solution.py:270
  8.3 0.0 copy-start
  8.3 0.0 copy-start.1
  8.3 0.0 copy-start.2
  8.3 4.3 %collective-permute-done.1.refs_9_ = f32[16,2048]{1,0:T(8,128)S(1)} collective-permute-done((f32[16,2048]{1,0:T(8,128)S(1)}, f32[16,2048]{1,0:T(8,128)S(1)}, u32[]{:S(2)}, u32[]{:S(2)}) %collective-permute-start.1) | collective-permute-done | bytes 131104 | tf_op jit(solution)/shard_map/ppermute | solution.py:262
  12.6 0.0 collective-permute-done.3.refs_8_
  12.6 0.5 %collective-permute-start.5 = (f32[16,2048]{1,0:T(8,128)S(1)}, f32[16,2048]{1,0:T(8,128)S(1)}, u32[]{:S(2)}, u32[]{:S(2)}) collective-permute-start(f32[16,2048]{1,0:T(8,128)S(1)} %collective-permute-done.3.refs_8_), channel_id=1, source_target_pairs={{0,1},{1,0},{2,3},{3,2},{4,5},{5,4},{6,7},{7,6},{8,9},{9,8},{10,11... | collective-permute-start | bytes 393224 | tf_op jit(solution)/shard_map/ppermute | solution.py:248
  13.1 0.0 collective-permute-done.2.refs_7_
  13.1 0.1 collective-permute-start.4
  13.2 0.4 collective-permute-start.6
  14.3 0.0 collective-permute-done.5.refs_11_
  14.3 0.2 collective-permute-done.4.refs_10_
  14.4 0.2 collective-permute-done.6.refs_12_
  14.6 0.0 slice-done
  14.6 0.0 slice-done.1
  14.6 0.0 slice-done.2
  14.6 0.0 slice-done.3
  14.7 2.6 %products.1 = (f32[4,8,2048]{2,1,0:T(8,128)S(1)}, f32[4,8,2048]{2,1,0:T(8,128)S(1)}, f32[4,8,2048]{2,1,0:T(8,128)S(1)}) custom-call(s32[1,1]{1,0:T(1,128)S(6)} %copy.12.refs_0_, f32[256,128,128]{2,1,0:T(8,128)S(1)} %bitcast.22, s32[1,1,256]{2,1,0:T(1,128)} %refs_2_.1, s32[1,1,256]{2,1,0:T(1,128)} %refs_3_.1, f32[1,2048]{1,0:T(1,128)} %bitcast.23, ...), custom_call_target="tpu_custom_call" | custom-call | tf_op jit(solution)/shard_map/products/pallas_call | solution.py:294
  17.3 0.4 collective-permute-start.7
  17.7 8.2 %collective-permute-start.13 = (f32[8,2048]{1,0:T(8,128)S(1)}, f32[8,2048]{1,0:T(8,128)S(1)}, u32[]{:S(2)}, u32[]{:S(2)}) collective-permute-start(f32[8,2048]{1,0:T(8,128)S(1)} %get-tuple-element.20), channel_id=1, source_target_pairs={{0,24},{8,16},{16,8},{24,0},{1,25},{9,17},{17,9},{25,1},{2,26},{10... | collective-permute-start | bytes 196616 | tf_op jit(solution)/shard_map/ppermute | solution.py:251
  25.9 0.0 collective-permute-start.12
  25.9 0.6 %collective-permute-start.11 = (f32[8,2048]{1,0:T(8,128)S(1)}, f32[8,2048]{1,0:T(8,128)S(1)}, u32[]{:S(2)}, u32[]{:S(2)}) collective-permute-start(f32[8,2048]{1,0:T(8,128)S(1)} %get-tuple-element.22), channel_id=1, source_target_pairs={{0,8},{8,0},{16,24},{24,16},{1,9},{9,1},{17,25},{25,17},{2,10},{10... | collective-permute-start | bytes 196616 | tf_op jit(solution)/shard_map/ppermute | solution.py:251
  26.5 0.0 collective-permute-done.7
  26.6 1.5 %collective-permute-start.10 = (f32[8,2048]{1,0:T(8,128)S(1)}, f32[8,2048]{1,0:T(8,128)S(1)}, u32[]{:S(2)}, u32[]{:S(2)}) collective-permute-start(f32[8,2048]{1,0:T(8,128)S(1)} %get-tuple-element.17), channel_id=1, source_target_pairs={{0,6},{1,7},{2,4},{3,5},{4,2},{5,3},{6,0},{7,1},{8,14},{9,15},{10,... | collective-permute-start | bytes 196616 | tf_op jit(solution)/shard_map/ppermute | solution.py:248
  28.1 0.6 %collective-permute-start.9 = (f32[8,2048]{1,0:T(8,128)S(1)}, f32[8,2048]{1,0:T(8,128)S(1)}, u32[]{:S(2)}, u32[]{:S(2)}) collective-permute-start(f32[8,2048]{1,0:T(8,128)S(1)} %get-tuple-element.18), channel_id=1, source_target_pairs={{0,4},{1,5},{2,6},{3,7},{4,0},{5,1},{6,2},{7,3},{8,12},{9,13},{10,... | collective-permute-start | bytes 196616 | tf_op jit(solution)/shard_map/ppermute | solution.py:248
  28.7 0.1 collective-permute-done.13.refs_11_
  28.8 1.4 %collective-permute-start.8 = (f32[8,2048]{1,0:T(8,128)S(1)}, f32[8,2048]{1,0:T(8,128)S(1)}, u32[]{:S(2)}, u32[]{:S(2)}) collective-permute-start(f32[8,2048]{1,0:T(8,128)S(1)} %get-tuple-element.19), channel_id=1, source_target_pairs={{0,2},{1,3},{2,0},{3,1},{4,6},{5,7},{6,4},{7,5},{8,10},{9,11},{10,... | collective-permute-start | bytes 196616 | tf_op jit(solution)/shard_map/ppermute | solution.py:248
  30.1 1.3 %collective-permute-done.12.refs_10_ = f32[8,2048]{1,0:T(8,128)S(1)} collective-permute-done((f32[8,2048]{1,0:T(8,128)S(1)}, f32[8,2048]{1,0:T(8,128)S(1)}, u32[]{:S(2)}, u32[]{:S(2)}) %collective-permute-start.12) | collective-permute-done | bytes 65568 | tf_op jit(solution)/shard_map/ppermute | solution.py:251
  31.4 0.2 collective-permute-done.11.refs_9_
  31.6 0.7 %collective-permute-done.10.refs_8_ = f32[8,2048]{1,0:T(8,128)S(1)} collective-permute-done((f32[8,2048]{1,0:T(8,128)S(1)}, f32[8,2048]{1,0:T(8,128)S(1)}, u32[]{:S(2)}, u32[]{:S(2)}) %collective-permute-start.10) | collective-permute-done | bytes 65568 | tf_op jit(solution)/shard_map/ppermute | solution.py:248
  32.3 0.4 collective-permute-done.9.refs_7_
  32.7 0.3 collective-permute-done.8.refs_6_
  33.0 0.0 copy-done
  33.0 0.0 copy-done.1
  33.0 0.4 image.1
  33.4 12.4 %all_to_all.5.sums_in = f32[32,4,128]{2,1,0:T(4,128)S(1)} all-to-all(f32[32,4,128]{2,1,0:T(4,128)S(1)} %get-tuple-element.15), channel_id=1, replica_groups=mesh['row'=4,'col'=8] {'row','col'}, dimensions={0} | all-to-all | bytes 131072 | tf_op jit(solution)/shard_map/all_to_all | solution.py:350
  45.8 0.0 copy-done.2
  45.8 2.1 %finish.1 = (f32[8,2048]{1,0:T(8,128)}, f32[8,8]{1,0:T(8,128)}, f32[8,8]{1,0:T(8,128)}) custom-call(f32[32,4,128]{2,1,0:T(4,128)S(1)} %all_to_all.5.sums_in, f32[8,2048]{1,0:T(8,128)S(1)} %get-tuple-element.16.image, f32[8,2048]{1,0:T(8,128)S(1)} %copy-done, f32[8,2048]{1,0:T(8,128)S(1)} %copy-done.1, f32[8,8]{1,0:T(8,128)S(1)} %copy-done.2), custom_call_target="tpu_custom_call" | custom-call | tf_op jit(solution)/shard_map/finish/pallas_call | solution.py:351
  (4 shorter events, 0.1 us)
Async XLA Ops:
  0.6 1.6 %collective-permute-start = (f32[8,2048]{1,0:T(8,128)}, f32[8,2048]{1,0:T(8,128)S(1)}, u32[]{:S(2)}, u32[]{:S(2)}) collective-permute-start(f32[8,2048]{1,0:T(8,128)} %now.3), channel_id=1, source_target_pairs={{0,1},{1,0},{2,3},{3,2},{4,5},{5,4},{6,7},{7,6},{8,9},{9,8},{10,11... | collective-permute-start | bytes 196616 | tf_op jit(solution)/shard_map/ppermute | solution.py:248
  2.3 12.4 %slice-start = ((s8[16777216]{0:T(1024)(128)(4,1)}), s8[4194304]{0:T(1024)(128)(4,1)S(1)}, s32[]{:S(2)}) async-start(s8[16777216]{0:T(1024)(128)(4,1)} %bitcast.20), calls=%async_computation.1 | async-start | bytes 8388608
  2.3 12.4 %slice-start.1 = ((s8[16777216]{0:T(1024)(128)(4,1)}), s8[4194304]{0:T(1024)(128)(4,1)S(1)}, s32[]{:S(2)}) async-start(s8[16777216]{0:T(1024)(128)(4,1)} %bitcast.20), calls=%async_computation.2 | async-start | bytes 8388608
  2.3 12.4 %slice-start.2 = ((s8[16777216]{0:T(1024)(128)(4,1)}), s8[4194304]{0:T(1024)(128)(4,1)S(1)}, s32[]{:S(2)}) async-start(s8[16777216]{0:T(1024)(128)(4,1)} %bitcast.20), calls=%async_computation.3 | async-start | bytes 8388608
  2.3 12.4 %slice-start.3 = ((s8[16777216]{0:T(1024)(128)(4,1)}), s8[4194304]{0:T(1024)(128)(4,1)S(1)}, s32[]{:S(2)}) async-start(s8[16777216]{0:T(1024)(128)(4,1)} %bitcast.20), calls=%async_computation.4 | async-start | bytes 8388608
  2.3 10.3 %collective-permute-start.3 = (f32[16,2048]{1,0:T(8,128)S(1)}, f32[16,2048]{1,0:T(8,128)S(1)}, u32[]{:S(2)}, u32[]{:S(2)}) collective-permute-start(f32[16,2048]{1,0:T(8,128)S(1)} %constant_dynamic-update-slice_fusion), channel_id=1, source_target_pairs={{0,4},{1,17},{2,6},{3,19},{4,0},{5,21},{6,2},{7,23},{8,12},{9,25},... | collective-permute-start | bytes 393224 | tf_op jit(solution)/shard_map/ppermute | solution.py:262
  5.2 7.9 %collective-permute-start.2 = (f32[16,2048]{1,0:T(8,128)S(1)}, f32[16,2048]{1,0:T(8,128)S(1)}, u32[]{:S(2)}, u32[]{:S(2)}) collective-permute-start(f32[16,2048]{1,0:T(8,128)S(1)} %constant_dynamic-update-slice_fusion), channel_id=1, source_target_pairs={{0,2},{1,9},{2,0},{3,11},{4,6},{5,13},{6,4},{7,15},{8,10},{9,1},{1... | collective-permute-start | bytes 393224 | tf_op jit(solution)/shard_map/ppermute | solution.py:262
  6.7 5.9 %collective-permute-start.1 = (f32[16,2048]{1,0:T(8,128)S(1)}, f32[16,2048]{1,0:T(8,128)S(1)}, u32[]{:S(2)}, u32[]{:S(2)}) collective-permute-start(f32[16,2048]{1,0:T(8,128)S(1)} %constant_dynamic-update-slice_fusion), channel_id=1, source_target_pairs={{0,6},{1,25},{2,4},{3,27},{4,2},{5,29},{6,0},{7,31},{8,14},{9,17},... | collective-permute-start | bytes 393224 | tf_op jit(solution)/shard_map/ppermute | solution.py:262
  8.3 24.7 %copy-start = (f32[8,2048]{1,0:T(8,128)S(1)}, f32[8,2048]{1,0:T(8,128)}, u32[]{:S(2)}) copy-start(f32[8,2048]{1,0:T(8,128)} %now.3) | copy-start | bytes 196612
  8.3 24.7 %copy-start.1 = (f32[8,2048]{1,0:T(8,128)S(1)}, f32[8,2048]{1,0:T(8,128)}, u32[]{:S(2)}) copy-start(f32[8,2048]{1,0:T(8,128)} %prev.3) | copy-start | bytes 196612
  8.3 37.5 %copy-start.2 = (f32[8,8]{1,0:T(8,128)S(1)}, f32[8,8]{1,0:T(8,128)}, u32[]{:S(2)}) copy-start(f32[8,8]{1,0:T(8,128)} %coupling.1) | copy-start | bytes 772
  12.6 1.7 %collective-permute-start.5 = (f32[16,2048]{1,0:T(8,128)S(1)}, f32[16,2048]{1,0:T(8,128)S(1)}, u32[]{:S(2)}, u32[]{:S(2)}) collective-permute-start(f32[16,2048]{1,0:T(8,128)S(1)} %collective-permute-done.3.refs_8_), channel_id=1, source_target_pairs={{0,1},{1,0},{2,3},{3,2},{4,5},{5,4},{6,7},{7,6},{8,9},{9,8},{10,11... | collective-permute-start | bytes 393224 | tf_op jit(solution)/shard_map/ppermute | solution.py:248
  13.1 1.3 %collective-permute-start.4 = (f32[16,2048]{1,0:T(8,128)S(1)}, f32[16,2048]{1,0:T(8,128)S(1)}, u32[]{:S(2)}, u32[]{:S(2)}) collective-permute-start(f32[16,2048]{1,0:T(8,128)S(1)} %collective-permute-done.2.refs_7_), channel_id=1, source_target_pairs={{0,1},{1,0},{2,3},{3,2},{4,5},{5,4},{6,7},{7,6},{8,9},{9,8},{10,11... | collective-permute-start | bytes 393224 | tf_op jit(solution)/shard_map/ppermute | solution.py:248
  13.2 1.5 %collective-permute-start.6 = (f32[16,2048]{1,0:T(8,128)S(1)}, f32[16,2048]{1,0:T(8,128)S(1)}, u32[]{:S(2)}, u32[]{:S(2)}) collective-permute-start(f32[16,2048]{1,0:T(8,128)S(1)} %collective-permute-done.1.refs_9_), channel_id=1, source_target_pairs={{0,1},{1,0},{2,3},{3,2},{4,5},{5,4},{6,7},{7,6},{8,9},{9,8},{10,11... | collective-permute-start | bytes 393224 | tf_op jit(solution)/shard_map/ppermute | solution.py:248
  17.3 9.2 %collective-permute-start.7 = (f32[4,8,2048]{2,1,0:T(8,128)S(1)}, f32[4,8,2048]{2,1,0:T(8,128)S(1)}, u32[]{:S(2)}, u32[]{:S(2)}) collective-permute-start(f32[4,8,2048]{2,1,0:T(8,128)S(1)} %get-tuple-element.13), channel_id=1, source_target_pairs={{0,1},{1,0},{2,3},{3,2},{4,5},{5,4},{6,7},{7,6},{8,9},{9,8},{10,11... | collective-permute-start | bytes 786440 | tf_op jit(solution)/shard_map/ppermute | solution.py:248
  17.7 11.0 %collective-permute-start.13 = (f32[8,2048]{1,0:T(8,128)S(1)}, f32[8,2048]{1,0:T(8,128)S(1)}, u32[]{:S(2)}, u32[]{:S(2)}) collective-permute-start(f32[8,2048]{1,0:T(8,128)S(1)} %get-tuple-element.20), channel_id=1, source_target_pairs={{0,24},{8,16},{16,8},{24,0},{1,25},{9,17},{17,9},{25,1},{2,26},{10... | collective-permute-start | bytes 196616 | tf_op jit(solution)/shard_map/ppermute | solution.py:251
  25.9 5.5 %collective-permute-start.12 = (f32[8,2048]{1,0:T(8,128)S(1)}, f32[8,2048]{1,0:T(8,128)S(1)}, u32[]{:S(2)}, u32[]{:S(2)}) collective-permute-start(f32[8,2048]{1,0:T(8,128)S(1)} %get-tuple-element.21), channel_id=1, source_target_pairs={{0,16},{8,24},{16,0},{24,8},{1,17},{9,25},{17,1},{25,9},{2,18},{10... | collective-permute-start | bytes 196616 | tf_op jit(solution)/shard_map/ppermute | solution.py:251
  25.9 5.7 %collective-permute-start.11 = (f32[8,2048]{1,0:T(8,128)S(1)}, f32[8,2048]{1,0:T(8,128)S(1)}, u32[]{:S(2)}, u32[]{:S(2)}) collective-permute-start(f32[8,2048]{1,0:T(8,128)S(1)} %get-tuple-element.22), channel_id=1, source_target_pairs={{0,8},{8,0},{16,24},{24,16},{1,9},{9,1},{17,25},{25,17},{2,10},{10... | collective-permute-start | bytes 196616 | tf_op jit(solution)/shard_map/ppermute | solution.py:251
  26.6 5.7 %collective-permute-start.10 = (f32[8,2048]{1,0:T(8,128)S(1)}, f32[8,2048]{1,0:T(8,128)S(1)}, u32[]{:S(2)}, u32[]{:S(2)}) collective-permute-start(f32[8,2048]{1,0:T(8,128)S(1)} %get-tuple-element.17), channel_id=1, source_target_pairs={{0,6},{1,7},{2,4},{3,5},{4,2},{5,3},{6,0},{7,1},{8,14},{9,15},{10,... | collective-permute-start | bytes 196616 | tf_op jit(solution)/shard_map/ppermute | solution.py:248
  28.1 4.6 %collective-permute-start.9 = (f32[8,2048]{1,0:T(8,128)S(1)}, f32[8,2048]{1,0:T(8,128)S(1)}, u32[]{:S(2)}, u32[]{:S(2)}) collective-permute-start(f32[8,2048]{1,0:T(8,128)S(1)} %get-tuple-element.18), channel_id=1, source_target_pairs={{0,4},{1,5},{2,6},{3,7},{4,0},{5,1},{6,2},{7,3},{8,12},{9,13},{10,... | collective-permute-start | bytes 196616 | tf_op jit(solution)/shard_map/ppermute | solution.py:248
  28.8 4.3 %collective-permute-start.8 = (f32[8,2048]{1,0:T(8,128)S(1)}, f32[8,2048]{1,0:T(8,128)S(1)}, u32[]{:S(2)}, u32[]{:S(2)}) collective-permute-start(f32[8,2048]{1,0:T(8,128)S(1)} %get-tuple-element.19), channel_id=1, source_target_pairs={{0,2},{1,3},{2,0},{3,1},{4,6},{5,7},{6,4},{7,5},{8,10},{9,11},{10,... | collective-permute-start | bytes 196616 | tf_op jit(solution)/shard_map/ppermute | solution.py:248

commit v6 on v5

--- a/solution.py
+++ b/solution.py
@@ -10,7 +10,7 @@
 
 VMEM = pltpu.VMEM
 SMEM = pltpu.SMEM
-GROUP = 32
+GROUP = 64
 WAIT_FLOPS = 20_000_000_000
 MIB = 1 << 20
 
@@ -39,9 +39,9 @@
 
 def products_kernel(rows, planes, group, *refs):
     peers = max(planes, rows) - 1
-    count, tiles, row_idx_hbm, col_idx_hbm, diag_hbm, own_hbm, beside = refs[:7]
-    fetched = refs[7 : 7 + peers]
-    passed = refs[7 + peers : 7 + 2 * peers]
+    count, tiles, row_idx_hbm, col_idx_hbm, diag_hbm, chip = refs[:6]
+    fetched = refs[6 : 6 + peers]
+    passed = refs[6 + peers : 6 + 2 * peers]
     (
         keep_out,
         send_out,
@@ -49,19 +49,18 @@
         row_idx,
         col_idx,
         diag,
-        own,
         vec_rows,
         vec_cols,
         acc_rows,
         acc_cols,
         small_sems,
-    ) = refs[7 + 2 * peers :]
+    ) = refs[6 + 2 * peers :]
     row = lax.axis_index("row")
     col = lax.axis_index("col")
     plane, core = col // 2, col % 2
-    vectors = own.shape[0]
+    vectors = chip.shape[0] // 2
     width = tiles.shape[-1]
-    piece_tiles = own.shape[1] // width
+    piece_tiles = chip.shape[1] // width
     first = core == 0
 
     small = [
@@ -70,7 +69,6 @@
             (
                 (row_idx_hbm, row_idx),
                 (col_idx_hbm, col_idx),
-                (own_hbm, own),
                 (diag_hbm, diag),
             )
         )
@@ -106,11 +104,11 @@
                 first, passed[s - 1][vectors:, at], fetched[s - 1][:vectors, at]
             ),
         )
-    store_split(vec_rows, (col + 1 - 2 * core) * piece_tiles, lambda at: beside[:, at])
-    for copy in small:
-        copy.wait()
-    store_split(vec_rows, col * piece_tiles, lambda at: own[:, at])
-    store_split(vec_cols, row * piece_tiles, lambda at: own[:, at])
+    store_split(vec_rows, col * piece_tiles, lambda at: chip[:vectors, at])
+    store_split(vec_rows, (col + 1 - 2 * core) * piece_tiles, lambda at: chip[vectors:, at])
+    store_split(vec_cols, row * piece_tiles, lambda at: chip[:vectors, at])
+    small[0].wait()
+    small[1].wait()
 
     spare_row = acc_rows.shape[0] - 1
     spare_col = acc_cols.shape[0] - 1
@@ -139,6 +137,7 @@
         return carry
 
     lax.fori_loop(0, groups, multiply, 0)
+    small[2].wait()
 
     for s in range(planes):
         base = jnp.bitwise_xor(plane, s) * 2 * piece_tiles
@@ -152,7 +151,7 @@
             at = slice(t * width, (t + 1) * width)
             piece = acc_cols[base + t]
             if s == 0:
-                piece = piece + own[:, at] * diag[:, at]
+                piece = piece + chip[:vectors, at] * diag[:, at]
             col_out[s, :, at] = piece
 
 
@@ -220,15 +219,14 @@
     eye = (row_at == col_at).astype(jnp.float32)
     alpha_out[...] = contract(eye, alpha_t)
     work = jnp.concatenate([gram, eye, -left], axis=1)
-    below = lax.broadcasted_iota(jnp.int32, (vectors, 1), 0)
-    pivots = jnp.zeros((vectors, 1), jnp.float32)
+    line_at = lax.broadcasted_iota(jnp.int32, work.shape, 0)
+    pivots = jnp.ones_like(work)
     for j in range(vectors):
-        pivot = work[j : j + 1, j : j + 1]
-        line = work[j : j + 1, :]
-        pivots = jnp.where(below == j, pivot, pivots)
-        if j + 1 < vectors:
-            factor = jnp.where(below > j, work[:, j : j + 1] / pivot, 0.0)
-            work = work - factor * line
+        column = jnp.broadcast_to(work[:, j : j + 1], work.shape)
+        line = jnp.broadcast_to(work[j : j + 1, :], work.shape)
+        pivot = jnp.broadcast_to(column[j : j + 1, :], work.shape)
+        pivots = jnp.where(line_at == j, pivot, pivots)
+        work = work - jnp.where(line_at > j, column, 0.0) * (line / pivot)
     work = work / jnp.sqrt(pivots)
     beta_out[...] = jnp.where(col_at >= row_at, work[:, :vectors], 0.0)
     next_out[...] = matmul(
@@ -286,7 +284,7 @@
     chip = jnp.concatenate([block_now, beside], axis=0)
     peers = range(1, max(planes, rows))
     fetched = [apart(chip, s) for s in peers]
-    fetched[-1], fixed = lax.optimization_barrier((fetched[-1], fixed))
+    fetched[0], fixed = lax.optimization_barrier((fetched[0], fixed))
     passed = [along_col(x, 1) for x in fetched]
 
     group = math.gcd(slots, GROUP)
@@ -300,19 +298,18 @@
         ),
         in_specs=[pl.BlockSpec(memory_space=SMEM)]
         + [in_vmem]
-        + [in_hbm] * 4
+        + [in_hbm] * 3
         + [in_vmem] * (1 + 2 * len(peers)),
         out_specs=(in_vmem,) * 3,
         scratch_shapes=[
             SMEM(tile_rows.shape, jnp.int32),
             SMEM(tile_cols.shape, jnp.int32),
             VMEM((1, piece), f32),
-            VMEM((vectors, piece), f32),
             VMEM((cols * piece_tiles, 2 * vectors, width), jnp.bfloat16),
             VMEM((rows * piece_tiles, 2 * vectors, width), jnp.bfloat16),
             VMEM((cols * piece_tiles + 1, vectors, width), f32),
             VMEM((rows * piece_tiles + 1, vectors, width), f32),
-            pltpu.SemaphoreType.DMA((4,)),
+            pltpu.SemaphoreType.DMA((3,)),
         ],
         compiler_params=pltpu.CompilerParams(vmem_limit_bytes=20 * MIB),
         name="products",
@@ -322,8 +319,7 @@
         stay(tile_rows),
         stay(tile_cols),
         stay(diag_energy.reshape(1, piece)),
-        stay(block_now),
-        beside,
+        chip,
         *fetched,
         *passed,
     )

time: 48.2 us -> 47.3 us (0.981)
  starting transfers between devices: 18.7 us -> 17.9 us
    ppermute x3, starting transfers between devices: 8.82 us -> 7.81 us  [along_row(): return lax.ppermute(x, 'row', [(i, i ^ s) for i in range(rows)])]
    ppermute x3, waiting for transfers between devices: 4.27 us -> 3.31 us  [apart(): return lax.ppermute(x, ('row', 'col'), pairs)]
    ppermute x8, waiting for transfers between devices: 2.09 us -> 2.88 us  [along_col(): return lax.ppermute(x, 'col', [(i, i ^ s) for i in range(cols)])]
  transfers between devices with their start and end apart: 14 -> 14, of which waited for: 10 -> 9; matrix products, arithmetic and copies ran while one was open for 2% -> 2% of each run, Pallas kernels for 3% -> 3%
where the time goes in v6:
time: 47.3 us; the launch traced here: 47 us
  starting transfers between devices  17.9 us (38%)
  blocking collectives  12.6 us (27%)
  waiting for transfers between devices  7.63 us (16%)
  Pallas kernels  6.55 us (14%)
  between operations  1.41 us (3%)
  local copies, waits for them, and re-layouts  0.9 us (2%)
    all_to_all x1, blocking collectives, local(): sums = lax.all_to_all(sums, ('row', 'col'), 0, 0)  12.6 us
    ppermute x3, starting transfers between devices, along_row(): return lax.ppermute(x, 'row', [(i, i ^ s) for i in range(rows)])  7.81 us
    ppermute x8, starting transfers between devices, along_col(): return lax.ppermute(x, 'col', [(i, i ^ s) for i in range(cols)])  5.58 us
    ppermute x3, starting transfers between devices, apart(): return lax.ppermute(x, ('row', 'col'), pairs)  4.51 us
    ppermute x3, waiting for transfers between devices, apart(): return lax.ppermute(x, ('row', 'col'), pairs)  3.31 us
    ppermute x8, waiting for transfers between devices, along_col(): return lax.ppermute(x, 'col', [(i, i ^ s) for i in range(cols)])  2.88 us
    pallas_call x1, Pallas kernels, local(): pl.pallas_call(functools.partial(products_kernel, rows, planes, group), o...  2.36 us
    pallas_call x1, Pallas kernels, local(): pl.pallas_call(functools.partial(finish_kernel, float(piece * devices)),...  2.32 us
  transfers between devices with their start and end apart: 14, of which 9 were waited for; matrix products, arithmetic and copies ran while one was open for 2% of the time, Pallas kernels for 3%

profile of v6, /device:TPU:0, one launch (start us, length us, event | category | flops | bytes accessed | tf_op | source)
XLA Modules:
  0.0 47.0 jit_solution(16846859434067499131)
XLA Ops:
  0.6 0.5 %collective-permute-start = (f32[8,2048]{1,0:T(8,128)}, f32[8,2048]{1,0:T(8,128)S(1)}, u32[]{:S(2)}, u32[]{:S(2)}) collective-permute-start(f32[8,2048]{1,0:T(8,128)} %now.3), channel_id=1, source_target_pairs={{0,1},{1,0},{2,3},{3,2},{4,5},{5,4},{6,7},{7,6},{8,9},{9,8},{10,11... | collective-permute-start | bytes 196616 | tf_op jit(solution)/shard_map/ppermute | solution.py:246
  1.1 0.8 %constant_dynamic-update-slice_fusion.1 = f32[16,2048]{1,0:T(8,128)S(1)} fusion(f32[8,2048]{1,0:T(8,128)} %now.3), kind=kLoop, calls=%fused_computation.13 | loop fusion | bytes 131072
  2.0 0.3 collective-permute-done
  2.3 0.0 slice-start
  2.3 0.0 slice-start.1
  2.3 0.0 slice-start.2
  2.3 0.0 slice-start.3
  2.3 3.9 %collective-permute-start.3 = (f32[16,2048]{1,0:T(8,128)S(1)}, f32[16,2048]{1,0:T(8,128)S(1)}, u32[]{:S(2)}, u32[]{:S(2)}) collective-permute-start(f32[16,2048]{1,0:T(8,128)S(1)} %constant_dynamic-update-slice_fusion.refs_5_), channel_id=1, source_target_pairs={{0,6},{1,25},{2,4},{3,27},{4,2},{5,29},{6,0},{7,31},{8,14},{9,17},... | collective-permute-start | bytes 393224 | tf_op jit(solution)/shard_map/ppermute | solution.py:260
  6.2 0.5 %collective-permute-start.2 = (f32[16,2048]{1,0:T(8,128)S(1)}, f32[16,2048]{1,0:T(8,128)S(1)}, u32[]{:S(2)}, u32[]{:S(2)}) collective-permute-start(f32[16,2048]{1,0:T(8,128)S(1)} %constant_dynamic-update-slice_fusion.refs_5_), channel_id=1, source_target_pairs={{0,4},{1,17},{2,6},{3,19},{4,0},{5,21},{6,2},{7,23},{8,12},{9,25},... | collective-permute-start | bytes 393224 | tf_op jit(solution)/shard_map/ppermute | solution.py:260
  6.7 0.1 collective-permute-start.1
  6.8 1.5 %fixed.1.refs_2_ = f32[16,16]{1,0:T(8,128)S(1)} custom-call(f32[8,2048]{1,0:T(8,128)} %now.3, f32[8,2048]{1,0:T(8,128)} %prev.3), custom_call_target="tpu_custom_call" | custom-call | flops 20000000000 | bytes 131072 | tf_op jit(solution)/shard_map/fixed/pallas_call | solution.py:268
  8.3 0.0 copy-start
  8.3 0.0 copy-start.1
  8.3 0.0 copy-start.2
  8.3 3.3 %collective-permute-done.1.refs_6_ = f32[16,2048]{1,0:T(8,128)S(1)} collective-permute-done((f32[16,2048]{1,0:T(8,128)S(1)}, f32[16,2048]{1,0:T(8,128)S(1)}, u32[]{:S(2)}, u32[]{:S(2)}) %collective-permute-start.1) | collective-permute-done | bytes 131104 | tf_op jit(solution)/shard_map/ppermute | solution.py:260
  11.6 0.0 collective-permute-done.3.refs_8_
  11.6 0.3 collective-permute-start.6
  12.0 0.0 collective-permute-done.2.refs_7_
  12.0 0.9 %collective-permute-start.5 = (f32[16,2048]{1,0:T(8,128)S(1)}, f32[16,2048]{1,0:T(8,128)S(1)}, u32[]{:S(2)}, u32[]{:S(2)}) collective-permute-start(f32[16,2048]{1,0:T(8,128)S(1)} %collective-permute-done.2.refs_7_), channel_id=1, source_target_pairs={{0,1},{1,0},{2,3},{3,2},{4,5},{5,4},{6,7},{7,6},{8,9},{9,8},{10,11... | collective-permute-start | bytes 393224 | tf_op jit(solution)/shard_map/ppermute | solution.py:246
  12.9 0.0 collective-permute-start.4
  13.6 0.0 collective-permute-done.6.refs_11_
  13.6 0.3 collective-permute-done.5.refs_10_
  13.9 0.4 collective-permute-done.4.refs_9_
  14.3 0.0 slice-done
  14.3 0.0 slice-done.1
  14.3 0.0 slice-done.2
  14.3 0.0 slice-done.3
  14.3 2.4 %products.1 = (f32[4,8,2048]{2,1,0:T(8,128)S(1)}, f32[4,8,2048]{2,1,0:T(8,128)S(1)}, f32[4,8,2048]{2,1,0:T(8,128)S(1)}) custom-call(s32[1,1]{1,0:T(1,128)S(6)} %copy.12.refs_0_, f32[256,128,128]{2,1,0:T(8,128)S(1)} %bitcast.22, s32[1,1,256]{2,1,0:T(1,128)} %refs_2_.1, s32[1,1,256]{2,1,0:T(1,128)} %refs_3_.1, f32[1,2048]{1,0:T(1,128)} %bitcast.23, ...), custom_call_target="tpu_custom_call" | custom-call | tf_op jit(solution)/shard_map/products/pallas_call | solution.py:292
  16.7 0.2 collective-permute-start.7
  16.9 7.2 %collective-permute-start.13 = (f32[8,2048]{1,0:T(8,128)S(1)}, f32[8,2048]{1,0:T(8,128)S(1)}, u32[]{:S(2)}, u32[]{:S(2)}) collective-permute-start(f32[8,2048]{1,0:T(8,128)S(1)} %get-tuple-element.20), channel_id=1, source_target_pairs={{0,24},{8,16},{16,8},{24,0},{1,25},{9,17},{17,9},{25,1},{2,26},{10... | collective-permute-start | bytes 196616 | tf_op jit(solution)/shard_map/ppermute | solution.py:249
  24.1 0.0 collective-permute-start.12
  24.1 0.6 %collective-permute-start.11 = (f32[8,2048]{1,0:T(8,128)S(1)}, f32[8,2048]{1,0:T(8,128)S(1)}, u32[]{:S(2)}, u32[]{:S(2)}) collective-permute-start(f32[8,2048]{1,0:T(8,128)S(1)} %get-tuple-element.22), channel_id=1, source_target_pairs={{0,8},{8,0},{16,24},{24,16},{1,9},{9,1},{17,25},{25,17},{2,10},{10... | collective-permute-start | bytes 196616 | tf_op jit(solution)/shard_map/ppermute | solution.py:249
  24.7 0.0 collective-permute-done.7
  24.8 2.1 %collective-permute-start.10 = (f32[8,2048]{1,0:T(8,128)S(1)}, f32[8,2048]{1,0:T(8,128)S(1)}, u32[]{:S(2)}, u32[]{:S(2)}) collective-permute-start(f32[8,2048]{1,0:T(8,128)S(1)} %get-tuple-element.17), channel_id=1, source_target_pairs={{0,6},{1,7},{2,4},{3,5},{4,2},{5,3},{6,0},{7,1},{8,14},{9,15},{10,... | collective-permute-start | bytes 196616 | tf_op jit(solution)/shard_map/ppermute | solution.py:246
  26.9 0.5 %collective-permute-start.9 = (f32[8,2048]{1,0:T(8,128)S(1)}, f32[8,2048]{1,0:T(8,128)S(1)}, u32[]{:S(2)}, u32[]{:S(2)}) collective-permute-start(f32[8,2048]{1,0:T(8,128)S(1)} %get-tuple-element.18), channel_id=1, source_target_pairs={{0,4},{1,5},{2,6},{3,7},{4,0},{5,1},{6,2},{7,3},{8,12},{9,13},{10,... | collective-permute-start | bytes 196616 | tf_op jit(solution)/shard_map/ppermute | solution.py:246
  27.4 0.0 collective-permute-done.13.refs_11_
  27.4 0.9 %collective-permute-start.8 = (f32[8,2048]{1,0:T(8,128)S(1)}, f32[8,2048]{1,0:T(8,128)S(1)}, u32[]{:S(2)}, u32[]{:S(2)}) collective-permute-start(f32[8,2048]{1,0:T(8,128)S(1)} %get-tuple-element.19), channel_id=1, source_target_pairs={{0,2},{1,3},{2,0},{3,1},{4,6},{5,7},{6,4},{7,5},{8,10},{9,11},{10,... | collective-permute-start | bytes 196616 | tf_op jit(solution)/shard_map/ppermute | solution.py:246
  28.3 1.3 %collective-permute-done.12.refs_10_ = f32[8,2048]{1,0:T(8,128)S(1)} collective-permute-done((f32[8,2048]{1,0:T(8,128)S(1)}, f32[8,2048]{1,0:T(8,128)S(1)}, u32[]{:S(2)}, u32[]{:S(2)}) %collective-permute-start.12) | collective-permute-done | bytes 65568 | tf_op jit(solution)/shard_map/ppermute | solution.py:249
  29.6 0.2 collective-permute-done.11.refs_9_
  29.8 0.3 collective-permute-done.10.refs_8_
  30.1 1.1 %collective-permute-done.9.refs_7_ = f32[8,2048]{1,0:T(8,128)S(1)} collective-permute-done((f32[8,2048]{1,0:T(8,128)S(1)}, f32[8,2048]{1,0:T(8,128)S(1)}, u32[]{:S(2)}, u32[]{:S(2)}) %collective-permute-start.9) | collective-permute-done | bytes 65568 | tf_op jit(solution)/shard_map/ppermute | solution.py:246
  31.2 0.5 %collective-permute-done.8.refs_6_ = f32[8,2048]{1,0:T(8,128)S(1)} collective-permute-done((f32[8,2048]{1,0:T(8,128)S(1)}, f32[8,2048]{1,0:T(8,128)S(1)}, u32[]{:S(2)}, u32[]{:S(2)}) %collective-permute-start.8) | collective-permute-done | bytes 65568 | tf_op jit(solution)/shard_map/ppermute | solution.py:246
  31.7 0.0 copy-done
  31.7 0.0 copy-done.1
  31.7 0.4 image.1
  32.1 12.6 %all_to_all.5.sums_in = f32[32,4,128]{2,1,0:T(4,128)S(1)} all-to-all(f32[32,4,128]{2,1,0:T(4,128)S(1)} %get-tuple-element.15), channel_id=1, replica_groups=mesh['row'=4,'col'=8] {'row','col'}, dimensions={0} | all-to-all | bytes 131072 | tf_op jit(solution)/shard_map/all_to_all | solution.py:346
  44.7 0.0 copy-done.2
  44.7 2.3 %finish.1 = (f32[8,2048]{1,0:T(8,128)}, f32[8,8]{1,0:T(8,128)}, f32[8,8]{1,0:T(8,128)}) custom-call(f32[32,4,128]{2,1,0:T(4,128)S(1)} %all_to_all.5.sums_in, f32[8,2048]{1,0:T(8,128)S(1)} %get-tuple-element.16.image, f32[8,2048]{1,0:T(8,128)S(1)} %copy-done, f32[8,2048]{1,0:T(8,128)S(1)} %copy-done.1, f32[8,8]{1,0:T(8,128)S(1)} %copy-done.2), custom_call_target="tpu_custom_call" | custom-call | tf_op jit(solution)/shard_map/finish/pallas_call | solution.py:347
  (4 shorter events, 0.1 us)
Async XLA Ops:
  0.6 1.6 %collective-permute-start = (f32[8,2048]{1,0:T(8,128)}, f32[8,2048]{1,0:T(8,128)S(1)}, u32[]{:S(2)}, u32[]{:S(2)}) collective-permute-start(f32[8,2048]{1,0:T(8,128)} %now.3), channel_id=1, source_target_pairs={{0,1},{1,0},{2,3},{3,2},{4,5},{5,4},{6,7},{7,6},{8,9},{9,8},{10,11... | collective-permute-start | bytes 196616 | tf_op jit(solution)/shard_map/ppermute | solution.py:246
  2.3 12.0 %slice-start = ((s8[16777216]{0:T(1024)(128)(4,1)}), s8[4194304]{0:T(1024)(128)(4,1)S(1)}, s32[]{:S(2)}) async-start(s8[16777216]{0:T(1024)(128)(4,1)} %bitcast.20), calls=%async_computation.1 | async-start | bytes 8388608
  2.3 12.0 %slice-start.1 = ((s8[16777216]{0:T(1024)(128)(4,1)}), s8[4194304]{0:T(1024)(128)(4,1)S(1)}, s32[]{:S(2)}) async-start(s8[16777216]{0:T(1024)(128)(4,1)} %bitcast.20), calls=%async_computation.2 | async-start | bytes 8388608
  2.3 12.0 %slice-start.2 = ((s8[16777216]{0:T(1024)(128)(4,1)}), s8[4194304]{0:T(1024)(128)(4,1)S(1)}, s32[]{:S(2)}) async-start(s8[16777216]{0:T(1024)(128)(4,1)} %bitcast.20), calls=%async_computation.3 | async-start | bytes 8388608
  2.3 12.0 %slice-start.3 = ((s8[16777216]{0:T(1024)(128)(4,1)}), s8[4194304]{0:T(1024)(128)(4,1)S(1)}, s32[]{:S(2)}) async-start(s8[16777216]{0:T(1024)(128)(4,1)} %bitcast.20), calls=%async_computation.4 | async-start | bytes 8388608
  2.3 9.3 %collective-permute-start.3 = (f32[16,2048]{1,0:T(8,128)S(1)}, f32[16,2048]{1,0:T(8,128)S(1)}, u32[]{:S(2)}, u32[]{:S(2)}) collective-permute-start(f32[16,2048]{1,0:T(8,128)S(1)} %constant_dynamic-update-slice_fusion.refs_5_), channel_id=1, source_target_pairs={{0,6},{1,25},{2,4},{3,27},{4,2},{5,29},{6,0},{7,31},{8,14},{9,17},... | collective-permute-start | bytes 393224 | tf_op jit(solution)/shard_map/ppermute | solution.py:260
  6.2 5.8 %collective-permute-start.2 = (f32[16,2048]{1,0:T(8,128)S(1)}, f32[16,2048]{1,0:T(8,128)S(1)}, u32[]{:S(2)}, u32[]{:S(2)}) collective-permute-start(f32[16,2048]{1,0:T(8,128)S(1)} %constant_dynamic-update-slice_fusion.refs_5_), channel_id=1, source_target_pairs={{0,4},{1,17},{2,6},{3,19},{4,0},{5,21},{6,2},{7,23},{8,12},{9,25},... | collective-permute-start | bytes 393224 | tf_op jit(solution)/shard_map/ppermute | solution.py:260
  6.7 5.0 %collective-permute-start.1 = (f32[16,2048]{1,0:T(8,128)S(1)}, f32[16,2048]{1,0:T(8,128)S(1)}, u32[]{:S(2)}, u32[]{:S(2)}) collective-permute-start(f32[16,2048]{1,0:T(8,128)S(1)} %constant_dynamic-update-slice_fusion.refs_5_), channel_id=1, source_target_pairs={{0,2},{1,9},{2,0},{3,11},{4,6},{5,13},{6,4},{7,15},{8,10},{9,1},{1... | collective-permute-start | bytes 393224 | tf_op jit(solution)/shard_map/ppermute | solution.py:260
  8.3 23.4 %copy-start = (f32[8,2048]{1,0:T(8,128)S(1)}, f32[8,2048]{1,0:T(8,128)}, u32[]{:S(2)}) copy-start(f32[8,2048]{1,0:T(8,128)} %now.3) | copy-start | bytes 196612
  8.3 23.4 %copy-start.1 = (f32[8,2048]{1,0:T(8,128)S(1)}, f32[8,2048]{1,0:T(8,128)}, u32[]{:S(2)}) copy-start(f32[8,2048]{1,0:T(8,128)} %prev.3) | copy-start | bytes 196612
  8.3 36.4 %copy-start.2 = (f32[8,8]{1,0:T(8,128)S(1)}, f32[8,8]{1,0:T(8,128)}, u32[]{:S(2)}) copy-start(f32[8,8]{1,0:T(8,128)} %coupling.1) | copy-start | bytes 772
  11.6 1.9 %collective-permute-start.6 = (f32[16,2048]{1,0:T(8,128)S(1)}, f32[16,2048]{1,0:T(8,128)S(1)}, u32[]{:S(2)}, u32[]{:S(2)}) collective-permute-start(f32[16,2048]{1,0:T(8,128)S(1)} %collective-permute-done.3.refs_8_), channel_id=1, source_target_pairs={{0,1},{1,0},{2,3},{3,2},{4,5},{5,4},{6,7},{7,6},{8,9},{9,8},{10,11... | collective-permute-start | bytes 393224 | tf_op jit(solution)/shard_map/ppermute | solution.py:246
  12.0 1.9 %collective-permute-start.5 = (f32[16,2048]{1,0:T(8,128)S(1)}, f32[16,2048]{1,0:T(8,128)S(1)}, u32[]{:S(2)}, u32[]{:S(2)}) collective-permute-start(f32[16,2048]{1,0:T(8,128)S(1)} %collective-permute-done.2.refs_7_), channel_id=1, source_target_pairs={{0,1},{1,0},{2,3},{3,2},{4,5},{5,4},{6,7},{7,6},{8,9},{9,8},{10,11... | collective-permute-start | bytes 393224 | tf_op jit(solution)/shard_map/ppermute | solution.py:246
  12.9 1.3 %collective-permute-start.4 = (f32[16,2048]{1,0:T(8,128)S(1)}, f32[16,2048]{1,0:T(8,128)S(1)}, u32[]{:S(2)}, u32[]{:S(2)}) collective-permute-start(f32[16,2048]{1,0:T(8,128)S(1)} %collective-permute-done.1.refs_6_), channel_id=1, source_target_pairs={{0,1},{1,0},{2,3},{3,2},{4,5},{5,4},{6,7},{7,6},{8,9},{9,8},{10,11... | collective-permute-start | bytes 393224 | tf_op jit(solution)/shard_map/ppermute | solution.py:246
  16.7 8.1 %collective-permute-start.7 = (f32[4,8,2048]{2,1,0:T(8,128)S(1)}, f32[4,8,2048]{2,1,0:T(8,128)S(1)}, u32[]{:S(2)}, u32[]{:S(2)}) collective-permute-start(f32[4,8,2048]{2,1,0:T(8,128)S(1)} %get-tuple-element.13), channel_id=1, source_target_pairs={{0,1},{1,0},{2,3},{3,2},{4,5},{5,4},{6,7},{7,6},{8,9},{9,8},{10,11... | collective-permute-start | bytes 786440 | tf_op jit(solution)/shard_map/ppermute | solution.py:246
  16.9 10.5 %collective-permute-start.13 = (f32[8,2048]{1,0:T(8,128)S(1)}, f32[8,2048]{1,0:T(8,128)S(1)}, u32[]{:S(2)}, u32[]{:S(2)}) collective-permute-start(f32[8,2048]{1,0:T(8,128)S(1)} %get-tuple-element.20), channel_id=1, source_target_pairs={{0,24},{8,16},{16,8},{24,0},{1,25},{9,17},{17,9},{25,1},{2,26},{10... | collective-permute-start | bytes 196616 | tf_op jit(solution)/shard_map/ppermute | solution.py:249
  24.1 5.5 %collective-permute-start.12 = (f32[8,2048]{1,0:T(8,128)S(1)}, f32[8,2048]{1,0:T(8,128)S(1)}, u32[]{:S(2)}, u32[]{:S(2)}) collective-permute-start(f32[8,2048]{1,0:T(8,128)S(1)} %get-tuple-element.21), channel_id=1, source_target_pairs={{0,16},{8,24},{16,0},{24,8},{1,17},{9,25},{17,1},{25,9},{2,18},{10... | collective-permute-start | bytes 196616 | tf_op jit(solution)/shard_map/ppermute | solution.py:249
  24.1 5.7 %collective-permute-start.11 = (f32[8,2048]{1,0:T(8,128)S(1)}, f32[8,2048]{1,0:T(8,128)S(1)}, u32[]{:S(2)}, u32[]{:S(2)}) collective-permute-start(f32[8,2048]{1,0:T(8,128)S(1)} %get-tuple-element.22), channel_id=1, source_target_pairs={{0,8},{8,0},{16,24},{24,16},{1,9},{9,1},{17,25},{25,17},{2,10},{10... | collective-permute-start | bytes 196616 | tf_op jit(solution)/shard_map/ppermute | solution.py:249
  24.8 5.3 %collective-permute-start.10 = (f32[8,2048]{1,0:T(8,128)S(1)}, f32[8,2048]{1,0:T(8,128)S(1)}, u32[]{:S(2)}, u32[]{:S(2)}) collective-permute-start(f32[8,2048]{1,0:T(8,128)S(1)} %get-tuple-element.17), channel_id=1, source_target_pairs={{0,6},{1,7},{2,4},{3,5},{4,2},{5,3},{6,0},{7,1},{8,14},{9,15},{10,... | collective-permute-start | bytes 196616 | tf_op jit(solution)/shard_map/ppermute | solution.py:246
  26.9 4.3 %collective-permute-start.9 = (f32[8,2048]{1,0:T(8,128)S(1)}, f32[8,2048]{1,0:T(8,128)S(1)}, u32[]{:S(2)}, u32[]{:S(2)}) collective-permute-start(f32[8,2048]{1,0:T(8,128)S(1)} %get-tuple-element.18), channel_id=1, source_target_pairs={{0,4},{1,5},{2,6},{3,7},{4,0},{5,1},{6,2},{7,3},{8,12},{9,13},{10,... | collective-permute-start | bytes 196616 | tf_op jit(solution)/shard_map/ppermute | solution.py:246
  27.4 4.3 %collective-permute-start.8 = (f32[8,2048]{1,0:T(8,128)S(1)}, f32[8,2048]{1,0:T(8,128)S(1)}, u32[]{:S(2)}, u32[]{:S(2)}) collective-permute-start(f32[8,2048]{1,0:T(8,128)S(1)} %get-tuple-element.19), channel_id=1, source_target_pairs={{0,2},{1,3},{2,0},{3,1},{4,6},{5,7},{6,4},{7,5},{8,10},{9,11},{10,... | collective-permute-start | bytes 196616 | tf_op jit(solution)/shard_map/ppermute | solution.py:246

commit v7 on v6

--- a/solution.py
+++ b/solution.py
@@ -219,14 +219,15 @@
     eye = (row_at == col_at).astype(jnp.float32)
     alpha_out[...] = contract(eye, alpha_t)
     work = jnp.concatenate([gram, eye, -left], axis=1)
-    line_at = lax.broadcasted_iota(jnp.int32, work.shape, 0)
-    pivots = jnp.ones_like(work)
+    below = lax.broadcasted_iota(jnp.int32, (vectors, 1), 0)
+    pivots = jnp.zeros((vectors, 1), jnp.float32)
     for j in range(vectors):
-        column = jnp.broadcast_to(work[:, j : j + 1], work.shape)
-        line = jnp.broadcast_to(work[j : j + 1, :], work.shape)
-        pivot = jnp.broadcast_to(column[j : j + 1, :], work.shape)
-        pivots = jnp.where(line_at == j, pivot, pivots)
-        work = work - jnp.where(line_at > j, column, 0.0) * (line / pivot)
+        pivot = work[j : j + 1, j : j + 1]
+        line = work[j : j + 1, :]
+        pivots = jnp.where(below == j, pivot, pivots)
+        if j + 1 < vectors:
+            factor = jnp.where(below > j, work[:, j : j + 1] / pivot, 0.0)
+            work = work - factor * line
     work = work / jnp.sqrt(pivots)
     beta_out[...] = jnp.where(col_at >= row_at, work[:, :vectors], 0.0)
     next_out[...] = matmul(
@@ -324,9 +325,11 @@
         *passed,
     )
 
-    back_rows = [along_row(col_parts[s], s) for s in range(1, rows)]
     from_core = along_col(send, 1)
     summed = [keep[s] + from_core[s] for s in range(1, planes)]
+    nearest, *summed = lax.optimization_barrier((col_parts[1], *summed))
+    back_rows = [along_row(nearest, 1)]
+    back_rows += [along_row(col_parts[s], s) for s in range(2, rows)]
     back_planes = [along_col(summed[s - 1], 2 * s) for s in range(1, planes)]
     terms = [keep[0], from_core[0], col_parts[0], *back_planes, *back_rows]
 

time: 47.3 us -> 47 us (level)
    ppermute x8, waiting for transfers between devices: 2.88 us -> 3.49 us  [along_col(): return lax.ppermute(x, 'col', [(i, i ^ s) for i in range(cols)])]
  transfers between devices with their start and end apart: 14 -> 14, of which waited for: 9 -> 7; matrix products, arithmetic and copies ran while one was open for 2% -> 2% of each run, Pallas kernels for 3% -> 3%
where the time goes in v7:
time: 47 us; the launch traced here: 46.8 us
  starting transfers between devices  17.9 us (38%)
  blocking collectives  12.2 us (26%)
  waiting for transfers between devices  7.95 us (17%)
  Pallas kernels  6.33 us (13%)
  between operations  1.41 us (3%)
  local copies, waits for them, and re-layouts  0.9 us (2%)
    all_to_all x1, blocking collectives, local(): sums = lax.all_to_all(sums, ('row', 'col'), 0, 0)  12.2 us
    ppermute x3, starting transfers between devices, along_row(): return lax.ppermute(x, 'row', [(i, i ^ s) for i in range(rows)])  7.82 us
    ppermute x8, starting transfers between devices, along_col(): return lax.ppermute(x, 'col', [(i, i ^ s) for i in range(cols)])  5.56 us
    ppermute x3, starting transfers between devices, apart(): return lax.ppermute(x, ('row', 'col'), pairs)  4.51 us
    ppermute x8, waiting for transfers between devices, along_col(): return lax.ppermute(x, 'col', [(i, i ^ s) for i in range(cols)])  3.49 us
    ppermute x3, waiting for transfers between devices, apart(): return lax.ppermute(x, ('row', 'col'), pairs)  3.31 us
    pallas_call x1, Pallas kernels, local(): pl.pallas_call(functools.partial(products_kernel, rows, planes, group), o...  2.36 us
    pallas_call x1, Pallas kernels, local(): pl.pallas_call(functools.partial(finish_kernel, float(piece * devices)),...  2.1 us
  transfers between devices with their start and end apart: 14, of which 7 were waited for; matrix products, arithmetic and copies ran while one was open for 2% of the time, Pallas kernels for 3%

profile of v7, /device:TPU:0, one launch (start us, length us, event | category | flops | bytes accessed | tf_op | source)
XLA Modules:
  0.0 46.8 jit_solution(4321622250471467253)
XLA Ops:
  0.6 0.5 %collective-permute-start = (f32[8,2048]{1,0:T(8,128)}, f32[8,2048]{1,0:T(8,128)S(1)}, u32[]{:S(2)}, u32[]{:S(2)}) collective-permute-start(f32[8,2048]{1,0:T(8,128)} %now.3), channel_id=1, source_target_pairs={{0,1},{1,0},{2,3},{3,2},{4,5},{5,4},{6,7},{7,6},{8,9},{9,8},{10,11... | collective-permute-start | bytes 196616 | tf_op jit(solution)/shard_map/ppermute | solution.py:247
  1.1 0.8 %constant_dynamic-update-slice_fusion.1 = f32[16,2048]{1,0:T(8,128)S(1)} fusion(f32[8,2048]{1,0:T(8,128)} %now.3), kind=kLoop, calls=%fused_computation.13 | loop fusion | bytes 131072
  2.0 0.3 collective-permute-done
  2.3 0.0 slice-start
  2.3 0.0 slice-start.1
  2.3 0.0 slice-start.2
  2.3 0.0 slice-start.3
  2.3 3.9 %collective-permute-start.3 = (f32[16,2048]{1,0:T(8,128)S(1)}, f32[16,2048]{1,0:T(8,128)S(1)}, u32[]{:S(2)}, u32[]{:S(2)}) collective-permute-start(f32[16,2048]{1,0:T(8,128)S(1)} %constant_dynamic-update-slice_fusion.refs_5_), channel_id=1, source_target_pairs={{0,6},{1,25},{2,4},{3,27},{4,2},{5,29},{6,0},{7,31},{8,14},{9,17},... | collective-permute-start | bytes 393224 | tf_op jit(solution)/shard_map/ppermute | solution.py:261
  6.2 0.5 %collective-permute-start.2 = (f32[16,2048]{1,0:T(8,128)S(1)}, f32[16,2048]{1,0:T(8,128)S(1)}, u32[]{:S(2)}, u32[]{:S(2)}) collective-permute-start(f32[16,2048]{1,0:T(8,128)S(1)} %constant_dynamic-update-slice_fusion.refs_5_), channel_id=1, source_target_pairs={{0,4},{1,17},{2,6},{3,19},{4,0},{5,21},{6,2},{7,23},{8,12},{9,25},... | collective-permute-start | bytes 393224 | tf_op jit(solution)/shard_map/ppermute | solution.py:261
  6.7 0.1 collective-permute-start.1
  6.8 1.5 %fixed.1.refs_2_ = f32[16,16]{1,0:T(8,128)S(1)} custom-call(f32[8,2048]{1,0:T(8,128)} %now.3, f32[8,2048]{1,0:T(8,128)} %prev.3), custom_call_target="tpu_custom_call" | custom-call | flops 20000000000 | bytes 131072 | tf_op jit(solution)/shard_map/fixed/pallas_call | solution.py:269
  8.3 0.0 copy-start
  8.3 0.0 copy-start.1
  8.3 0.0 copy-start.2
  8.3 3.3 %collective-permute-done.1.refs_6_ = f32[16,2048]{1,0:T(8,128)S(1)} collective-permute-done((f32[16,2048]{1,0:T(8,128)S(1)}, f32[16,2048]{1,0:T(8,128)S(1)}, u32[]{:S(2)}, u32[]{:S(2)}) %collective-permute-start.1) | collective-permute-done | bytes 131104 | tf_op jit(solution)/shard_map/ppermute | solution.py:261
  11.6 0.0 collective-permute-done.3.refs_8_
  11.6 0.3 collective-permute-start.6
  12.0 0.0 collective-permute-done.2.refs_7_
  12.0 0.9 %collective-permute-start.5 = (f32[16,2048]{1,0:T(8,128)S(1)}, f32[16,2048]{1,0:T(8,128)S(1)}, u32[]{:S(2)}, u32[]{:S(2)}) collective-permute-start(f32[16,2048]{1,0:T(8,128)S(1)} %collective-permute-done.2.refs_7_), channel_id=1, source_target_pairs={{0,1},{1,0},{2,3},{3,2},{4,5},{5,4},{6,7},{7,6},{8,9},{9,8},{10,11... | collective-permute-start | bytes 393224 | tf_op jit(solution)/shard_map/ppermute | solution.py:247
  12.9 0.0 collective-permute-start.4
  13.6 0.0 collective-permute-done.6.refs_11_
  13.6 0.3 collective-permute-done.5.refs_10_
  13.9 0.4 collective-permute-done.4.refs_9_
  14.3 0.0 slice-done
  14.3 0.0 slice-done.1
  14.3 0.0 slice-done.2
  14.3 0.0 slice-done.3
  14.3 2.4 %products.1 = (f32[4,8,2048]{2,1,0:T(8,128)S(1)}, f32[4,8,2048]{2,1,0:T(8,128)S(1)}, f32[4,8,2048]{2,1,0:T(8,128)S(1)}) custom-call(s32[1,1]{1,0:T(1,128)S(6)} %copy.12.refs_0_, f32[256,128,128]{2,1,0:T(8,128)S(1)} %bitcast.22, s32[1,1,256]{2,1,0:T(1,128)} %refs_2_.1, s32[1,1,256]{2,1,0:T(1,128)} %refs_3_.1, f32[1,2048]{1,0:T(1,128)} %bitcast.23, ...), custom_call_target="tpu_custom_call" | custom-call | tf_op jit(solution)/shard_map/products/pallas_call | solution.py:293
  16.7 0.2 collective-permute-start.7
  16.9 7.2 %collective-permute-start.13 = (f32[8,2048]{1,0:T(8,128)S(1)}, f32[8,2048]{1,0:T(8,128)S(1)}, u32[]{:S(2)}, u32[]{:S(2)}) collective-permute-start(f32[8,2048]{1,0:T(8,128)S(1)} %get-tuple-element.28), channel_id=1, source_target_pairs={{0,24},{8,16},{16,8},{24,0},{1,25},{9,17},{17,9},{25,1},{2,26},{10... | collective-permute-start | bytes 196616 | tf_op jit(solution)/shard_map/ppermute | solution.py:250
  24.1 0.0 collective-permute-start.12
  24.1 0.0 collective-permute-done.7
  24.1 1.2 %collective-permute-start.8 = (f32[8,2048]{1,0:T(8,128)S(1)}, f32[8,2048]{1,0:T(8,128)S(1)}, u32[]{:S(2)}, u32[]{:S(2)}) collective-permute-start(f32[8,2048]{1,0:T(8,128)S(1)} %get-tuple-element.19), channel_id=1, source_target_pairs={{0,2},{1,3},{2,0},{3,1},{4,6},{5,7},{6,4},{7,5},{8,10},{9,11},{10,... | collective-permute-start | bytes 196616 | tf_op jit(solution)/shard_map/ppermute | solution.py:247
  25.3 1.5 %collective-permute-start.9 = (f32[8,2048]{1,0:T(8,128)S(1)}, f32[8,2048]{1,0:T(8,128)S(1)}, u32[]{:S(2)}, u32[]{:S(2)}) collective-permute-start(f32[8,2048]{1,0:T(8,128)S(1)} %get-tuple-element.20), channel_id=1, source_target_pairs={{0,4},{1,5},{2,6},{3,7},{4,0},{5,1},{6,2},{7,3},{8,12},{9,13},{10,... | collective-permute-start | bytes 196616 | tf_op jit(solution)/shard_map/ppermute | solution.py:247
  26.9 0.8 %collective-permute-start.10 = (f32[8,2048]{1,0:T(8,128)S(1)}, f32[8,2048]{1,0:T(8,128)S(1)}, u32[]{:S(2)}, u32[]{:S(2)}) collective-permute-start(f32[8,2048]{1,0:T(8,128)S(1)} %get-tuple-element.21), channel_id=1, source_target_pairs={{0,6},{1,7},{2,4},{3,5},{4,2},{5,3},{6,0},{7,1},{8,14},{9,15},{10,... | collective-permute-start | bytes 196616 | tf_op jit(solution)/shard_map/ppermute | solution.py:247
  27.7 0.0 collective-permute-done.13.refs_11_
  27.7 0.6 %collective-permute-start.11 = (f32[8,2048]{1,0:T(8,128)S(1)}, f32[8,2048]{1,0:T(8,128)S(1)}, u32[]{:S(2)}, u32[]{:S(2)}) collective-permute-start(f32[8,2048]{1,0:T(8,128)S(1)} %get-tuple-element.22), channel_id=1, source_target_pairs={{0,8},{8,0},{16,24},{24,16},{1,9},{9,1},{17,25},{25,17},{2,10},{10... | collective-permute-start | bytes 196616 | tf_op jit(solution)/shard_map/ppermute | solution.py:250
  28.3 1.1 %collective-permute-done.12.refs_10_ = f32[8,2048]{1,0:T(8,128)S(1)} collective-permute-done((f32[8,2048]{1,0:T(8,128)S(1)}, f32[8,2048]{1,0:T(8,128)S(1)}, u32[]{:S(2)}, u32[]{:S(2)}) %collective-permute-start.12) | collective-permute-done | bytes 65568 | tf_op jit(solution)/shard_map/ppermute | solution.py:250
  29.5 0.0 collective-permute-done.8.refs_6_
  29.5 0.1 collective-permute-done.9.refs_7_
  29.6 2.4 %collective-permute-done.10.refs_8_ = f32[8,2048]{1,0:T(8,128)S(1)} collective-permute-done((f32[8,2048]{1,0:T(8,128)S(1)}, f32[8,2048]{1,0:T(8,128)S(1)}, u32[]{:S(2)}, u32[]{:S(2)}) %collective-permute-start.10) | collective-permute-done | bytes 65568 | tf_op jit(solution)/shard_map/ppermute | solution.py:247
  32.0 0.0 collective-permute-done.11.refs_9_
  32.0 0.0 copy-done
  32.0 0.0 copy-done.1
  32.0 0.4 image.1
  32.4 12.2 %all_to_all.5.sums_in = f32[32,4,128]{2,1,0:T(4,128)S(1)} all-to-all(f32[32,4,128]{2,1,0:T(4,128)S(1)} %get-tuple-element.23), channel_id=1, replica_groups=mesh['row'=4,'col'=8] {'row','col'}, dimensions={0} | all-to-all | bytes 131072 | tf_op jit(solution)/shard_map/all_to_all | solution.py:349
  44.7 0.0 copy-done.2
  44.7 2.1 %finish.1 = (f32[8,2048]{1,0:T(8,128)}, f32[8,8]{1,0:T(8,128)}, f32[8,8]{1,0:T(8,128)}) custom-call(f32[32,4,128]{2,1,0:T(4,128)S(1)} %all_to_all.5.sums_in, f32[8,2048]{1,0:T(8,128)S(1)} %get-tuple-element.24.image, f32[8,2048]{1,0:T(8,128)S(1)} %copy-done, f32[8,2048]{1,0:T(8,128)S(1)} %copy-done.1, f32[8,8]{1,0:T(8,128)S(1)} %copy-done.2), custom_call_target="tpu_custom_call" | custom-call | tf_op jit(solution)/shard_map/finish/pallas_call | solution.py:350
  (4 shorter events, 0.1 us)
Async XLA Ops:
  0.6 1.6 %collective-permute-start = (f32[8,2048]{1,0:T(8,128)}, f32[8,2048]{1,0:T(8,128)S(1)}, u32[]{:S(2)}, u32[]{:S(2)}) collective-permute-start(f32[8,2048]{1,0:T(8,128)} %now.3), channel_id=1, source_target_pairs={{0,1},{1,0},{2,3},{3,2},{4,5},{5,4},{6,7},{7,6},{8,9},{9,8},{10,11... | collective-permute-start | bytes 196616 | tf_op jit(solution)/shard_map/ppermute | solution.py:247
  2.3 12.0 %slice-start = ((s8[16777216]{0:T(1024)(128)(4,1)}), s8[4194304]{0:T(1024)(128)(4,1)S(1)}, s32[]{:S(2)}) async-start(s8[16777216]{0:T(1024)(128)(4,1)} %bitcast.20), calls=%async_computation.1 | async-start | bytes 8388608
  2.3 12.0 %slice-start.1 = ((s8[16777216]{0:T(1024)(128)(4,1)}), s8[4194304]{0:T(1024)(128)(4,1)S(1)}, s32[]{:S(2)}) async-start(s8[16777216]{0:T(1024)(128)(4,1)} %bitcast.20), calls=%async_computation.2 | async-start | bytes 8388608
  2.3 12.0 %slice-start.2 = ((s8[16777216]{0:T(1024)(128)(4,1)}), s8[4194304]{0:T(1024)(128)(4,1)S(1)}, s32[]{:S(2)}) async-start(s8[16777216]{0:T(1024)(128)(4,1)} %bitcast.20), calls=%async_computation.3 | async-start | bytes 8388608
  2.3 12.0 %slice-start.3 = ((s8[16777216]{0:T(1024)(128)(4,1)}), s8[4194304]{0:T(1024)(128)(4,1)S(1)}, s32[]{:S(2)}) async-start(s8[16777216]{0:T(1024)(128)(4,1)} %bitcast.20), calls=%async_computation.4 | async-start | bytes 8388608
  2.3 9.3 %collective-permute-start.3 = (f32[16,2048]{1,0:T(8,128)S(1)}, f32[16,2048]{1,0:T(8,128)S(1)}, u32[]{:S(2)}, u32[]{:S(2)}) collective-permute-start(f32[16,2048]{1,0:T(8,128)S(1)} %constant_dynamic-update-slice_fusion.refs_5_), channel_id=1, source_target_pairs={{0,6},{1,25},{2,4},{3,27},{4,2},{5,29},{6,0},{7,31},{8,14},{9,17},... | collective-permute-start | bytes 393224 | tf_op jit(solution)/shard_map/ppermute | solution.py:261
  6.2 5.8 %collective-permute-start.2 = (f32[16,2048]{1,0:T(8,128)S(1)}, f32[16,2048]{1,0:T(8,128)S(1)}, u32[]{:S(2)}, u32[]{:S(2)}) collective-permute-start(f32[16,2048]{1,0:T(8,128)S(1)} %constant_dynamic-update-slice_fusion.refs_5_), channel_id=1, source_target_pairs={{0,4},{1,17},{2,6},{3,19},{4,0},{5,21},{6,2},{7,23},{8,12},{9,25},... | collective-permute-start | bytes 393224 | tf_op jit(solution)/shard_map/ppermute | solution.py:261
  6.7 5.0 %collective-permute-start.1 = (f32[16,2048]{1,0:T(8,128)S(1)}, f32[16,2048]{1,0:T(8,128)S(1)}, u32[]{:S(2)}, u32[]{:S(2)}) collective-permute-start(f32[16,2048]{1,0:T(8,128)S(1)} %constant_dynamic-update-slice_fusion.refs_5_), channel_id=1, source_target_pairs={{0,2},{1,9},{2,0},{3,11},{4,6},{5,13},{6,4},{7,15},{8,10},{9,1},{1... | collective-permute-start | bytes 393224 | tf_op jit(solution)/shard_map/ppermute | solution.py:261
  8.3 23.7 %copy-start = (f32[8,2048]{1,0:T(8,128)S(1)}, f32[8,2048]{1,0:T(8,128)}, u32[]{:S(2)}) copy-start(f32[8,2048]{1,0:T(8,128)} %now.3) | copy-start | bytes 196612
  8.3 23.7 %copy-start.1 = (f32[8,2048]{1,0:T(8,128)S(1)}, f32[8,2048]{1,0:T(8,128)}, u32[]{:S(2)}) copy-start(f32[8,2048]{1,0:T(8,128)} %prev.3) | copy-start | bytes 196612
  8.3 36.4 %copy-start.2 = (f32[8,8]{1,0:T(8,128)S(1)}, f32[8,8]{1,0:T(8,128)}, u32[]{:S(2)}) copy-start(f32[8,8]{1,0:T(8,128)} %coupling.1) | copy-start | bytes 772
  11.6 1.9 %collective-permute-start.6 = (f32[16,2048]{1,0:T(8,128)S(1)}, f32[16,2048]{1,0:T(8,128)S(1)}, u32[]{:S(2)}, u32[]{:S(2)}) collective-permute-start(f32[16,2048]{1,0:T(8,128)S(1)} %collective-permute-done.3.refs_8_), channel_id=1, source_target_pairs={{0,1},{1,0},{2,3},{3,2},{4,5},{5,4},{6,7},{7,6},{8,9},{9,8},{10,11... | collective-permute-start | bytes 393224 | tf_op jit(solution)/shard_map/ppermute | solution.py:247
  12.0 1.9 %collective-permute-start.5 = (f32[16,2048]{1,0:T(8,128)S(1)}, f32[16,2048]{1,0:T(8,128)S(1)}, u32[]{:S(2)}, u32[]{:S(2)}) collective-permute-start(f32[16,2048]{1,0:T(8,128)S(1)} %collective-permute-done.2.refs_7_), channel_id=1, source_target_pairs={{0,1},{1,0},{2,3},{3,2},{4,5},{5,4},{6,7},{7,6},{8,9},{9,8},{10,11... | collective-permute-start | bytes 393224 | tf_op jit(solution)/shard_map/ppermute | solution.py:247
  12.9 1.3 %collective-permute-start.4 = (f32[16,2048]{1,0:T(8,128)S(1)}, f32[16,2048]{1,0:T(8,128)S(1)}, u32[]{:S(2)}, u32[]{:S(2)}) collective-permute-start(f32[16,2048]{1,0:T(8,128)S(1)} %collective-permute-done.1.refs_6_), channel_id=1, source_target_pairs={{0,1},{1,0},{2,3},{3,2},{4,5},{5,4},{6,7},{7,6},{8,9},{9,8},{10,11... | collective-permute-start | bytes 393224 | tf_op jit(solution)/shard_map/ppermute | solution.py:247
  16.7 7.4 %collective-permute-start.7 = (f32[4,8,2048]{2,1,0:T(8,128)S(1)}, f32[4,8,2048]{2,1,0:T(8,128)S(1)}, u32[]{:S(2)}, u32[]{:S(2)}) collective-permute-start(f32[4,8,2048]{2,1,0:T(8,128)S(1)} %get-tuple-element.17), channel_id=1, source_target_pairs={{0,1},{1,0},{2,3},{3,2},{4,5},{5,4},{6,7},{7,6},{8,9},{9,8},{10,11... | collective-permute-start | bytes 786440 | tf_op jit(solution)/shard_map/ppermute | solution.py:247
  16.9 10.8 %collective-permute-start.13 = (f32[8,2048]{1,0:T(8,128)S(1)}, f32[8,2048]{1,0:T(8,128)S(1)}, u32[]{:S(2)}, u32[]{:S(2)}) collective-permute-start(f32[8,2048]{1,0:T(8,128)S(1)} %get-tuple-element.28), channel_id=1, source_target_pairs={{0,24},{8,16},{16,8},{24,0},{1,25},{9,17},{17,9},{25,1},{2,26},{10... | collective-permute-start | bytes 196616 | tf_op jit(solution)/shard_map/ppermute | solution.py:250
  24.1 5.4 %collective-permute-start.12 = (f32[8,2048]{1,0:T(8,128)S(1)}, f32[8,2048]{1,0:T(8,128)S(1)}, u32[]{:S(2)}, u32[]{:S(2)}) collective-permute-start(f32[8,2048]{1,0:T(8,128)S(1)} %get-tuple-element.29), channel_id=1, source_target_pairs={{0,16},{8,24},{16,0},{24,8},{1,17},{9,25},{17,1},{25,9},{2,18},{10... | collective-permute-start | bytes 196616 | tf_op jit(solution)/shard_map/ppermute | solution.py:250
  24.1 5.3 %collective-permute-start.8 = (f32[8,2048]{1,0:T(8,128)S(1)}, f32[8,2048]{1,0:T(8,128)S(1)}, u32[]{:S(2)}, u32[]{:S(2)}) collective-permute-start(f32[8,2048]{1,0:T(8,128)S(1)} %get-tuple-element.19), channel_id=1, source_target_pairs={{0,2},{1,3},{2,0},{3,1},{4,6},{5,7},{6,4},{7,5},{8,10},{9,11},{10,... | collective-permute-start | bytes 196616 | tf_op jit(solution)/shard_map/ppermute | solution.py:247
  25.3 4.3 %collective-permute-start.9 = (f32[8,2048]{1,0:T(8,128)S(1)}, f32[8,2048]{1,0:T(8,128)S(1)}, u32[]{:S(2)}, u32[]{:S(2)}) collective-permute-start(f32[8,2048]{1,0:T(8,128)S(1)} %get-tuple-element.20), channel_id=1, source_target_pairs={{0,4},{1,5},{2,6},{3,7},{4,0},{5,1},{6,2},{7,3},{8,12},{9,13},{10,... | collective-permute-start | bytes 196616 | tf_op jit(solution)/shard_map/ppermute | solution.py:247
  26.9 5.2 %collective-permute-start.10 = (f32[8,2048]{1,0:T(8,128)S(1)}, f32[8,2048]{1,0:T(8,128)S(1)}, u32[]{:S(2)}, u32[]{:S(2)}) collective-permute-start(f32[8,2048]{1,0:T(8,128)S(1)} %get-tuple-element.21), channel_id=1, source_target_pairs={{0,6},{1,7},{2,4},{3,5},{4,2},{5,3},{6,0},{7,1},{8,14},{9,15},{10,... | collective-permute-start | bytes 196616 | tf_op jit(solution)/shard_map/ppermute | solution.py:247
  27.7 4.3 %collective-permute-start.11 = (f32[8,2048]{1,0:T(8,128)S(1)}, f32[8,2048]{1,0:T(8,128)S(1)}, u32[]{:S(2)}, u32[]{:S(2)}) collective-permute-start(f32[8,2048]{1,0:T(8,128)S(1)} %get-tuple-element.22), channel_id=1, source_target_pairs={{0,8},{8,0},{16,24},{24,16},{1,9},{9,1},{17,25},{25,17},{2,10},{10... | collective-permute-start | bytes 196616 | tf_op jit(solution)/shard_map/ppermute | solution.py:250

commit v8 on v7

--- a/solution.py
+++ b/solution.py
@@ -166,6 +166,19 @@
     for copy in copies:
         copy.wait()
     out[...] = contract(both[...], both[...])
+
+
+def add_kernel(block, arriving, out):
+    half = out.shape[0]
+    for s in range(half):
+        out[s] = block[s] + arriving[s]
+
+
+def sum_kernel(*refs):
+    total = refs[0][...]
+    for ref in refs[1:-1]:
+        total = total + ref[...]
+    refs[-1][...] = total
 
 
 def image_kernel(copies, *refs):
@@ -325,13 +338,38 @@
         *passed,
     )
 
+    block, half = col_parts, rows // 2
+    arriving = along_row(block[half:], half)
     from_core = along_col(send, 1)
     summed = [keep[s] + from_core[s] for s in range(1, planes)]
-    nearest, *summed = lax.optimization_barrier((col_parts[1], *summed))
-    back_rows = [along_row(nearest, 1)]
-    back_rows += [along_row(col_parts[s], s) for s in range(2, rows)]
-    back_planes = [along_col(summed[s - 1], 2 * s) for s in range(1, planes)]
-    terms = [keep[0], from_core[0], col_parts[0], *back_planes, *back_rows]
+    arriving, *_ = lax.optimization_barrier((arriving, *summed))
+    back_planes = [along_col(x, 2 * s) for s, x in enumerate(summed, 1)]
+    while half > 1:
+        block = pl.pallas_call(
+            add_kernel,
+            out_shape=jax.ShapeDtypeStruct((half, vectors, piece), f32),
+            in_specs=[in_vmem] * 2,
+            out_specs=in_vmem,
+            compiler_params=pltpu.CompilerParams(vmem_limit_bytes=16 * MIB),
+            cost_estimate=pl.CostEstimate(
+                flops=WAIT_FLOPS, bytes_accessed=3 * half * vectors * piece * 4, transcendentals=0
+            ),
+            name="add",
+        )(block, arriving)
+        half //= 2
+        arriving = along_row(block[half:], half)
+    most = pl.pallas_call(
+        sum_kernel,
+        out_shape=piece_shape,
+        in_specs=[in_vmem] * (2 + planes),
+        out_specs=in_vmem,
+        compiler_params=pltpu.CompilerParams(vmem_limit_bytes=16 * MIB),
+        cost_estimate=pl.CostEstimate(
+            flops=WAIT_FLOPS, bytes_accessed=(3 + planes) * vectors * piece * 4, transcendentals=0
+        ),
+        name="sum",
+    )(keep[0], from_core[0], block[0], *back_planes)
+    terms = [most, arriving[0]]
 
     devices = rows * cols
     image, sums = pl.pallas_call(

time: 47 us -> 47.7 us (1.015)
  waiting for transfers between devices: 7.95 us -> 11 us
  starting transfers between devices: 17.9 us -> 15.7 us
    ppermute x3 -> x2, waiting for transfers between devices: 1.15 us -> 6.66 us  [along_row(): return lax.ppermute(x, 'row', [(i, i ^ s) for i in range(rows)])]
    ppermute x8, waiting for transfers between devices: 3.49 us -> 0.96 us  [along_col(): return lax.ppermute(x, 'col', [(i, i ^ s) for i in range(cols)])]
    ppermute x3 -> x2, starting transfers between devices: 7.82 us -> 5.57 us  [along_row(): return lax.ppermute(x, 'row', [(i, i ^ s) for i in range(rows)])]
  transfers between devices with their start and end apart: 14 -> 13, of which waited for: 7 -> 6; matrix products, arithmetic and copies ran while one was open for 2% -> 2% of each run, Pallas kernels for 3% -> 3%
where the time goes in v8:
time: 47.7 us; the launch traced here: 47.5 us
  starting transfers between devices  15.7 us (33%)
  blocking collectives  12.1 us (25%)
  waiting for transfers between devices  11 us (23%)
  Pallas kernels  6.35 us (13%)
  between operations  1.43 us (3%)
  local copies, waits for them, and re-layouts  0.91 us (2%)
    all_to_all x1, blocking collectives, local(): sums = lax.all_to_all(sums, ('row', 'col'), 0, 0)  12.1 us
    ppermute x2, waiting for transfers between devices, along_row(): return lax.ppermute(x, 'row', [(i, i ^ s) for i in range(rows)])  6.66 us
    ppermute x8, starting transfers between devices, along_col(): return lax.ppermute(x, 'col', [(i, i ^ s) for i in range(cols)])  5.58 us
    ppermute x2, starting transfers between devices, along_row(): return lax.ppermute(x, 'row', [(i, i ^ s) for i in range(rows)])  5.57 us
    ppermute x3, starting transfers between devices, apart(): return lax.ppermute(x, ('row', 'col'), pairs)  4.51 us
    ppermute x3, waiting for transfers between devices, apart(): return lax.ppermute(x, ('row', 'col'), pairs)  3.35 us
    pallas_call x1, Pallas kernels, local(): pl.pallas_call(functools.partial(products_kernel, rows, planes, group), o...  2.35 us
    pallas_call x1, Pallas kernels, local(): pl.pallas_call(functools.partial(finish_kernel, float(piece * devices)),...  2.1 us
  transfers between devices with their start and end apart: 13, of which 6 were waited for; matrix products, arithmetic and copies ran while one was open for 2% of the time, Pallas kernels for 3%

profile of v8, /device:TPU:0, one launch (start us, length us, event | category | flops | bytes accessed | tf_op | source)
XLA Modules:
  0.0 47.5 jit_solution(9715405127878392534)
XLA Ops:
  0.6 0.5 %collective-permute-start = (f32[8,2048]{1,0:T(8,128)}, f32[8,2048]{1,0:T(8,128)S(1)}, u32[]{:S(2)}, u32[]{:S(2)}) collective-permute-start(f32[8,2048]{1,0:T(8,128)} %now.3), channel_id=1, source_target_pairs={{0,1},{1,0},{2,3},{3,2},{4,5},{5,4},{6,7},{7,6},{8,9},{9,8},{10,11... | collective-permute-start | bytes 196616 | tf_op jit(solution)/shard_map/ppermute | solution.py:260
  1.1 0.8 %constant_dynamic-update-slice_fusion.1 = f32[16,2048]{1,0:T(8,128)S(1)} fusion(f32[8,2048]{1,0:T(8,128)} %now.3), kind=kLoop, calls=%fused_computation.10 | loop fusion | bytes 131072
  2.0 0.3 collective-permute-done
  2.3 0.0 slice-start
  2.3 0.0 slice-start.1
  2.3 0.0 slice-start.2
  2.3 0.0 slice-start.3
  2.3 3.9 %collective-permute-start.3 = (f32[16,2048]{1,0:T(8,128)S(1)}, f32[16,2048]{1,0:T(8,128)S(1)}, u32[]{:S(2)}, u32[]{:S(2)}) collective-permute-start(f32[16,2048]{1,0:T(8,128)S(1)} %constant_dynamic-update-slice_fusion.refs_5_), channel_id=1, source_target_pairs={{0,6},{1,25},{2,4},{3,27},{4,2},{5,29},{6,0},{7,31},{8,14},{9,17},... | collective-permute-start | bytes 393224 | tf_op jit(solution)/shard_map/ppermute | solution.py:274
  6.2 0.5 %collective-permute-start.2 = (f32[16,2048]{1,0:T(8,128)S(1)}, f32[16,2048]{1,0:T(8,128)S(1)}, u32[]{:S(2)}, u32[]{:S(2)}) collective-permute-start(f32[16,2048]{1,0:T(8,128)S(1)} %constant_dynamic-update-slice_fusion.refs_5_), channel_id=1, source_target_pairs={{0,4},{1,17},{2,6},{3,19},{4,0},{5,21},{6,2},{7,23},{8,12},{9,25},... | collective-permute-start | bytes 393224 | tf_op jit(solution)/shard_map/ppermute | solution.py:274
  6.7 0.1 collective-permute-start.1
  6.8 1.5 %fixed.1.refs_2_ = f32[16,16]{1,0:T(8,128)S(1)} custom-call(f32[8,2048]{1,0:T(8,128)} %now.3, f32[8,2048]{1,0:T(8,128)} %prev.3), custom_call_target="tpu_custom_call" | custom-call | flops 20000000000 | bytes 131072 | tf_op jit(solution)/shard_map/fixed/pallas_call | solution.py:282
  8.3 3.3 %collective-permute-done.1.refs_6_ = f32[16,2048]{1,0:T(8,128)S(1)} collective-permute-done((f32[16,2048]{1,0:T(8,128)S(1)}, f32[16,2048]{1,0:T(8,128)S(1)}, u32[]{:S(2)}, u32[]{:S(2)}) %collective-permute-start.1) | collective-permute-done | bytes 131104 | tf_op jit(solution)/shard_map/ppermute | solution.py:274
  11.6 0.0 collective-permute-done.3.refs_8_
  11.6 0.3 collective-permute-start.6
  12.0 0.0 collective-permute-done.2.refs_7_
  12.0 0.9 %collective-permute-start.5 = (f32[16,2048]{1,0:T(8,128)S(1)}, f32[16,2048]{1,0:T(8,128)S(1)}, u32[]{:S(2)}, u32[]{:S(2)}) collective-permute-start(f32[16,2048]{1,0:T(8,128)S(1)} %collective-permute-done.2.refs_7_), channel_id=1, source_target_pairs={{0,1},{1,0},{2,3},{3,2},{4,5},{5,4},{6,7},{7,6},{8,9},{9,8},{10,11... | collective-permute-start | bytes 393224 | tf_op jit(solution)/shard_map/ppermute | solution.py:260
  12.9 0.0 collective-permute-start.4
  13.6 0.0 collective-permute-done.6.refs_11_
  13.6 0.3 collective-permute-done.5.refs_10_
  13.9 0.4 collective-permute-done.4.refs_9_
  14.3 0.0 slice-done
  14.3 0.0 slice-done.1
  14.3 0.0 slice-done.2
  14.3 0.0 slice-done.3
  14.3 2.4 %products.1 = (f32[4,8,2048]{2,1,0:T(8,128)S(1)}, f32[4,8,2048]{2,1,0:T(8,128)S(1)}, f32[4,8,2048]{2,1,0:T(8,128)S(1)}) custom-call(s32[1,1]{1,0:T(1,128)S(6)} %copy.12.refs_0_, f32[256,128,128]{2,1,0:T(8,128)S(1)} %bitcast.17, s32[1,1,256]{2,1,0:T(1,128)} %refs_2_.1, s32[1,1,256]{2,1,0:T(1,128)} %refs_3_.1, f32[1,2048]{1,0:T(1,128)} %bitcast.19, ...), custom_call_target="tpu_custom_call" | custom-call | tf_op jit(solution)/shard_map/products/pallas_call | solution.py:306
  16.7 0.2 collective-permute-start.7
  16.9 4.8 %collective-permute-start.8 = (f32[2,8,2048]{2,1,0:T(8,128)S(1)}, f32[2,8,2048]{2,1,0:T(8,128)S(1)}, u32[]{:S(2)}, u32[]{:S(2)}) collective-permute-start(f32[2,8,2048]{2,1,0:T(8,128)S(1)} %slice.35), channel_id=1, source_target_pairs={{0,16},{8,24},{16,0},{24,8},{1,17},{9,25},{17,1},{25,9},{2,18},{10... | collective-permute-start | bytes 393224 | tf_op jit(solution)/shard_map/ppermute | solution.py:263
  21.7 0.0 collective-permute-done.7
  21.7 1.7 %collective-permute-start.11 = (f32[8,2048]{1,0:T(8,128)S(1)}, f32[8,2048]{1,0:T(8,128)S(1)}, u32[]{:S(2)}, u32[]{:S(2)}) collective-permute-start(f32[8,2048]{1,0:T(8,128)S(1)} %get-tuple-element.19), channel_id=1, source_target_pairs={{0,6},{1,7},{2,4},{3,5},{4,2},{5,3},{6,0},{7,1},{8,14},{9,15},{10,... | collective-permute-start | bytes 196616 | tf_op jit(solution)/shard_map/ppermute | solution.py:260
  23.4 0.7 %collective-permute-start.10 = (f32[8,2048]{1,0:T(8,128)S(1)}, f32[8,2048]{1,0:T(8,128)S(1)}, u32[]{:S(2)}, u32[]{:S(2)}) collective-permute-start(f32[8,2048]{1,0:T(8,128)S(1)} %get-tuple-element.20), channel_id=1, source_target_pairs={{0,4},{1,5},{2,6},{3,7},{4,0},{5,1},{6,2},{7,3},{8,12},{9,13},{10,... | collective-permute-start | bytes 196616 | tf_op jit(solution)/shard_map/ppermute | solution.py:260
  24.2 1.1 %collective-permute-start.9 = (f32[8,2048]{1,0:T(8,128)S(1)}, f32[8,2048]{1,0:T(8,128)S(1)}, u32[]{:S(2)}, u32[]{:S(2)}) collective-permute-start(f32[8,2048]{1,0:T(8,128)S(1)} %get-tuple-element.21), channel_id=1, source_target_pairs={{0,2},{1,3},{2,0},{3,1},{4,6},{5,7},{6,4},{7,5},{8,10},{9,11},{10,... | collective-permute-start | bytes 196616 | tf_op jit(solution)/shard_map/ppermute | solution.py:260
  25.3 3.2 %collective-permute-done.8.arriving = f32[2,8,2048]{2,1,0:T(8,128)S(1)} collective-permute-done((f32[2,8,2048]{2,1,0:T(8,128)S(1)}, f32[2,8,2048]{2,1,0:T(8,128)S(1)}, u32[]{:S(2)}, u32[]{:S(2)}) %collective-permute-start.8) | collective-permute-done | bytes 131104 | tf_op jit(solution)/shard_map/ppermute | solution.py:263
  28.5 0.8 %collective-permute-start.12 = (f32[1,8,2048]{2,1,0:T(8,128)S(1)}, f32[1,8,2048]{2,1,0:T(8,128)S(1)}, u32[]{:S(2)}, u32[]{:S(2)}) collective-permute-start(f32[1,8,2048]{2,1,0:T(8,128)S(1)} %get-tuple-element.24), channel_id=1, source_target_pairs={{0,8},{8,0},{16,24},{24,16},{1,9},{9,1},{17,25},{25,17},{2,10},{10... | collective-permute-start | bytes 196616 | tf_op jit(solution)/shard_map/ppermute | solution.py:263
  29.3 0.0 collective-permute-done.11.refs_5_
  29.3 0.0 collective-permute-done.10.refs_4_
  29.3 0.0 collective-permute-done.9.refs_3_
  29.3 0.0 copy-start
  29.4 0.0 copy-start.1
  29.4 0.0 copy-start.2
  29.4 3.4 %collective-permute-done.12 = f32[1,8,2048]{2,1,0:T(8,128)S(1)} collective-permute-done((f32[1,8,2048]{2,1,0:T(8,128)S(1)}, f32[1,8,2048]{2,1,0:T(8,128)S(1)}, u32[]{:S(2)}, u32[]{:S(2)}) %collective-permute-start.12) | collective-permute-done | bytes 65568 | tf_op jit(solution)/shard_map/ppermute | solution.py:263
  32.9 0.0 copy-done
  32.9 0.0 copy-done.1
  32.9 0.4 image.1
  33.2 12.1 %all_to_all.5.sums_in = f32[32,4,128]{2,1,0:T(4,128)S(1)} all-to-all(f32[32,4,128]{2,1,0:T(4,128)S(1)} %get-tuple-element.17), channel_id=1, replica_groups=mesh['row'=4,'col'=8] {'row','col'}, dimensions={0} | all-to-all | bytes 131072 | tf_op jit(solution)/shard_map/all_to_all | solution.py:387
  45.4 0.0 copy-done.2
  45.4 2.1 %finish.1 = (f32[8,2048]{1,0:T(8,128)}, f32[8,8]{1,0:T(8,128)}, f32[8,8]{1,0:T(8,128)}) custom-call(f32[32,4,128]{2,1,0:T(4,128)S(1)} %all_to_all.5.sums_in, f32[8,2048]{1,0:T(8,128)S(1)} %get-tuple-element.18.image, f32[8,2048]{1,0:T(8,128)S(1)} %copy-done, f32[8,2048]{1,0:T(8,128)S(1)} %copy-done.1, f32[8,8]{1,0:T(8,128)S(1)} %copy-done.2), custom_call_target="tpu_custom_call" | custom-call | tf_op jit(solution)/shard_map/finish/pallas_call | solution.py:388
  (7 shorter events, 0.1 us)
Async XLA Ops:
  0.6 1.6 %collective-permute-start = (f32[8,2048]{1,0:T(8,128)}, f32[8,2048]{1,0:T(8,128)S(1)}, u32[]{:S(2)}, u32[]{:S(2)}) collective-permute-start(f32[8,2048]{1,0:T(8,128)} %now.3), channel_id=1, source_target_pairs={{0,1},{1,0},{2,3},{3,2},{4,5},{5,4},{6,7},{7,6},{8,9},{9,8},{10,11... | collective-permute-start | bytes 196616 | tf_op jit(solution)/shard_map/ppermute | solution.py:260
  2.3 12.0 %slice-start = ((s8[16777216]{0:T(1024)(128)(4,1)}), s8[4194304]{0:T(1024)(128)(4,1)S(1)}, s32[]{:S(2)}) async-start(s8[16777216]{0:T(1024)(128)(4,1)} %bitcast.15), calls=%async_computation.1 | async-start | bytes 8388608
  2.3 12.0 %slice-start.1 = ((s8[16777216]{0:T(1024)(128)(4,1)}), s8[4194304]{0:T(1024)(128)(4,1)S(1)}, s32[]{:S(2)}) async-start(s8[16777216]{0:T(1024)(128)(4,1)} %bitcast.15), calls=%async_computation.2 | async-start | bytes 8388608
  2.3 12.0 %slice-start.2 = ((s8[16777216]{0:T(1024)(128)(4,1)}), s8[4194304]{0:T(1024)(128)(4,1)S(1)}, s32[]{:S(2)}) async-start(s8[16777216]{0:T(1024)(128)(4,1)} %bitcast.15), calls=%async_computation.3 | async-start | bytes 8388608
  2.3 12.0 %slice-start.3 = ((s8[16777216]{0:T(1024)(128)(4,1)}), s8[4194304]{0:T(1024)(128)(4,1)S(1)}, s32[]{:S(2)}) async-start(s8[16777216]{0:T(1024)(128)(4,1)} %bitcast.15), calls=%async_computation.4 | async-start | bytes 8388608
  2.3 9.3 %collective-permute-start.3 = (f32[16,2048]{1,0:T(8,128)S(1)}, f32[16,2048]{1,0:T(8,128)S(1)}, u32[]{:S(2)}, u32[]{:S(2)}) collective-permute-start(f32[16,2048]{1,0:T(8,128)S(1)} %constant_dynamic-update-slice_fusion.refs_5_), channel_id=1, source_target_pairs={{0,6},{1,25},{2,4},{3,27},{4,2},{5,29},{6,0},{7,31},{8,14},{9,17},... | collective-permute-start | bytes 393224 | tf_op jit(solution)/shard_map/ppermute | solution.py:274
  6.2 5.8 %collective-permute-start.2 = (f32[16,2048]{1,0:T(8,128)S(1)}, f32[16,2048]{1,0:T(8,128)S(1)}, u32[]{:S(2)}, u32[]{:S(2)}) collective-permute-start(f32[16,2048]{1,0:T(8,128)S(1)} %constant_dynamic-update-slice_fusion.refs_5_), channel_id=1, source_target_pairs={{0,4},{1,17},{2,6},{3,19},{4,0},{5,21},{6,2},{7,23},{8,12},{9,25},... | collective-permute-start | bytes 393224 | tf_op jit(solution)/shard_map/ppermute | solution.py:274
  6.7 5.0 %collective-permute-start.1 = (f32[16,2048]{1,0:T(8,128)S(1)}, f32[16,2048]{1,0:T(8,128)S(1)}, u32[]{:S(2)}, u32[]{:S(2)}) collective-permute-start(f32[16,2048]{1,0:T(8,128)S(1)} %constant_dynamic-update-slice_fusion.refs_5_), channel_id=1, source_target_pairs={{0,2},{1,9},{2,0},{3,11},{4,6},{5,13},{6,4},{7,15},{8,10},{9,1},{1... | collective-permute-start | bytes 393224 | tf_op jit(solution)/shard_map/ppermute | solution.py:274
  11.6 1.9 %collective-permute-start.6 = (f32[16,2048]{1,0:T(8,128)S(1)}, f32[16,2048]{1,0:T(8,128)S(1)}, u32[]{:S(2)}, u32[]{:S(2)}) collective-permute-start(f32[16,2048]{1,0:T(8,128)S(1)} %collective-permute-done.3.refs_8_), channel_id=1, source_target_pairs={{0,1},{1,0},{2,3},{3,2},{4,5},{5,4},{6,7},{7,6},{8,9},{9,8},{10,11... | collective-permute-start | bytes 393224 | tf_op jit(solution)/shard_map/ppermute | solution.py:260
  12.0 1.9 %collective-permute-start.5 = (f32[16,2048]{1,0:T(8,128)S(1)}, f32[16,2048]{1,0:T(8,128)S(1)}, u32[]{:S(2)}, u32[]{:S(2)}) collective-permute-start(f32[16,2048]{1,0:T(8,128)S(1)} %collective-permute-done.2.refs_7_), channel_id=1, source_target_pairs={{0,1},{1,0},{2,3},{3,2},{4,5},{5,4},{6,7},{7,6},{8,9},{9,8},{10,11... | collective-permute-start | bytes 393224 | tf_op jit(solution)/shard_map/ppermute | solution.py:260
  12.9 1.3 %collective-permute-start.4 = (f32[16,2048]{1,0:T(8,128)S(1)}, f32[16,2048]{1,0:T(8,128)S(1)}, u32[]{:S(2)}, u32[]{:S(2)}) collective-permute-start(f32[16,2048]{1,0:T(8,128)S(1)} %collective-permute-done.1.refs_6_), channel_id=1, source_target_pairs={{0,1},{1,0},{2,3},{3,2},{4,5},{5,4},{6,7},{7,6},{8,9},{9,8},{10,11... | collective-permute-start | bytes 393224 | tf_op jit(solution)/shard_map/ppermute | solution.py:260
  16.7 5.0 %collective-permute-start.7 = (f32[4,8,2048]{2,1,0:T(8,128)S(1)}, f32[4,8,2048]{2,1,0:T(8,128)S(1)}, u32[]{:S(2)}, u32[]{:S(2)}) collective-permute-start(f32[4,8,2048]{2,1,0:T(8,128)S(1)} %get-tuple-element.14), channel_id=1, source_target_pairs={{0,1},{1,0},{2,3},{3,2},{4,5},{5,4},{6,7},{7,6},{8,9},{9,8},{10,11... | collective-permute-start | bytes 786440 | tf_op jit(solution)/shard_map/ppermute | solution.py:260
  16.9 11.6 %collective-permute-start.8 = (f32[2,8,2048]{2,1,0:T(8,128)S(1)}, f32[2,8,2048]{2,1,0:T(8,128)S(1)}, u32[]{:S(2)}, u32[]{:S(2)}) collective-permute-start(f32[2,8,2048]{2,1,0:T(8,128)S(1)} %slice.35), channel_id=1, source_target_pairs={{0,16},{8,24},{16,0},{24,8},{1,17},{9,25},{17,1},{25,9},{2,18},{10... | collective-permute-start | bytes 393224 | tf_op jit(solution)/shard_map/ppermute | solution.py:263
  21.7 7.6 %collective-permute-start.11 = (f32[8,2048]{1,0:T(8,128)S(1)}, f32[8,2048]{1,0:T(8,128)S(1)}, u32[]{:S(2)}, u32[]{:S(2)}) collective-permute-start(f32[8,2048]{1,0:T(8,128)S(1)} %get-tuple-element.19), channel_id=1, source_target_pairs={{0,6},{1,7},{2,4},{3,5},{4,2},{5,3},{6,0},{7,1},{8,14},{9,15},{10,... | collective-permute-start | bytes 196616 | tf_op jit(solution)/shard_map/ppermute | solution.py:260
  23.4 5.9 %collective-permute-start.10 = (f32[8,2048]{1,0:T(8,128)S(1)}, f32[8,2048]{1,0:T(8,128)S(1)}, u32[]{:S(2)}, u32[]{:S(2)}) collective-permute-start(f32[8,2048]{1,0:T(8,128)S(1)} %get-tuple-element.20), channel_id=1, source_target_pairs={{0,4},{1,5},{2,6},{3,7},{4,0},{5,1},{6,2},{7,3},{8,12},{9,13},{10,... | collective-permute-start | bytes 196616 | tf_op jit(solution)/shard_map/ppermute | solution.py:260
  24.2 5.2 %collective-permute-start.9 = (f32[8,2048]{1,0:T(8,128)S(1)}, f32[8,2048]{1,0:T(8,128)S(1)}, u32[]{:S(2)}, u32[]{:S(2)}) collective-permute-start(f32[8,2048]{1,0:T(8,128)S(1)} %get-tuple-element.21), channel_id=1, source_target_pairs={{0,2},{1,3},{2,0},{3,1},{4,6},{5,7},{6,4},{7,5},{8,10},{9,11},{10,... | collective-permute-start | bytes 196616 | tf_op jit(solution)/shard_map/ppermute | solution.py:260
  28.5 4.3 %collective-permute-start.12 = (f32[1,8,2048]{2,1,0:T(8,128)S(1)}, f32[1,8,2048]{2,1,0:T(8,128)S(1)}, u32[]{:S(2)}, u32[]{:S(2)}) collective-permute-start(f32[1,8,2048]{2,1,0:T(8,128)S(1)} %get-tuple-element.24), channel_id=1, source_target_pairs={{0,8},{8,0},{16,24},{24,16},{1,9},{9,1},{17,25},{25,17},{2,10},{10... | collective-permute-start | bytes 196616 | tf_op jit(solution)/shard_map/ppermute | solution.py:263
  29.3 3.5 %copy-start = (f32[8,2048]{1,0:T(8,128)S(1)}, f32[8,2048]{1,0:T(8,128)}, u32[]{:S(2)}) copy-start(f32[8,2048]{1,0:T(8,128)} %now.3) | copy-start | bytes 196612
  29.4 3.5 %copy-start.1 = (f32[8,2048]{1,0:T(8,128)S(1)}, f32[8,2048]{1,0:T(8,128)}, u32[]{:S(2)}) copy-start(f32[8,2048]{1,0:T(8,128)} %prev.3) | copy-start | bytes 196612
  29.4 16.0 %copy-start.2 = (f32[8,8]{1,0:T(8,128)S(1)}, f32[8,8]{1,0:T(8,128)}, u32[]{:S(2)}) copy-start(f32[8,8]{1,0:T(8,128)} %coupling.1) | copy-start | bytes 772

commit v9 on v7

--- a/solution.py
+++ b/solution.py
@@ -155,7 +155,7 @@
             col_out[s, :, at] = piece
 
 
-def fixed_kernel(now, prev, out, both, sems):
+def fixed_kernel(count, now, prev, out, both, sems):
     vectors = now.shape[0]
     copies = [
         pltpu.make_async_copy(now, both.at[pl.ds(0, vectors)], sems.at[0]),
@@ -269,7 +269,7 @@
     fixed = pl.pallas_call(
         fixed_kernel,
         out_shape=jax.ShapeDtypeStruct((2 * vectors, 2 * vectors), f32),
-        in_specs=[in_hbm] * 2,
+        in_specs=[pl.BlockSpec(memory_space=SMEM)] + [in_hbm] * 2,
         out_specs=in_vmem,
         scratch_shapes=[
             VMEM((2 * vectors, piece), f32),
@@ -280,7 +280,7 @@
             flops=WAIT_FLOPS, bytes_accessed=2 * vectors * piece * 4, transcendentals=0
         ),
         name="fixed",
-    )(stay(block_now), stay(block_prev))
+    )(tile_counts, stay(block_now), stay(block_prev))
     beside = along_col(block_now, 1)
     chip = jnp.concatenate([block_now, beside], axis=0)
     peers = range(1, max(planes, rows))
@@ -331,7 +331,8 @@
     back_rows = [along_row(nearest, 1)]
     back_rows += [along_row(col_parts[s], s) for s in range(2, rows)]
     back_planes = [along_col(summed[s - 1], 2 * s) for s in range(1, planes)]
-    terms = [keep[0], from_core[0], col_parts[0], *back_planes, *back_rows]
+    terms = [keep[0], from_core[0], col_parts[0], *back_planes[:-1]]
+    terms += [back_rows[0], back_planes[-1], *back_rows[1:]]
 
     devices = rows * cols
     image, sums = pl.pallas_call(

time: 47 us -> 48.3 us (1.028)
  starting transfers between devices: 17.9 us -> 18.6 us
    ppermute x8, starting transfers between devices: 5.56 us -> 6.96 us  [along_col(): return lax.ppermute(x, 'col', [(i, i ^ s) for i in range(cols)])]
    ppermute x3, waiting for transfers between devices: 1.15 us -> 1.67 us  [along_row(): return lax.ppermute(x, 'row', [(i, i ^ s) for i in range(rows)])]
  transfers between devices with their start and end apart: 14 -> 14, of which waited for: 7 -> 7; matrix products, arithmetic and copies ran while one was open for 2% -> 2% of each run, Pallas kernels for 3% -> 4%
where the time goes in v9:
time: 48.3 us; the launch traced here: 48.1 us
  starting transfers between devices  18.6 us (39%)
  blocking collectives  12.5 us (26%)
  waiting for transfers between devices  7.97 us (17%)
  Pallas kernels  6.64 us (14%)
  between operations  1.42 us (3%)
  local copies, waits for them, and re-layouts  0.91 us (2%)
    all_to_all x1, blocking collectives, local(): sums = lax.all_to_all(sums, ('row', 'col'), 0, 0)  12.5 us
    ppermute x3, starting transfers between devices, along_row(): return lax.ppermute(x, 'row', [(i, i ^ s) for i in range(rows)])  7.46 us
    ppermute x8, starting transfers between devices, along_col(): return lax.ppermute(x, 'col', [(i, i ^ s) for i in range(cols)])  6.96 us
    ppermute x3, starting transfers between devices, apart(): return lax.ppermute(x, ('row', 'col'), pairs)  4.17 us
    ppermute x8, waiting for transfers between devices, along_col(): return lax.ppermute(x, 'col', [(i, i ^ s) for i in range(cols)])  3.31 us
    ppermute x3, waiting for transfers between devices, apart(): return lax.ppermute(x, ('row', 'col'), pairs)  2.99 us
    pallas_call x1, Pallas kernels, local(): pl.pallas_call(functools.partial(products_kernel, rows, planes, group), o...  2.36 us
    pallas_call x1, Pallas kernels, local(): pl.pallas_call(functools.partial(finish_kernel, float(piece * devices)),...  2.1 us
  transfers between devices with their start and end apart: 14, of which 7 were waited for; matrix products, arithmetic and copies ran while one was open for 2% of the time, Pallas kernels for 4%

profile of v9, /device:TPU:0, one launch (start us, length us, event | category | flops | bytes accessed | tf_op | source)
XLA Modules:
  0.0 48.1 jit_solution(16899926669098193906)
XLA Ops:
  0.6 0.5 %collective-permute-start = (f32[8,2048]{1,0:T(8,128)}, f32[8,2048]{1,0:T(8,128)S(1)}, u32[]{:S(2)}, u32[]{:S(2)}) collective-permute-start(f32[8,2048]{1,0:T(8,128)} %now.3), channel_id=1, source_target_pairs={{0,1},{1,0},{2,3},{3,2},{4,5},{5,4},{6,7},{7,6},{8,9},{9,8},{10,11... | collective-permute-start | bytes 196616 | tf_op jit(solution)/shard_map/ppermute | solution.py:247
  1.1 0.8 %constant_dynamic-update-slice_fusion.1 = f32[16,2048]{1,0:T(8,128)S(1)} fusion(f32[8,2048]{1,0:T(8,128)} %now.3), kind=kLoop, calls=%fused_computation.13 | loop fusion | bytes 131072
  2.6 0.0 collective-permute-done
  2.7 0.0 slice-start
  2.7 0.0 slice-start.1
  2.7 0.0 slice-start.2
  2.7 0.0 slice-start.3
  2.7 3.5 %collective-permute-start.3 = (f32[16,2048]{1,0:T(8,128)S(1)}, f32[16,2048]{1,0:T(8,128)S(1)}, u32[]{:S(2)}, u32[]{:S(2)}) collective-permute-start(f32[16,2048]{1,0:T(8,128)S(1)} %constant_dynamic-update-slice_fusion.refs_5_), channel_id=1, source_target_pairs={{0,6},{1,25},{2,4},{3,27},{4,2},{5,29},{6,0},{7,31},{8,14},{9,17},... | collective-permute-start | bytes 393224 | tf_op jit(solution)/shard_map/ppermute | solution.py:261
  6.2 0.5 %collective-permute-start.2 = (f32[16,2048]{1,0:T(8,128)S(1)}, f32[16,2048]{1,0:T(8,128)S(1)}, u32[]{:S(2)}, u32[]{:S(2)}) collective-permute-start(f32[16,2048]{1,0:T(8,128)S(1)} %constant_dynamic-update-slice_fusion.refs_5_), channel_id=1, source_target_pairs={{0,4},{1,17},{2,6},{3,19},{4,0},{5,21},{6,2},{7,23},{8,12},{9,25},... | collective-permute-start | bytes 393224 | tf_op jit(solution)/shard_map/ppermute | solution.py:261
  6.7 0.1 collective-permute-start.1
  6.9 1.8 %fixed.1.refs_2_ = f32[16,16]{1,0:T(8,128)S(1)} custom-call(s32[1,1]{1,0:T(1,128)S(6)} %copy.12.count.refs_0_, f32[8,2048]{1,0:T(8,128)} %now.3, f32[8,2048]{1,0:T(8,128)} %prev.3), custom_call_target="tpu_custom_call" | custom-call | flops 20000000000 | bytes 131072 | tf_op jit(solution)/shard_map/fixed/pallas_call | solution.py:269
  8.7 0.0 copy-start
  8.7 0.0 copy-start.1
  8.7 0.0 copy-start.2
  8.7 3.0 %collective-permute-done.1.refs_6_ = f32[16,2048]{1,0:T(8,128)S(1)} collective-permute-done((f32[16,2048]{1,0:T(8,128)S(1)}, f32[16,2048]{1,0:T(8,128)S(1)}, u32[]{:S(2)}, u32[]{:S(2)}) %collective-permute-start.1) | collective-permute-done | bytes 131104 | tf_op jit(solution)/shard_map/ppermute | solution.py:261
  11.7 0.0 collective-permute-done.3.refs_8_
  11.7 0.7 %collective-permute-start.6 = (f32[16,2048]{1,0:T(8,128)S(1)}, f32[16,2048]{1,0:T(8,128)S(1)}, u32[]{:S(2)}, u32[]{:S(2)}) collective-permute-start(f32[16,2048]{1,0:T(8,128)S(1)} %collective-permute-done.3.refs_8_), channel_id=1, source_target_pairs={{0,1},{1,0},{2,3},{3,2},{4,5},{5,4},{6,7},{7,6},{8,9},{9,8},{10,11... | collective-permute-start | bytes 393224 | tf_op jit(solution)/shard_map/ppermute | solution.py:247
  12.4 0.0 collective-permute-done.2.refs_7_
  12.4 0.9 %collective-permute-start.5 = (f32[16,2048]{1,0:T(8,128)S(1)}, f32[16,2048]{1,0:T(8,128)S(1)}, u32[]{:S(2)}, u32[]{:S(2)}) collective-permute-start(f32[16,2048]{1,0:T(8,128)S(1)} %collective-permute-done.2.refs_7_), channel_id=1, source_target_pairs={{0,1},{1,0},{2,3},{3,2},{4,5},{5,4},{6,7},{7,6},{8,9},{9,8},{10,11... | collective-permute-start | bytes 393224 | tf_op jit(solution)/shard_map/ppermute | solution.py:247
  13.3 0.0 collective-permute-start.4
  13.3 0.0 collective-permute-done.6.refs_11_
  13.4 1.0 %collective-permute-done.5.refs_10_ = f32[16,2048]{1,0:T(8,128)S(1)} collective-permute-done((f32[16,2048]{1,0:T(8,128)S(1)}, f32[16,2048]{1,0:T(8,128)S(1)}, u32[]{:S(2)}, u32[]{:S(2)}) %collective-permute-start.5) | collective-permute-done | bytes 131104 | tf_op jit(solution)/shard_map/ppermute | solution.py:247
  14.3 0.4 collective-permute-done.4.refs_9_
  14.7 0.0 slice-done
  14.7 0.0 slice-done.1
  14.7 0.0 slice-done.2
  14.7 0.0 slice-done.3
  14.7 2.4 %products.1 = (f32[4,8,2048]{2,1,0:T(8,128)S(1)}, f32[4,8,2048]{2,1,0:T(8,128)S(1)}, f32[4,8,2048]{2,1,0:T(8,128)S(1)}) custom-call(s32[1,1]{1,0:T(1,128)S(6)} %copy.12.count.refs_0_, f32[256,128,128]{2,1,0:T(8,128)S(1)} %bitcast.22, s32[1,1,256]{2,1,0:T(1,128)} %refs_2_.1, s32[1,1,256]{2,1,0:T(1,128)} %refs_3_.1, f32[1,2048]{1,0:T(1,128)} %bitcast.23, ...), custom_call_target="tpu_custom_call" | custom-call | tf_op jit(solution)/shard_map/products/pallas_call | solution.py:293
  17.1 0.2 collective-permute-start.7
  17.3 6.8 %collective-permute-start.13 = (f32[8,2048]{1,0:T(8,128)S(1)}, f32[8,2048]{1,0:T(8,128)S(1)}, u32[]{:S(2)}, u32[]{:S(2)}) collective-permute-start(f32[8,2048]{1,0:T(8,128)S(1)} %get-tuple-element.28), channel_id=1, source_target_pairs={{0,24},{8,16},{16,8},{24,0},{1,25},{9,17},{17,9},{25,1},{2,26},{10... | collective-permute-start | bytes 196616 | tf_op jit(solution)/shard_map/ppermute | solution.py:250
  24.2 0.0 collective-permute-start.12
  24.2 0.0 collective-permute-done.7
  24.2 1.5 %collective-permute-start.8 = (f32[8,2048]{1,0:T(8,128)S(1)}, f32[8,2048]{1,0:T(8,128)S(1)}, u32[]{:S(2)}, u32[]{:S(2)}) collective-permute-start(f32[8,2048]{1,0:T(8,128)S(1)} %get-tuple-element.19), channel_id=1, source_target_pairs={{0,2},{1,3},{2,0},{3,1},{4,6},{5,7},{6,4},{7,5},{8,10},{9,11},{10,... | collective-permute-start | bytes 196616 | tf_op jit(solution)/shard_map/ppermute | solution.py:247
  25.7 1.5 %collective-permute-start.9 = (f32[8,2048]{1,0:T(8,128)S(1)}, f32[8,2048]{1,0:T(8,128)S(1)}, u32[]{:S(2)}, u32[]{:S(2)}) collective-permute-start(f32[8,2048]{1,0:T(8,128)S(1)} %get-tuple-element.20), channel_id=1, source_target_pairs={{0,4},{1,5},{2,6},{3,7},{4,0},{5,1},{6,2},{7,3},{8,12},{9,13},{10,... | collective-permute-start | bytes 196616 | tf_op jit(solution)/shard_map/ppermute | solution.py:247
  27.3 0.6 %collective-permute-start.10 = (f32[8,2048]{1,0:T(8,128)S(1)}, f32[8,2048]{1,0:T(8,128)S(1)}, u32[]{:S(2)}, u32[]{:S(2)}) collective-permute-start(f32[8,2048]{1,0:T(8,128)S(1)} %get-tuple-element.21), channel_id=1, source_target_pairs={{0,8},{8,0},{16,24},{24,16},{1,9},{9,1},{17,25},{25,17},{2,10},{10... | collective-permute-start | bytes 196616 | tf_op jit(solution)/shard_map/ppermute | solution.py:250
  27.9 0.0 collective-permute-done.13.refs_11_
  27.9 1.5 %collective-permute-start.11 = (f32[8,2048]{1,0:T(8,128)S(1)}, f32[8,2048]{1,0:T(8,128)S(1)}, u32[]{:S(2)}, u32[]{:S(2)}) collective-permute-start(f32[8,2048]{1,0:T(8,128)S(1)} %get-tuple-element.22), channel_id=1, source_target_pairs={{0,6},{1,7},{2,4},{3,5},{4,2},{5,3},{6,0},{7,1},{8,14},{9,15},{10,... | collective-permute-start | bytes 196616 | tf_op jit(solution)/shard_map/ppermute | solution.py:247
  29.4 0.1 collective-permute-done.12.refs_10_
  29.6 0.0 collective-permute-done.8.refs_6_
  29.6 0.4 collective-permute-done.9.refs_7_
  30.0 1.5 %collective-permute-done.10.refs_8_ = f32[8,2048]{1,0:T(8,128)S(1)} collective-permute-done((f32[8,2048]{1,0:T(8,128)S(1)}, f32[8,2048]{1,0:T(8,128)S(1)}, u32[]{:S(2)}, u32[]{:S(2)}) %collective-permute-start.10) | collective-permute-done | bytes 65568 | tf_op jit(solution)/shard_map/ppermute | solution.py:250
  31.5 1.5 %collective-permute-done.11.refs_9_ = f32[8,2048]{1,0:T(8,128)S(1)} collective-permute-done((f32[8,2048]{1,0:T(8,128)S(1)}, f32[8,2048]{1,0:T(8,128)S(1)}, u32[]{:S(2)}, u32[]{:S(2)}) %collective-permute-start.11) | collective-permute-done | bytes 65568 | tf_op jit(solution)/shard_map/ppermute | solution.py:247
  33.1 0.0 copy-done
  33.1 0.0 copy-done.1
  33.1 0.4 image.1
  33.5 12.5 %all_to_all.5.sums_in = f32[32,4,128]{2,1,0:T(4,128)S(1)} all-to-all(f32[32,4,128]{2,1,0:T(4,128)S(1)} %get-tuple-element.23), channel_id=1, replica_groups=mesh['row'=4,'col'=8] {'row','col'}, dimensions={0} | all-to-all | bytes 131072 | tf_op jit(solution)/shard_map/all_to_all | solution.py:350
  46.0 0.0 copy-done.2
  46.0 2.1 %finish.1 = (f32[8,2048]{1,0:T(8,128)}, f32[8,8]{1,0:T(8,128)}, f32[8,8]{1,0:T(8,128)}) custom-call(f32[32,4,128]{2,1,0:T(4,128)S(1)} %all_to_all.5.sums_in, f32[8,2048]{1,0:T(8,128)S(1)} %get-tuple-element.24.image, f32[8,2048]{1,0:T(8,128)S(1)} %copy-done, f32[8,2048]{1,0:T(8,128)S(1)} %copy-done.1, f32[8,8]{1,0:T(8,128)S(1)} %copy-done.2), custom_call_target="tpu_custom_call" | custom-call | tf_op jit(solution)/shard_map/finish/pallas_call | solution.py:351
  (4 shorter events, 0.1 us)
Async XLA Ops:
  0.6 2.0 %collective-permute-start = (f32[8,2048]{1,0:T(8,128)}, f32[8,2048]{1,0:T(8,128)S(1)}, u32[]{:S(2)}, u32[]{:S(2)}) collective-permute-start(f32[8,2048]{1,0:T(8,128)} %now.3), channel_id=1, source_target_pairs={{0,1},{1,0},{2,3},{3,2},{4,5},{5,4},{6,7},{7,6},{8,9},{9,8},{10,11... | collective-permute-start | bytes 196616 | tf_op jit(solution)/shard_map/ppermute | solution.py:247
  2.7 12.0 %slice-start = ((s8[16777216]{0:T(1024)(128)(4,1)}), s8[4194304]{0:T(1024)(128)(4,1)S(1)}, s32[]{:S(2)}) async-start(s8[16777216]{0:T(1024)(128)(4,1)} %bitcast.20), calls=%async_computation.1 | async-start | bytes 8388608
  2.7 12.0 %slice-start.1 = ((s8[16777216]{0:T(1024)(128)(4,1)}), s8[4194304]{0:T(1024)(128)(4,1)S(1)}, s32[]{:S(2)}) async-start(s8[16777216]{0:T(1024)(128)(4,1)} %bitcast.20), calls=%async_computation.2 | async-start | bytes 8388608
  2.7 12.0 %slice-start.2 = ((s8[16777216]{0:T(1024)(128)(4,1)}), s8[4194304]{0:T(1024)(128)(4,1)S(1)}, s32[]{:S(2)}) async-start(s8[16777216]{0:T(1024)(128)(4,1)} %bitcast.20), calls=%async_computation.3 | async-start | bytes 8388608
  2.7 12.0 %slice-start.3 = ((s8[16777216]{0:T(1024)(128)(4,1)}), s8[4194304]{0:T(1024)(128)(4,1)S(1)}, s32[]{:S(2)}) async-start(s8[16777216]{0:T(1024)(128)(4,1)} %bitcast.20), calls=%async_computation.4 | async-start | bytes 8388608
  2.7 9.0 %collective-permute-start.3 = (f32[16,2048]{1,0:T(8,128)S(1)}, f32[16,2048]{1,0:T(8,128)S(1)}, u32[]{:S(2)}, u32[]{:S(2)}) collective-permute-start(f32[16,2048]{1,0:T(8,128)S(1)} %constant_dynamic-update-slice_fusion.refs_5_), channel_id=1, source_target_pairs={{0,6},{1,25},{2,4},{3,27},{4,2},{5,29},{6,0},{7,31},{8,14},{9,17},... | collective-permute-start | bytes 393224 | tf_op jit(solution)/shard_map/ppermute | solution.py:261
  6.2 6.1 %collective-permute-start.2 = (f32[16,2048]{1,0:T(8,128)S(1)}, f32[16,2048]{1,0:T(8,128)S(1)}, u32[]{:S(2)}, u32[]{:S(2)}) collective-permute-start(f32[16,2048]{1,0:T(8,128)S(1)} %constant_dynamic-update-slice_fusion.refs_5_), channel_id=1, source_target_pairs={{0,4},{1,17},{2,6},{3,19},{4,0},{5,21},{6,2},{7,23},{8,12},{9,25},... | collective-permute-start | bytes 393224 | tf_op jit(solution)/shard_map/ppermute | solution.py:261
  6.7 5.0 %collective-permute-start.1 = (f32[16,2048]{1,0:T(8,128)S(1)}, f32[16,2048]{1,0:T(8,128)S(1)}, u32[]{:S(2)}, u32[]{:S(2)}) collective-permute-start(f32[16,2048]{1,0:T(8,128)S(1)} %constant_dynamic-update-slice_fusion.refs_5_), channel_id=1, source_target_pairs={{0,2},{1,9},{2,0},{3,11},{4,6},{5,13},{6,4},{7,15},{8,10},{9,1},{1... | collective-permute-start | bytes 393224 | tf_op jit(solution)/shard_map/ppermute | solution.py:261
  8.7 24.4 %copy-start = (f32[8,2048]{1,0:T(8,128)S(1)}, f32[8,2048]{1,0:T(8,128)}, u32[]{:S(2)}) copy-start(f32[8,2048]{1,0:T(8,128)} %now.3) | copy-start | bytes 196612
  8.7 24.4 %copy-start.1 = (f32[8,2048]{1,0:T(8,128)S(1)}, f32[8,2048]{1,0:T(8,128)}, u32[]{:S(2)}) copy-start(f32[8,2048]{1,0:T(8,128)} %prev.3) | copy-start | bytes 196612
  8.7 37.3 %copy-start.2 = (f32[8,8]{1,0:T(8,128)S(1)}, f32[8,8]{1,0:T(8,128)}, u32[]{:S(2)}) copy-start(f32[8,8]{1,0:T(8,128)} %coupling.1) | copy-start | bytes 772
  11.7 1.6 %collective-permute-start.6 = (f32[16,2048]{1,0:T(8,128)S(1)}, f32[16,2048]{1,0:T(8,128)S(1)}, u32[]{:S(2)}, u32[]{:S(2)}) collective-permute-start(f32[16,2048]{1,0:T(8,128)S(1)} %collective-permute-done.3.refs_8_), channel_id=1, source_target_pairs={{0,1},{1,0},{2,3},{3,2},{4,5},{5,4},{6,7},{7,6},{8,9},{9,8},{10,11... | collective-permute-start | bytes 393224 | tf_op jit(solution)/shard_map/ppermute | solution.py:247
  12.4 1.9 %collective-permute-start.5 = (f32[16,2048]{1,0:T(8,128)S(1)}, f32[16,2048]{1,0:T(8,128)S(1)}, u32[]{:S(2)}, u32[]{:S(2)}) collective-permute-start(f32[16,2048]{1,0:T(8,128)S(1)} %collective-permute-done.2.refs_7_), channel_id=1, source_target_pairs={{0,1},{1,0},{2,3},{3,2},{4,5},{5,4},{6,7},{7,6},{8,9},{9,8},{10,11... | collective-permute-start | bytes 393224 | tf_op jit(solution)/shard_map/ppermute | solution.py:247
  13.3 1.3 %collective-permute-start.4 = (f32[16,2048]{1,0:T(8,128)S(1)}, f32[16,2048]{1,0:T(8,128)S(1)}, u32[]{:S(2)}, u32[]{:S(2)}) collective-permute-start(f32[16,2048]{1,0:T(8,128)S(1)} %collective-permute-done.1.refs_6_), channel_id=1, source_target_pairs={{0,1},{1,0},{2,3},{3,2},{4,5},{5,4},{6,7},{7,6},{8,9},{9,8},{10,11... | collective-permute-start | bytes 393224 | tf_op jit(solution)/shard_map/ppermute | solution.py:247
  17.1 7.1 %collective-permute-start.7 = (f32[4,8,2048]{2,1,0:T(8,128)S(1)}, f32[4,8,2048]{2,1,0:T(8,128)S(1)}, u32[]{:S(2)}, u32[]{:S(2)}) collective-permute-start(f32[4,8,2048]{2,1,0:T(8,128)S(1)} %get-tuple-element.17), channel_id=1, source_target_pairs={{0,1},{1,0},{2,3},{3,2},{4,5},{5,4},{6,7},{7,6},{8,9},{9,8},{10,11... | collective-permute-start | bytes 786440 | tf_op jit(solution)/shard_map/ppermute | solution.py:247
  17.3 10.6 %collective-permute-start.13 = (f32[8,2048]{1,0:T(8,128)S(1)}, f32[8,2048]{1,0:T(8,128)S(1)}, u32[]{:S(2)}, u32[]{:S(2)}) collective-permute-start(f32[8,2048]{1,0:T(8,128)S(1)} %get-tuple-element.28), channel_id=1, source_target_pairs={{0,24},{8,16},{16,8},{24,0},{1,25},{9,17},{17,9},{25,1},{2,26},{10... | collective-permute-start | bytes 196616 | tf_op jit(solution)/shard_map/ppermute | solution.py:250
  24.2 5.4 %collective-permute-start.12 = (f32[8,2048]{1,0:T(8,128)S(1)}, f32[8,2048]{1,0:T(8,128)S(1)}, u32[]{:S(2)}, u32[]{:S(2)}) collective-permute-start(f32[8,2048]{1,0:T(8,128)S(1)} %get-tuple-element.29), channel_id=1, source_target_pairs={{0,16},{8,24},{16,0},{24,8},{1,17},{9,25},{17,1},{25,9},{2,18},{10... | collective-permute-start | bytes 196616 | tf_op jit(solution)/shard_map/ppermute | solution.py:250
  24.2 5.4 %collective-permute-start.8 = (f32[8,2048]{1,0:T(8,128)S(1)}, f32[8,2048]{1,0:T(8,128)S(1)}, u32[]{:S(2)}, u32[]{:S(2)}) collective-permute-start(f32[8,2048]{1,0:T(8,128)S(1)} %get-tuple-element.19), channel_id=1, source_target_pairs={{0,2},{1,3},{2,0},{3,1},{4,6},{5,7},{6,4},{7,5},{8,10},{9,11},{10,... | collective-permute-start | bytes 196616 | tf_op jit(solution)/shard_map/ppermute | solution.py:247
  25.7 4.3 %collective-permute-start.9 = (f32[8,2048]{1,0:T(8,128)S(1)}, f32[8,2048]{1,0:T(8,128)S(1)}, u32[]{:S(2)}, u32[]{:S(2)}) collective-permute-start(f32[8,2048]{1,0:T(8,128)S(1)} %get-tuple-element.20), channel_id=1, source_target_pairs={{0,4},{1,5},{2,6},{3,7},{4,0},{5,1},{6,2},{7,3},{8,12},{9,13},{10,... | collective-permute-start | bytes 196616 | tf_op jit(solution)/shard_map/ppermute | solution.py:247
  27.3 4.3 %collective-permute-start.10 = (f32[8,2048]{1,0:T(8,128)S(1)}, f32[8,2048]{1,0:T(8,128)S(1)}, u32[]{:S(2)}, u32[]{:S(2)}) collective-permute-start(f32[8,2048]{1,0:T(8,128)S(1)} %get-tuple-element.21), channel_id=1, source_target_pairs={{0,8},{8,0},{16,24},{24,16},{1,9},{9,1},{17,25},{25,17},{2,10},{10... | collective-permute-start | bytes 196616 | tf_op jit(solution)/shard_map/ppermute | solution.py:250
  27.9 5.2 %collective-permute-start.11 = (f32[8,2048]{1,0:T(8,128)S(1)}, f32[8,2048]{1,0:T(8,128)S(1)}, u32[]{:S(2)}, u32[]{:S(2)}) collective-permute-start(f32[8,2048]{1,0:T(8,128)S(1)} %get-tuple-element.22), channel_id=1, source_target_pairs={{0,6},{1,7},{2,4},{3,5},{4,2},{5,3},{6,0},{7,1},{8,14},{9,15},{10,... | collective-permute-start | bytes 196616 | tf_op jit(solution)/shard_map/ppermute | solution.py:247

commit v10 on v7

--- a/solution.py
+++ b/solution.py
@@ -146,7 +146,7 @@
             keep_out[s, :, at] = acc_rows[base + core * piece_tiles + t]
             send_out[s, :, at] = acc_rows[base + (1 - core) * piece_tiles + t]
     for s in range(rows):
-        base = jnp.bitwise_xor(row, s) * piece_tiles
+        base = lax.rem(row + rows - s, rows) * piece_tiles
         for t in range(piece_tiles):
             at = slice(t * width, (t + 1) * width)
             piece = acc_cols[base + t]
@@ -247,7 +247,7 @@
         return lax.ppermute(x, "col", [(i, i ^ s) for i in range(cols)])
 
     def along_row(x, s):
-        return lax.ppermute(x, "row", [(i, i ^ s) for i in range(rows)])
+        return lax.ppermute(x, "row", [(i, (i - s) % rows) for i in range(rows)])
 
     def apart(x, s):
         pairs = []
@@ -325,11 +325,9 @@
         *passed,
     )
 
+    back_rows = [along_row(col_parts[s], s) for s in range(1, rows)]
     from_core = along_col(send, 1)
     summed = [keep[s] + from_core[s] for s in range(1, planes)]
-    nearest, *summed = lax.optimization_barrier((col_parts[1], *summed))
-    back_rows = [along_row(nearest, 1)]
-    back_rows += [along_row(col_parts[s], s) for s in range(2, rows)]
     back_planes = [along_col(summed[s - 1], 2 * s) for s in range(1, planes)]
     terms = [keep[0], from_core[0], col_parts[0], *back_planes, *back_rows]
 

time: 47 us -> 45.7 us (0.972)
  blocking collectives: 12.2 us -> 11.3 us
    ppermute x8, waiting for transfers between devices: 3.49 us -> 2.48 us  [along_col(): return lax.ppermute(x, 'col', [(i, i ^ s) for i in range(cols)])]
    all_to_all x1, blocking collectives: 12.2 us -> 11.3 us  [local(): sums = lax.all_to_all(sums, ('row', 'col'), 0, 0)]
    ppermute x3, waiting for transfers between devices: 1.15 us -> 1.83 us  [along_row(): return lax.ppermute(x, 'row', [(i, (i - s) % rows) for i in range(rows)])]
  transfers between devices with their start and end apart: 14 -> 14, of which waited for: 7 -> 8; matrix products, arithmetic and copies ran while one was open for 2% -> 2% of each run, Pallas kernels for 3% -> 3%
where the time goes in v10:
time: 45.7 us; the launch traced here: 45.4 us
  starting transfers between devices  17.8 us (39%)
  blocking collectives  11.3 us (25%)
  waiting for transfers between devices  7.62 us (17%)
  Pallas kernels  6.32 us (14%)
  between operations  1.41 us (3%)
  local copies, waits for them, and re-layouts  0.9 us (2%)
    all_to_all x1, blocking collectives, local(): sums = lax.all_to_all(sums, ('row', 'col'), 0, 0)  11.3 us
    ppermute x3, starting transfers between devices, along_row(): return lax.ppermute(x, 'row', [(i, (i - s) % rows) for i in range(rows)])  7.72 us
    ppermute x8, starting transfers between devices, along_col(): return lax.ppermute(x, 'col', [(i, i ^ s) for i in range(cols)])  5.6 us
    ppermute x3, starting transfers between devices, apart(): return lax.ppermute(x, ('row', 'col'), pairs)  4.51 us
    ppermute x3, waiting for transfers between devices, apart(): return lax.ppermute(x, ('row', 'col'), pairs)  3.31 us
    ppermute x8, waiting for transfers between devices, along_col(): return lax.ppermute(x, 'col', [(i, i ^ s) for i in range(cols)])  2.48 us
    pallas_call x1, Pallas kernels, local(): pl.pallas_call(functools.partial(products_kernel, rows, planes, group), o...  2.35 us
    pallas_call x1, Pallas kernels, local(): pl.pallas_call(functools.partial(finish_kernel, float(piece * devices)),...  2.1 us
  transfers between devices with their start and end apart: 14, of which 8 were waited for; matrix products, arithmetic and copies ran while one was open for 2% of the time, Pallas kernels for 3%

profile of v10, /device:TPU:0, one launch (start us, length us, event | category | flops | bytes accessed | tf_op | source)
XLA Modules:
  0.0 45.4 jit_solution(2338545505185772676)
XLA Ops:
  0.6 0.5 %collective-permute-start = (f32[8,2048]{1,0:T(8,128)}, f32[8,2048]{1,0:T(8,128)S(1)}, u32[]{:S(2)}, u32[]{:S(2)}) collective-permute-start(f32[8,2048]{1,0:T(8,128)} %now.3), channel_id=1, source_target_pairs={{0,1},{1,0},{2,3},{3,2},{4,5},{5,4},{6,7},{7,6},{8,9},{9,8},{10,11... | collective-permute-start | bytes 196616 | tf_op jit(solution)/shard_map/ppermute | solution.py:247
  1.1 0.8 %constant_dynamic-update-slice_fusion.1 = f32[16,2048]{1,0:T(8,128)S(1)} fusion(f32[8,2048]{1,0:T(8,128)} %now.3), kind=kLoop, calls=%fused_computation.13 | loop fusion | bytes 131072
  2.0 0.3 collective-permute-done
  2.3 0.0 slice-start
  2.3 0.0 slice-start.1
  2.3 0.0 slice-start.2
  2.3 0.0 slice-start.3
  2.3 3.9 %collective-permute-start.3 = (f32[16,2048]{1,0:T(8,128)S(1)}, f32[16,2048]{1,0:T(8,128)S(1)}, u32[]{:S(2)}, u32[]{:S(2)}) collective-permute-start(f32[16,2048]{1,0:T(8,128)S(1)} %constant_dynamic-update-slice_fusion.refs_5_), channel_id=1, source_target_pairs={{0,6},{1,25},{2,4},{3,27},{4,2},{5,29},{6,0},{7,31},{8,14},{9,17},... | collective-permute-start | bytes 393224 | tf_op jit(solution)/shard_map/ppermute | solution.py:261
  6.2 0.5 %collective-permute-start.2 = (f32[16,2048]{1,0:T(8,128)S(1)}, f32[16,2048]{1,0:T(8,128)S(1)}, u32[]{:S(2)}, u32[]{:S(2)}) collective-permute-start(f32[16,2048]{1,0:T(8,128)S(1)} %constant_dynamic-update-slice_fusion.refs_5_), channel_id=1, source_target_pairs={{0,4},{1,17},{2,6},{3,19},{4,0},{5,21},{6,2},{7,23},{8,12},{9,25},... | collective-permute-start | bytes 393224 | tf_op jit(solution)/shard_map/ppermute | solution.py:261
  6.7 0.1 collective-permute-start.1
  6.8 1.5 %fixed.1.refs_2_ = f32[16,16]{1,0:T(8,128)S(1)} custom-call(f32[8,2048]{1,0:T(8,128)} %now.3, f32[8,2048]{1,0:T(8,128)} %prev.3), custom_call_target="tpu_custom_call" | custom-call | flops 20000000000 | bytes 131072 | tf_op jit(solution)/shard_map/fixed/pallas_call | solution.py:269
  8.3 0.0 copy-start
  8.3 0.0 copy-start.1
  8.3 0.0 copy-start.2
  8.3 3.3 %collective-permute-done.1.refs_6_ = f32[16,2048]{1,0:T(8,128)S(1)} collective-permute-done((f32[16,2048]{1,0:T(8,128)S(1)}, f32[16,2048]{1,0:T(8,128)S(1)}, u32[]{:S(2)}, u32[]{:S(2)}) %collective-permute-start.1) | collective-permute-done | bytes 131104 | tf_op jit(solution)/shard_map/ppermute | solution.py:261
  11.6 0.0 collective-permute-done.3.refs_8_
  11.6 0.3 collective-permute-start.6
  12.0 0.0 collective-permute-done.2.refs_7_
  12.0 0.9 %collective-permute-start.5 = (f32[16,2048]{1,0:T(8,128)S(1)}, f32[16,2048]{1,0:T(8,128)S(1)}, u32[]{:S(2)}, u32[]{:S(2)}) collective-permute-start(f32[16,2048]{1,0:T(8,128)S(1)} %collective-permute-done.2.refs_7_), channel_id=1, source_target_pairs={{0,1},{1,0},{2,3},{3,2},{4,5},{5,4},{6,7},{7,6},{8,9},{9,8},{10,11... | collective-permute-start | bytes 393224 | tf_op jit(solution)/shard_map/ppermute | solution.py:247
  12.9 0.0 collective-permute-start.4
  13.6 0.0 collective-permute-done.6.refs_11_
  13.6 0.3 collective-permute-done.5.refs_10_
  13.9 0.4 collective-permute-done.4.refs_9_
  14.3 0.0 slice-done
  14.3 0.0 slice-done.1
  14.3 0.0 slice-done.2
  14.3 0.0 slice-done.3
  14.3 2.4 %products.1 = (f32[4,8,2048]{2,1,0:T(8,128)S(1)}, f32[4,8,2048]{2,1,0:T(8,128)S(1)}, f32[4,8,2048]{2,1,0:T(8,128)S(1)}) custom-call(s32[1,1]{1,0:T(1,128)S(6)} %copy.12.refs_0_, f32[256,128,128]{2,1,0:T(8,128)S(1)} %bitcast.22, s32[1,1,256]{2,1,0:T(1,128)} %refs_2_.1, s32[1,1,256]{2,1,0:T(1,128)} %refs_3_.1, f32[1,2048]{1,0:T(1,128)} %bitcast.23, ...), custom_call_target="tpu_custom_call" | custom-call | tf_op jit(solution)/shard_map/products/pallas_call | solution.py:293
  16.7 0.3 collective-permute-start.7
  16.9 3.0 %collective-permute-start.13 = (f32[8,2048]{1,0:T(8,128)S(1)}, f32[8,2048]{1,0:T(8,128)S(1)}, u32[]{:S(2)}, u32[]{:S(2)}) collective-permute-start(f32[8,2048]{1,0:T(8,128)S(1)} %get-tuple-element.20), channel_id=1, source_target_pairs={{0,8},{8,16},{16,24},{24,0},{1,9},{9,17},{17,25},{25,1},{2,10},{10... | collective-permute-start | bytes 196616 | tf_op jit(solution)/shard_map/ppermute | solution.py:250
  20.0 4.7 %collective-permute-start.12 = (f32[8,2048]{1,0:T(8,128)S(1)}, f32[8,2048]{1,0:T(8,128)S(1)}, u32[]{:S(2)}, u32[]{:S(2)}) collective-permute-start(f32[8,2048]{1,0:T(8,128)S(1)} %get-tuple-element.21), channel_id=1, source_target_pairs={{0,16},{8,24},{16,0},{24,8},{1,17},{9,25},{17,1},{25,9},{2,18},{10... | collective-permute-start | bytes 196616 | tf_op jit(solution)/shard_map/ppermute | solution.py:250
  24.6 0.0 collective-permute-start.11
  24.7 0.0 collective-permute-done.7
  24.7 2.1 %collective-permute-start.10 = (f32[8,2048]{1,0:T(8,128)S(1)}, f32[8,2048]{1,0:T(8,128)S(1)}, u32[]{:S(2)}, u32[]{:S(2)}) collective-permute-start(f32[8,2048]{1,0:T(8,128)S(1)} %get-tuple-element.17), channel_id=1, source_target_pairs={{0,6},{1,7},{2,4},{3,5},{4,2},{5,3},{6,0},{7,1},{8,14},{9,15},{10,... | collective-permute-start | bytes 196616 | tf_op jit(solution)/shard_map/ppermute | solution.py:247
  26.8 0.5 %collective-permute-start.9 = (f32[8,2048]{1,0:T(8,128)S(1)}, f32[8,2048]{1,0:T(8,128)S(1)}, u32[]{:S(2)}, u32[]{:S(2)}) collective-permute-start(f32[8,2048]{1,0:T(8,128)S(1)} %get-tuple-element.18), channel_id=1, source_target_pairs={{0,4},{1,5},{2,6},{3,7},{4,0},{5,1},{6,2},{7,3},{8,12},{9,13},{10,... | collective-permute-start | bytes 196616 | tf_op jit(solution)/shard_map/ppermute | solution.py:247
  27.3 0.0 collective-permute-done.13.refs_11_
  27.3 0.9 %collective-permute-start.8 = (f32[8,2048]{1,0:T(8,128)S(1)}, f32[8,2048]{1,0:T(8,128)S(1)}, u32[]{:S(2)}, u32[]{:S(2)}) collective-permute-start(f32[8,2048]{1,0:T(8,128)S(1)} %get-tuple-element.19), channel_id=1, source_target_pairs={{0,2},{1,3},{2,0},{3,1},{4,6},{5,7},{6,4},{7,5},{8,10},{9,11},{10,... | collective-permute-start | bytes 196616 | tf_op jit(solution)/shard_map/ppermute | solution.py:247
  28.3 1.3 %collective-permute-done.12.refs_10_ = f32[8,2048]{1,0:T(8,128)S(1)} collective-permute-done((f32[8,2048]{1,0:T(8,128)S(1)}, f32[8,2048]{1,0:T(8,128)S(1)}, u32[]{:S(2)}, u32[]{:S(2)}) %collective-permute-start.12) | collective-permute-done | bytes 65568 | tf_op jit(solution)/shard_map/ppermute | solution.py:250
  29.6 0.5 %collective-permute-done.11.refs_9_ = f32[8,2048]{1,0:T(8,128)S(1)} collective-permute-done((f32[8,2048]{1,0:T(8,128)S(1)}, f32[8,2048]{1,0:T(8,128)S(1)}, u32[]{:S(2)}, u32[]{:S(2)}) %collective-permute-start.11) | collective-permute-done | bytes 65568 | tf_op jit(solution)/shard_map/ppermute | solution.py:250
  30.1 0.0 collective-permute-done.10.refs_8_
  30.1 1.0 %collective-permute-done.9.refs_7_ = f32[8,2048]{1,0:T(8,128)S(1)} collective-permute-done((f32[8,2048]{1,0:T(8,128)S(1)}, f32[8,2048]{1,0:T(8,128)S(1)}, u32[]{:S(2)}, u32[]{:S(2)}) %collective-permute-start.9) | collective-permute-done | bytes 65568 | tf_op jit(solution)/shard_map/ppermute | solution.py:247
  31.1 0.5 %collective-permute-done.8.refs_6_ = f32[8,2048]{1,0:T(8,128)S(1)} collective-permute-done((f32[8,2048]{1,0:T(8,128)S(1)}, f32[8,2048]{1,0:T(8,128)S(1)}, u32[]{:S(2)}, u32[]{:S(2)}) %collective-permute-start.8) | collective-permute-done | bytes 65568 | tf_op jit(solution)/shard_map/ppermute | solution.py:247
  31.6 0.0 copy-done
  31.6 0.0 copy-done.1
  31.6 0.4 image.1
  32.0 11.3 %all_to_all.5.sums_in = f32[32,4,128]{2,1,0:T(4,128)S(1)} all-to-all(f32[32,4,128]{2,1,0:T(4,128)S(1)} %get-tuple-element.15), channel_id=1, replica_groups=mesh['row'=4,'col'=8] {'row','col'}, dimensions={0} | all-to-all | bytes 131072 | tf_op jit(solution)/shard_map/all_to_all | solution.py:347
  43.3 0.0 copy-done.2
  43.3 2.1 %finish.1 = (f32[8,2048]{1,0:T(8,128)}, f32[8,8]{1,0:T(8,128)}, f32[8,8]{1,0:T(8,128)}) custom-call(f32[32,4,128]{2,1,0:T(4,128)S(1)} %all_to_all.5.sums_in, f32[8,2048]{1,0:T(8,128)S(1)} %get-tuple-element.16.image, f32[8,2048]{1,0:T(8,128)S(1)} %copy-done, f32[8,2048]{1,0:T(8,128)S(1)} %copy-done.1, f32[8,8]{1,0:T(8,128)S(1)} %copy-done.2), custom_call_target="tpu_custom_call" | custom-call | tf_op jit(solution)/shard_map/finish/pallas_call | solution.py:348
  (4 shorter events, 0.1 us)
Async XLA Ops:
  0.6 1.6 %collective-permute-start = (f32[8,2048]{1,0:T(8,128)}, f32[8,2048]{1,0:T(8,128)S(1)}, u32[]{:S(2)}, u32[]{:S(2)}) collective-permute-start(f32[8,2048]{1,0:T(8,128)} %now.3), channel_id=1, source_target_pairs={{0,1},{1,0},{2,3},{3,2},{4,5},{5,4},{6,7},{7,6},{8,9},{9,8},{10,11... | collective-permute-start | bytes 196616 | tf_op jit(solution)/shard_map/ppermute | solution.py:247
  2.3 12.0 %slice-start = ((s8[16777216]{0:T(1024)(128)(4,1)}), s8[4194304]{0:T(1024)(128)(4,1)S(1)}, s32[]{:S(2)}) async-start(s8[16777216]{0:T(1024)(128)(4,1)} %bitcast.20), calls=%async_computation.1 | async-start | bytes 8388608
  2.3 12.0 %slice-start.1 = ((s8[16777216]{0:T(1024)(128)(4,1)}), s8[4194304]{0:T(1024)(128)(4,1)S(1)}, s32[]{:S(2)}) async-start(s8[16777216]{0:T(1024)(128)(4,1)} %bitcast.20), calls=%async_computation.2 | async-start | bytes 8388608
  2.3 12.0 %slice-start.2 = ((s8[16777216]{0:T(1024)(128)(4,1)}), s8[4194304]{0:T(1024)(128)(4,1)S(1)}, s32[]{:S(2)}) async-start(s8[16777216]{0:T(1024)(128)(4,1)} %bitcast.20), calls=%async_computation.3 | async-start | bytes 8388608
  2.3 12.0 %slice-start.3 = ((s8[16777216]{0:T(1024)(128)(4,1)}), s8[4194304]{0:T(1024)(128)(4,1)S(1)}, s32[]{:S(2)}) async-start(s8[16777216]{0:T(1024)(128)(4,1)} %bitcast.20), calls=%async_computation.4 | async-start | bytes 8388608
  2.3 9.3 %collective-permute-start.3 = (f32[16,2048]{1,0:T(8,128)S(1)}, f32[16,2048]{1,0:T(8,128)S(1)}, u32[]{:S(2)}, u32[]{:S(2)}) collective-permute-start(f32[16,2048]{1,0:T(8,128)S(1)} %constant_dynamic-update-slice_fusion.refs_5_), channel_id=1, source_target_pairs={{0,6},{1,25},{2,4},{3,27},{4,2},{5,29},{6,0},{7,31},{8,14},{9,17},... | collective-permute-start | bytes 393224 | tf_op jit(solution)/shard_map/ppermute | solution.py:261
  6.2 5.8 %collective-permute-start.2 = (f32[16,2048]{1,0:T(8,128)S(1)}, f32[16,2048]{1,0:T(8,128)S(1)}, u32[]{:S(2)}, u32[]{:S(2)}) collective-permute-start(f32[16,2048]{1,0:T(8,128)S(1)} %constant_dynamic-update-slice_fusion.refs_5_), channel_id=1, source_target_pairs={{0,4},{1,17},{2,6},{3,19},{4,0},{5,21},{6,2},{7,23},{8,12},{9,25},... | collective-permute-start | bytes 393224 | tf_op jit(solution)/shard_map/ppermute | solution.py:261
  6.7 5.0 %collective-permute-start.1 = (f32[16,2048]{1,0:T(8,128)S(1)}, f32[16,2048]{1,0:T(8,128)S(1)}, u32[]{:S(2)}, u32[]{:S(2)}) collective-permute-start(f32[16,2048]{1,0:T(8,128)S(1)} %constant_dynamic-update-slice_fusion.refs_5_), channel_id=1, source_target_pairs={{0,2},{1,9},{2,0},{3,11},{4,6},{5,13},{6,4},{7,15},{8,10},{9,1},{1... | collective-permute-start | bytes 393224 | tf_op jit(solution)/shard_map/ppermute | solution.py:261
  8.3 23.3 %copy-start = (f32[8,2048]{1,0:T(8,128)S(1)}, f32[8,2048]{1,0:T(8,128)}, u32[]{:S(2)}) copy-start(f32[8,2048]{1,0:T(8,128)} %now.3) | copy-start | bytes 196612
  8.3 23.3 %copy-start.1 = (f32[8,2048]{1,0:T(8,128)S(1)}, f32[8,2048]{1,0:T(8,128)}, u32[]{:S(2)}) copy-start(f32[8,2048]{1,0:T(8,128)} %prev.3) | copy-start | bytes 196612
  8.3 35.0 %copy-start.2 = (f32[8,8]{1,0:T(8,128)S(1)}, f32[8,8]{1,0:T(8,128)}, u32[]{:S(2)}) copy-start(f32[8,8]{1,0:T(8,128)} %coupling.1) | copy-start | bytes 772
  11.6 1.9 %collective-permute-start.6 = (f32[16,2048]{1,0:T(8,128)S(1)}, f32[16,2048]{1,0:T(8,128)S(1)}, u32[]{:S(2)}, u32[]{:S(2)}) collective-permute-start(f32[16,2048]{1,0:T(8,128)S(1)} %collective-permute-done.3.refs_8_), channel_id=1, source_target_pairs={{0,1},{1,0},{2,3},{3,2},{4,5},{5,4},{6,7},{7,6},{8,9},{9,8},{10,11... | collective-permute-start | bytes 393224 | tf_op jit(solution)/shard_map/ppermute | solution.py:247
  12.0 1.9 %collective-permute-start.5 = (f32[16,2048]{1,0:T(8,128)S(1)}, f32[16,2048]{1,0:T(8,128)S(1)}, u32[]{:S(2)}, u32[]{:S(2)}) collective-permute-start(f32[16,2048]{1,0:T(8,128)S(1)} %collective-permute-done.2.refs_7_), channel_id=1, source_target_pairs={{0,1},{1,0},{2,3},{3,2},{4,5},{5,4},{6,7},{7,6},{8,9},{9,8},{10,11... | collective-permute-start | bytes 393224 | tf_op jit(solution)/shard_map/ppermute | solution.py:247
  12.9 1.3 %collective-permute-start.4 = (f32[16,2048]{1,0:T(8,128)S(1)}, f32[16,2048]{1,0:T(8,128)S(1)}, u32[]{:S(2)}, u32[]{:S(2)}) collective-permute-start(f32[16,2048]{1,0:T(8,128)S(1)} %collective-permute-done.1.refs_6_), channel_id=1, source_target_pairs={{0,1},{1,0},{2,3},{3,2},{4,5},{5,4},{6,7},{7,6},{8,9},{9,8},{10,11... | collective-permute-start | bytes 393224 | tf_op jit(solution)/shard_map/ppermute | solution.py:247
  16.7 8.0 %collective-permute-start.7 = (f32[4,8,2048]{2,1,0:T(8,128)S(1)}, f32[4,8,2048]{2,1,0:T(8,128)S(1)}, u32[]{:S(2)}, u32[]{:S(2)}) collective-permute-start(f32[4,8,2048]{2,1,0:T(8,128)S(1)} %get-tuple-element.13), channel_id=1, source_target_pairs={{0,1},{1,0},{2,3},{3,2},{4,5},{5,4},{6,7},{7,6},{8,9},{9,8},{10,11... | collective-permute-start | bytes 786440 | tf_op jit(solution)/shard_map/ppermute | solution.py:247
  16.9 10.4 %collective-permute-start.13 = (f32[8,2048]{1,0:T(8,128)S(1)}, f32[8,2048]{1,0:T(8,128)S(1)}, u32[]{:S(2)}, u32[]{:S(2)}) collective-permute-start(f32[8,2048]{1,0:T(8,128)S(1)} %get-tuple-element.20), channel_id=1, source_target_pairs={{0,8},{8,16},{16,24},{24,0},{1,9},{9,17},{17,25},{25,1},{2,10},{10... | collective-permute-start | bytes 196616 | tf_op jit(solution)/shard_map/ppermute | solution.py:250
  20.0 9.6 %collective-permute-start.12 = (f32[8,2048]{1,0:T(8,128)S(1)}, f32[8,2048]{1,0:T(8,128)S(1)}, u32[]{:S(2)}, u32[]{:S(2)}) collective-permute-start(f32[8,2048]{1,0:T(8,128)S(1)} %get-tuple-element.21), channel_id=1, source_target_pairs={{0,16},{8,24},{16,0},{24,8},{1,17},{9,25},{17,1},{25,9},{2,18},{10... | collective-permute-start | bytes 196616 | tf_op jit(solution)/shard_map/ppermute | solution.py:250
  24.6 5.4 %collective-permute-start.11 = (f32[8,2048]{1,0:T(8,128)S(1)}, f32[8,2048]{1,0:T(8,128)S(1)}, u32[]{:S(2)}, u32[]{:S(2)}) collective-permute-start(f32[8,2048]{1,0:T(8,128)S(1)} %get-tuple-element.22), channel_id=1, source_target_pairs={{0,24},{8,0},{16,8},{24,16},{1,25},{9,1},{17,9},{25,17},{2,26},{10... | collective-permute-start | bytes 196616 | tf_op jit(solution)/shard_map/ppermute | solution.py:250
  24.7 5.4 %collective-permute-start.10 = (f32[8,2048]{1,0:T(8,128)S(1)}, f32[8,2048]{1,0:T(8,128)S(1)}, u32[]{:S(2)}, u32[]{:S(2)}) collective-permute-start(f32[8,2048]{1,0:T(8,128)S(1)} %get-tuple-element.17), channel_id=1, source_target_pairs={{0,6},{1,7},{2,4},{3,5},{4,2},{5,3},{6,0},{7,1},{8,14},{9,15},{10,... | collective-permute-start | bytes 196616 | tf_op jit(solution)/shard_map/ppermute | solution.py:247
  26.8 4.3 %collective-permute-start.9 = (f32[8,2048]{1,0:T(8,128)S(1)}, f32[8,2048]{1,0:T(8,128)S(1)}, u32[]{:S(2)}, u32[]{:S(2)}) collective-permute-start(f32[8,2048]{1,0:T(8,128)S(1)} %get-tuple-element.18), channel_id=1, source_target_pairs={{0,4},{1,5},{2,6},{3,7},{4,0},{5,1},{6,2},{7,3},{8,12},{9,13},{10,... | collective-permute-start | bytes 196616 | tf_op jit(solution)/shard_map/ppermute | solution.py:247
  27.3 4.3 %collective-permute-start.8 = (f32[8,2048]{1,0:T(8,128)S(1)}, f32[8,2048]{1,0:T(8,128)S(1)}, u32[]{:S(2)}, u32[]{:S(2)}) collective-permute-start(f32[8,2048]{1,0:T(8,128)S(1)} %get-tuple-element.19), channel_id=1, source_target_pairs={{0,2},{1,3},{2,0},{3,1},{4,6},{5,7},{6,4},{7,5},{8,10},{9,11},{10,... | collective-permute-start | bytes 196616 | tf_op jit(solution)/shard_map/ppermute | solution.py:247

commit v11 on v10

--- a/solution.py
+++ b/solution.py
@@ -99,7 +99,7 @@
     for s in range(1, rows):
         store_split(
             vec_cols,
-            jnp.bitwise_xor(row, s) * piece_tiles,
+            lax.rem(row + s, rows) * piece_tiles,
             lambda at: jnp.where(
                 first, passed[s - 1][vectors:, at], fetched[s - 1][:vectors, at]
             ),
@@ -256,7 +256,7 @@
                 if c % 2 == 0:
                     to = (r, c ^ (2 * s) if s < planes else c)
                 else:
-                    to = (r ^ s if s < rows else r, c)
+                    to = ((r - s) % rows if s < rows else r, c)
                 pairs.append((r * cols + c, to[0] * cols + to[1]))
         return lax.ppermute(x, ("row", "col"), pairs)
 

time: 45.7 us -> 45.6 us (level)
  no operation moved by 1% of the time
where the time goes in v11:
time: 45.6 us; the launch traced here: 45.4 us
  starting transfers between devices  18.1 us (40%)
  blocking collectives  11.3 us (25%)
  waiting for transfers between devices  7.28 us (16%)
  Pallas kernels  6.33 us (14%)
  between operations  1.41 us (3%)
  local copies, waits for them, and re-layouts  0.9 us (2%)
    all_to_all x1, blocking collectives, local(): sums = lax.all_to_all(sums, ('row', 'col'), 0, 0)  11.3 us
    ppermute x3, starting transfers between devices, along_row(): return lax.ppermute(x, 'row', [(i, (i - s) % rows) for i in range(rows)])  7.71 us
    ppermute x8, starting transfers between devices, along_col(): return lax.ppermute(x, 'col', [(i, i ^ s) for i in range(cols)])  5.94 us
    ppermute x3, starting transfers between devices, apart(): return lax.ppermute(x, ('row', 'col'), pairs)  4.49 us
    ppermute x3, waiting for transfers between devices, apart(): return lax.ppermute(x, ('row', 'col'), pairs)  3.29 us
    pallas_call x1, Pallas kernels, local(): pl.pallas_call(functools.partial(products_kernel, rows, planes, group), o...  2.35 us
    ppermute x8, waiting for transfers between devices, along_col(): return lax.ppermute(x, 'col', [(i, i ^ s) for i in range(cols)])  2.15 us
    pallas_call x1, Pallas kernels, local(): pl.pallas_call(functools.partial(finish_kernel, float(piece * devices)),...  2.1 us
  transfers between devices with their start and end apart: 14, of which 8 were waited for; matrix products, arithmetic and copies ran while one was open for 2% of the time, Pallas kernels for 3%

profile of v11, /device:TPU:0, one launch (start us, length us, event | category | flops | bytes accessed | tf_op | source)
XLA Modules:
  0.0 45.4 jit_solution(6495735479287382414)
XLA Ops:
  0.6 0.5 %collective-permute-start = (f32[8,2048]{1,0:T(8,128)}, f32[8,2048]{1,0:T(8,128)S(1)}, u32[]{:S(2)}, u32[]{:S(2)}) collective-permute-start(f32[8,2048]{1,0:T(8,128)} %now.3), channel_id=1, source_target_pairs={{0,1},{1,0},{2,3},{3,2},{4,5},{5,4},{6,7},{7,6},{8,9},{9,8},{10,11... | collective-permute-start | bytes 196616 | tf_op jit(solution)/shard_map/ppermute | solution.py:247
  1.1 0.8 %constant_dynamic-update-slice_fusion.1 = f32[16,2048]{1,0:T(8,128)S(1)} fusion(f32[8,2048]{1,0:T(8,128)} %now.3), kind=kLoop, calls=%fused_computation.13 | loop fusion | bytes 131072
  2.0 0.3 collective-permute-done
  2.3 0.0 slice-start
  2.3 0.0 slice-start.1
  2.3 0.0 slice-start.2
  2.3 0.0 slice-start.3
  2.3 3.9 %collective-permute-start.3 = (f32[16,2048]{1,0:T(8,128)S(1)}, f32[16,2048]{1,0:T(8,128)S(1)}, u32[]{:S(2)}, u32[]{:S(2)}) collective-permute-start(f32[16,2048]{1,0:T(8,128)S(1)} %constant_dynamic-update-slice_fusion.refs_5_), channel_id=1, source_target_pairs={{0,6},{1,9},{2,4},{3,11},{4,2},{5,13},{6,0},{7,15},{8,14},{9,17},{... | collective-permute-start | bytes 393224 | tf_op jit(solution)/shard_map/ppermute | solution.py:261
  6.2 0.5 %collective-permute-start.2 = (f32[16,2048]{1,0:T(8,128)S(1)}, f32[16,2048]{1,0:T(8,128)S(1)}, u32[]{:S(2)}, u32[]{:S(2)}) collective-permute-start(f32[16,2048]{1,0:T(8,128)S(1)} %constant_dynamic-update-slice_fusion.refs_5_), channel_id=1, source_target_pairs={{0,4},{1,17},{2,6},{3,19},{4,0},{5,21},{6,2},{7,23},{8,12},{9,25},... | collective-permute-start | bytes 393224 | tf_op jit(solution)/shard_map/ppermute | solution.py:261
  6.7 0.1 collective-permute-start.1
  6.8 1.5 %fixed.1.refs_2_ = f32[16,16]{1,0:T(8,128)S(1)} custom-call(f32[8,2048]{1,0:T(8,128)} %now.3, f32[8,2048]{1,0:T(8,128)} %prev.3), custom_call_target="tpu_custom_call" | custom-call | flops 20000000000 | bytes 131072 | tf_op jit(solution)/shard_map/fixed/pallas_call | solution.py:269
  8.3 0.0 copy-start
  8.3 0.0 copy-start.1
  8.3 0.0 copy-start.2
  8.3 3.3 %collective-permute-done.1.refs_6_ = f32[16,2048]{1,0:T(8,128)S(1)} collective-permute-done((f32[16,2048]{1,0:T(8,128)S(1)}, f32[16,2048]{1,0:T(8,128)S(1)}, u32[]{:S(2)}, u32[]{:S(2)}) %collective-permute-start.1) | collective-permute-done | bytes 131104 | tf_op jit(solution)/shard_map/ppermute | solution.py:261
  11.6 0.0 collective-permute-done.3.refs_8_
  11.6 1.0 %collective-permute-start.6 = (f32[16,2048]{1,0:T(8,128)S(1)}, f32[16,2048]{1,0:T(8,128)S(1)}, u32[]{:S(2)}, u32[]{:S(2)}) collective-permute-start(f32[16,2048]{1,0:T(8,128)S(1)} %collective-permute-done.3.refs_8_), channel_id=1, source_target_pairs={{0,1},{1,0},{2,3},{3,2},{4,5},{5,4},{6,7},{7,6},{8,9},{9,8},{10,11... | collective-permute-start | bytes 393224 | tf_op jit(solution)/shard_map/ppermute | solution.py:247
  12.6 0.0 collective-permute-done.2.refs_7_
  12.6 0.1 collective-permute-start.5
  12.7 0.4 collective-permute-start.4
  13.8 0.0 collective-permute-done.6.refs_11_
  13.8 0.2 collective-permute-done.5.refs_10_
  13.9 0.2 collective-permute-done.4.refs_9_
  14.1 0.0 slice-done
  14.1 0.0 slice-done.1
  14.1 0.0 slice-done.2
  14.1 0.0 slice-done.3
  14.2 2.3 %products.1 = (f32[4,8,2048]{2,1,0:T(8,128)S(1)}, f32[4,8,2048]{2,1,0:T(8,128)S(1)}, f32[4,8,2048]{2,1,0:T(8,128)S(1)}) custom-call(s32[1,1]{1,0:T(1,128)S(6)} %copy.12.refs_0_, f32[256,128,128]{2,1,0:T(8,128)S(1)} %bitcast.22, s32[1,1,256]{2,1,0:T(1,128)} %refs_2_.1, s32[1,1,256]{2,1,0:T(1,128)} %refs_3_.1, f32[1,2048]{1,0:T(1,128)} %bitcast.23, ...), custom_call_target="tpu_custom_call" | custom-call | tf_op jit(solution)/shard_map/products/pallas_call | solution.py:293
  16.5 0.4 collective-permute-start.7
  16.9 3.2 %collective-permute-start.13 = (f32[8,2048]{1,0:T(8,128)S(1)}, f32[8,2048]{1,0:T(8,128)S(1)}, u32[]{:S(2)}, u32[]{:S(2)}) collective-permute-start(f32[8,2048]{1,0:T(8,128)S(1)} %get-tuple-element.20), channel_id=1, source_target_pairs={{0,8},{8,16},{16,24},{24,0},{1,9},{9,17},{17,25},{25,1},{2,10},{10... | collective-permute-start | bytes 196616 | tf_op jit(solution)/shard_map/ppermute | solution.py:250
  20.2 4.5 %collective-permute-start.12 = (f32[8,2048]{1,0:T(8,128)S(1)}, f32[8,2048]{1,0:T(8,128)S(1)}, u32[]{:S(2)}, u32[]{:S(2)}) collective-permute-start(f32[8,2048]{1,0:T(8,128)S(1)} %get-tuple-element.21), channel_id=1, source_target_pairs={{0,16},{8,24},{16,0},{24,8},{1,17},{9,25},{17,1},{25,9},{2,18},{10... | collective-permute-start | bytes 196616 | tf_op jit(solution)/shard_map/ppermute | solution.py:250
  24.6 0.0 collective-permute-start.11
  24.6 0.0 collective-permute-done.7
  24.7 2.1 %collective-permute-start.10 = (f32[8,2048]{1,0:T(8,128)S(1)}, f32[8,2048]{1,0:T(8,128)S(1)}, u32[]{:S(2)}, u32[]{:S(2)}) collective-permute-start(f32[8,2048]{1,0:T(8,128)S(1)} %get-tuple-element.17), channel_id=1, source_target_pairs={{0,6},{1,7},{2,4},{3,5},{4,2},{5,3},{6,0},{7,1},{8,14},{9,15},{10,... | collective-permute-start | bytes 196616 | tf_op jit(solution)/shard_map/ppermute | solution.py:247
  26.8 0.5 %collective-permute-start.9 = (f32[8,2048]{1,0:T(8,128)S(1)}, f32[8,2048]{1,0:T(8,128)S(1)}, u32[]{:S(2)}, u32[]{:S(2)}) collective-permute-start(f32[8,2048]{1,0:T(8,128)S(1)} %get-tuple-element.18), channel_id=1, source_target_pairs={{0,4},{1,5},{2,6},{3,7},{4,0},{5,1},{6,2},{7,3},{8,12},{9,13},{10,... | collective-permute-start | bytes 196616 | tf_op jit(solution)/shard_map/ppermute | solution.py:247
  27.3 0.0 collective-permute-done.13.refs_11_
  27.3 0.9 %collective-permute-start.8 = (f32[8,2048]{1,0:T(8,128)S(1)}, f32[8,2048]{1,0:T(8,128)S(1)}, u32[]{:S(2)}, u32[]{:S(2)}) collective-permute-start(f32[8,2048]{1,0:T(8,128)S(1)} %get-tuple-element.19), channel_id=1, source_target_pairs={{0,2},{1,3},{2,0},{3,1},{4,6},{5,7},{6,4},{7,5},{8,10},{9,11},{10,... | collective-permute-start | bytes 196616 | tf_op jit(solution)/shard_map/ppermute | solution.py:247
  28.2 1.3 %collective-permute-done.12.refs_10_ = f32[8,2048]{1,0:T(8,128)S(1)} collective-permute-done((f32[8,2048]{1,0:T(8,128)S(1)}, f32[8,2048]{1,0:T(8,128)S(1)}, u32[]{:S(2)}, u32[]{:S(2)}) %collective-permute-start.12) | collective-permute-done | bytes 65568 | tf_op jit(solution)/shard_map/ppermute | solution.py:250
  29.6 0.5 %collective-permute-done.11.refs_9_ = f32[8,2048]{1,0:T(8,128)S(1)} collective-permute-done((f32[8,2048]{1,0:T(8,128)S(1)}, f32[8,2048]{1,0:T(8,128)S(1)}, u32[]{:S(2)}, u32[]{:S(2)}) %collective-permute-start.11) | collective-permute-done | bytes 65568 | tf_op jit(solution)/shard_map/ppermute | solution.py:250
  30.1 0.0 collective-permute-done.10.refs_8_
  30.1 1.0 %collective-permute-done.9.refs_7_ = f32[8,2048]{1,0:T(8,128)S(1)} collective-permute-done((f32[8,2048]{1,0:T(8,128)S(1)}, f32[8,2048]{1,0:T(8,128)S(1)}, u32[]{:S(2)}, u32[]{:S(2)}) %collective-permute-start.9) | collective-permute-done | bytes 65568 | tf_op jit(solution)/shard_map/ppermute | solution.py:247
  31.1 0.5 %collective-permute-done.8.refs_6_ = f32[8,2048]{1,0:T(8,128)S(1)} collective-permute-done((f32[8,2048]{1,0:T(8,128)S(1)}, f32[8,2048]{1,0:T(8,128)S(1)}, u32[]{:S(2)}, u32[]{:S(2)}) %collective-permute-start.8) | collective-permute-done | bytes 65568 | tf_op jit(solution)/shard_map/ppermute | solution.py:247
  31.6 0.0 copy-done
  31.6 0.0 copy-done.1
  31.6 0.4 image.1
  32.0 11.3 %all_to_all.5.sums_in = f32[32,4,128]{2,1,0:T(4,128)S(1)} all-to-all(f32[32,4,128]{2,1,0:T(4,128)S(1)} %get-tuple-element.15), channel_id=1, replica_groups=mesh['row'=4,'col'=8] {'row','col'}, dimensions={0} | all-to-all | bytes 131072 | tf_op jit(solution)/shard_map/all_to_all | solution.py:347
  43.3 0.0 copy-done.2
  43.3 2.1 %finish.1 = (f32[8,2048]{1,0:T(8,128)}, f32[8,8]{1,0:T(8,128)}, f32[8,8]{1,0:T(8,128)}) custom-call(f32[32,4,128]{2,1,0:T(4,128)S(1)} %all_to_all.5.sums_in, f32[8,2048]{1,0:T(8,128)S(1)} %get-tuple-element.16.image, f32[8,2048]{1,0:T(8,128)S(1)} %copy-done, f32[8,2048]{1,0:T(8,128)S(1)} %copy-done.1, f32[8,8]{1,0:T(8,128)S(1)} %copy-done.2), custom_call_target="tpu_custom_call" | custom-call | tf_op jit(solution)/shard_map/finish/pallas_call | solution.py:348
  (4 shorter events, 0.1 us)
Async XLA Ops:
  0.6 1.6 %collective-permute-start = (f32[8,2048]{1,0:T(8,128)}, f32[8,2048]{1,0:T(8,128)S(1)}, u32[]{:S(2)}, u32[]{:S(2)}) collective-permute-start(f32[8,2048]{1,0:T(8,128)} %now.3), channel_id=1, source_target_pairs={{0,1},{1,0},{2,3},{3,2},{4,5},{5,4},{6,7},{7,6},{8,9},{9,8},{10,11... | collective-permute-start | bytes 196616 | tf_op jit(solution)/shard_map/ppermute | solution.py:247
  2.3 11.9 %slice-start = ((s8[16777216]{0:T(1024)(128)(4,1)}), s8[4194304]{0:T(1024)(128)(4,1)S(1)}, s32[]{:S(2)}) async-start(s8[16777216]{0:T(1024)(128)(4,1)} %bitcast.20), calls=%async_computation.1 | async-start | bytes 8388608
  2.3 11.9 %slice-start.1 = ((s8[16777216]{0:T(1024)(128)(4,1)}), s8[4194304]{0:T(1024)(128)(4,1)S(1)}, s32[]{:S(2)}) async-start(s8[16777216]{0:T(1024)(128)(4,1)} %bitcast.20), calls=%async_computation.2 | async-start | bytes 8388608
  2.3 11.9 %slice-start.2 = ((s8[16777216]{0:T(1024)(128)(4,1)}), s8[4194304]{0:T(1024)(128)(4,1)S(1)}, s32[]{:S(2)}) async-start(s8[16777216]{0:T(1024)(128)(4,1)} %bitcast.20), calls=%async_computation.3 | async-start | bytes 8388608
  2.3 11.9 %slice-start.3 = ((s8[16777216]{0:T(1024)(128)(4,1)}), s8[4194304]{0:T(1024)(128)(4,1)S(1)}, s32[]{:S(2)}) async-start(s8[16777216]{0:T(1024)(128)(4,1)} %bitcast.20), calls=%async_computation.4 | async-start | bytes 8388608
  2.3 9.3 %collective-permute-start.3 = (f32[16,2048]{1,0:T(8,128)S(1)}, f32[16,2048]{1,0:T(8,128)S(1)}, u32[]{:S(2)}, u32[]{:S(2)}) collective-permute-start(f32[16,2048]{1,0:T(8,128)S(1)} %constant_dynamic-update-slice_fusion.refs_5_), channel_id=1, source_target_pairs={{0,6},{1,9},{2,4},{3,11},{4,2},{5,13},{6,0},{7,15},{8,14},{9,17},{... | collective-permute-start | bytes 393224 | tf_op jit(solution)/shard_map/ppermute | solution.py:261
  6.2 6.4 %collective-permute-start.2 = (f32[16,2048]{1,0:T(8,128)S(1)}, f32[16,2048]{1,0:T(8,128)S(1)}, u32[]{:S(2)}, u32[]{:S(2)}) collective-permute-start(f32[16,2048]{1,0:T(8,128)S(1)} %constant_dynamic-update-slice_fusion.refs_5_), channel_id=1, source_target_pairs={{0,4},{1,17},{2,6},{3,19},{4,0},{5,21},{6,2},{7,23},{8,12},{9,25},... | collective-permute-start | bytes 393224 | tf_op jit(solution)/shard_map/ppermute | solution.py:261
  6.7 5.0 %collective-permute-start.1 = (f32[16,2048]{1,0:T(8,128)S(1)}, f32[16,2048]{1,0:T(8,128)S(1)}, u32[]{:S(2)}, u32[]{:S(2)}) collective-permute-start(f32[16,2048]{1,0:T(8,128)S(1)} %constant_dynamic-update-slice_fusion.refs_5_), channel_id=1, source_target_pairs={{0,2},{1,25},{2,0},{3,27},{4,6},{5,29},{6,4},{7,31},{8,10},{9,1},{... | collective-permute-start | bytes 393224 | tf_op jit(solution)/shard_map/ppermute | solution.py:261
  8.3 23.3 %copy-start = (f32[8,2048]{1,0:T(8,128)S(1)}, f32[8,2048]{1,0:T(8,128)}, u32[]{:S(2)}) copy-start(f32[8,2048]{1,0:T(8,128)} %now.3) | copy-start | bytes 196612
  8.3 23.3 %copy-start.1 = (f32[8,2048]{1,0:T(8,128)S(1)}, f32[8,2048]{1,0:T(8,128)}, u32[]{:S(2)}) copy-start(f32[8,2048]{1,0:T(8,128)} %prev.3) | copy-start | bytes 196612
  8.3 35.0 %copy-start.2 = (f32[8,8]{1,0:T(8,128)S(1)}, f32[8,8]{1,0:T(8,128)}, u32[]{:S(2)}) copy-start(f32[8,8]{1,0:T(8,128)} %coupling.1) | copy-start | bytes 772
  11.6 2.1 %collective-permute-start.6 = (f32[16,2048]{1,0:T(8,128)S(1)}, f32[16,2048]{1,0:T(8,128)S(1)}, u32[]{:S(2)}, u32[]{:S(2)}) collective-permute-start(f32[16,2048]{1,0:T(8,128)S(1)} %collective-permute-done.3.refs_8_), channel_id=1, source_target_pairs={{0,1},{1,0},{2,3},{3,2},{4,5},{5,4},{6,7},{7,6},{8,9},{9,8},{10,11... | collective-permute-start | bytes 393224 | tf_op jit(solution)/shard_map/ppermute | solution.py:247
  12.6 1.3 %collective-permute-start.5 = (f32[16,2048]{1,0:T(8,128)S(1)}, f32[16,2048]{1,0:T(8,128)S(1)}, u32[]{:S(2)}, u32[]{:S(2)}) collective-permute-start(f32[16,2048]{1,0:T(8,128)S(1)} %collective-permute-done.2.refs_7_), channel_id=1, source_target_pairs={{0,1},{1,0},{2,3},{3,2},{4,5},{5,4},{6,7},{7,6},{8,9},{9,8},{10,11... | collective-permute-start | bytes 393224 | tf_op jit(solution)/shard_map/ppermute | solution.py:247
  12.7 1.5 %collective-permute-start.4 = (f32[16,2048]{1,0:T(8,128)S(1)}, f32[16,2048]{1,0:T(8,128)S(1)}, u32[]{:S(2)}, u32[]{:S(2)}) collective-permute-start(f32[16,2048]{1,0:T(8,128)S(1)} %collective-permute-done.1.refs_6_), channel_id=1, source_target_pairs={{0,1},{1,0},{2,3},{3,2},{4,5},{5,4},{6,7},{7,6},{8,9},{9,8},{10,11... | collective-permute-start | bytes 393224 | tf_op jit(solution)/shard_map/ppermute | solution.py:247
  16.5 8.1 %collective-permute-start.7 = (f32[4,8,2048]{2,1,0:T(8,128)S(1)}, f32[4,8,2048]{2,1,0:T(8,128)S(1)}, u32[]{:S(2)}, u32[]{:S(2)}) collective-permute-start(f32[4,8,2048]{2,1,0:T(8,128)S(1)} %get-tuple-element.13), channel_id=1, source_target_pairs={{0,1},{1,0},{2,3},{3,2},{4,5},{5,4},{6,7},{7,6},{8,9},{9,8},{10,11... | collective-permute-start | bytes 786440 | tf_op jit(solution)/shard_map/ppermute | solution.py:247
  16.9 10.4 %collective-permute-start.13 = (f32[8,2048]{1,0:T(8,128)S(1)}, f32[8,2048]{1,0:T(8,128)S(1)}, u32[]{:S(2)}, u32[]{:S(2)}) collective-permute-start(f32[8,2048]{1,0:T(8,128)S(1)} %get-tuple-element.20), channel_id=1, source_target_pairs={{0,8},{8,16},{16,24},{24,0},{1,9},{9,17},{17,25},{25,1},{2,10},{10... | collective-permute-start | bytes 196616 | tf_op jit(solution)/shard_map/ppermute | solution.py:250
  20.2 9.4 %collective-permute-start.12 = (f32[8,2048]{1,0:T(8,128)S(1)}, f32[8,2048]{1,0:T(8,128)S(1)}, u32[]{:S(2)}, u32[]{:S(2)}) collective-permute-start(f32[8,2048]{1,0:T(8,128)S(1)} %get-tuple-element.21), channel_id=1, source_target_pairs={{0,16},{8,24},{16,0},{24,8},{1,17},{9,25},{17,1},{25,9},{2,18},{10... | collective-permute-start | bytes 196616 | tf_op jit(solution)/shard_map/ppermute | solution.py:250
  24.6 5.4 %collective-permute-start.11 = (f32[8,2048]{1,0:T(8,128)S(1)}, f32[8,2048]{1,0:T(8,128)S(1)}, u32[]{:S(2)}, u32[]{:S(2)}) collective-permute-start(f32[8,2048]{1,0:T(8,128)S(1)} %get-tuple-element.22), channel_id=1, source_target_pairs={{0,24},{8,0},{16,8},{24,16},{1,25},{9,1},{17,9},{25,17},{2,26},{10... | collective-permute-start | bytes 196616 | tf_op jit(solution)/shard_map/ppermute | solution.py:250
  24.7 5.4 %collective-permute-start.10 = (f32[8,2048]{1,0:T(8,128)S(1)}, f32[8,2048]{1,0:T(8,128)S(1)}, u32[]{:S(2)}, u32[]{:S(2)}) collective-permute-start(f32[8,2048]{1,0:T(8,128)S(1)} %get-tuple-element.17), channel_id=1, source_target_pairs={{0,6},{1,7},{2,4},{3,5},{4,2},{5,3},{6,0},{7,1},{8,14},{9,15},{10,... | collective-permute-start | bytes 196616 | tf_op jit(solution)/shard_map/ppermute | solution.py:247
  26.8 4.3 %collective-permute-start.9 = (f32[8,2048]{1,0:T(8,128)S(1)}, f32[8,2048]{1,0:T(8,128)S(1)}, u32[]{:S(2)}, u32[]{:S(2)}) collective-permute-start(f32[8,2048]{1,0:T(8,128)S(1)} %get-tuple-element.18), channel_id=1, source_target_pairs={{0,4},{1,5},{2,6},{3,7},{4,0},{5,1},{6,2},{7,3},{8,12},{9,13},{10,... | collective-permute-start | bytes 196616 | tf_op jit(solution)/shard_map/ppermute | solution.py:247
  27.3 4.3 %collective-permute-start.8 = (f32[8,2048]{1,0:T(8,128)S(1)}, f32[8,2048]{1,0:T(8,128)S(1)}, u32[]{:S(2)}, u32[]{:S(2)}) collective-permute-start(f32[8,2048]{1,0:T(8,128)S(1)} %get-tuple-element.19), channel_id=1, source_target_pairs={{0,2},{1,3},{2,0},{3,1},{4,6},{5,7},{6,4},{7,5},{8,10},{9,11},{10,... | collective-permute-start | bytes 196616 | tf_op jit(solution)/shard_map/ppermute | solution.py:247

commit v12 on v11

--- a/solution.py
+++ b/solution.py
@@ -10,7 +10,7 @@
 
 VMEM = pltpu.VMEM
 SMEM = pltpu.SMEM
-GROUP = 64
+GROUP = 128
 WAIT_FLOPS = 20_000_000_000
 MIB = 1 << 20
 

time: 45.6 us -> 45.2 us (level)
  Pallas kernels: 6.33 us -> 7.65 us
  blocking collectives: 11.3 us -> 10 us
    ppermute x3, waiting for transfers between devices: 1.83 us -> 0.04 us  [along_row(): return lax.ppermute(x, 'row', [(i, (i - s) % rows) for i in range(rows)])]
    ppermute x8, waiting for transfers between devices: 2.15 us -> 3.77 us  [along_col(): return lax.ppermute(x, 'col', [(i, i ^ s) for i in range(cols)])]
    pallas_call x1, Pallas kernels: 2.35 us -> 3.66 us  [local(): pl.pallas_call(functools.partial(products_kernel, rows, planes, group), o...]
    all_to_all x1, blocking collectives: 11.3 us -> 10 us  [local(): sums = lax.all_to_all(sums, ('row', 'col'), 0, 0)]
  transfers between devices with their start and end apart: 14 -> 14, of which waited for: 8 -> 7; matrix products, arithmetic and copies ran while one was open for 2% -> 2% of each run, Pallas kernels for 3% -> 3%
where the time goes in v12:
time: 45.2 us; the launch traced here: 45 us
  starting transfers between devices  17.9 us (40%)
  blocking collectives  10 us (22%)
  Pallas kernels  7.65 us (17%)
  waiting for transfers between devices  7.1 us (16%)
  between operations  1.41 us (3%)
  local copies, waits for them, and re-layouts  0.9 us (2%)
    all_to_all x1, blocking collectives, local(): sums = lax.all_to_all(sums, ('row', 'col'), 0, 0)  10 us
    ppermute x3, starting transfers between devices, along_row(): return lax.ppermute(x, 'row', [(i, (i - s) % rows) for i in range(rows)])  7.45 us
    ppermute x8, starting transfers between devices, along_col(): return lax.ppermute(x, 'col', [(i, i ^ s) for i in range(cols)])  5.96 us
    ppermute x3, starting transfers between devices, apart(): return lax.ppermute(x, ('row', 'col'), pairs)  4.49 us
    ppermute x8, waiting for transfers between devices, along_col(): return lax.ppermute(x, 'col', [(i, i ^ s) for i in range(cols)])  3.77 us
    pallas_call x1, Pallas kernels, local(): pl.pallas_call(functools.partial(products_kernel, rows, planes, group), o...  3.66 us
    ppermute x3, waiting for transfers between devices, apart(): return lax.ppermute(x, ('row', 'col'), pairs)  3.29 us
    pallas_call x1, Pallas kernels, local(): pl.pallas_call(functools.partial(finish_kernel, float(piece * devices)),...  2.1 us
  transfers between devices with their start and end apart: 14, of which 7 were waited for; matrix products, arithmetic and copies ran while one was open for 2% of the time, Pallas kernels for 3%

profile of v12, /device:TPU:0, one launch (start us, length us, event | category | flops | bytes accessed | tf_op | source)
XLA Modules:
  0.0 45.0 jit_solution(17662894153365144219)
XLA Ops:
  0.6 0.5 %collective-permute-start = (f32[8,2048]{1,0:T(8,128)}, f32[8,2048]{1,0:T(8,128)S(1)}, u32[]{:S(2)}, u32[]{:S(2)}) collective-permute-start(f32[8,2048]{1,0:T(8,128)} %now.3), channel_id=1, source_target_pairs={{0,1},{1,0},{2,3},{3,2},{4,5},{5,4},{6,7},{7,6},{8,9},{9,8},{10,11... | collective-permute-start | bytes 196616 | tf_op jit(solution)/shard_map/ppermute | solution.py:247
  1.1 0.8 %constant_dynamic-update-slice_fusion.1 = f32[16,2048]{1,0:T(8,128)S(1)} fusion(f32[8,2048]{1,0:T(8,128)} %now.3), kind=kLoop, calls=%fused_computation.13 | loop fusion | bytes 131072
  2.0 0.3 collective-permute-done
  2.3 0.0 slice-start
  2.3 0.0 slice-start.1
  2.3 0.0 slice-start.2
  2.3 0.0 slice-start.3
  2.3 3.9 %collective-permute-start.3 = (f32[16,2048]{1,0:T(8,128)S(1)}, f32[16,2048]{1,0:T(8,128)S(1)}, u32[]{:S(2)}, u32[]{:S(2)}) collective-permute-start(f32[16,2048]{1,0:T(8,128)S(1)} %constant_dynamic-update-slice_fusion.refs_5_), channel_id=1, source_target_pairs={{0,6},{1,9},{2,4},{3,11},{4,2},{5,13},{6,0},{7,15},{8,14},{9,17},{... | collective-permute-start | bytes 393224 | tf_op jit(solution)/shard_map/ppermute | solution.py:261
  6.2 0.5 %collective-permute-start.2 = (f32[16,2048]{1,0:T(8,128)S(1)}, f32[16,2048]{1,0:T(8,128)S(1)}, u32[]{:S(2)}, u32[]{:S(2)}) collective-permute-start(f32[16,2048]{1,0:T(8,128)S(1)} %constant_dynamic-update-slice_fusion.refs_5_), channel_id=1, source_target_pairs={{0,4},{1,17},{2,6},{3,19},{4,0},{5,21},{6,2},{7,23},{8,12},{9,25},... | collective-permute-start | bytes 393224 | tf_op jit(solution)/shard_map/ppermute | solution.py:261
  6.7 0.1 collective-permute-start.1
  6.8 1.5 %fixed.1.refs_2_ = f32[16,16]{1,0:T(8,128)S(1)} custom-call(f32[8,2048]{1,0:T(8,128)} %now.3, f32[8,2048]{1,0:T(8,128)} %prev.3), custom_call_target="tpu_custom_call" | custom-call | flops 20000000000 | bytes 131072 | tf_op jit(solution)/shard_map/fixed/pallas_call | solution.py:269
  8.3 0.0 copy-start
  8.3 0.0 copy-start.1
  8.3 0.0 copy-start.2
  8.3 3.3 %collective-permute-done.1.refs_6_ = f32[16,2048]{1,0:T(8,128)S(1)} collective-permute-done((f32[16,2048]{1,0:T(8,128)S(1)}, f32[16,2048]{1,0:T(8,128)S(1)}, u32[]{:S(2)}, u32[]{:S(2)}) %collective-permute-start.1) | collective-permute-done | bytes 131104 | tf_op jit(solution)/shard_map/ppermute | solution.py:261
  11.6 0.0 collective-permute-done.3.refs_8_
  11.6 1.0 %collective-permute-start.6 = (f32[16,2048]{1,0:T(8,128)S(1)}, f32[16,2048]{1,0:T(8,128)S(1)}, u32[]{:S(2)}, u32[]{:S(2)}) collective-permute-start(f32[16,2048]{1,0:T(8,128)S(1)} %collective-permute-done.3.refs_8_), channel_id=1, source_target_pairs={{0,1},{1,0},{2,3},{3,2},{4,5},{5,4},{6,7},{7,6},{8,9},{9,8},{10,11... | collective-permute-start | bytes 393224 | tf_op jit(solution)/shard_map/ppermute | solution.py:247
  12.6 0.0 collective-permute-done.2.refs_7_
  12.6 0.1 collective-permute-start.5
  12.7 0.4 collective-permute-start.4
  13.8 0.0 collective-permute-done.6.refs_11_
  13.8 0.2 collective-permute-done.5.refs_10_
  13.9 0.2 collective-permute-done.4.refs_9_
  14.1 0.0 slice-done
  14.1 0.0 slice-done.1
  14.1 0.0 slice-done.2
  14.1 0.0 slice-done.3
  14.2 3.7 %products.1 = (f32[4,8,2048]{2,1,0:T(8,128)S(1)}, f32[4,8,2048]{2,1,0:T(8,128)S(1)}, f32[4,8,2048]{2,1,0:T(8,128)S(1)}) custom-call(s32[1,1]{1,0:T(1,128)S(6)} %copy.12.refs_0_, f32[256,128,128]{2,1,0:T(8,128)S(1)} %bitcast.22, s32[1,1,256]{2,1,0:T(1,128)} %refs_2_.1, s32[1,1,256]{2,1,0:T(1,128)} %refs_3_.1, f32[1,2048]{1,0:T(1,128)} %bitcast.23, ...), custom_call_target="tpu_custom_call" | custom-call | tf_op jit(solution)/shard_map/products/pallas_call | solution.py:293
  17.8 0.4 collective-permute-start.7
  18.3 1.7 %collective-permute-start.13 = (f32[8,2048]{1,0:T(8,128)S(1)}, f32[8,2048]{1,0:T(8,128)S(1)}, u32[]{:S(2)}, u32[]{:S(2)}) collective-permute-start(f32[8,2048]{1,0:T(8,128)S(1)} %get-tuple-element.20), channel_id=1, source_target_pairs={{0,8},{8,16},{16,24},{24,0},{1,9},{9,17},{17,25},{25,1},{2,10},{10... | collective-permute-start | bytes 196616 | tf_op jit(solution)/shard_map/ppermute | solution.py:250
  20.0 4.2 %collective-permute-start.12 = (f32[8,2048]{1,0:T(8,128)S(1)}, f32[8,2048]{1,0:T(8,128)S(1)}, u32[]{:S(2)}, u32[]{:S(2)}) collective-permute-start(f32[8,2048]{1,0:T(8,128)S(1)} %get-tuple-element.21), channel_id=1, source_target_pairs={{0,16},{8,24},{16,0},{24,8},{1,17},{9,25},{17,1},{25,9},{2,18},{10... | collective-permute-start | bytes 196616 | tf_op jit(solution)/shard_map/ppermute | solution.py:250
  24.2 1.5 %collective-permute-start.11 = (f32[8,2048]{1,0:T(8,128)S(1)}, f32[8,2048]{1,0:T(8,128)S(1)}, u32[]{:S(2)}, u32[]{:S(2)}) collective-permute-start(f32[8,2048]{1,0:T(8,128)S(1)} %get-tuple-element.22), channel_id=1, source_target_pairs={{0,24},{8,0},{16,8},{24,16},{1,25},{9,1},{17,9},{25,17},{2,26},{10... | collective-permute-start | bytes 196616 | tf_op jit(solution)/shard_map/ppermute | solution.py:250
  25.7 0.0 collective-permute-done.7
  25.8 1.7 %collective-permute-start.10 = (f32[8,2048]{1,0:T(8,128)S(1)}, f32[8,2048]{1,0:T(8,128)S(1)}, u32[]{:S(2)}, u32[]{:S(2)}) collective-permute-start(f32[8,2048]{1,0:T(8,128)S(1)} %get-tuple-element.17), channel_id=1, source_target_pairs={{0,6},{1,7},{2,4},{3,5},{4,2},{5,3},{6,0},{7,1},{8,14},{9,15},{10,... | collective-permute-start | bytes 196616 | tf_op jit(solution)/shard_map/ppermute | solution.py:247
  27.5 0.7 %collective-permute-start.9 = (f32[8,2048]{1,0:T(8,128)S(1)}, f32[8,2048]{1,0:T(8,128)S(1)}, u32[]{:S(2)}, u32[]{:S(2)}) collective-permute-start(f32[8,2048]{1,0:T(8,128)S(1)} %get-tuple-element.18), channel_id=1, source_target_pairs={{0,4},{1,5},{2,6},{3,7},{4,0},{5,1},{6,2},{7,3},{8,12},{9,13},{10,... | collective-permute-start | bytes 196616 | tf_op jit(solution)/shard_map/ppermute | solution.py:247
  28.2 0.0 collective-permute-done.13.refs_11_
  28.2 1.1 %collective-permute-start.8 = (f32[8,2048]{1,0:T(8,128)S(1)}, f32[8,2048]{1,0:T(8,128)S(1)}, u32[]{:S(2)}, u32[]{:S(2)}) collective-permute-start(f32[8,2048]{1,0:T(8,128)S(1)} %get-tuple-element.19), channel_id=1, source_target_pairs={{0,2},{1,3},{2,0},{3,1},{4,6},{5,7},{6,4},{7,5},{8,10},{9,11},{10,... | collective-permute-start | bytes 196616 | tf_op jit(solution)/shard_map/ppermute | solution.py:247
  29.3 0.0 collective-permute-done.12.refs_10_
  29.3 0.0 collective-permute-done.11.refs_9_
  29.4 2.3 %collective-permute-done.10.refs_8_ = f32[8,2048]{1,0:T(8,128)S(1)} collective-permute-done((f32[8,2048]{1,0:T(8,128)S(1)}, f32[8,2048]{1,0:T(8,128)S(1)}, u32[]{:S(2)}, u32[]{:S(2)}) %collective-permute-start.10) | collective-permute-done | bytes 65568 | tf_op jit(solution)/shard_map/ppermute | solution.py:247
  31.7 0.4 collective-permute-done.9.refs_7_
  32.1 0.4 collective-permute-done.8.refs_6_
  32.5 0.0 copy-done
  32.5 0.0 copy-done.1
  32.5 0.4 image.1
  32.9 10.0 %all_to_all.5.sums_in = f32[32,4,128]{2,1,0:T(4,128)S(1)} all-to-all(f32[32,4,128]{2,1,0:T(4,128)S(1)} %get-tuple-element.15), channel_id=1, replica_groups=mesh['row'=4,'col'=8] {'row','col'}, dimensions={0} | all-to-all | bytes 131072 | tf_op jit(solution)/shard_map/all_to_all | solution.py:347
  42.9 0.0 copy-done.2
  42.9 2.1 %finish.1 = (f32[8,2048]{1,0:T(8,128)}, f32[8,8]{1,0:T(8,128)}, f32[8,8]{1,0:T(8,128)}) custom-call(f32[32,4,128]{2,1,0:T(4,128)S(1)} %all_to_all.5.sums_in, f32[8,2048]{1,0:T(8,128)S(1)} %get-tuple-element.16.image, f32[8,2048]{1,0:T(8,128)S(1)} %copy-done, f32[8,2048]{1,0:T(8,128)S(1)} %copy-done.1, f32[8,8]{1,0:T(8,128)S(1)} %copy-done.2), custom_call_target="tpu_custom_call" | custom-call | tf_op jit(solution)/shard_map/finish/pallas_call | solution.py:348
  (4 shorter events, 0.1 us)
Async XLA Ops:
  0.6 1.6 %collective-permute-start = (f32[8,2048]{1,0:T(8,128)}, f32[8,2048]{1,0:T(8,128)S(1)}, u32[]{:S(2)}, u32[]{:S(2)}) collective-permute-start(f32[8,2048]{1,0:T(8,128)} %now.3), channel_id=1, source_target_pairs={{0,1},{1,0},{2,3},{3,2},{4,5},{5,4},{6,7},{7,6},{8,9},{9,8},{10,11... | collective-permute-start | bytes 196616 | tf_op jit(solution)/shard_map/ppermute | solution.py:247
  2.3 11.9 %slice-start = ((s8[16777216]{0:T(1024)(128)(4,1)}), s8[4194304]{0:T(1024)(128)(4,1)S(1)}, s32[]{:S(2)}) async-start(s8[16777216]{0:T(1024)(128)(4,1)} %bitcast.20), calls=%async_computation.1 | async-start | bytes 8388608
  2.3 11.9 %slice-start.1 = ((s8[16777216]{0:T(1024)(128)(4,1)}), s8[4194304]{0:T(1024)(128)(4,1)S(1)}, s32[]{:S(2)}) async-start(s8[16777216]{0:T(1024)(128)(4,1)} %bitcast.20), calls=%async_computation.2 | async-start | bytes 8388608
  2.3 11.9 %slice-start.2 = ((s8[16777216]{0:T(1024)(128)(4,1)}), s8[4194304]{0:T(1024)(128)(4,1)S(1)}, s32[]{:S(2)}) async-start(s8[16777216]{0:T(1024)(128)(4,1)} %bitcast.20), calls=%async_computation.3 | async-start | bytes 8388608
  2.3 11.9 %slice-start.3 = ((s8[16777216]{0:T(1024)(128)(4,1)}), s8[4194304]{0:T(1024)(128)(4,1)S(1)}, s32[]{:S(2)}) async-start(s8[16777216]{0:T(1024)(128)(4,1)} %bitcast.20), calls=%async_computation.4 | async-start | bytes 8388608
  2.3 9.3 %collective-permute-start.3 = (f32[16,2048]{1,0:T(8,128)S(1)}, f32[16,2048]{1,0:T(8,128)S(1)}, u32[]{:S(2)}, u32[]{:S(2)}) collective-permute-start(f32[16,2048]{1,0:T(8,128)S(1)} %constant_dynamic-update-slice_fusion.refs_5_), channel_id=1, source_target_pairs={{0,6},{1,9},{2,4},{3,11},{4,2},{5,13},{6,0},{7,15},{8,14},{9,17},{... | collective-permute-start | bytes 393224 | tf_op jit(solution)/shard_map/ppermute | solution.py:261
  6.2 6.4 %collective-permute-start.2 = (f32[16,2048]{1,0:T(8,128)S(1)}, f32[16,2048]{1,0:T(8,128)S(1)}, u32[]{:S(2)}, u32[]{:S(2)}) collective-permute-start(f32[16,2048]{1,0:T(8,128)S(1)} %constant_dynamic-update-slice_fusion.refs_5_), channel_id=1, source_target_pairs={{0,4},{1,17},{2,6},{3,19},{4,0},{5,21},{6,2},{7,23},{8,12},{9,25},... | collective-permute-start | bytes 393224 | tf_op jit(solution)/shard_map/ppermute | solution.py:261
  6.7 5.0 %collective-permute-start.1 = (f32[16,2048]{1,0:T(8,128)S(1)}, f32[16,2048]{1,0:T(8,128)S(1)}, u32[]{:S(2)}, u32[]{:S(2)}) collective-permute-start(f32[16,2048]{1,0:T(8,128)S(1)} %constant_dynamic-update-slice_fusion.refs_5_), channel_id=1, source_target_pairs={{0,2},{1,25},{2,0},{3,27},{4,6},{5,29},{6,4},{7,31},{8,10},{9,1},{... | collective-permute-start | bytes 393224 | tf_op jit(solution)/shard_map/ppermute | solution.py:261
  8.3 24.2 %copy-start = (f32[8,2048]{1,0:T(8,128)S(1)}, f32[8,2048]{1,0:T(8,128)}, u32[]{:S(2)}) copy-start(f32[8,2048]{1,0:T(8,128)} %now.3) | copy-start | bytes 196612
  8.3 24.2 %copy-start.1 = (f32[8,2048]{1,0:T(8,128)S(1)}, f32[8,2048]{1,0:T(8,128)}, u32[]{:S(2)}) copy-start(f32[8,2048]{1,0:T(8,128)} %prev.3) | copy-start | bytes 196612
  8.3 34.6 %copy-start.2 = (f32[8,8]{1,0:T(8,128)S(1)}, f32[8,8]{1,0:T(8,128)}, u32[]{:S(2)}) copy-start(f32[8,8]{1,0:T(8,128)} %coupling.1) | copy-start | bytes 772
  11.6 2.1 %collective-permute-start.6 = (f32[16,2048]{1,0:T(8,128)S(1)}, f32[16,2048]{1,0:T(8,128)S(1)}, u32[]{:S(2)}, u32[]{:S(2)}) collective-permute-start(f32[16,2048]{1,0:T(8,128)S(1)} %collective-permute-done.3.refs_8_), channel_id=1, source_target_pairs={{0,1},{1,0},{2,3},{3,2},{4,5},{5,4},{6,7},{7,6},{8,9},{9,8},{10,11... | collective-permute-start | bytes 393224 | tf_op jit(solution)/shard_map/ppermute | solution.py:247
  12.6 1.3 %collective-permute-start.5 = (f32[16,2048]{1,0:T(8,128)S(1)}, f32[16,2048]{1,0:T(8,128)S(1)}, u32[]{:S(2)}, u32[]{:S(2)}) collective-permute-start(f32[16,2048]{1,0:T(8,128)S(1)} %collective-permute-done.2.refs_7_), channel_id=1, source_target_pairs={{0,1},{1,0},{2,3},{3,2},{4,5},{5,4},{6,7},{7,6},{8,9},{9,8},{10,11... | collective-permute-start | bytes 393224 | tf_op jit(solution)/shard_map/ppermute | solution.py:247
  12.7 1.5 %collective-permute-start.4 = (f32[16,2048]{1,0:T(8,128)S(1)}, f32[16,2048]{1,0:T(8,128)S(1)}, u32[]{:S(2)}, u32[]{:S(2)}) collective-permute-start(f32[16,2048]{1,0:T(8,128)S(1)} %collective-permute-done.1.refs_6_), channel_id=1, source_target_pairs={{0,1},{1,0},{2,3},{3,2},{4,5},{5,4},{6,7},{7,6},{8,9},{9,8},{10,11... | collective-permute-start | bytes 393224 | tf_op jit(solution)/shard_map/ppermute | solution.py:247
  17.8 7.9 %collective-permute-start.7 = (f32[4,8,2048]{2,1,0:T(8,128)S(1)}, f32[4,8,2048]{2,1,0:T(8,128)S(1)}, u32[]{:S(2)}, u32[]{:S(2)}) collective-permute-start(f32[4,8,2048]{2,1,0:T(8,128)S(1)} %get-tuple-element.13), channel_id=1, source_target_pairs={{0,1},{1,0},{2,3},{3,2},{4,5},{5,4},{6,7},{7,6},{8,9},{9,8},{10,11... | collective-permute-start | bytes 786440 | tf_op jit(solution)/shard_map/ppermute | solution.py:247
  18.3 10.0 %collective-permute-start.13 = (f32[8,2048]{1,0:T(8,128)S(1)}, f32[8,2048]{1,0:T(8,128)S(1)}, u32[]{:S(2)}, u32[]{:S(2)}) collective-permute-start(f32[8,2048]{1,0:T(8,128)S(1)} %get-tuple-element.20), channel_id=1, source_target_pairs={{0,8},{8,16},{16,24},{24,0},{1,9},{9,17},{17,25},{25,1},{2,10},{10... | collective-permute-start | bytes 196616 | tf_op jit(solution)/shard_map/ppermute | solution.py:250
  20.0 9.3 %collective-permute-start.12 = (f32[8,2048]{1,0:T(8,128)S(1)}, f32[8,2048]{1,0:T(8,128)S(1)}, u32[]{:S(2)}, u32[]{:S(2)}) collective-permute-start(f32[8,2048]{1,0:T(8,128)S(1)} %get-tuple-element.21), channel_id=1, source_target_pairs={{0,16},{8,24},{16,0},{24,8},{1,17},{9,25},{17,1},{25,9},{2,18},{10... | collective-permute-start | bytes 196616 | tf_op jit(solution)/shard_map/ppermute | solution.py:250
  24.2 5.1 %collective-permute-start.11 = (f32[8,2048]{1,0:T(8,128)S(1)}, f32[8,2048]{1,0:T(8,128)S(1)}, u32[]{:S(2)}, u32[]{:S(2)}) collective-permute-start(f32[8,2048]{1,0:T(8,128)S(1)} %get-tuple-element.22), channel_id=1, source_target_pairs={{0,24},{8,0},{16,8},{24,16},{1,25},{9,1},{17,9},{25,17},{2,26},{10... | collective-permute-start | bytes 196616 | tf_op jit(solution)/shard_map/ppermute | solution.py:250
  25.8 5.9 %collective-permute-start.10 = (f32[8,2048]{1,0:T(8,128)S(1)}, f32[8,2048]{1,0:T(8,128)S(1)}, u32[]{:S(2)}, u32[]{:S(2)}) collective-permute-start(f32[8,2048]{1,0:T(8,128)S(1)} %get-tuple-element.17), channel_id=1, source_target_pairs={{0,6},{1,7},{2,4},{3,5},{4,2},{5,3},{6,0},{7,1},{8,14},{9,15},{10,... | collective-permute-start | bytes 196616 | tf_op jit(solution)/shard_map/ppermute | solution.py:247
  27.5 4.6 %collective-permute-start.9 = (f32[8,2048]{1,0:T(8,128)S(1)}, f32[8,2048]{1,0:T(8,128)S(1)}, u32[]{:S(2)}, u32[]{:S(2)}) collective-permute-start(f32[8,2048]{1,0:T(8,128)S(1)} %get-tuple-element.18), channel_id=1, source_target_pairs={{0,4},{1,5},{2,6},{3,7},{4,0},{5,1},{6,2},{7,3},{8,12},{9,13},{10,... | collective-permute-start | bytes 196616 | tf_op jit(solution)/shard_map/ppermute | solution.py:247
  28.2 4.3 %collective-permute-start.8 = (f32[8,2048]{1,0:T(8,128)S(1)}, f32[8,2048]{1,0:T(8,128)S(1)}, u32[]{:S(2)}, u32[]{:S(2)}) collective-permute-start(f32[8,2048]{1,0:T(8,128)S(1)} %get-tuple-element.19), channel_id=1, source_target_pairs={{0,2},{1,3},{2,0},{3,1},{4,6},{5,7},{6,4},{7,5},{8,10},{9,11},{10,... | collective-permute-start | bytes 196616 | tf_op jit(solution)/shard_map/ppermute | solution.py:247

commit v13 on v12

--- a/solution.py
+++ b/solution.py
@@ -10,7 +10,7 @@
 
 VMEM = pltpu.VMEM
 SMEM = pltpu.SMEM
-GROUP = 128
+GROUP = 256
 WAIT_FLOPS = 20_000_000_000
 MIB = 1 << 20
 

time: 45.2 us -> 45.7 us (1.011)
  starting transfers between devices: 17.9 us -> 15.1 us
  Pallas kernels: 7.65 us -> 10.4 us
  blocking collectives: 10 us -> 10.5 us
    ppermute x3, starting transfers between devices: 7.45 us -> 4.58 us  [along_row(): return lax.ppermute(x, 'row', [(i, (i - s) % rows) for i in range(rows)])]
    pallas_call x1, Pallas kernels: 3.66 us -> 6.38 us  [local(): pl.pallas_call(functools.partial(products_kernel, rows, planes, group), o...]
    ppermute x8, waiting for transfers between devices: 3.77 us -> 3.15 us  [along_col(): return lax.ppermute(x, 'col', [(i, i ^ s) for i in range(cols)])]
    ppermute x3, waiting for transfers between devices: 0.04 us -> 0.66 us  [along_row(): return lax.ppermute(x, 'row', [(i, (i - s) % rows) for i in range(rows)])]
    all_to_all x1, blocking collectives: 10 us -> 10.5 us  [local(): sums = lax.all_to_all(sums, ('row', 'col'), 0, 0)]
  transfers between devices with their start and end apart: 14 -> 14, of which waited for: 7 -> 8; matrix products, arithmetic and copies ran while one was open for 2% -> 2% of each run, Pallas kernels for 3% -> 3%
where the time goes in v13:
time: 45.7 us; the launch traced here: 45.4 us
  starting transfers between devices  15.1 us (33%)
  blocking collectives  10.5 us (23%)
  Pallas kernels  10.4 us (23%)
  waiting for transfers between devices  7.1 us (16%)
  between operations  1.41 us (3%)
  local copies, waits for them, and re-layouts  0.9 us (2%)
    all_to_all x1, blocking collectives, local(): sums = lax.all_to_all(sums, ('row', 'col'), 0, 0)  10.5 us
    pallas_call x1, Pallas kernels, local(): pl.pallas_call(functools.partial(products_kernel, rows, planes, group), o...  6.38 us
    ppermute x8, starting transfers between devices, along_col(): return lax.ppermute(x, 'col', [(i, i ^ s) for i in range(cols)])  6.03 us
    ppermute x3, starting transfers between devices, along_row(): return lax.ppermute(x, 'row', [(i, (i - s) % rows) for i in range(rows)])  4.58 us
    ppermute x3, starting transfers between devices, apart(): return lax.ppermute(x, ('row', 'col'), pairs)  4.49 us
    ppermute x3, waiting for transfers between devices, apart(): return lax.ppermute(x, ('row', 'col'), pairs)  3.29 us
    ppermute x8, waiting for transfers between devices, along_col(): return lax.ppermute(x, 'col', [(i, i ^ s) for i in range(cols)])  3.15 us
    pallas_call x1, Pallas kernels, local(): pl.pallas_call(functools.partial(finish_kernel, float(piece * devices)),...  2.1 us
  transfers between devices with their start and end apart: 14, of which 8 were waited for; matrix products, arithmetic and copies ran while one was open for 2% of the time, Pallas kernels for 3%

profile of v13, /device:TPU:0, one launch (start us, length us, event | category | flops | bytes accessed | tf_op | source)
XLA Modules:
  0.0 45.4 jit_solution(14364529839633079608)
XLA Ops:
  0.6 0.5 %collective-permute-start = (f32[8,2048]{1,0:T(8,128)}, f32[8,2048]{1,0:T(8,128)S(1)}, u32[]{:S(2)}, u32[]{:S(2)}) collective-permute-start(f32[8,2048]{1,0:T(8,128)} %now.3), channel_id=1, source_target_pairs={{0,1},{1,0},{2,3},{3,2},{4,5},{5,4},{6,7},{7,6},{8,9},{9,8},{10,11... | collective-permute-start | bytes 196616 | tf_op jit(solution)/shard_map/ppermute | solution.py:247
  1.1 0.8 %constant_dynamic-update-slice_fusion.1 = f32[16,2048]{1,0:T(8,128)S(1)} fusion(f32[8,2048]{1,0:T(8,128)} %now.3), kind=kLoop, calls=%fused_computation.13 | loop fusion | bytes 131072
  2.0 0.3 collective-permute-done
  2.3 0.0 slice-start
  2.3 0.0 slice-start.1
  2.3 0.0 slice-start.2
  2.3 0.0 slice-start.3
  2.3 3.9 %collective-permute-start.3 = (f32[16,2048]{1,0:T(8,128)S(1)}, f32[16,2048]{1,0:T(8,128)S(1)}, u32[]{:S(2)}, u32[]{:S(2)}) collective-permute-start(f32[16,2048]{1,0:T(8,128)S(1)} %constant_dynamic-update-slice_fusion.refs_5_), channel_id=1, source_target_pairs={{0,6},{1,9},{2,4},{3,11},{4,2},{5,13},{6,0},{7,15},{8,14},{9,17},{... | collective-permute-start | bytes 393224 | tf_op jit(solution)/shard_map/ppermute | solution.py:261
  6.2 0.5 %collective-permute-start.2 = (f32[16,2048]{1,0:T(8,128)S(1)}, f32[16,2048]{1,0:T(8,128)S(1)}, u32[]{:S(2)}, u32[]{:S(2)}) collective-permute-start(f32[16,2048]{1,0:T(8,128)S(1)} %constant_dynamic-update-slice_fusion.refs_5_), channel_id=1, source_target_pairs={{0,4},{1,17},{2,6},{3,19},{4,0},{5,21},{6,2},{7,23},{8,12},{9,25},... | collective-permute-start | bytes 393224 | tf_op jit(solution)/shard_map/ppermute | solution.py:261
  6.7 0.1 collective-permute-start.1
  6.8 1.5 %fixed.1.refs_2_ = f32[16,16]{1,0:T(8,128)S(1)} custom-call(f32[8,2048]{1,0:T(8,128)} %now.3, f32[8,2048]{1,0:T(8,128)} %prev.3), custom_call_target="tpu_custom_call" | custom-call | flops 20000000000 | bytes 131072 | tf_op jit(solution)/shard_map/fixed/pallas_call | solution.py:269
  8.3 0.0 copy-start
  8.3 0.0 copy-start.1
  8.3 0.0 copy-start.2
  8.3 3.3 %collective-permute-done.1.refs_6_ = f32[16,2048]{1,0:T(8,128)S(1)} collective-permute-done((f32[16,2048]{1,0:T(8,128)S(1)}, f32[16,2048]{1,0:T(8,128)S(1)}, u32[]{:S(2)}, u32[]{:S(2)}) %collective-permute-start.1) | collective-permute-done | bytes 131104 | tf_op jit(solution)/shard_map/ppermute | solution.py:261
  11.6 0.0 collective-permute-done.3.refs_8_
  11.6 1.0 %collective-permute-start.6 = (f32[16,2048]{1,0:T(8,128)S(1)}, f32[16,2048]{1,0:T(8,128)S(1)}, u32[]{:S(2)}, u32[]{:S(2)}) collective-permute-start(f32[16,2048]{1,0:T(8,128)S(1)} %collective-permute-done.3.refs_8_), channel_id=1, source_target_pairs={{0,1},{1,0},{2,3},{3,2},{4,5},{5,4},{6,7},{7,6},{8,9},{9,8},{10,11... | collective-permute-start | bytes 393224 | tf_op jit(solution)/shard_map/ppermute | solution.py:247
  12.6 0.0 collective-permute-done.2.refs_7_
  12.6 0.1 collective-permute-start.5
  12.7 0.4 collective-permute-start.4
  13.8 0.0 collective-permute-done.6.refs_11_
  13.8 0.2 collective-permute-done.5.refs_10_
  13.9 0.2 collective-permute-done.4.refs_9_
  14.1 0.0 slice-done
  14.1 0.0 slice-done.1
  14.1 0.0 slice-done.2
  14.1 0.0 slice-done.3
  14.2 6.4 %products.1 = (f32[4,8,2048]{2,1,0:T(8,128)S(1)}, f32[4,8,2048]{2,1,0:T(8,128)S(1)}, f32[4,8,2048]{2,1,0:T(8,128)S(1)}) custom-call(s32[1,1]{1,0:T(1,128)S(6)} %copy.12.refs_0_, f32[256,128,128]{2,1,0:T(8,128)S(1)} %bitcast.22, s32[1,1,256]{2,1,0:T(1,128)} %refs_2_.1, s32[1,1,256]{2,1,0:T(1,128)} %refs_3_.1, f32[1,2048]{1,0:T(1,128)} %bitcast.23, ...), custom_call_target="tpu_custom_call" | custom-call | tf_op jit(solution)/shard_map/products/pallas_call | solution.py:293
  20.5 0.4 collective-permute-start.7
  20.9 1.7 %collective-permute-start.13 = (f32[8,2048]{1,0:T(8,128)S(1)}, f32[8,2048]{1,0:T(8,128)S(1)}, u32[]{:S(2)}, u32[]{:S(2)}) collective-permute-start(f32[8,2048]{1,0:T(8,128)S(1)} %get-tuple-element.20), channel_id=1, source_target_pairs={{0,8},{8,16},{16,24},{24,0},{1,9},{9,17},{17,25},{25,1},{2,10},{10... | collective-permute-start | bytes 196616 | tf_op jit(solution)/shard_map/ppermute | solution.py:250
  22.6 1.4 %collective-permute-start.12 = (f32[8,2048]{1,0:T(8,128)S(1)}, f32[8,2048]{1,0:T(8,128)S(1)}, u32[]{:S(2)}, u32[]{:S(2)}) collective-permute-start(f32[8,2048]{1,0:T(8,128)S(1)} %get-tuple-element.21), channel_id=1, source_target_pairs={{0,16},{8,24},{16,0},{24,8},{1,17},{9,25},{17,1},{25,9},{2,18},{10... | collective-permute-start | bytes 196616 | tf_op jit(solution)/shard_map/ppermute | solution.py:250
  24.1 1.5 %collective-permute-start.11 = (f32[8,2048]{1,0:T(8,128)S(1)}, f32[8,2048]{1,0:T(8,128)S(1)}, u32[]{:S(2)}, u32[]{:S(2)}) collective-permute-start(f32[8,2048]{1,0:T(8,128)S(1)} %get-tuple-element.22), channel_id=1, source_target_pairs={{0,24},{8,0},{16,8},{24,16},{1,25},{9,1},{17,9},{25,17},{2,26},{10... | collective-permute-start | bytes 196616 | tf_op jit(solution)/shard_map/ppermute | solution.py:250
  25.5 0.0 collective-permute-done.7
  25.6 2.1 %collective-permute-start.10 = (f32[8,2048]{1,0:T(8,128)S(1)}, f32[8,2048]{1,0:T(8,128)S(1)}, u32[]{:S(2)}, u32[]{:S(2)}) collective-permute-start(f32[8,2048]{1,0:T(8,128)S(1)} %get-tuple-element.17), channel_id=1, source_target_pairs={{0,6},{1,7},{2,4},{3,5},{4,2},{5,3},{6,0},{7,1},{8,14},{9,15},{10,... | collective-permute-start | bytes 196616 | tf_op jit(solution)/shard_map/ppermute | solution.py:247
  27.7 0.5 %collective-permute-start.9 = (f32[8,2048]{1,0:T(8,128)S(1)}, f32[8,2048]{1,0:T(8,128)S(1)}, u32[]{:S(2)}, u32[]{:S(2)}) collective-permute-start(f32[8,2048]{1,0:T(8,128)S(1)} %get-tuple-element.18), channel_id=1, source_target_pairs={{0,4},{1,5},{2,6},{3,7},{4,0},{5,1},{6,2},{7,3},{8,12},{9,13},{10,... | collective-permute-start | bytes 196616 | tf_op jit(solution)/shard_map/ppermute | solution.py:247
  28.1 0.0 collective-permute-done.13.refs_11_
  28.1 1.1 %collective-permute-start.8 = (f32[8,2048]{1,0:T(8,128)S(1)}, f32[8,2048]{1,0:T(8,128)S(1)}, u32[]{:S(2)}, u32[]{:S(2)}) collective-permute-start(f32[8,2048]{1,0:T(8,128)S(1)} %get-tuple-element.19), channel_id=1, source_target_pairs={{0,2},{1,3},{2,0},{3,1},{4,6},{5,7},{6,4},{7,5},{8,10},{9,11},{10,... | collective-permute-start | bytes 196616 | tf_op jit(solution)/shard_map/ppermute | solution.py:247
  29.2 0.7 %collective-permute-done.12.refs_10_ = f32[8,2048]{1,0:T(8,128)S(1)} collective-permute-done((f32[8,2048]{1,0:T(8,128)S(1)}, f32[8,2048]{1,0:T(8,128)S(1)}, u32[]{:S(2)}, u32[]{:S(2)}) %collective-permute-start.12) | collective-permute-done | bytes 65568 | tf_op jit(solution)/shard_map/ppermute | solution.py:250
  29.9 0.0 collective-permute-done.11.refs_9_
  29.9 1.0 %collective-permute-done.10.refs_8_ = f32[8,2048]{1,0:T(8,128)S(1)} collective-permute-done((f32[8,2048]{1,0:T(8,128)S(1)}, f32[8,2048]{1,0:T(8,128)S(1)}, u32[]{:S(2)}, u32[]{:S(2)}) %collective-permute-start.10) | collective-permute-done | bytes 65568 | tf_op jit(solution)/shard_map/ppermute | solution.py:247
  30.9 1.0 %collective-permute-done.9.refs_7_ = f32[8,2048]{1,0:T(8,128)S(1)} collective-permute-done((f32[8,2048]{1,0:T(8,128)S(1)}, f32[8,2048]{1,0:T(8,128)S(1)}, u32[]{:S(2)}, u32[]{:S(2)}) %collective-permute-start.9) | collective-permute-done | bytes 65568 | tf_op jit(solution)/shard_map/ppermute | solution.py:247
  31.9 0.5 %collective-permute-done.8.refs_6_ = f32[8,2048]{1,0:T(8,128)S(1)} collective-permute-done((f32[8,2048]{1,0:T(8,128)S(1)}, f32[8,2048]{1,0:T(8,128)S(1)}, u32[]{:S(2)}, u32[]{:S(2)}) %collective-permute-start.8) | collective-permute-done | bytes 65568 | tf_op jit(solution)/shard_map/ppermute | solution.py:247
  32.4 0.0 copy-done
  32.4 0.0 copy-done.1
  32.4 0.4 image.1
  32.8 10.5 %all_to_all.5.sums_in = f32[32,4,128]{2,1,0:T(4,128)S(1)} all-to-all(f32[32,4,128]{2,1,0:T(4,128)S(1)} %get-tuple-element.15), channel_id=1, replica_groups=mesh['row'=4,'col'=8] {'row','col'}, dimensions={0} | all-to-all | bytes 131072 | tf_op jit(solution)/shard_map/all_to_all | solution.py:347
  43.3 0.0 copy-done.2
  43.3 2.1 %finish.1 = (f32[8,2048]{1,0:T(8,128)}, f32[8,8]{1,0:T(8,128)}, f32[8,8]{1,0:T(8,128)}) custom-call(f32[32,4,128]{2,1,0:T(4,128)S(1)} %all_to_all.5.sums_in, f32[8,2048]{1,0:T(8,128)S(1)} %get-tuple-element.16.image, f32[8,2048]{1,0:T(8,128)S(1)} %copy-done, f32[8,2048]{1,0:T(8,128)S(1)} %copy-done.1, f32[8,8]{1,0:T(8,128)S(1)} %copy-done.2), custom_call_target="tpu_custom_call" | custom-call | tf_op jit(solution)/shard_map/finish/pallas_call | solution.py:348
  (4 shorter events, 0.1 us)
Async XLA Ops:
  0.6 1.6 %collective-permute-start = (f32[8,2048]{1,0:T(8,128)}, f32[8,2048]{1,0:T(8,128)S(1)}, u32[]{:S(2)}, u32[]{:S(2)}) collective-permute-start(f32[8,2048]{1,0:T(8,128)} %now.3), channel_id=1, source_target_pairs={{0,1},{1,0},{2,3},{3,2},{4,5},{5,4},{6,7},{7,6},{8,9},{9,8},{10,11... | collective-permute-start | bytes 196616 | tf_op jit(solution)/shard_map/ppermute | solution.py:247
  2.3 11.9 %slice-start = ((s8[16777216]{0:T(1024)(128)(4,1)}), s8[4194304]{0:T(1024)(128)(4,1)S(1)}, s32[]{:S(2)}) async-start(s8[16777216]{0:T(1024)(128)(4,1)} %bitcast.20), calls=%async_computation.1 | async-start | bytes 8388608
  2.3 11.9 %slice-start.1 = ((s8[16777216]{0:T(1024)(128)(4,1)}), s8[4194304]{0:T(1024)(128)(4,1)S(1)}, s32[]{:S(2)}) async-start(s8[16777216]{0:T(1024)(128)(4,1)} %bitcast.20), calls=%async_computation.2 | async-start | bytes 8388608
  2.3 11.9 %slice-start.2 = ((s8[16777216]{0:T(1024)(128)(4,1)}), s8[4194304]{0:T(1024)(128)(4,1)S(1)}, s32[]{:S(2)}) async-start(s8[16777216]{0:T(1024)(128)(4,1)} %bitcast.20), calls=%async_computation.3 | async-start | bytes 8388608
  2.3 11.9 %slice-start.3 = ((s8[16777216]{0:T(1024)(128)(4,1)}), s8[4194304]{0:T(1024)(128)(4,1)S(1)}, s32[]{:S(2)}) async-start(s8[16777216]{0:T(1024)(128)(4,1)} %bitcast.20), calls=%async_computation.4 | async-start | bytes 8388608
  2.3 9.3 %collective-permute-start.3 = (f32[16,2048]{1,0:T(8,128)S(1)}, f32[16,2048]{1,0:T(8,128)S(1)}, u32[]{:S(2)}, u32[]{:S(2)}) collective-permute-start(f32[16,2048]{1,0:T(8,128)S(1)} %constant_dynamic-update-slice_fusion.refs_5_), channel_id=1, source_target_pairs={{0,6},{1,9},{2,4},{3,11},{4,2},{5,13},{6,0},{7,15},{8,14},{9,17},{... | collective-permute-start | bytes 393224 | tf_op jit(solution)/shard_map/ppermute | solution.py:261
  6.2 6.4 %collective-permute-start.2 = (f32[16,2048]{1,0:T(8,128)S(1)}, f32[16,2048]{1,0:T(8,128)S(1)}, u32[]{:S(2)}, u32[]{:S(2)}) collective-permute-start(f32[16,2048]{1,0:T(8,128)S(1)} %constant_dynamic-update-slice_fusion.refs_5_), channel_id=1, source_target_pairs={{0,4},{1,17},{2,6},{3,19},{4,0},{5,21},{6,2},{7,23},{8,12},{9,25},... | collective-permute-start | bytes 393224 | tf_op jit(solution)/shard_map/ppermute | solution.py:261
  6.7 5.0 %collective-permute-start.1 = (f32[16,2048]{1,0:T(8,128)S(1)}, f32[16,2048]{1,0:T(8,128)S(1)}, u32[]{:S(2)}, u32[]{:S(2)}) collective-permute-start(f32[16,2048]{1,0:T(8,128)S(1)} %constant_dynamic-update-slice_fusion.refs_5_), channel_id=1, source_target_pairs={{0,2},{1,25},{2,0},{3,27},{4,6},{5,29},{6,4},{7,31},{8,10},{9,1},{... | collective-permute-start | bytes 393224 | tf_op jit(solution)/shard_map/ppermute | solution.py:261
  8.3 24.1 %copy-start = (f32[8,2048]{1,0:T(8,128)S(1)}, f32[8,2048]{1,0:T(8,128)}, u32[]{:S(2)}) copy-start(f32[8,2048]{1,0:T(8,128)} %now.3) | copy-start | bytes 196612
  8.3 24.1 %copy-start.1 = (f32[8,2048]{1,0:T(8,128)S(1)}, f32[8,2048]{1,0:T(8,128)}, u32[]{:S(2)}) copy-start(f32[8,2048]{1,0:T(8,128)} %prev.3) | copy-start | bytes 196612
  8.3 35.0 %copy-start.2 = (f32[8,8]{1,0:T(8,128)S(1)}, f32[8,8]{1,0:T(8,128)}, u32[]{:S(2)}) copy-start(f32[8,8]{1,0:T(8,128)} %coupling.1) | copy-start | bytes 772
  11.6 2.1 %collective-permute-start.6 = (f32[16,2048]{1,0:T(8,128)S(1)}, f32[16,2048]{1,0:T(8,128)S(1)}, u32[]{:S(2)}, u32[]{:S(2)}) collective-permute-start(f32[16,2048]{1,0:T(8,128)S(1)} %collective-permute-done.3.refs_8_), channel_id=1, source_target_pairs={{0,1},{1,0},{2,3},{3,2},{4,5},{5,4},{6,7},{7,6},{8,9},{9,8},{10,11... | collective-permute-start | bytes 393224 | tf_op jit(solution)/shard_map/ppermute | solution.py:247
  12.6 1.3 %collective-permute-start.5 = (f32[16,2048]{1,0:T(8,128)S(1)}, f32[16,2048]{1,0:T(8,128)S(1)}, u32[]{:S(2)}, u32[]{:S(2)}) collective-permute-start(f32[16,2048]{1,0:T(8,128)S(1)} %collective-permute-done.2.refs_7_), channel_id=1, source_target_pairs={{0,1},{1,0},{2,3},{3,2},{4,5},{5,4},{6,7},{7,6},{8,9},{9,8},{10,11... | collective-permute-start | bytes 393224 | tf_op jit(solution)/shard_map/ppermute | solution.py:247
  12.7 1.5 %collective-permute-start.4 = (f32[16,2048]{1,0:T(8,128)S(1)}, f32[16,2048]{1,0:T(8,128)S(1)}, u32[]{:S(2)}, u32[]{:S(2)}) collective-permute-start(f32[16,2048]{1,0:T(8,128)S(1)} %collective-permute-done.1.refs_6_), channel_id=1, source_target_pairs={{0,1},{1,0},{2,3},{3,2},{4,5},{5,4},{6,7},{7,6},{8,9},{9,8},{10,11... | collective-permute-start | bytes 393224 | tf_op jit(solution)/shard_map/ppermute | solution.py:247
  20.5 5.0 %collective-permute-start.7 = (f32[4,8,2048]{2,1,0:T(8,128)S(1)}, f32[4,8,2048]{2,1,0:T(8,128)S(1)}, u32[]{:S(2)}, u32[]{:S(2)}) collective-permute-start(f32[4,8,2048]{2,1,0:T(8,128)S(1)} %get-tuple-element.13), channel_id=1, source_target_pairs={{0,1},{1,0},{2,3},{3,2},{4,5},{5,4},{6,7},{7,6},{8,9},{9,8},{10,11... | collective-permute-start | bytes 786440 | tf_op jit(solution)/shard_map/ppermute | solution.py:247
  20.9 7.2 %collective-permute-start.13 = (f32[8,2048]{1,0:T(8,128)S(1)}, f32[8,2048]{1,0:T(8,128)S(1)}, u32[]{:S(2)}, u32[]{:S(2)}) collective-permute-start(f32[8,2048]{1,0:T(8,128)S(1)} %get-tuple-element.20), channel_id=1, source_target_pairs={{0,8},{8,16},{16,24},{24,0},{1,9},{9,17},{17,25},{25,1},{2,10},{10... | collective-permute-start | bytes 196616 | tf_op jit(solution)/shard_map/ppermute | solution.py:250
  22.6 7.3 %collective-permute-start.12 = (f32[8,2048]{1,0:T(8,128)S(1)}, f32[8,2048]{1,0:T(8,128)S(1)}, u32[]{:S(2)}, u32[]{:S(2)}) collective-permute-start(f32[8,2048]{1,0:T(8,128)S(1)} %get-tuple-element.21), channel_id=1, source_target_pairs={{0,16},{8,24},{16,0},{24,8},{1,17},{9,25},{17,1},{25,9},{2,18},{10... | collective-permute-start | bytes 196616 | tf_op jit(solution)/shard_map/ppermute | solution.py:250
  24.1 5.8 %collective-permute-start.11 = (f32[8,2048]{1,0:T(8,128)S(1)}, f32[8,2048]{1,0:T(8,128)S(1)}, u32[]{:S(2)}, u32[]{:S(2)}) collective-permute-start(f32[8,2048]{1,0:T(8,128)S(1)} %get-tuple-element.22), channel_id=1, source_target_pairs={{0,24},{8,0},{16,8},{24,16},{1,25},{9,1},{17,9},{25,17},{2,26},{10... | collective-permute-start | bytes 196616 | tf_op jit(solution)/shard_map/ppermute | solution.py:250
  25.6 5.3 %collective-permute-start.10 = (f32[8,2048]{1,0:T(8,128)S(1)}, f32[8,2048]{1,0:T(8,128)S(1)}, u32[]{:S(2)}, u32[]{:S(2)}) collective-permute-start(f32[8,2048]{1,0:T(8,128)S(1)} %get-tuple-element.17), channel_id=1, source_target_pairs={{0,6},{1,7},{2,4},{3,5},{4,2},{5,3},{6,0},{7,1},{8,14},{9,15},{10,... | collective-permute-start | bytes 196616 | tf_op jit(solution)/shard_map/ppermute | solution.py:247
  27.7 4.3 %collective-permute-start.9 = (f32[8,2048]{1,0:T(8,128)S(1)}, f32[8,2048]{1,0:T(8,128)S(1)}, u32[]{:S(2)}, u32[]{:S(2)}) collective-permute-start(f32[8,2048]{1,0:T(8,128)S(1)} %get-tuple-element.18), channel_id=1, source_target_pairs={{0,4},{1,5},{2,6},{3,7},{4,0},{5,1},{6,2},{7,3},{8,12},{9,13},{10,... | collective-permute-start | bytes 196616 | tf_op jit(solution)/shard_map/ppermute | solution.py:247
  28.1 4.3 %collective-permute-start.8 = (f32[8,2048]{1,0:T(8,128)S(1)}, f32[8,2048]{1,0:T(8,128)S(1)}, u32[]{:S(2)}, u32[]{:S(2)}) collective-permute-start(f32[8,2048]{1,0:T(8,128)S(1)} %get-tuple-element.19), channel_id=1, source_target_pairs={{0,2},{1,3},{2,0},{3,1},{4,6},{5,7},{6,4},{7,5},{8,10},{9,11},{10,... | collective-permute-start | bytes 196616 | tf_op jit(solution)/shard_map/ppermute | solution.py:247

commit v14 on v12

--- a/solution.py
+++ b/solution.py
@@ -329,7 +329,7 @@
     from_core = along_col(send, 1)
     summed = [keep[s] + from_core[s] for s in range(1, planes)]
     back_planes = [along_col(summed[s - 1], 2 * s) for s in range(1, planes)]
-    terms = [keep[0], from_core[0], col_parts[0], *back_planes, *back_rows]
+    terms = [keep[0], from_core[0], col_parts[0], *back_planes[::-1], *back_rows]
 
     devices = rows * cols
     image, sums = pl.pallas_call(

time: 45.2 us -> 46.2 us (1.022)
  waiting for transfers between devices: 7.1 us -> 7.81 us
    ppermute x8, waiting for transfers between devices: 3.77 us -> 4.51 us  [along_col(): return lax.ppermute(x, 'col', [(i, i ^ s) for i in range(cols)])]
where the time goes in v14:
time: 46.2 us; the launch traced here: 45.9 us
  starting transfers between devices  17.9 us (39%)
  blocking collectives  10.2 us (22%)
  waiting for transfers between devices  7.81 us (17%)
  Pallas kernels  7.69 us (17%)
  between operations  1.41 us (3%)
  local copies, waits for them, and re-layouts  0.9 us (2%)
    all_to_all x1, blocking collectives, local(): sums = lax.all_to_all(sums, ('row', 'col'), 0, 0)  10.2 us
    ppermute x3, starting transfers between devices, along_row(): return lax.ppermute(x, 'row', [(i, (i - s) % rows) for i in range(rows)])  7.45 us
    ppermute x8, starting transfers between devices, along_col(): return lax.ppermute(x, 'col', [(i, i ^ s) for i in range(cols)])  5.93 us
    ppermute x8, waiting for transfers between devices, along_col(): return lax.ppermute(x, 'col', [(i, i ^ s) for i in range(cols)])  4.51 us
    ppermute x3, starting transfers between devices, apart(): return lax.ppermute(x, ('row', 'col'), pairs)  4.49 us
    pallas_call x1, Pallas kernels, local(): pl.pallas_call(functools.partial(products_kernel, rows, planes, group), o...  3.71 us
    ppermute x3, waiting for transfers between devices, apart(): return lax.ppermute(x, ('row', 'col'), pairs)  3.29 us
    pallas_call x1, Pallas kernels, local(): pl.pallas_call(functools.partial(finish_kernel, float(piece * devices)),...  2.1 us
  transfers between devices with their start and end apart: 14, of which 7 were waited for; matrix products, arithmetic and copies ran while one was open for 2% of the time, Pallas kernels for 3%

profile of v14, /device:TPU:0, one launch (start us, length us, event | category | flops | bytes accessed | tf_op | source)
XLA Modules:
  0.0 45.9 jit_solution(2981639031613676685)
XLA Ops:
  0.6 0.5 %collective-permute-start = (f32[8,2048]{1,0:T(8,128)}, f32[8,2048]{1,0:T(8,128)S(1)}, u32[]{:S(2)}, u32[]{:S(2)}) collective-permute-start(f32[8,2048]{1,0:T(8,128)} %now.3), channel_id=1, source_target_pairs={{0,1},{1,0},{2,3},{3,2},{4,5},{5,4},{6,7},{7,6},{8,9},{9,8},{10,11... | collective-permute-start | bytes 196616 | tf_op jit(solution)/shard_map/ppermute | solution.py:247
  1.1 0.8 %constant_dynamic-update-slice_fusion.1 = f32[16,2048]{1,0:T(8,128)S(1)} fusion(f32[8,2048]{1,0:T(8,128)} %now.3), kind=kLoop, calls=%fused_computation.13 | loop fusion | bytes 131072
  2.0 0.3 collective-permute-done
  2.3 0.0 slice-start
  2.3 0.0 slice-start.1
  2.3 0.0 slice-start.2
  2.3 0.0 slice-start.3
  2.3 3.9 %collective-permute-start.3 = (f32[16,2048]{1,0:T(8,128)S(1)}, f32[16,2048]{1,0:T(8,128)S(1)}, u32[]{:S(2)}, u32[]{:S(2)}) collective-permute-start(f32[16,2048]{1,0:T(8,128)S(1)} %constant_dynamic-update-slice_fusion.refs_5_), channel_id=1, source_target_pairs={{0,6},{1,9},{2,4},{3,11},{4,2},{5,13},{6,0},{7,15},{8,14},{9,17},{... | collective-permute-start | bytes 393224 | tf_op jit(solution)/shard_map/ppermute | solution.py:261
  6.2 0.5 %collective-permute-start.2 = (f32[16,2048]{1,0:T(8,128)S(1)}, f32[16,2048]{1,0:T(8,128)S(1)}, u32[]{:S(2)}, u32[]{:S(2)}) collective-permute-start(f32[16,2048]{1,0:T(8,128)S(1)} %constant_dynamic-update-slice_fusion.refs_5_), channel_id=1, source_target_pairs={{0,4},{1,17},{2,6},{3,19},{4,0},{5,21},{6,2},{7,23},{8,12},{9,25},... | collective-permute-start | bytes 393224 | tf_op jit(solution)/shard_map/ppermute | solution.py:261
  6.7 0.1 collective-permute-start.1
  6.8 1.5 %fixed.1.refs_2_ = f32[16,16]{1,0:T(8,128)S(1)} custom-call(f32[8,2048]{1,0:T(8,128)} %now.3, f32[8,2048]{1,0:T(8,128)} %prev.3), custom_call_target="tpu_custom_call" | custom-call | flops 20000000000 | bytes 131072 | tf_op jit(solution)/shard_map/fixed/pallas_call | solution.py:269
  8.3 0.0 copy-start
  8.3 0.0 copy-start.1
  8.3 0.0 copy-start.2
  8.3 3.3 %collective-permute-done.1.refs_6_ = f32[16,2048]{1,0:T(8,128)S(1)} collective-permute-done((f32[16,2048]{1,0:T(8,128)S(1)}, f32[16,2048]{1,0:T(8,128)S(1)}, u32[]{:S(2)}, u32[]{:S(2)}) %collective-permute-start.1) | collective-permute-done | bytes 131104 | tf_op jit(solution)/shard_map/ppermute | solution.py:261
  11.6 0.0 collective-permute-done.3.refs_8_
  11.6 1.0 %collective-permute-start.6 = (f32[16,2048]{1,0:T(8,128)S(1)}, f32[16,2048]{1,0:T(8,128)S(1)}, u32[]{:S(2)}, u32[]{:S(2)}) collective-permute-start(f32[16,2048]{1,0:T(8,128)S(1)} %collective-permute-done.3.refs_8_), channel_id=1, source_target_pairs={{0,1},{1,0},{2,3},{3,2},{4,5},{5,4},{6,7},{7,6},{8,9},{9,8},{10,11... | collective-permute-start | bytes 393224 | tf_op jit(solution)/shard_map/ppermute | solution.py:247
  12.6 0.0 collective-permute-done.2.refs_7_
  12.6 0.1 collective-permute-start.5
  12.7 0.4 collective-permute-start.4
  13.8 0.0 collective-permute-done.6.refs_11_
  13.8 0.2 collective-permute-done.5.refs_10_
  13.9 0.2 collective-permute-done.4.refs_9_
  14.1 0.0 slice-done
  14.1 0.0 slice-done.1
  14.1 0.0 slice-done.2
  14.1 0.0 slice-done.3
  14.2 3.7 %products.1 = (f32[4,8,2048]{2,1,0:T(8,128)S(1)}, f32[4,8,2048]{2,1,0:T(8,128)S(1)}, f32[4,8,2048]{2,1,0:T(8,128)S(1)}) custom-call(s32[1,1]{1,0:T(1,128)S(6)} %copy.12.refs_0_, f32[256,128,128]{2,1,0:T(8,128)S(1)} %bitcast.22, s32[1,1,256]{2,1,0:T(1,128)} %refs_2_.1, s32[1,1,256]{2,1,0:T(1,128)} %refs_3_.1, f32[1,2048]{1,0:T(1,128)} %bitcast.23, ...), custom_call_target="tpu_custom_call" | custom-call | tf_op jit(solution)/shard_map/products/pallas_call | solution.py:293
  17.9 0.4 collective-permute-start.7
  18.3 1.7 %collective-permute-start.13 = (f32[8,2048]{1,0:T(8,128)S(1)}, f32[8,2048]{1,0:T(8,128)S(1)}, u32[]{:S(2)}, u32[]{:S(2)}) collective-permute-start(f32[8,2048]{1,0:T(8,128)S(1)} %get-tuple-element.20), channel_id=1, source_target_pairs={{0,8},{8,16},{16,24},{24,0},{1,9},{9,17},{17,25},{25,1},{2,10},{10... | collective-permute-start | bytes 196616 | tf_op jit(solution)/shard_map/ppermute | solution.py:250
  20.0 4.3 %collective-permute-start.12 = (f32[8,2048]{1,0:T(8,128)S(1)}, f32[8,2048]{1,0:T(8,128)S(1)}, u32[]{:S(2)}, u32[]{:S(2)}) collective-permute-start(f32[8,2048]{1,0:T(8,128)S(1)} %get-tuple-element.21), channel_id=1, source_target_pairs={{0,16},{8,24},{16,0},{24,8},{1,17},{9,25},{17,1},{25,9},{2,18},{10... | collective-permute-start | bytes 196616 | tf_op jit(solution)/shard_map/ppermute | solution.py:250
  24.2 1.5 %collective-permute-start.11 = (f32[8,2048]{1,0:T(8,128)S(1)}, f32[8,2048]{1,0:T(8,128)S(1)}, u32[]{:S(2)}, u32[]{:S(2)}) collective-permute-start(f32[8,2048]{1,0:T(8,128)S(1)} %get-tuple-element.22), channel_id=1, source_target_pairs={{0,24},{8,0},{16,8},{24,16},{1,25},{9,1},{17,9},{25,17},{2,26},{10... | collective-permute-start | bytes 196616 | tf_op jit(solution)/shard_map/ppermute | solution.py:250
  25.7 0.0 collective-permute-done.7
  25.8 1.0 %collective-permute-start.10 = (f32[8,2048]{1,0:T(8,128)S(1)}, f32[8,2048]{1,0:T(8,128)S(1)}, u32[]{:S(2)}, u32[]{:S(2)}) collective-permute-start(f32[8,2048]{1,0:T(8,128)S(1)} %get-tuple-element.17), channel_id=1, source_target_pairs={{0,2},{1,3},{2,0},{3,1},{4,6},{5,7},{6,4},{7,5},{8,10},{9,11},{10,... | collective-permute-start | bytes 196616 | tf_op jit(solution)/shard_map/ppermute | solution.py:247
  26.8 1.3 %collective-permute-start.9 = (f32[8,2048]{1,0:T(8,128)S(1)}, f32[8,2048]{1,0:T(8,128)S(1)}, u32[]{:S(2)}, u32[]{:S(2)}) collective-permute-start(f32[8,2048]{1,0:T(8,128)S(1)} %get-tuple-element.18), channel_id=1, source_target_pairs={{0,4},{1,5},{2,6},{3,7},{4,0},{5,1},{6,2},{7,3},{8,12},{9,13},{10,... | collective-permute-start | bytes 196616 | tf_op jit(solution)/shard_map/ppermute | solution.py:247
  28.0 0.0 collective-permute-done.13.refs_11_
  28.0 1.3 %collective-permute-start.8 = (f32[8,2048]{1,0:T(8,128)S(1)}, f32[8,2048]{1,0:T(8,128)S(1)}, u32[]{:S(2)}, u32[]{:S(2)}) collective-permute-start(f32[8,2048]{1,0:T(8,128)S(1)} %get-tuple-element.19), channel_id=1, source_target_pairs={{0,6},{1,7},{2,4},{3,5},{4,2},{5,3},{6,0},{7,1},{8,14},{9,15},{10,... | collective-permute-start | bytes 196616 | tf_op jit(solution)/shard_map/ppermute | solution.py:247
  29.3 0.0 collective-permute-done.12.refs_10_
  29.3 0.0 collective-permute-done.11.refs_9_
  29.3 1.1 %collective-permute-done.10.refs_8_ = f32[8,2048]{1,0:T(8,128)S(1)} collective-permute-done((f32[8,2048]{1,0:T(8,128)S(1)}, f32[8,2048]{1,0:T(8,128)S(1)}, u32[]{:S(2)}, u32[]{:S(2)}) %collective-permute-start.10) | collective-permute-done | bytes 65568 | tf_op jit(solution)/shard_map/ppermute | solution.py:247
  30.5 1.2 %collective-permute-done.9.refs_7_ = f32[8,2048]{1,0:T(8,128)S(1)} collective-permute-done((f32[8,2048]{1,0:T(8,128)S(1)}, f32[8,2048]{1,0:T(8,128)S(1)}, u32[]{:S(2)}, u32[]{:S(2)}) %collective-permute-start.9) | collective-permute-done | bytes 65568 | tf_op jit(solution)/shard_map/ppermute | solution.py:247
  31.7 1.5 %collective-permute-done.8.refs_6_ = f32[8,2048]{1,0:T(8,128)S(1)} collective-permute-done((f32[8,2048]{1,0:T(8,128)S(1)}, f32[8,2048]{1,0:T(8,128)S(1)}, u32[]{:S(2)}, u32[]{:S(2)}) %collective-permute-start.8) | collective-permute-done | bytes 65568 | tf_op jit(solution)/shard_map/ppermute | solution.py:247
  33.2 0.0 copy-done
  33.2 0.0 copy-done.1
  33.2 0.4 image.1
  33.6 10.2 %all_to_all.5.sums_in = f32[32,4,128]{2,1,0:T(4,128)S(1)} all-to-all(f32[32,4,128]{2,1,0:T(4,128)S(1)} %get-tuple-element.15), channel_id=1, replica_groups=mesh['row'=4,'col'=8] {'row','col'}, dimensions={0} | all-to-all | bytes 131072 | tf_op jit(solution)/shard_map/all_to_all | solution.py:347
  43.8 0.0 copy-done.2
  43.8 2.1 %finish.1 = (f32[8,2048]{1,0:T(8,128)}, f32[8,8]{1,0:T(8,128)}, f32[8,8]{1,0:T(8,128)}) custom-call(f32[32,4,128]{2,1,0:T(4,128)S(1)} %all_to_all.5.sums_in, f32[8,2048]{1,0:T(8,128)S(1)} %get-tuple-element.16.image, f32[8,2048]{1,0:T(8,128)S(1)} %copy-done, f32[8,2048]{1,0:T(8,128)S(1)} %copy-done.1, f32[8,8]{1,0:T(8,128)S(1)} %copy-done.2), custom_call_target="tpu_custom_call" | custom-call | tf_op jit(solution)/shard_map/finish/pallas_call | solution.py:348
  (4 shorter events, 0.1 us)
Async XLA Ops:
  0.6 1.6 %collective-permute-start = (f32[8,2048]{1,0:T(8,128)}, f32[8,2048]{1,0:T(8,128)S(1)}, u32[]{:S(2)}, u32[]{:S(2)}) collective-permute-start(f32[8,2048]{1,0:T(8,128)} %now.3), channel_id=1, source_target_pairs={{0,1},{1,0},{2,3},{3,2},{4,5},{5,4},{6,7},{7,6},{8,9},{9,8},{10,11... | collective-permute-start | bytes 196616 | tf_op jit(solution)/shard_map/ppermute | solution.py:247
  2.3 11.9 %slice-start = ((s8[16777216]{0:T(1024)(128)(4,1)}), s8[4194304]{0:T(1024)(128)(4,1)S(1)}, s32[]{:S(2)}) async-start(s8[16777216]{0:T(1024)(128)(4,1)} %bitcast.20), calls=%async_computation.1 | async-start | bytes 8388608
  2.3 11.9 %slice-start.1 = ((s8[16777216]{0:T(1024)(128)(4,1)}), s8[4194304]{0:T(1024)(128)(4,1)S(1)}, s32[]{:S(2)}) async-start(s8[16777216]{0:T(1024)(128)(4,1)} %bitcast.20), calls=%async_computation.2 | async-start | bytes 8388608
  2.3 11.9 %slice-start.2 = ((s8[16777216]{0:T(1024)(128)(4,1)}), s8[4194304]{0:T(1024)(128)(4,1)S(1)}, s32[]{:S(2)}) async-start(s8[16777216]{0:T(1024)(128)(4,1)} %bitcast.20), calls=%async_computation.3 | async-start | bytes 8388608
  2.3 11.9 %slice-start.3 = ((s8[16777216]{0:T(1024)(128)(4,1)}), s8[4194304]{0:T(1024)(128)(4,1)S(1)}, s32[]{:S(2)}) async-start(s8[16777216]{0:T(1024)(128)(4,1)} %bitcast.20), calls=%async_computation.4 | async-start | bytes 8388608
  2.3 9.3 %collective-permute-start.3 = (f32[16,2048]{1,0:T(8,128)S(1)}, f32[16,2048]{1,0:T(8,128)S(1)}, u32[]{:S(2)}, u32[]{:S(2)}) collective-permute-start(f32[16,2048]{1,0:T(8,128)S(1)} %constant_dynamic-update-slice_fusion.refs_5_), channel_id=1, source_target_pairs={{0,6},{1,9},{2,4},{3,11},{4,2},{5,13},{6,0},{7,15},{8,14},{9,17},{... | collective-permute-start | bytes 393224 | tf_op jit(solution)/shard_map/ppermute | solution.py:261
  6.2 6.4 %collective-permute-start.2 = (f32[16,2048]{1,0:T(8,128)S(1)}, f32[16,2048]{1,0:T(8,128)S(1)}, u32[]{:S(2)}, u32[]{:S(2)}) collective-permute-start(f32[16,2048]{1,0:T(8,128)S(1)} %constant_dynamic-update-slice_fusion.refs_5_), channel_id=1, source_target_pairs={{0,4},{1,17},{2,6},{3,19},{4,0},{5,21},{6,2},{7,23},{8,12},{9,25},... | collective-permute-start | bytes 393224 | tf_op jit(solution)/shard_map/ppermute | solution.py:261
  6.7 5.0 %collective-permute-start.1 = (f32[16,2048]{1,0:T(8,128)S(1)}, f32[16,2048]{1,0:T(8,128)S(1)}, u32[]{:S(2)}, u32[]{:S(2)}) collective-permute-start(f32[16,2048]{1,0:T(8,128)S(1)} %constant_dynamic-update-slice_fusion.refs_5_), channel_id=1, source_target_pairs={{0,2},{1,25},{2,0},{3,27},{4,6},{5,29},{6,4},{7,31},{8,10},{9,1},{... | collective-permute-start | bytes 393224 | tf_op jit(solution)/shard_map/ppermute | solution.py:261
  8.3 24.9 %copy-start = (f32[8,2048]{1,0:T(8,128)S(1)}, f32[8,2048]{1,0:T(8,128)}, u32[]{:S(2)}) copy-start(f32[8,2048]{1,0:T(8,128)} %now.3) | copy-start | bytes 196612
  8.3 24.9 %copy-start.1 = (f32[8,2048]{1,0:T(8,128)S(1)}, f32[8,2048]{1,0:T(8,128)}, u32[]{:S(2)}) copy-start(f32[8,2048]{1,0:T(8,128)} %prev.3) | copy-start | bytes 196612
  8.3 35.5 %copy-start.2 = (f32[8,8]{1,0:T(8,128)S(1)}, f32[8,8]{1,0:T(8,128)}, u32[]{:S(2)}) copy-start(f32[8,8]{1,0:T(8,128)} %coupling.1) | copy-start | bytes 772
  11.6 2.1 %collective-permute-start.6 = (f32[16,2048]{1,0:T(8,128)S(1)}, f32[16,2048]{1,0:T(8,128)S(1)}, u32[]{:S(2)}, u32[]{:S(2)}) collective-permute-start(f32[16,2048]{1,0:T(8,128)S(1)} %collective-permute-done.3.refs_8_), channel_id=1, source_target_pairs={{0,1},{1,0},{2,3},{3,2},{4,5},{5,4},{6,7},{7,6},{8,9},{9,8},{10,11... | collective-permute-start | bytes 393224 | tf_op jit(solution)/shard_map/ppermute | solution.py:247
  12.6 1.3 %collective-permute-start.5 = (f32[16,2048]{1,0:T(8,128)S(1)}, f32[16,2048]{1,0:T(8,128)S(1)}, u32[]{:S(2)}, u32[]{:S(2)}) collective-permute-start(f32[16,2048]{1,0:T(8,128)S(1)} %collective-permute-done.2.refs_7_), channel_id=1, source_target_pairs={{0,1},{1,0},{2,3},{3,2},{4,5},{5,4},{6,7},{7,6},{8,9},{9,8},{10,11... | collective-permute-start | bytes 393224 | tf_op jit(solution)/shard_map/ppermute | solution.py:247
  12.7 1.5 %collective-permute-start.4 = (f32[16,2048]{1,0:T(8,128)S(1)}, f32[16,2048]{1,0:T(8,128)S(1)}, u32[]{:S(2)}, u32[]{:S(2)}) collective-permute-start(f32[16,2048]{1,0:T(8,128)S(1)} %collective-permute-done.1.refs_6_), channel_id=1, source_target_pairs={{0,1},{1,0},{2,3},{3,2},{4,5},{5,4},{6,7},{7,6},{8,9},{9,8},{10,11... | collective-permute-start | bytes 393224 | tf_op jit(solution)/shard_map/ppermute | solution.py:247
  17.9 7.9 %collective-permute-start.7 = (f32[4,8,2048]{2,1,0:T(8,128)S(1)}, f32[4,8,2048]{2,1,0:T(8,128)S(1)}, u32[]{:S(2)}, u32[]{:S(2)}) collective-permute-start(f32[4,8,2048]{2,1,0:T(8,128)S(1)} %get-tuple-element.13), channel_id=1, source_target_pairs={{0,1},{1,0},{2,3},{3,2},{4,5},{5,4},{6,7},{7,6},{8,9},{9,8},{10,11... | collective-permute-start | bytes 786440 | tf_op jit(solution)/shard_map/ppermute | solution.py:247
  18.3 9.8 %collective-permute-start.13 = (f32[8,2048]{1,0:T(8,128)S(1)}, f32[8,2048]{1,0:T(8,128)S(1)}, u32[]{:S(2)}, u32[]{:S(2)}) collective-permute-start(f32[8,2048]{1,0:T(8,128)S(1)} %get-tuple-element.20), channel_id=1, source_target_pairs={{0,8},{8,16},{16,24},{24,0},{1,9},{9,17},{17,25},{25,1},{2,10},{10... | collective-permute-start | bytes 196616 | tf_op jit(solution)/shard_map/ppermute | solution.py:250
  20.0 9.3 %collective-permute-start.12 = (f32[8,2048]{1,0:T(8,128)S(1)}, f32[8,2048]{1,0:T(8,128)S(1)}, u32[]{:S(2)}, u32[]{:S(2)}) collective-permute-start(f32[8,2048]{1,0:T(8,128)S(1)} %get-tuple-element.21), channel_id=1, source_target_pairs={{0,16},{8,24},{16,0},{24,8},{1,17},{9,25},{17,1},{25,9},{2,18},{10... | collective-permute-start | bytes 196616 | tf_op jit(solution)/shard_map/ppermute | solution.py:250
  24.2 5.1 %collective-permute-start.11 = (f32[8,2048]{1,0:T(8,128)S(1)}, f32[8,2048]{1,0:T(8,128)S(1)}, u32[]{:S(2)}, u32[]{:S(2)}) collective-permute-start(f32[8,2048]{1,0:T(8,128)S(1)} %get-tuple-element.22), channel_id=1, source_target_pairs={{0,24},{8,0},{16,8},{24,16},{1,25},{9,1},{17,9},{25,17},{2,26},{10... | collective-permute-start | bytes 196616 | tf_op jit(solution)/shard_map/ppermute | solution.py:250
  25.8 4.7 %collective-permute-start.10 = (f32[8,2048]{1,0:T(8,128)S(1)}, f32[8,2048]{1,0:T(8,128)S(1)}, u32[]{:S(2)}, u32[]{:S(2)}) collective-permute-start(f32[8,2048]{1,0:T(8,128)S(1)} %get-tuple-element.17), channel_id=1, source_target_pairs={{0,2},{1,3},{2,0},{3,1},{4,6},{5,7},{6,4},{7,5},{8,10},{9,11},{10,... | collective-permute-start | bytes 196616 | tf_op jit(solution)/shard_map/ppermute | solution.py:247
  26.8 5.0 %collective-permute-start.9 = (f32[8,2048]{1,0:T(8,128)S(1)}, f32[8,2048]{1,0:T(8,128)S(1)}, u32[]{:S(2)}, u32[]{:S(2)}) collective-permute-start(f32[8,2048]{1,0:T(8,128)S(1)} %get-tuple-element.18), channel_id=1, source_target_pairs={{0,4},{1,5},{2,6},{3,7},{4,0},{5,1},{6,2},{7,3},{8,12},{9,13},{10,... | collective-permute-start | bytes 196616 | tf_op jit(solution)/shard_map/ppermute | solution.py:247
  28.0 5.2 %collective-permute-start.8 = (f32[8,2048]{1,0:T(8,128)S(1)}, f32[8,2048]{1,0:T(8,128)S(1)}, u32[]{:S(2)}, u32[]{:S(2)}) collective-permute-start(f32[8,2048]{1,0:T(8,128)S(1)} %get-tuple-element.19), channel_id=1, source_target_pairs={{0,6},{1,7},{2,4},{3,5},{4,2},{5,3},{6,0},{7,1},{8,14},{9,15},{10,... | collective-permute-start | bytes 196616 | tf_op jit(solution)/shard_map/ppermute | solution.py:247
